TPU v7x, 256 devices: a whole 4x4x8 slice. The times are simulated.
256 devices in a mesh: seq: 32 (over z, y), tp: 8 (over x, core).
Axes of the slice: x: 4, y: 4, z: 8, core: 2. Of those that a mesh axis runs over, the one named last changes fastest.
Arguments:
- inner_x: bfloat16 [8192, 8192], P('seq', 'tp'), may hold values from -6 to 6
- in_b: bfloat16 [8192, 1024], P('seq', 'tp'), may hold values from -6 to 6
- in_c: bfloat16 [8192, 1024], P('seq', 'tp'), may hold values from -6 to 6
- log_decay: float32 [128, 8192], P('tp', 'seq'), may hold values from -2 to 0
- doc_lengths: int32 [4], replicated, may hold values from 1 to 4096, 8192 in all
- out_grad: bfloat16 [8192, 8192], P('seq', 'tp'), may hold values from -0.0016937256 to 0.0016937256
- w_b: bfloat16 [8192, 1024], P(None, 'tp'), may hold values from -0.09375 to 0.09375
- w_c: bfloat16 [8192, 1024], P(None, 'tp'), may hold values from -0.0625 to 0.0625
Outputs:
- grad_x: bfloat16 [8192, 8192], P('seq', 'tp')
- grad_input: bfloat16 [8192, 8192], P('seq', 'tp')
Inputs may be any that keep to these rules, and one draw needn't show every extreme that they name: `doc_lengths`: the lengths sum to 8192; the longest is exactly half of 8192.
All inputs are finite; a program needn't handle non-finite values.
Results may differ from a plain program's by a relative error of at most 0.023.
Values may be sent and summed in bfloat16 or wider, within the bound.
No kernel may reach another device: no remote copies, remote signals or barrier semaphores. Data moves between devices by JAX's collectives and lax.ppermute only.
A program may use at most 128 MiB of HBM per device.

v0:
```python
import jax
import jax.numpy as jnp
from jax import lax
from jax.sharding import PartitionSpec as P

SPACE_HEADS = 128
HEAD_DIM = 64
STATE = 128
GROUPS = 8
SPAN = 128


def entering(x, axis, combine, identity, reverse):
    devices, index = (lax.axis_size(axis), lax.axis_index(axis))
    everything = jax.tree.map(
        lambda part, kind: lax.all_gather(part.astype(kind), axis),
        x,
        jax.tree.map(lambda a: jnp.bfloat16 if a.dtype == jnp.float32 else a.dtype, x),
    )
    start = jax.tree.map(
        lambda part, zero: jnp.broadcast_to(jnp.asarray(zero, part.dtype), part.shape), x, identity
    )

    def step(k, before):
        at = devices - 1 - k if reverse else k
        reached = at > index if reverse else at < index
        new = combine(
            before, jax.tree.map(lambda part, own: part[at].astype(own.dtype), everything, x)
        )
        return jax.tree.map(lambda a, b: jnp.where(reached, a, b), new, before)

    return lax.fori_loop(0, devices, step, start)


def doc_ids(doc_lengths, positions):
    doc_ends = jnp.cumsum(doc_lengths)[:-1]
    return jnp.sum((positions[:, None] >= doc_ends[None, :]).astype(jnp.int32), axis=1)


def span_vectors(log_part, doc_part, doc_prior):
    cumulative = jnp.cumsum(log_part, axis=-1)
    decay_enter = jnp.where(doc_part == doc_prior, jnp.exp(cumulative), 0.0)
    decay_leave = jnp.where(
        doc_part == doc_part[-1], jnp.exp(cumulative[..., -1:] - cumulative), 0.0
    )
    decay_total = jnp.where(doc_part[-1] == doc_prior, jnp.exp(cumulative[..., -1]), 0.0)
    return (decay_enter, decay_leave, decay_total)


def span_within(log_part, doc_part):
    cumulative = jnp.cumsum(log_part, axis=-1)
    span_len = doc_part.shape[0]
    row_ids = jnp.arange(span_len)
    same_doc = (doc_part[:, None] == doc_part[None, :]) & (row_ids[:, None] >= row_ids[None, :])
    log_gaps = cumulative[..., :, None] - cumulative[..., None, :]
    return jnp.where(same_doc, jnp.exp(jnp.where(same_doc, log_gaps, 0.0)), 0.0)


def weigh_rows(x_part, dy_part, decay_enter, decay_leave):
    leave_rows = jnp.transpose(decay_leave, (2, 0, 1))[..., None]
    enter_rows = jnp.transpose(decay_enter, (2, 0, 1))[..., None]
    x_weighted = (x_part.astype(jnp.float32) * leave_rows).astype(jnp.bfloat16)
    dy_weighted = (dy_part.astype(jnp.float32) * enter_rows).astype(jnp.bfloat16)
    return (x_weighted, dy_weighted)


def span_summary(x_weighted, dy_weighted, b_part, c_part):
    local_state = jnp.einsum(
        "lghp,lgn->ghpn", x_weighted, b_part, preferred_element_type=jnp.float32
    )
    local_grad = jnp.einsum(
        "lghp,lgn->ghpn", dy_weighted, c_part, preferred_element_type=jnp.float32
    )
    return (local_state, local_grad)


def span_grads(
    x_part,
    dy_part,
    b_part,
    c_part,
    x_weighted,
    dy_weighted,
    within,
    decay_leave,
    start_state,
    end_grad,
):
    pair_scores = jnp.einsum("ign,jgn->gij", c_part, b_part, preferred_element_type=jnp.float32)
    inner_dots = jnp.einsum("ighp,jghp->ghij", dy_part, x_part, preferred_element_type=jnp.float32)
    score_low = (within * pair_scores[:, None]).astype(jnp.bfloat16)
    leave_rows = jnp.transpose(decay_leave, (2, 0, 1))[..., None]
    end_low = end_grad.astype(jnp.bfloat16)
    start_low = start_state.astype(jnp.bfloat16)
    grad_x = jnp.einsum("ghij,ighp->jghp", score_low, dy_part, preferred_element_type=jnp.float32)
    grad_x = (
        grad_x
        + jnp.einsum("jgn,ghpn->jghp", b_part, end_low, preferred_element_type=jnp.float32)
        * leave_rows
    )
    mixed_low = jnp.sum(within * inner_dots, axis=1).astype(jnp.bfloat16)
    grad_c = jnp.einsum("gij,jgn->ign", mixed_low, b_part, preferred_element_type=jnp.float32)
    grad_c = grad_c + jnp.einsum(
        "ighp,ghpn->ign", dy_weighted, start_low, preferred_element_type=jnp.float32
    )
    grad_b = jnp.einsum("gij,ign->jgn", mixed_low, c_part, preferred_element_type=jnp.float32)
    grad_b = grad_b + jnp.einsum(
        "jghp,ghpn->jgn", x_weighted, end_low, preferred_element_type=jnp.float32
    )
    return (grad_x, grad_b, grad_c)


def combine(earlier_one, later_one):
    return (
        earlier_one[0] * later_one[0],
        later_one[1] + later_one[0][..., None, None] * earlier_one[1],
    )


def per_device(inner_x, in_b, in_c, log_decay, doc_lengths, out_grad, w_b, w_c):
    tok_count = inner_x.shape[0]
    group_count = in_b.shape[1] // STATE
    per_group = SPACE_HEADS // GROUPS
    span_count = tok_count // SPAN
    first_row = lax.axis_index("seq") * tok_count
    positions = first_row + jnp.arange(tok_count, dtype=jnp.int32)
    doc_local = doc_ids(doc_lengths, positions)
    doc_before = doc_ids(doc_lengths, jnp.reshape(first_row - 1, (1,)))[0]
    doc_before = jnp.where(first_row > 0, doc_before, -1)
    x_all = inner_x.reshape(tok_count, group_count, per_group, HEAD_DIM)
    dy_all = out_grad.reshape(tok_count, group_count, per_group, HEAD_DIM)
    b_all = in_b.reshape(tok_count, group_count, STATE)
    c_all = in_c.reshape(tok_count, group_count, STATE)
    log_all = log_decay.reshape(group_count, per_group, tok_count)
    vectors = []
    weighted_rows = []
    summaries = []
    for number in range(span_count):
        low = number * SPAN
        high = low + SPAN
        doc_prior = doc_before if number == 0 else doc_local[low - 1]
        span_vec = span_vectors(log_all[..., low:high], doc_local[low:high], doc_prior)
        vectors.append(span_vec)
        rows_pair = weigh_rows(x_all[low:high], dy_all[low:high], span_vec[0], span_vec[1])
        weighted_rows.append(rows_pair)
        summaries.append(span_summary(rows_pair[0], rows_pair[1], b_all[low:high], c_all[low:high]))
    forward_sum = (vectors[0][2], summaries[0][0])
    number = 1
    forward_sum = combine(forward_sum, (vectors[number][2], summaries[number][0]))
    backward_sum = (vectors[-1][2], summaries[-1][1])
    number = 0
    backward_sum = combine(backward_sum, (vectors[number][2], summaries[number][1]))
    identity = (jnp.ones_like(forward_sum[0]), jnp.zeros_like(forward_sum[1]))
    incoming = entering(forward_sum, "seq", combine, identity, False)
    outgoing = entering(backward_sum, "seq", combine, identity, True)
    start_states = [incoming[1]]
    number = 0
    start_states.append(
        vectors[number][2][..., None, None] * start_states[number] + summaries[number][0]
    )
    end_grads = [outgoing[1]]
    number = 1
    end_grads.insert(0, vectors[number][2][..., None, None] * end_grads[0] + summaries[number][1])
    x_pieces = []
    b_pieces = []
    c_pieces = []
    for number in range(span_count):
        low = number * SPAN
        high = low + SPAN
        within = span_within(log_all[..., low:high], doc_local[low:high])
        grads = span_grads(
            x_all[low:high],
            dy_all[low:high],
            b_all[low:high],
            c_all[low:high],
            weighted_rows[number][0],
            weighted_rows[number][1],
            within,
            vectors[number][1],
            start_states[number],
            end_grads[number],
        )
        x_pieces.append(grads[0].reshape(SPAN, group_count * per_group * HEAD_DIM))
        b_pieces.append(grads[1].reshape(SPAN, group_count * STATE))
        c_pieces.append(grads[2].reshape(SPAN, group_count * STATE))
    grad_x = jnp.concatenate(x_pieces, axis=0).astype(jnp.bfloat16)
    grad_b = jnp.concatenate(b_pieces, axis=0).astype(jnp.bfloat16)
    grad_c = jnp.concatenate(c_pieces, axis=0).astype(jnp.bfloat16)
    partial_value = lax.dot_general(
        grad_b, w_b, (((1,), (1,)), ((), ())), preferred_element_type=jnp.float32
    )
    partial_value = partial_value + lax.dot_general(
        grad_c, w_c, (((1,), (1,)), ((), ())), preferred_element_type=jnp.float32
    )
    grad_input = lax.psum_scatter(
        partial_value.astype(jnp.bfloat16), "tp", scatter_dimension=1, tiled=True
    )
    return (grad_x, grad_input)


def solution(mesh):
    placed = (
        P("seq", "tp"),
        P("seq", "tp"),
        P("seq", "tp"),
        P("tp", "seq"),
        P(),
        P("seq", "tp"),
        P(None, "tp"),
        P(None, "tp"),
    )
    return jax.shard_map(
        per_device,
        mesh=mesh,
        in_specs=placed,
        out_specs=(P("seq", "tp"), P("seq", "tp")),
        check_vma=False,
    )
```

profile of v0, /device:TPU:1, one launch (start us, length us, event | category | flops | bytes accessed | tf_op | source)
XLA Modules:
  0.0 330.3 jit_solution(12250906708368210000)
XLA Ops:
  11.4 1.2 broadcast_compare_fusion.1
  14.3 1.1 fusion.93
  24.9 1.3 copy.57
  26.2 39.6 %all-gather.1 = bf16[32,16,1]{1,2,0:T(2,128)(2,1)} all-gather(bf16[1,16,1]{1,2,0:T(2,128)(2,1)} %copy.57), channel_id=3, replica_groups=mesh['seq'=32,'tp'=8] {'seq'}, dimensions={0}, use_global_device_ids=true | all-gather | bytes 1056 | tf_op jit(solution)/shard_map/all_gather | solution.py:16
  65.8 1.4 copy.58
  67.2 1.4 copy.60
  70.0 2.2 fusion.4
  72.2 2.2 fusion.3
  74.4 47.6 %all-gather.8.cloned.1.call-done = bf16[512,64,128]{2,1,0:T(8,128)(2,1)} async-done(((bf16[16,64,128]{2,1,0:T(8,128)(2,1)}), bf16[512,64,128]{2,1,0:T(8,128)(2,1)}) %all-gather.8.cloned.1.call-update) | async-done | bytes 8388624 | tf_op jit(solution)/shard_map/all_gather | solution.py:16
  122.0 56.3 %while.31 = (s32[]{:T(128)}, f32[1,16,64,128]{3,2,1,0:T(8,128)S(1)}, s32[]{:T(128)}, bf16[32,1,16,64,128]{4,3,2,1,0:T(8,128)(2,1)}, bf16[32,1,16]{2,1,0:T(2,128)(2,1)}, /*index=5*/s32[]{:T(128)}, s32[]{:T(128)}) while((s32[]{:T(128)}, f32[1,16,64,128]{3,2,1,0:T(8,128)S(1)}, s32[]{:T(128)}, ...), condition=%wide.region_10.11_spmd.clone, body=%wide.region_9.10_spmd.clone.sunk | while | flops 655380 | bytes 1310993 | solution.py:32
  122.6 1.1 fusion.123
  124.4 1.1 fusion.123
  126.1 1.1 fusion.123
  127.9 1.1 fusion.123
  129.7 1.1 fusion.123
  131.5 1.1 fusion.123
  133.2 1.1 fusion.123
  135.0 1.1 fusion.123
  136.8 1.1 fusion.123
  138.5 1.1 fusion.123
  140.2 1.1 fusion.123
  142.0 1.1 fusion.123
  143.8 1.1 fusion.123
  145.5 1.1 fusion.123
  147.3 1.1 fusion.123
  149.1 1.1 fusion.123
  150.9 1.1 fusion.123
  152.7 1.1 fusion.123
  154.4 1.1 fusion.123
  156.2 1.1 fusion.123
  157.9 1.1 fusion.123
  159.7 1.1 fusion.123
  161.4 1.1 fusion.123
  163.2 1.1 fusion.123
  164.9 1.1 fusion.123
  166.7 1.1 fusion.123
  173.7 1.1 fusion.123
  178.3 1.9 convolution_bitcast_fusion.9
  180.2 2.0 convolution_bitcast_fusion.8
  182.2 38.1 %all-gather.6.cloned.1.call-done = bf16[512,64,128]{2,1,0:T(8,128)(2,1)} async-done(((bf16[16,64,128]{2,1,0:T(8,128)(2,1)}), bf16[512,64,128]{2,1,0:T(8,128)(2,1)}) %all-gather.6.cloned.1.call-update) | async-done | bytes 8388624 | tf_op jit(solution)/shard_map/all_gather | solution.py:16
  220.2 56.4 %while.30 = (s32[]{:T(128)}, f32[1,16,64,128]{3,2,1,0:T(8,128)S(1)}, s32[]{:T(128)}, bf16[32,1,16,64,128]{4,3,2,1,0:T(8,128)(2,1)}, bf16[32,1,16]{2,1,0:T(2,128)...) while((s32[]{:T(128)}, f32[1,16,64,128]{3,2,1,0:T(8,128)S(1)}, s32[]{:T(128)}, ...), condition=%wide.region_6.7_spmd.clone, body=%wide.region_5.6_spmd.clone.sunk | while | flops 655384 | bytes 1311055 | solution.py:32
  277.4 1.2 convolution_bitcast_fusion.10
  278.7 1.2 convolution_bitcast_fusion.11
  283.8 1.3 fusion.51
  285.4 3.2 fusion.2
  290.6 1.3 fusion.9
  292.9 1.3 fusion.10
  295.2 28.6 %reduce-scatter.2.cloned.1.call-done = bf16[256,1024]{1,0:T(8,128)(2,1)} async-done(((bf16[256,8192]{1,0:T(8,128)(2,1)}), bf16[256,1024]{1,0:T(8,128)(2,1)}) %reduce-scatter.2.cloned.1.call-update) | async-done | bytes 524304 | tf_op jit(solution)/shard_map/reduce_scatter | solution.py:195
  (198 shorter events, 104.4 us)
Async XLA Ops:
  7.2 276.6 %copy-start = (bf16[8192,128]{1,0:T(8,128)(2,1)S(1)}, bf16[8192,128]{1,0:T(8,128)(2,1)}, u32[]{:S(2)}) copy-start(bf16[8192,128]{1,0:T(8,128)(2,1)} %param.18) | copy-start | bytes 6291460
  7.2 11.8 %copy-start.8 = (bf16[256,128]{1,0:T(8,128)(2,1)S(1)}, bf16[256,128]{1,0:T(8,128)(2,1)}, u32[]{:S(2)}) copy-start(bf16[256,128]{1,0:T(8,128)(2,1)} %param.13) | copy-start | bytes 196612
  7.2 114.8 %all-gather.8.cloned.1.call-start = ((), (), s32[]{:S(2)}) async-start(), calls=%async_computation.3 | async-start | bytes 8650752 | tf_op jit(solution)/shard_map/all_gather | solution.py:16
  8.9 6.4 %copy-start.21 = (s32[256]{0:T(256)}, s32[256]{0:T(256)S(1)}, u32[]{:S(2)}) copy-start(s32[256]{0:T(256)S(1)} %convert_reduce_fusion) | copy-start | bytes 3076
  14.3 7.9 %copy-start.15 = (bf16[256,128]{1,0:T(8,128)(2,1)S(1)}, bf16[256,128]{1,0:T(8,128)(2,1)}, u32[]{:S(2)}) copy-start(bf16[256,128]{1,0:T(8,128)(2,1)} %param.14) | copy-start | bytes 196612
  15.6 6.2 %copy-start.13 = (bf16[128,1024]{0,1:T(8,128)(2,1)}, bf16[128,1024]{0,1:T(8,128)(2,1)S(1)}, u32[]{:S(2)}) copy-start(bf16[128,1024]{0,1:T(8,128)(2,1)S(1)} %copy.69) | copy-start | bytes 786436
  15.7 5.8 %copy-start.14 = (bf16[128,1024]{0,1:T(8,128)(2,1)}, bf16[128,1024]{0,1:T(8,128)(2,1)S(1)}, u32[]{:S(2)}) copy-start(bf16[128,1024]{0,1:T(8,128)(2,1)S(1)} %copy.70) | copy-start | bytes 786436
  15.8 8.3 %copy-start.23 = (f32[16]{0:T(128)}, f32[16]{0:T(128)S(1)}, u32[]{:S(2)}) copy-start(f32[16]{0:T(128)S(1)} %broadcast_select_fusion.1) | copy-start | bytes 196
  15.9 0.6 copy-start.16
  15.9 4.1 %copy-start.17 = (f32[128,16]{0,1:T(8,128)}, f32[128,16]{0,1:T(8,128)S(1)}, u32[]{:S(2)}) copy-start(f32[128,16]{0,1:T(8,128)S(1)} %get-tuple-element.346) | copy-start | bytes 24580
  15.9 2.2 copy-start.5
  16.5 0.7 copy-start.4
  18.1 0.8 copy-start.3
  19.9 200.3 %all-gather.6.cloned.1.call-start = ((), (), s32[]{:S(2)}) async-start(), calls=%async_computation.2 | async-start | bytes 8650752 | tf_op jit(solution)/shard_map/all_gather | solution.py:16
  21.8 2.4 copy-start.11
  21.9 2.2 copy-start.9
  22.1 0.7 copy-start.6
  22.1 2.1 copy-start.22
  22.3 0.8 copy-start.1
  24.1 299.6 %reduce-scatter.2.cloned.1.call-start = ((), (), s32[]{:S(2)}) async-start(), calls=%async_computation.1 | async-start | bytes 4718592 | tf_op jit(solution)/shard_map/reduce_scatter | solution.py:195
  69.4 0.6 copy-start.20
  69.5 2.8 copy-start.19
  182.2 94.5 %copy-start.2 = (f32[16,64,128]{2,1,0:T(8,128)S(1)}, f32[16,64,128]{2,1,0:T(8,128)}, u32[]{:S(2)}) copy-start(f32[16,64,128]{2,1,0:T(8,128)} %copy-done.1) | copy-start | bytes 1572868
  283.8 1.6 copy-start.7
  288.6 1.9 copy-start.12
  288.6 4.3 %copy-start.10 = (bf16[128,1024]{0,1:T(8,128)(2,1)S(1)}, bf16[128,1024]{0,1:T(8,128)(2,1)}, u32[]{:S(2)}) copy-start(bf16[128,1024]{0,1:T(8,128)(2,1)} %copy-done.9) | copy-start | bytes 786436
  289.6 3.3 %copy-start.18 = (f32[128,128]{1,0:T(8,128)S(1)}, f32[128,128]{1,0:T(8,128)}, u32[]{:S(2)}) copy-start(f32[128,128]{1,0:T(8,128)} %fusion.74) | copy-start | bytes 196612
Sparse Core Ops, SparseCore 0:
  20.0 101.9 all-gather.7
  124.6 95.5 all-gather.5
  288.8 34.9 reduce-scatter.1
where the time goes:
time: 336 us; the launch traced here: 330 us
  other arithmetic  117 us (35%)
  waiting for transfers between devices  114 us (34%)
  blocking collectives  39.6 us (12%)
  matrix products  27.4 us (8%)
  between operations  16.7 us (5%)
  local copies, waits for them, and re-layouts  13.3 us (4%)
    all_gather x2, waiting for transfers between devices, entering(): lax.all_gather(part.astype(kind), axis)  85.7 us
    select_n x64, other arithmetic, step(): return jax.tree.map(lambda a, b: jnp.where(reached, a, b), new, before)  69.7 us
    convert_element_type x64, other arithmetic, step(): part[at].astype(own.dtype)  41.2 us
    all_gather x1, blocking collectives, entering(): lax.all_gather(part.astype(kind), axis)  39.6 us
    reduce_scatter x1, waiting for transfers between devices, per_device(): lax.psum_scatter(partial_value.astype(jnp.bfloat16), 'tp', scatter_dimens...  28.6 us
  transfers between devices with their start and end apart: 3, of which 3 were waited for; matrix products, arithmetic and copies ran while one was open for 24% of the time, Pallas kernels for 0%

commit v1 on v0

v1 whole, which is shorter than its diff:
```python
import functools

import jax
import jax.numpy as jnp
from jax import lax
from jax.experimental import pallas as pl
from jax.experimental.pallas import tpu as pltpu
from jax.sharding import PartitionSpec as P

HEAD_DIM = 64
STATE = 128
SPAN = 128
HEADS = 16
LANES = 128
WIDE = HEADS * HEAD_DIM
PAIRS = WIDE // LANES
LOW = jnp.bfloat16
FULL = jnp.float32
NN = (((1,), (0,)), ((), ()))
NT = (((1,), (1,)), ((), ()))
TN = (((0,), (0,)), ((), ()))
VMEM_BYTES = 48 * 1024 * 1024


def mul(a, b, dims=NN):
    return lax.dot_general(a, b, dims, preferred_element_type=FULL)


def iota(shape, axis):
    return lax.broadcasted_iota(jnp.int32, shape, axis)


def doc_of(positions, ends):
    return sum((positions >= end).astype(jnp.int32) for end in ends)


def doc_ends(lengths_ref):
    first = lengths_ref[0]
    second = first + lengths_ref[1]
    return (first, second, second + lengths_ref[2])


def token_vectors(log_ref, lengths_ref):
    tokens = log_ref.shape[1]
    first_row = lax.axis_index("seq") * tokens
    ends = doc_ends(lengths_ref)
    upper = (iota((tokens, tokens), 0) <= iota((tokens, tokens), 1)).astype(FULL)
    cumulative = lax.dot_general(
        log_ref[...], upper, NN, precision=lax.Precision.HIGHEST, preferred_element_type=FULL
    )
    docs = doc_of(first_row + iota((HEADS, tokens), 1), ends)
    prior = jnp.where(first_row > 0, doc_of(first_row - 1, ends), -1)
    last = doc_of(first_row + tokens - 1, ends)
    cum_last = cumulative[:, tokens - 1 :]
    enter = jnp.where(docs == prior, jnp.exp(cumulative), 0.0)
    leave = jnp.where(docs == last, jnp.exp(cum_last - cumulative), 0.0)
    total = jnp.where(last == prior, jnp.exp(cum_last), 0.0)
    return first_row, ends, cumulative, docs, enter, leave, total


def split_columns(rows):
    high = rows.astype(LOW).astype(FULL)
    both = jnp.concatenate([high, rows - high], axis=0)
    return both.T.astype(LOW)


def spread(columns, low, width):
    head = (low + iota((2 * HEADS, width), 1)) // HEAD_DIM
    pick = (head == iota((2 * HEADS, width), 0) % HEADS).astype(FULL).astype(LOW)
    return mul(columns, pick)


def summary_kernel(lengths_ref, x_ref, dy_ref, b_ref, c_ref, log_ref, out_ref):
    slices = out_ref.shape[0]
    rows = WIDE // slices
    _, _, _, _, enter, leave, total = token_vectors(log_ref, lengths_ref)
    enter_cols = split_columns(enter)
    leave_cols = split_columns(leave)
    b, c = b_ref[...], c_ref[...]
    width = 2 * LANES
    for chunk in range(WIDE // width):
        low = chunk * width
        span = slice(low, low + width)
        at = slice(low // rows, (low + width) // rows)
        weighted = (x_ref[:, span].astype(FULL) * spread(leave_cols, low, width)).astype(LOW)
        out_ref[at, 0:rows, :] = mul(weighted, b, TN).astype(LOW).reshape(width // rows, rows, STATE)
        weighted = (dy_ref[:, span].astype(FULL) * spread(enter_cols, low, width)).astype(LOW)
        out_ref[at, rows : 2 * rows, :] = (
            mul(weighted, c, TN).astype(LOW).reshape(width // rows, rows, STATE)
        )
    total = jnp.broadcast_to(total, (HEADS, STATE))
    high = total.astype(LOW).astype(FULL)
    per_head = slices // HEADS
    for head in range(HEADS):
        rest = jnp.broadcast_to((total - high)[head : head + 1], (8, STATE))
        tile = jnp.where(iota((8, STATE), 0) == 0, high[head : head + 1], rest).astype(LOW)
        for part in range(per_head):
            out_ref[head * per_head + part, 2 * rows : 2 * rows + 8, :] = tile


def scan_kernel(in_ref, out_ref):
    devices, rows = out_ref.shape[0], out_ref.shape[1] // 2
    decays = []
    for at in range(devices):
        pair = in_ref[at, 2 * rows : 2 * rows + 8, :].astype(FULL)
        decays.append(pair[0:1] + pair[1:2])
    state = jnp.zeros((rows, STATE), FULL)
    for at in range(devices):
        out_ref[at, 0:rows, :] = state.astype(LOW)
        state = decays[at] * state + in_ref[at, 0:rows, :].astype(FULL)
    state = jnp.zeros((rows, STATE), FULL)
    for at in reversed(range(devices)):
        out_ref[at, rows : 2 * rows, :] = state.astype(LOW)
        state = decays[at] * state + in_ref[at, rows : 2 * rows, :].astype(FULL)


def grads_kernel(
    lengths_ref, x_ref, dy_ref, b_ref, c_ref, log_ref, edge_ref, grad_x_ref, grad_bc_ref
):
    slices, rows = edge_ref.shape[0], edge_ref.shape[1] // 2
    first_row, ends, cumulative, docs, enter, leave, _ = token_vectors(log_ref, lengths_ref)
    cum_cols = cumulative.T
    enter_cols, leave_cols = split_columns(enter), split_columns(leave)
    middle = doc_of(first_row + SPAN - 1, ends)
    cum_middle = cumulative[:, SPAN - 1 : SPAN]
    leave_first = jnp.where(
        docs[:, :SPAN] == middle, jnp.exp(cum_middle - cumulative[:, :SPAN]), 0.0
    )
    enter_second = jnp.where(
        docs[:, SPAN:] == middle, jnp.exp(cumulative[:, SPAN:] - cum_middle), 0.0
    )
    leave_first, enter_second = split_columns(leave_first), split_columns(enter_second)
    b, c = b_ref[...], c_ref[...]
    scores = mul(b, c, NT)
    cross_scores = scores[:SPAN, SPAN:].astype(LOW)
    is_left = iota((SPAN, LANES), 1) < HEAD_DIM
    masks = []
    for number in range(2):
        base = first_row + number * SPAN
        same = doc_of(base + iota((SPAN, SPAN), 0), ends) == doc_of(
            base + iota((SPAN, SPAN), 1), ends
        )
        masks.append(same & (iota((SPAN, SPAN), 0) <= iota((SPAN, SPAN), 1)))

    def halves(value):
        zero = jnp.zeros_like(value)
        return jnp.concatenate(
            [jnp.where(is_left, value, zero), jnp.where(is_left, zero, value)], axis=0
        )

    mixed = [jnp.zeros((SPAN, SPAN), FULL), jnp.zeros((SPAN, SPAN), FULL)]
    mixed_cross = jnp.zeros((SPAN, SPAN), FULL)
    grad_b = jnp.zeros((2 * SPAN, STATE), FULL)
    grad_c = jnp.zeros((2 * SPAN, STATE), FULL)
    for pair in range(PAIRS):
        low = pair * LANES
        x, dy = x_ref[:, low : low + LANES], dy_ref[:, low : low + LANES]
        at = slice(low // rows, (low + LANES) // rows)
        start = edge_ref[at, 0:rows, :].reshape(LANES, STATE)
        end = edge_ref[at, rows : 2 * rows, :].reshape(LANES, STATE)
        leave_wide = spread(leave_cols, low, LANES)
        weighted = (x.astype(FULL) * leave_wide).astype(LOW)
        grad_b += mul(weighted, end)
        weighted = (dy.astype(FULL) * spread(enter_cols, low, LANES)).astype(LOW)
        grad_c += mul(weighted, start)
        grad_x = leave_wide * mul(b, end, NT)
        first_wide = spread(leave_first, low, LANES)
        x_first = (x[:SPAN].astype(FULL) * first_wide).astype(LOW)
        dy_second = (dy[SPAN:].astype(FULL) * spread(enter_second, low, LANES)).astype(LOW)
        mixed_cross += mul(x_first, dy_second, NT)
        pieces = [first_wide * mul(cross_scores, dy_second), 0.0]
        for number in range(2):
            span = slice(number * SPAN, (number + 1) * SPAN)
            inner = mul(halves(x[span]), dy[span], NT)
            low_scores = []
            for side in range(2):
                head = 2 * pair + side
                gaps = cumulative[head : head + 1, span] - cum_cols[span, head : head + 1]
                within = jnp.exp(jnp.where(masks[number], gaps, -1e30))
                mixed[number] += within * inner[side * SPAN : (side + 1) * SPAN]
                low_scores.append((within * scores[span, span]).astype(LOW))
            pieces[number] += mul(jnp.concatenate(low_scores, axis=1), halves(dy[span]))
            grad_x_ref[span, low : low + LANES] = (grad_x[span] + pieces[number]).astype(LOW)
    nothing = jnp.zeros((SPAN, SPAN), FULL)
    table = jnp.concatenate(
        [
            jnp.concatenate([mixed[0], mixed_cross], axis=1),
            jnp.concatenate([nothing, mixed[1]], axis=1),
        ],
        axis=0,
    )
    grad_bc_ref[:, :STATE] = (grad_b + mul(table.astype(LOW), c)).astype(LOW)
    grad_bc_ref[:, STATE:] = (grad_c + mul(table.T.astype(LOW), b)).astype(LOW)


def call(body, out_shape, specs, flops, moved):
    return pl.pallas_call(
        body,
        out_shape=out_shape,
        in_specs=specs,
        out_specs=jax.tree.map(lambda _: pl.BlockSpec(memory_space=pltpu.VMEM), out_shape),
        compiler_params=pltpu.CompilerParams(vmem_limit_bytes=VMEM_BYTES),
        cost_estimate=pl.CostEstimate(flops=flops, bytes_accessed=moved, transcendentals=0),
    )


def per_device(inner_x, in_b, in_c, log_decay, doc_lengths, out_grad, w_b, w_c):
    tokens = inner_x.shape[0]
    devices = lax.axis_size("seq")
    rows = WIDE // devices
    small = pl.BlockSpec(memory_space=pltpu.SMEM)
    block = pl.BlockSpec(memory_space=pltpu.VMEM)
    local = (doc_lengths, inner_x, out_grad, in_b, in_c, log_decay)
    summary = call(
        summary_kernel,
        jax.ShapeDtypeStruct((devices, 2 * rows + 8, STATE), LOW),
        [small] + [block] * 5,
        2 * 10**8,
        2 * 10**6,
    )(*local)
    summary = lax.all_to_all(summary, "seq", 0, 0)
    edges = call(
        scan_kernel,
        jax.ShapeDtypeStruct((devices, 2 * rows, STATE), LOW),
        [block],
        10**6,
        10**6,
    )(summary)
    edges = lax.all_to_all(edges, "seq", 0, 0)
    grad_x, grad_bc = call(
        grads_kernel,
        (
            jax.ShapeDtypeStruct((tokens, WIDE), LOW),
            jax.ShapeDtypeStruct((tokens, 2 * STATE), LOW),
        ),
        [small] + [block] * 6,
        4 * 10**8,
        3 * 10**6,
    )(*local, edges)
    partial_value = lax.dot_general(grad_bc[:, :STATE], w_b, NT, preferred_element_type=FULL)
    partial_value = partial_value + lax.dot_general(
        grad_bc[:, STATE:], w_c, NT, preferred_element_type=FULL
    )
    grad_input = lax.psum_scatter(
        partial_value.astype(LOW), "tp", scatter_dimension=1, tiled=True
    )
    return grad_x, grad_input


def solution(mesh):
    placed = (
        P("seq", "tp"),
        P("seq", "tp"),
        P("seq", "tp"),
        P("tp", "seq"),
        P(),
        P("seq", "tp"),
        P(None, "tp"),
        P(None, "tp"),
    )
    return jax.shard_map(
        per_device,
        mesh=mesh,
        in_specs=placed,
        out_specs=(P("seq", "tp"), P("seq", "tp")),
        check_vma=False,
    )
```

time: 336 us -> 121 us (0.36)
  the two profiles are of different devices: /device:TPU:1 before, /device:TPU:8 now
where the time goes in v1:
time: 121 us
  blocking collectives  51.2 us (42%)
  waiting for transfers between devices  37.4 us (31%)
  between operations  14.1 us (12%)
  Pallas kernels  7.83 us (6%)
  local copies, waits for them, and re-layouts  5.63 us (5%)
  matrix products  4.46 us (4%)
    reduce_scatter x1, waiting for transfers between devices, per_device(): lax.psum_scatter(partial_value.astype(LOW), 'tp', scatter_dimension=1, ti...  37.4 us
    all_to_all x1, blocking collectives, per_device(): summary = lax.all_to_all(summary, 'seq', 0, 0)  29.9 us
    all_to_all x1, blocking collectives, per_device(): edges = lax.all_to_all(edges, 'seq', 0, 0)  21.3 us
    unnamed x24, local copies, waits for them, and re-layouts  5.63 us
    pallas_call x1, Pallas kernels, per_device(): call(grads_kernel, (jax.ShapeDtypeStruct((tokens, WIDE), LOW), jax.ShapeD...  5.41 us
    dot_general x1, matrix products, per_device(): lax.dot_general(grad_bc[:, STATE:], w_c, NT, preferred_element_type=FULL)  3.2 us
  transfers between devices with their start and end apart: 1, of which 1 were waited for; matrix products, arithmetic and copies ran while one was open for 0% of the time, Pallas kernels for 0%

profile of v1, /device:TPU:8, one launch (start us, length us, event | category | flops | bytes accessed | tf_op | source)
XLA Modules:
  0.0 120.7 jit_solution(2311777133435733743)
XLA Ops:
  7.2 0.0 copy-start
  7.2 0.0 reduce-scatter.2.cloned.1.call-start
  7.2 0.0 copy-start.1
  7.2 1.2 copy-done.1
  8.4 0.0 copy-start.3
  8.4 1.0 copy-done.3
  9.5 0.0 copy-start.5
  9.5 0.8 copy-done.5
  10.3 0.0 copy-start.7
  10.3 0.8 copy-done.7
  11.1 0.0 copy-start.8
  11.1 0.7 copy-done.8
  11.8 0.0 copy-start.9
  11.9 0.7 copy-done.9
  12.5 2.3 %shard_map.95 = bf16[32,72,128]{2,1,0:T(8,128)(2,1)S(1)} custom-call(s32[4]{0:T(128)S(1)} %copy-done.9, bf16[256,1024]{1,0:T(8,128)(2,1)S(1)} %copy-done.1, bf16[256,1024]{1,0:T(8,128)(2,1)S(1)} %copy-done.3, bf16[256,128]{1,0:T(8,128)(2,1)S(1)} %copy-done.5, bf16[256,128]{1,0:T(8,128)(2,1)S(1)} %copy-done.7, f32[16,256]{1,0:T(8,128)S(1)} %copy-done.8), custom_call_target="tpu_custom_call" | custom-call | flops 200000000 | bytes 2000000 | tf_op jit(solution)/shard_map/pallas_call | solution.py:214
  14.8 0.0 copy-start.2
  14.8 0.0 copy-start.4
  14.8 0.0 copy-start.6
  14.8 0.0 copy-start.10
  14.8 29.9 %all_to_all.10.in_ref = bf16[32,72,128]{2,1,0:T(8,128)(2,1)S(1)} all-to-all(bf16[32,72,128]{2,1,0:T(8,128)(2,1)S(1)} %shard_map.95), channel_id=1, replica_groups=mesh['seq'=32,'tp'=8] {'seq'}, dimensions={0} | all-to-all | bytes 1179648 | tf_op jit(solution)/shard_map/all_to_all | solution.py:221
  44.7 0.1 shard_map.96
  44.9 21.3 %all_to_all.11.edge_ref = bf16[32,64,128]{2,1,0:T(8,128)(2,1)S(1)} all-to-all(bf16[32,64,128]{2,1,0:T(8,128)(2,1)S(1)} %shard_map.96), channel_id=1, replica_groups=mesh['seq'=32,'tp'=8] {'seq'}, dimensions={0} | all-to-all | bytes 1048576 | tf_op jit(solution)/shard_map/all_to_all | solution.py:229
  66.2 0.0 copy-done.2
  66.2 0.0 copy-done.4
  66.2 0.0 copy-done.6
  66.2 0.0 copy-done.10
  66.2 5.4 %shard_map.97 = (bf16[256,1024]{1,0:T(8,128)(2,1)}, bf16[256,256]{1,0:T(8,128)(2,1)S(1)}) custom-call(s32[4]{0:T(128)S(1)} %copy-done.10, bf16[256,1024]{1,0:T(8,128)(2,1)S(1)} %copy-done.2, bf16[256,1024]{1,0:T(8,128)(2,1)S(1)} %copy-done.4, bf16[256,128]{1,0:T(8,128)(2,1)S(1)} %copy-done.6, bf16[256,128]{1,0:T(8,128)(2,1)S(1)} %copy-done.7, ...), custom_call_target="tpu_custom_call" | custom-call | flops 400000000 | bytes 3000000 | tf_op jit(solution)/shard_map/pallas_call | solution.py:230
  71.6 0.0 copy-done
  71.6 0.0 copy-start.11
  71.6 1.3 %fusion.2 = f32[256,8192]{1,0:T(8,128)S(1)} fusion(bf16[8192,128]{1,0:T(8,128)(2,1)S(1)} %copy-done, bf16[256,256]{1,0:T(8,128)(2,1)S(1)} %get-tuple-element.5), kind=kOutput, calls=%fused_computation.3 | convolution fusion | flops 536870912 | bytes 10551296 | tf_op jit(solution)/shard_map/dot_general | solution.py:240
  72.9 0.3 copy-done.11
  73.2 3.2 %fusion = bf16[256,8192]{1,0:T(8,128)(2,1)} fusion(f32[256,8192]{1,0:T(8,128)S(1)} %fusion.2, bf16[8192,128]{1,0:T(8,128)(2,1)S(1)} %copy-done.11, bf16[256,256]{1,0:T(8,128)(2,1)S(1)} %get-tuple-element.5), kind=kOutput, calls=%fused_computation.1 | convolution fusion | flops 541065216 | bytes 14745600 | tf_op jit(solution)/shard_map/dot_general | solution.py:241
  76.4 0.0 reduce-scatter.2.cloned.1.call-update
  76.4 37.4 %reduce-scatter.2.cloned.1.call-done = bf16[256,1024]{1,0:T(8,128)(2,1)} async-done(((bf16[256,8192]{1,0:T(8,128)(2,1)}), bf16[256,1024]{1,0:T(8,128)(2,1)}) %reduce-scatter.2.cloned.1.call-update) | async-done | bytes 524304 | tf_op jit(solution)/shard_map/reduce_scatter | solution.py:244
Async XLA Ops:
  7.2 64.5 %copy-start = (bf16[8192,128]{1,0:T(8,128)(2,1)S(1)}, bf16[8192,128]{1,0:T(8,128)(2,1)}, u32[]{:S(2)}) copy-start(bf16[8192,128]{1,0:T(8,128)(2,1)} %param.14) | copy-start | bytes 6291460
  7.2 106.7 %reduce-scatter.2.cloned.1.call-start = ((), (), s32[]{:S(2)}) async-start(), calls=%async_computation.3 | async-start | bytes 4718592 | tf_op jit(solution)/shard_map/reduce_scatter | solution.py:244
  7.2 1.2 copy-start.1
  8.4 1.0 copy-start.3
  9.5 0.8 copy-start.5
  10.3 0.8 copy-start.7
  11.1 0.7 copy-start.8
  11.8 0.7 copy-start.9
  14.8 51.4 %copy-start.2 = (bf16[256,1024]{1,0:T(8,128)(2,1)S(1)}, bf16[256,1024]{1,0:T(8,128)(2,1)}, u32[]{:S(2)}) copy-start(bf16[256,1024]{1,0:T(8,128)(2,1)} %x_ref.3) | copy-start | bytes 1572868
  14.8 51.4 %copy-start.4 = (bf16[256,1024]{1,0:T(8,128)(2,1)S(1)}, bf16[256,1024]{1,0:T(8,128)(2,1)}, u32[]{:S(2)}) copy-start(bf16[256,1024]{1,0:T(8,128)(2,1)} %dy_ref.3) | copy-start | bytes 1572868
  14.8 51.4 %copy-start.6 = (bf16[256,128]{1,0:T(8,128)(2,1)S(1)}, bf16[256,128]{1,0:T(8,128)(2,1)}, u32[]{:S(2)}) copy-start(bf16[256,128]{1,0:T(8,128)(2,1)} %b_ref.3) | copy-start | bytes 196612
  14.8 51.4 %copy-start.10 = (s32[4]{0:T(128)S(1)}, s32[4]{0:T(128)}, u32[]{:S(2)}) copy-start(s32[4]{0:T(128)} %lengths_ref.3) | copy-start | bytes 52
  71.6 1.6 %copy-start.11 = (bf16[8192,128]{1,0:T(8,128)(2,1)S(1)}, bf16[8192,128]{1,0:T(8,128)(2,1)}, u32[]{:S(2)}) copy-start(bf16[8192,128]{1,0:T(8,128)(2,1)} %param.15) | copy-start | bytes 6291460
Sparse Core Ops, SparseCore 0:
  76.6 37.2 reduce-scatter.1

commit v2 on v1

--- a/solution.py
+++ b/solution.py
@@ -14,12 +14,14 @@
 LANES = 128
 WIDE = HEADS * HEAD_DIM
 PAIRS = WIDE // LANES
+CORES = 2
 LOW = jnp.bfloat16
 FULL = jnp.float32
 NN = (((1,), (0,)), ((), ()))
 NT = (((1,), (1,)), ((), ()))
 TN = (((0,), (0,)), ((), ()))
-VMEM_BYTES = 48 * 1024 * 1024
+MIB = 1024 * 1024
+LARGE_VMEM = 56 * MIB
 
 
 def mul(a, b, dims=NN):
@@ -70,24 +72,75 @@
     return mul(columns, pick)
 
 
-def summary_kernel(lengths_ref, x_ref, dy_ref, b_ref, c_ref, log_ref, out_ref):
+def fetch(pairs, sems):
+    copies = [
+        pltpu.make_async_copy(source, target, sems.at[at])
+        for at, (source, target) in enumerate(pairs)
+    ]
+    for copy in copies:
+        copy.start()
+    return copies
+
+
+def summary_kernel(
+    lengths_hbm,
+    log_hbm,
+    x_hbm,
+    b_hbm,
+    dy_hbm,
+    c_hbm,
+    w_b_hbm,
+    w_c_hbm,
+    out_ref,
+    *refs,
+):
+    sent_refs = refs[:-8]
+    lengths_ref, log_ref, x_ref, b_ref, dy_ref, c_ref, sems, sent_sems = refs[-8:]
+    loads = fetch(
+        [
+            (lengths_hbm, lengths_ref),
+            (log_hbm, log_ref),
+            (x_hbm, x_ref),
+            (b_hbm, b_ref),
+            (dy_hbm, dy_ref),
+            (c_hbm, c_ref),
+        ],
+        sems,
+    )
+    columns = sent_refs[0].shape[0]
+    steps = len(sent_refs) // CORES
+    me = lax.axis_index("tp")
+    core = lax.rem(me, CORES)
+    pairs = []
+    for at, sent_ref in enumerate(sent_refs):
+        half = 1 - core if at < steps else core
+        target = lax.rem(me // CORES + at % steps + 1, steps + 1)
+        from_row = pl.ds(pl.multiple_of((target * CORES + half) * columns, columns), columns)
+        pairs.append((w_b_hbm.at[from_row, :], sent_ref.at[:, pl.ds(0, STATE)]))
+        pairs.append((w_c_hbm.at[from_row, :], sent_ref.at[:, pl.ds(STATE, STATE)]))
+    sends = fetch(pairs, sent_sems)
     slices = out_ref.shape[0]
     rows = WIDE // slices
+    loads[0].wait()
+    loads[1].wait()
     _, _, _, _, enter, leave, total = token_vectors(log_ref, lengths_ref)
     enter_cols = split_columns(enter)
     leave_cols = split_columns(leave)
-    b, c = b_ref[...], c_ref[...]
     width = 2 * LANES
-    for chunk in range(WIDE // width):
-        low = chunk * width
-        span = slice(low, low + width)
-        at = slice(low // rows, (low + width) // rows)
-        weighted = (x_ref[:, span].astype(FULL) * spread(leave_cols, low, width)).astype(LOW)
-        out_ref[at, 0:rows, :] = mul(weighted, b, TN).astype(LOW).reshape(width // rows, rows, STATE)
-        weighted = (dy_ref[:, span].astype(FULL) * spread(enter_cols, low, width)).astype(LOW)
-        out_ref[at, rows : 2 * rows, :] = (
-            mul(weighted, c, TN).astype(LOW).reshape(width // rows, rows, STATE)
-        )
+    for side, (wide_ref, narrow_ref, cols) in enumerate(
+        ((x_ref, b_ref, leave_cols), (dy_ref, c_ref, enter_cols))
+    ):
+        loads[2 + 2 * side].wait()
+        loads[3 + 2 * side].wait()
+        narrow = narrow_ref[...]
+        for chunk in range(WIDE // width):
+            low = chunk * width
+            at = slice(low // rows, (low + width) // rows)
+            weighted = wide_ref[:, low : low + width].astype(FULL) * spread(cols, low, width)
+            product = mul(weighted.astype(LOW), narrow, TN).astype(LOW)
+            out_ref[at, side * rows : (side + 1) * rows, :] = product.reshape(
+                width // rows, rows, STATE
+            )
     total = jnp.broadcast_to(total, (HEADS, STATE))
     high = total.astype(LOW).astype(FULL)
     per_head = slices // HEADS
@@ -96,9 +149,12 @@
         tile = jnp.where(iota((8, STATE), 0) == 0, high[head : head + 1], rest).astype(LOW)
         for part in range(per_head):
             out_ref[head * per_head + part, 2 * rows : 2 * rows + 8, :] = tile
-
-
-def scan_kernel(in_ref, out_ref):
+    for send in sends:
+        send.wait()
+
+
+def scan_kernel(in_ref, *refs):
+    out_ref = refs[-1]
     devices, rows = out_ref.shape[0], out_ref.shape[1] // 2
     decays = []
     for at in range(devices):
@@ -114,13 +170,43 @@
         state = decays[at] * state + in_ref[at, rows : 2 * rows, :].astype(FULL)
 
 
-def grads_kernel(
-    lengths_ref, x_ref, dy_ref, b_ref, c_ref, log_ref, edge_ref, grad_x_ref, grad_bc_ref
+def local_kernel(
+    lengths_hbm,
+    log_hbm,
+    x_hbm,
+    b_hbm,
+    dy_hbm,
+    c_hbm,
+    grad_x_ref,
+    grad_bc_ref,
+    x_weighted_ref,
+    dy_weighted_ref,
+    leave_ref,
+    lengths_ref,
+    log_ref,
+    x_ref,
+    b_ref,
+    dy_ref,
+    c_ref,
+    sems,
 ):
-    slices, rows = edge_ref.shape[0], edge_ref.shape[1] // 2
+    loads = fetch(
+        [
+            (lengths_hbm, lengths_ref),
+            (log_hbm, log_ref),
+            (x_hbm, x_ref),
+            (b_hbm, b_ref),
+            (dy_hbm, dy_ref),
+            (c_hbm, c_ref),
+        ],
+        sems,
+    )
+    for load in loads:
+        load.wait()
     first_row, ends, cumulative, docs, enter, leave, _ = token_vectors(log_ref, lengths_ref)
+    enter_cols, leave_cols = split_columns(enter), split_columns(leave)
+    leave_ref[...] = leave_cols
     cum_cols = cumulative.T
-    enter_cols, leave_cols = split_columns(enter), split_columns(leave)
     middle = doc_of(first_row + SPAN - 1, ends)
     cum_middle = cumulative[:, SPAN - 1 : SPAN]
     leave_first = jnp.where(
@@ -150,20 +236,15 @@
 
     mixed = [jnp.zeros((SPAN, SPAN), FULL), jnp.zeros((SPAN, SPAN), FULL)]
     mixed_cross = jnp.zeros((SPAN, SPAN), FULL)
-    grad_b = jnp.zeros((2 * SPAN, STATE), FULL)
-    grad_c = jnp.zeros((2 * SPAN, STATE), FULL)
     for pair in range(PAIRS):
         low = pair * LANES
         x, dy = x_ref[:, low : low + LANES], dy_ref[:, low : low + LANES]
-        at = slice(low // rows, (low + LANES) // rows)
-        start = edge_ref[at, 0:rows, :].reshape(LANES, STATE)
-        end = edge_ref[at, rows : 2 * rows, :].reshape(LANES, STATE)
-        leave_wide = spread(leave_cols, low, LANES)
-        weighted = (x.astype(FULL) * leave_wide).astype(LOW)
-        grad_b += mul(weighted, end)
-        weighted = (dy.astype(FULL) * spread(enter_cols, low, LANES)).astype(LOW)
-        grad_c += mul(weighted, start)
-        grad_x = leave_wide * mul(b, end, NT)
+        for wide, cols, weighted_ref in (
+            (x, leave_cols, x_weighted_ref),
+            (dy, enter_cols, dy_weighted_ref),
+        ):
+            weighted = (wide.astype(FULL) * spread(cols, low, LANES)).astype(LOW)
+            weighted_ref[:, low : low + LANES] = weighted
         first_wide = spread(leave_first, low, LANES)
         x_first = (x[:SPAN].astype(FULL) * first_wide).astype(LOW)
         dy_second = (dy[SPAN:].astype(FULL) * spread(enter_second, low, LANES)).astype(LOW)
@@ -179,8 +260,9 @@
                 within = jnp.exp(jnp.where(masks[number], gaps, -1e30))
                 mixed[number] += within * inner[side * SPAN : (side + 1) * SPAN]
                 low_scores.append((within * scores[span, span]).astype(LOW))
-            pieces[number] += mul(jnp.concatenate(low_scores, axis=1), halves(dy[span]))
-            grad_x_ref[span, low : low + LANES] = (grad_x[span] + pieces[number]).astype(LOW)
+            grad_x_ref[span, low : low + LANES] = pieces[number] + mul(
+                jnp.concatenate(low_scores, axis=1), halves(dy[span])
+            )
     nothing = jnp.zeros((SPAN, SPAN), FULL)
     table = jnp.concatenate(
         [
@@ -189,61 +271,164 @@
         ],
         axis=0,
     )
-    grad_bc_ref[:, :STATE] = (grad_b + mul(table.astype(LOW), c)).astype(LOW)
-    grad_bc_ref[:, STATE:] = (grad_c + mul(table.T.astype(LOW), b)).astype(LOW)
-
-
-def call(body, out_shape, specs, flops, moved):
+    grad_bc_ref[:, :STATE] = mul(table.astype(LOW), c)
+    grad_bc_ref[:, STATE:] = mul(table.T.astype(LOW), b)
+
+
+def grad_bc_kernel(x_weighted_ref, dy_weighted_ref, local_ref, edge_ref, *refs):
+    out_ref = refs[-1]
+    rows = edge_ref.shape[1] // 2
+    start = edge_ref[:, 0:rows, :].reshape(WIDE, STATE)
+    end = edge_ref[:, rows : 2 * rows, :].reshape(WIDE, STATE)
+    out_ref[:, :STATE] = (local_ref[:, :STATE] + mul(x_weighted_ref[...], end)).astype(LOW)
+    out_ref[:, STATE:] = (local_ref[:, STATE:] + mul(dy_weighted_ref[...], start)).astype(LOW)
+
+
+def grad_x_kernel(b_ref, leave_ref, local_ref, edge_ref, out_ref):
+    rows = edge_ref.shape[1] // 2
+    width = 2 * LANES
+    for chunk in range(WIDE // width):
+        low = chunk * width
+        at = slice(low // rows, (low + width) // rows)
+        end = edge_ref[at, rows : 2 * rows, :].reshape(width, STATE)
+        later = spread(leave_ref[...], low, width) * mul(b_ref[...], end, NT)
+        out_ref[:, low : low + width] = (local_ref[:, low : low + width] + later).astype(LOW)
+
+
+def project_kernel(w_b_hbm, w_c_hbm, *refs, sibling):
+    terms = (len(refs) - 3) // 2
+    grads, weights = refs[:terms], refs[terms : 2 * terms - 1]
+    out_ref, grads_ref, weights_ref, sems = refs[-4:]
+    columns = out_ref.shape[1]
+    me = lax.axis_index("tp")
+    core = lax.rem(me, CORES)
+    half = 1 - core if sibling else core
+    from_row = pl.ds(pl.multiple_of((me - core + half) * columns, columns), columns)
+    pairs = [
+        (w_b_hbm.at[from_row, :], weights_ref.at[0, :, pl.ds(0, STATE)]),
+        (w_c_hbm.at[from_row, :], weights_ref.at[0, :, pl.ds(STATE, STATE)]),
+    ]
+    for at in range(terms):
+        pairs.append((grads[at], grads_ref.at[at]))
+        if at:
+            pairs.append((weights[at - 1], weights_ref.at[at]))
+    loads = fetch(pairs, sems)
+    total = 0.0
+    for at in range(terms):
+        for load in loads[:3] if at == 0 else loads[1 + 2 * at : 3 + 2 * at]:
+            load.wait()
+        total += mul(grads_ref[at], weights_ref[at], NT)
+    out_ref[...] = total.astype(out_ref.dtype)
+
+
+BLOCK = pl.BlockSpec(memory_space=pltpu.VMEM)
+WHERE = pl.BlockSpec(memory_space=pl.ANY)
+HBM = pl.BlockSpec(memory_space=pltpu.HBM)
+
+
+def call(body, out_shape, specs, vmem, flops, moved, out_specs=BLOCK, scratch=()):
     return pl.pallas_call(
         body,
         out_shape=out_shape,
         in_specs=specs,
-        out_specs=jax.tree.map(lambda _: pl.BlockSpec(memory_space=pltpu.VMEM), out_shape),
-        compiler_params=pltpu.CompilerParams(vmem_limit_bytes=VMEM_BYTES),
+        out_specs=out_specs,
+        scratch_shapes=scratch,
+        compiler_params=pltpu.CompilerParams(vmem_limit_bytes=vmem),
         cost_estimate=pl.CostEstimate(flops=flops, bytes_accessed=moved, transcendentals=0),
+    )
+
+
+def along_x(value, step):
+    devices = lax.axis_size("tp")
+    return lax.ppermute(
+        value, "tp", [(at, (at + CORES * step) % devices) for at in range(devices)]
     )
 
 
 def per_device(inner_x, in_b, in_c, log_decay, doc_lengths, out_grad, w_b, w_c):
     tokens = inner_x.shape[0]
     devices = lax.axis_size("seq")
+    steps = lax.axis_size("tp") // CORES - 1
     rows = WIDE // devices
-    small = pl.BlockSpec(memory_space=pltpu.SMEM)
-    block = pl.BlockSpec(memory_space=pltpu.VMEM)
-    local = (doc_lengths, inner_x, out_grad, in_b, in_c, log_decay)
-    summary = call(
+    columns = w_b.shape[0] // lax.axis_size("tp")
+    local = (doc_lengths, log_decay, inner_x, in_b, out_grad, in_c)
+    dma = pltpu.SemaphoreType.DMA
+    shape = jax.ShapeDtypeStruct
+    held = [pltpu.SMEM(doc_lengths.shape, doc_lengths.dtype)] + [
+        pltpu.VMEM(a.shape, a.dtype) for a in local[1:]
+    ]
+    sends = CORES * steps
+    summary, *sent = call(
         summary_kernel,
-        jax.ShapeDtypeStruct((devices, 2 * rows + 8, STATE), LOW),
-        [small] + [block] * 5,
+        [shape((devices, 2 * rows + 8, STATE), LOW)]
+        + [shape((columns, 2 * STATE), LOW)] * sends,
+        [HBM] * 8,
+        LARGE_VMEM,
         2 * 10**8,
-        2 * 10**6,
-    )(*local)
+        8 * 10**6,
+        [BLOCK] + [HBM] * sends,
+        held + [dma((6,)), dma((2 * sends,))],
+    )(*local, w_b, w_c)
+    weights = [along_x(value, at % steps + 1) for at, value in enumerate(sent)]
     summary = lax.all_to_all(summary, "seq", 0, 0)
     edges = call(
         scan_kernel,
-        jax.ShapeDtypeStruct((devices, 2 * rows, STATE), LOW),
-        [block],
+        shape((devices, 2 * rows, STATE), LOW),
+        [BLOCK] + [WHERE] * steps,
+        4 * MIB,
         10**6,
         10**6,
-    )(summary)
+    )(summary, *weights[:steps])
     edges = lax.all_to_all(edges, "seq", 0, 0)
-    grad_x, grad_bc = call(
-        grads_kernel,
-        (
-            jax.ShapeDtypeStruct((tokens, WIDE), LOW),
-            jax.ShapeDtypeStruct((tokens, 2 * STATE), LOW),
-        ),
-        [small] + [block] * 6,
+    grad_x, grad_bc, x_weighted, dy_weighted, leave_cols = call(
+        local_kernel,
+        [
+            shape((tokens, WIDE), FULL),
+            shape((tokens, 2 * STATE), FULL),
+            shape((tokens, WIDE), LOW),
+            shape((tokens, WIDE), LOW),
+            shape((tokens, 2 * HEADS), LOW),
+        ],
+        [HBM] * 6,
+        16 * MIB,
         4 * 10**8,
         3 * 10**6,
-    )(*local, edges)
-    partial_value = lax.dot_general(grad_bc[:, :STATE], w_b, NT, preferred_element_type=FULL)
-    partial_value = partial_value + lax.dot_general(
-        grad_bc[:, STATE:], w_c, NT, preferred_element_type=FULL
-    )
-    grad_input = lax.psum_scatter(
-        partial_value.astype(LOW), "tp", scatter_dimension=1, tiled=True
-    )
+        [BLOCK] * 5,
+        held + [dma((6,))],
+    )(*local)
+    grad_bc = call(
+        grad_bc_kernel,
+        shape((tokens, 2 * STATE), LOW),
+        [BLOCK] * 4 + [WHERE] * steps,
+        8 * MIB,
+        2 * 10**8,
+        10**6,
+    )(x_weighted, dy_weighted, grad_bc, edges, *weights[steps:])
+    others = [along_x(grad_bc, step + 1) for step in range(steps)]
+    grad_x = call(
+        grad_x_kernel, shape((tokens, WIDE), LOW), [BLOCK] * 4, 8 * MIB, 10**8, 3 * 10**6
+    )(in_b, leave_cols, grad_x, edges)
+
+    def project(sibling, kind):
+        terms = steps + 1
+        return call(
+            functools.partial(project_kernel, sibling=sibling),
+            shape((tokens, columns), kind),
+            [HBM] * (2 * terms + 1),
+            LARGE_VMEM,
+            6 * 10**8,
+            3 * 10**6,
+            BLOCK,
+            [
+                pltpu.VMEM((terms, tokens, 2 * STATE), LOW),
+                pltpu.VMEM((terms, columns, 2 * STATE), LOW),
+                dma((2 * terms + 1,)),
+            ],
+        )(w_b, w_c, grad_bc, *others, *(weights[:steps] if sibling else weights[steps:]))
+
+    partner = [(at, at ^ 1) for at in range(lax.axis_size("tp"))]
+    received = lax.ppermute(project(True, LOW), "tp", partner)
+    grad_input = (project(False, FULL) + received.astype(FULL)).astype(LOW)
     return grad_x, grad_input
 
 

time: 121 us -> 200 us (1.65)
  the two profiles are of different devices: /device:TPU:8 before, /device:TPU:1 now
where the time goes in v2:
time: 200 us; the launch traced here: 199 us
  Pallas kernels  110 us (55%)
  waiting for transfers between devices  40.3 us (20%)
  starting transfers between devices  36.2 us (18%)
  local copies, waits for them, and re-layouts  9.69 us (5%)
  other arithmetic  2.17 us (1%)
    pallas_call x1, Pallas kernels, per_device(): call(summary_kernel, [shape((devices, 2 * rows + 8, STATE), LOW)] + [shap...  97.4 us
    ppermute x9, waiting for transfers between devices, along_x(): lax.ppermute(value, 'tp', [(at, (at + CORES * step) % devices) for at in...  40.3 us
    ppermute x9, starting transfers between devices, along_x(): lax.ppermute(value, 'tp', [(at, (at + CORES * step) % devices) for at in...  13.6 us
    all_to_all x1, starting transfers between devices, per_device(): summary = lax.all_to_all(summary, 'seq', 0, 0)  12 us
    unnamed x48, local copies, waits for them, and re-layouts  9.69 us
    all_to_all x1, starting transfers between devices, per_device(): edges = lax.all_to_all(edges, 'seq', 0, 0)  9.09 us
    pallas_call x2, Pallas kernels, project(): call(functools.partial(project_kernel, sibling=sibling), shape((tokens, c...  6.3 us
  transfers between devices with their start and end apart: 12, of which 5 were waited for; matrix products, arithmetic and copies ran while one was open for 0% of the time, Pallas kernels for 4%

profile of v2, /device:TPU:1, one launch (start us, length us, event | category | flops | bytes accessed | tf_op | source)
XLA Modules:
  0.0 199.2 jit_solution(17775593872654920197)
XLA Ops:
  0.6 97.4 %shard_map.96 = (bf16[32,72,128]{2,1,0:T(8,128)(2,1)}, bf16[1024,256]{1,0:T(8,128)(2,1)}, bf16[1024,256]{1,0:T(8,128)(2,1)}, bf16[1024,256]{1,0:T(8,128)(2,1)}, ...) custom-call(s32[4]{0:T(128)} %lengths_hbm.3, f32[16,256]{1,0:T(8,128)} %log_hbm.3, ...), custom_call_target="tpu_custom_call" | custom-call | flops 200000000 | bytes 8000000 | tf_op jit(solution)/shard_map/pallas_call | solution.py:361
  98.0 12.0 %all-to-all-start = ((bf16[32,72,128]{2,1,0:T(8,128)(2,1)}), bf16[32,72,128]{2,1,0:T(8,128)(2,1)S(1)}, u32[]{:S(2)}, u32[]{:S(2)}) async-start(bf16[32,72,128]{2,1,0:T(8,128)(2,1)} %get-tuple-element.16), calls=%async_computation | async-start | bytes 1179648 | tf_op jit(solution)/shard_map/all_to_all | solution.py:373
  110.1 0.0 copy-start.15
  110.1 0.0 copy-start.16
  110.1 0.0 copy-start.19
  110.1 1.3 collective-permute-start
  111.4 2.5 %collective-permute-start.1 = (bf16[1024,256]{1,0:T(8,128)(2,1)}, bf16[1024,256]{1,0:T(8,128)(2,1)S(1)}, u32[]{:S(2)}, u32[]{:S(2)}) collective-permute-start(bf16[1024,256]{1,0:T(8,128)(2,1)} %get-tuple-element.18), channel_id=1, source_target_pairs={{0,4},{1,5},{2,6},{3,7},{4,0},{5,1},{6,2},{7,3},{8,12},{9,13},{10,... | collective-permute-start | bytes 1572872 | tf_op jit(solution)/shard_map/ppermute | solution.py:343
  113.9 1.2 collective-permute-start.2
  115.0 9.1 %collective-permute-done.refs_0_.refs_4_ = bf16[1024,256]{1,0:T(8,128)(2,1)S(1)} collective-permute-done((bf16[1024,256]{1,0:T(8,128)(2,1)}, bf16[1024,256]{1,0:T(8,128)(2,1)S(1)}, u32[]{:S(2)}, u32[]{:S(2)}) %collective-permute-start) | collective-permute-done | bytes 524320 | tf_op jit(solution)/shard_map/ppermute | solution.py:343
  124.1 12.2 %collective-permute-done.1.refs_1_.refs_5_ = bf16[1024,256]{1,0:T(8,128)(2,1)S(1)} collective-permute-done((bf16[1024,256]{1,0:T(8,128)(2,1)}, bf16[1024,256]{1,0:T(8,128)(2,1)S(1)}, u32[]{:S(2)}, u32[]{:S(2)}) %collective-permute-start.1) | collective-permute-done | bytes 524320 | tf_op jit(solution)/shard_map/ppermute | solution.py:343
  136.3 0.0 collective-permute-done.2.refs_2_.refs_6_
  136.4 0.0 all-to-all-done.in_ref
  136.4 1.1 shard_map.97
  137.5 9.1 %all-to-all-start.1 = ((bf16[32,64,128]{2,1,0:T(8,128)(2,1)}), bf16[32,64,128]{2,1,0:T(8,128)(2,1)S(1)}, u32[]{:S(2)}, u32[]{:S(2)}) async-start(bf16[32,64,128]{2,1,0:T(8,128)(2,1)} %shard_map.97), calls=%async_computation.1 | async-start | bytes 1048576 | tf_op jit(solution)/shard_map/all_to_all | solution.py:382
  146.6 0.0 copy-done.5
  146.6 1.7 collective-permute-start.3
  148.3 2.8 %collective-permute-start.4 = (bf16[1024,256]{1,0:T(8,128)(2,1)}, bf16[1024,256]{1,0:T(8,128)(2,1)S(1)}, u32[]{:S(2)}, u32[]{:S(2)}) collective-permute-start(bf16[1024,256]{1,0:T(8,128)(2,1)} %get-tuple-element.24), channel_id=1, source_target_pairs={{0,4},{1,5},{2,6},{3,7},{4,0},{5,1},{6,2},{7,3},{8,12},{9,13},{10,... | collective-permute-start | bytes 1572872 | tf_op jit(solution)/shard_map/ppermute | solution.py:343
  151.1 0.0 collective-permute-start.5
  151.2 0.0 copy-start.13
  151.2 1.0 copy-done.13
  152.2 1.0 copy-done.14
  153.2 0.7 copy-done.20
  153.9 3.7 %shard_map.95 = (f32[256,1024]{1,0:T(8,128)S(1)}, f32[256,256]{1,0:T(8,128)S(1)}, bf16[256,1024]{1,0:T(8,128)(2,1)S(1)}, bf16[256,1024]{1,0:T(8,128)(2,1)S(1)}, bf16[256,32]{1,0:T(8,128)(2,1)S(1)}) custom-call(s32[4]{0:T(128)S(1)} %copy-done.20, f32[16,256]{1,0:T(8,128)S(1)} %copy-done.19, bf16[256,1024]{1,0:T(8,128)(2,1)S(1)} %copy-done.13, ...), custom_call_target="tpu_custom_call" | custom-call | flops 400000000 | bytes 3000000 | tf_op jit(solution)/shard_map/pallas_call | solution.py:383
  157.6 1.0 copy-done.7
  158.6 0.8 copy-done.9
  159.4 0.8 copy-done.11
  160.2 0.6 copy-done.17
  160.8 0.0 collective-permute-done.3.refs_0_.refs_4_
  160.8 13.0 %collective-permute-done.4.refs_1_.refs_5_ = bf16[1024,256]{1,0:T(8,128)(2,1)S(1)} collective-permute-done((bf16[1024,256]{1,0:T(8,128)(2,1)}, bf16[1024,256]{1,0:T(8,128)(2,1)S(1)}, u32[]{:S(2)}, u32[]{:S(2)}) %collective-permute-start.4) | collective-permute-done | bytes 524320 | tf_op jit(solution)/shard_map/ppermute | solution.py:343
  173.8 0.0 collective-permute-done.5.refs_2_.refs_6_
  173.8 0.0 all-to-all-done.1.edge_ref
  173.8 1.4 copy-done.10
  175.2 1.0 copy-done.12
  176.3 0.4 shard_map.99.refs_0_
  176.7 1.3 collective-permute-start.6
  178.0 2.8 %collective-permute-start.7 = (bf16[256,256]{1,0:T(8,128)(2,1)S(1)}, bf16[256,256]{1,0:T(8,128)(2,1)S(1)}, u32[]{:S(2)}, u32[]{:S(2)}) collective-permute-start(bf16[256,256]{1,0:T(8,128)(2,1)S(1)} %shard_map.99.refs_0_), channel_id=1, source_target_pairs={{0,4},{1,5},{2,6},{3,7},{4,0},{5,1},{6,2},{7,3},{8,12},{9,13},{10,... | collective-permute-start | bytes 393224 | tf_op jit(solution)/shard_map/ppermute | solution.py:343
  180.8 0.0 collective-permute-start.8
  180.8 1.2 collective-permute-done.6.refs_1_
  182.0 4.7 %collective-permute-done.7.refs_2_ = bf16[256,256]{1,0:T(8,128)(2,1)S(1)} collective-permute-done((bf16[256,256]{1,0:T(8,128)(2,1)S(1)}, bf16[256,256]{1,0:T(8,128)(2,1)S(1)}, u32[]{:S(2)}, u32[]{:S(2)}) %collective-permute-start.7) | collective-permute-done | bytes 131104 | tf_op jit(solution)/shard_map/ppermute | solution.py:343
  186.8 0.0 collective-permute-done.8.refs_3_
  186.8 0.6 copy-done.22
  187.4 0.6 copy-done.23
  188.1 3.1 %shard_map.101 = bf16[256,1024]{1,0:T(8,128)(2,1)} custom-call(bf16[8192,128]{1,0:T(8,128)(2,1)} %w_b_hbm.5, bf16[8192,128]{1,0:T(8,128)(2,1)} %w_c_hbm.5, bf16[256,256]{1,0:T(8,128)(2,1)} %copy-done.6, bf16[256,256]{1,0:T(8,128)(2,1)} %copy-done.21, bf16[256,256]{1,0:T(8,128)(2,1)} %copy-done.22, bf16[256,256]{1,0:T(8,128)(2,1)} %copy-done.23, ...), custom_call_target="tpu_custom_call" | custom-call | flops 600000000 | bytes 3000000 | tf_op jit(solution)/shard_map/pallas_call | solution.py:414
  191.2 1.4 collective-permute-start.9
  192.6 1.2 shard_map.98
  193.8 3.2 %shard_map.100 = f32[256,1024]{1,0:T(8,128)} custom-call(bf16[8192,128]{1,0:T(8,128)(2,1)} %w_b_hbm.5, bf16[8192,128]{1,0:T(8,128)(2,1)} %w_c_hbm.5, bf16[256,256]{1,0:T(8,128)(2,1)} %copy-done.6, bf16[256,256]{1,0:T(8,128)(2,1)} %copy-done.21, bf16[256,256]{1,0:T(8,128)(2,1)} %copy-done.22, bf16[256,256]{1,0:T(8,128)(2,1)} %copy-done.23, ...), custom_call_target="tpu_custom_call" | custom-call | flops 600000000 | bytes 3000000 | tf_op jit(solution)/shard_map/pallas_call | solution.py:414
  197.1 0.0 collective-permute-done.9
  197.1 2.2 %add_convert_fusion = bf16[256,1024]{1,0:T(8,128)(2,1)} fusion(f32[256,1024]{1,0:T(8,128)} %shard_map.100, bf16[256,1024]{1,0:T(8,128)(2,1)S(1)} %collective-permute-done.9), kind=kLoop, calls=%fused_computation | loop fusion | flops 786432 | bytes 2097152 | tf_op jit(solution)/shard_map/convert_element_type | solution.py:431
  (32 shorter events, 0.1 us)
Async XLA Ops:
  98.0 38.3 %all-to-all-start = ((bf16[32,72,128]{2,1,0:T(8,128)(2,1)}), bf16[32,72,128]{2,1,0:T(8,128)(2,1)S(1)}, u32[]{:S(2)}, u32[]{:S(2)}) async-start(bf16[32,72,128]{2,1,0:T(8,128)(2,1)} %get-tuple-element.16), calls=%async_computation | async-start | bytes 1179648 | tf_op jit(solution)/shard_map/all_to_all | solution.py:373
  110.1 41.0 %copy-start.15 = (bf16[256,128]{1,0:T(8,128)(2,1)S(1)}, bf16[256,128]{1,0:T(8,128)(2,1)}, u32[]{:S(2)}) copy-start(bf16[256,128]{1,0:T(8,128)(2,1)} %b_ref.1) | copy-start | bytes 196612
  110.1 41.0 %copy-start.16 = (bf16[256,128]{1,0:T(8,128)(2,1)S(1)}, bf16[256,128]{1,0:T(8,128)(2,1)}, u32[]{:S(2)}) copy-start(bf16[256,128]{1,0:T(8,128)(2,1)} %c_hbm.3) | copy-start | bytes 196612
  110.1 41.0 %copy-start.19 = (f32[16,256]{1,0:T(8,128)S(1)}, f32[16,256]{1,0:T(8,128)}, u32[]{:S(2)}) copy-start(f32[16,256]{1,0:T(8,128)} %log_hbm.3) | copy-start | bytes 49156
  110.1 14.0 %collective-permute-start = (bf16[1024,256]{1,0:T(8,128)(2,1)}, bf16[1024,256]{1,0:T(8,128)(2,1)S(1)}, u32[]{:S(2)}, u32[]{:S(2)}) collective-permute-start(bf16[1024,256]{1,0:T(8,128)(2,1)} %get-tuple-element.17), channel_id=1, source_target_pairs={{0,2},{1,3},{2,4},{3,5},{4,6},{5,7},{6,0},{7,1},{8,10},{9,11},{10,... | collective-permute-start | bytes 1572872 | tf_op jit(solution)/shard_map/ppermute | solution.py:343
  111.4 24.9 %collective-permute-start.1 = (bf16[1024,256]{1,0:T(8,128)(2,1)}, bf16[1024,256]{1,0:T(8,128)(2,1)S(1)}, u32[]{:S(2)}, u32[]{:S(2)}) collective-permute-start(bf16[1024,256]{1,0:T(8,128)(2,1)} %get-tuple-element.18), channel_id=1, source_target_pairs={{0,4},{1,5},{2,6},{3,7},{4,0},{5,1},{6,2},{7,3},{8,12},{9,13},{10,... | collective-permute-start | bytes 1572872 | tf_op jit(solution)/shard_map/ppermute | solution.py:343
  113.9 22.5 %collective-permute-start.2 = (bf16[1024,256]{1,0:T(8,128)(2,1)}, bf16[1024,256]{1,0:T(8,128)(2,1)S(1)}, u32[]{:S(2)}, u32[]{:S(2)}) collective-permute-start(bf16[1024,256]{1,0:T(8,128)(2,1)} %get-tuple-element.19), channel_id=1, source_target_pairs={{0,6},{1,7},{2,0},{3,1},{4,2},{5,3},{6,4},{7,5},{8,14},{9,15},{10,... | collective-permute-start | bytes 1572872 | tf_op jit(solution)/shard_map/ppermute | solution.py:343
  124.1 33.5 %copy-start.3 = (bf16[1024,256]{1,0:T(8,128)(2,1)}, bf16[1024,256]{1,0:T(8,128)(2,1)S(1)}, u32[]{:S(2)}) copy-start(bf16[1024,256]{1,0:T(8,128)(2,1)S(1)} %collective-permute-done.refs_0_.refs_4_) | copy-start | bytes 1572868
  136.3 21.3 %copy-start.4 = (bf16[1024,256]{1,0:T(8,128)(2,1)}, bf16[1024,256]{1,0:T(8,128)(2,1)S(1)}, u32[]{:S(2)}) copy-start(bf16[1024,256]{1,0:T(8,128)(2,1)S(1)} %collective-permute-done.1.refs_1_.refs_5_) | copy-start | bytes 1572868
  136.4 10.2 %copy-start.5 = (bf16[1024,256]{1,0:T(8,128)(2,1)}, bf16[1024,256]{1,0:T(8,128)(2,1)S(1)}, u32[]{:S(2)}) copy-start(bf16[1024,256]{1,0:T(8,128)(2,1)S(1)} %collective-permute-done.2.refs_2_.refs_6_) | copy-start | bytes 1572868
  137.5 36.3 %all-to-all-start.1 = ((bf16[32,64,128]{2,1,0:T(8,128)(2,1)}), bf16[32,64,128]{2,1,0:T(8,128)(2,1)S(1)}, u32[]{:S(2)}, u32[]{:S(2)}) async-start(bf16[32,64,128]{2,1,0:T(8,128)(2,1)} %shard_map.97), calls=%async_computation.1 | async-start | bytes 1048576 | tf_op jit(solution)/shard_map/all_to_all | solution.py:382
  146.6 14.2 %collective-permute-start.3 = (bf16[1024,256]{1,0:T(8,128)(2,1)}, bf16[1024,256]{1,0:T(8,128)(2,1)S(1)}, u32[]{:S(2)}, u32[]{:S(2)}) collective-permute-start(bf16[1024,256]{1,0:T(8,128)(2,1)} %get-tuple-element.23), channel_id=1, source_target_pairs={{0,2},{1,3},{2,4},{3,5},{4,6},{5,7},{6,0},{7,1},{8,10},{9,11},{10,... | collective-permute-start | bytes 1572872 | tf_op jit(solution)/shard_map/ppermute | solution.py:343
  148.3 25.5 %collective-permute-start.4 = (bf16[1024,256]{1,0:T(8,128)(2,1)}, bf16[1024,256]{1,0:T(8,128)(2,1)S(1)}, u32[]{:S(2)}, u32[]{:S(2)}) collective-permute-start(bf16[1024,256]{1,0:T(8,128)(2,1)} %get-tuple-element.24), channel_id=1, source_target_pairs={{0,4},{1,5},{2,6},{3,7},{4,0},{5,1},{6,2},{7,3},{8,12},{9,13},{10,... | collective-permute-start | bytes 1572872 | tf_op jit(solution)/shard_map/ppermute | solution.py:343
  151.1 22.7 %collective-permute-start.5 = (bf16[1024,256]{1,0:T(8,128)(2,1)}, bf16[1024,256]{1,0:T(8,128)(2,1)S(1)}, u32[]{:S(2)}, u32[]{:S(2)}) collective-permute-start(bf16[1024,256]{1,0:T(8,128)(2,1)} %get-tuple-element.25), channel_id=1, source_target_pairs={{0,6},{1,7},{2,0},{3,1},{4,2},{5,3},{6,4},{7,5},{8,14},{9,15},{10,... | collective-permute-start | bytes 1572872 | tf_op jit(solution)/shard_map/ppermute | solution.py:343
  151.2 1.0 copy-start.13
  152.2 1.0 copy-start.14
  153.2 0.7 copy-start.20
  157.6 1.0 copy-start.7
  158.6 0.8 copy-start.9
  159.4 0.8 copy-start.11
  160.2 0.6 copy-start.17
  160.8 30.3 %copy-start = (bf16[1024,256]{1,0:T(8,128)(2,1)}, bf16[1024,256]{1,0:T(8,128)(2,1)S(1)}, u32[]{:S(2)}) copy-start(bf16[1024,256]{1,0:T(8,128)(2,1)S(1)} %collective-permute-done.3.refs_0_.refs_4_) | copy-start | bytes 1572868
  173.8 17.3 %copy-start.1 = (bf16[1024,256]{1,0:T(8,128)(2,1)}, bf16[1024,256]{1,0:T(8,128)(2,1)S(1)}, u32[]{:S(2)}) copy-start(bf16[1024,256]{1,0:T(8,128)(2,1)S(1)} %collective-permute-done.4.refs_1_.refs_5_) | copy-start | bytes 1572868
  173.8 17.3 %copy-start.2 = (bf16[1024,256]{1,0:T(8,128)(2,1)}, bf16[1024,256]{1,0:T(8,128)(2,1)S(1)}, u32[]{:S(2)}) copy-start(bf16[1024,256]{1,0:T(8,128)(2,1)S(1)} %collective-permute-done.5.refs_2_.refs_6_) | copy-start | bytes 1572868
  173.8 1.4 copy-start.10
  175.2 1.0 copy-start.12
  176.7 10.1 %copy-start.6 = (bf16[256,256]{1,0:T(8,128)(2,1)}, bf16[256,256]{1,0:T(8,128)(2,1)S(1)}, u32[]{:S(2)}) copy-start(bf16[256,256]{1,0:T(8,128)(2,1)S(1)} %shard_map.99.refs_0_) | copy-start | bytes 393220
  176.7 15.9 %copy-start.8 = (f32[256,1024]{1,0:T(8,128)S(1)}, f32[256,1024]{1,0:T(8,128)}, u32[]{:S(2)}) copy-start(f32[256,1024]{1,0:T(8,128)} %copy-done.7) | copy-start | bytes 3145732
  176.7 15.9 %copy-start.18 = (bf16[256,32]{1,0:T(8,128)(2,1)S(1)}, bf16[256,32]{1,0:T(8,128)(2,1)}, u32[]{:S(2)}) copy-start(bf16[256,32]{1,0:T(8,128)(2,1)} %copy-done.17) | copy-start | bytes 49156
  176.7 5.3 %collective-permute-start.6 = (bf16[256,256]{1,0:T(8,128)(2,1)S(1)}, bf16[256,256]{1,0:T(8,128)(2,1)S(1)}, u32[]{:S(2)}, u32[]{:S(2)}) collective-permute-start(bf16[256,256]{1,0:T(8,128)(2,1)S(1)} %shard_map.99.refs_0_), channel_id=1, source_target_pairs={{0,2},{1,3},{2,4},{3,5},{4,6},{5,7},{6,0},{7,1},{8,10},{9,11},{10,... | collective-permute-start | bytes 393224 | tf_op jit(solution)/shard_map/ppermute | solution.py:343
  178.0 8.8 %collective-permute-start.7 = (bf16[256,256]{1,0:T(8,128)(2,1)S(1)}, bf16[256,256]{1,0:T(8,128)(2,1)S(1)}, u32[]{:S(2)}, u32[]{:S(2)}) collective-permute-start(bf16[256,256]{1,0:T(8,128)(2,1)S(1)} %shard_map.99.refs_0_), channel_id=1, source_target_pairs={{0,4},{1,5},{2,6},{3,7},{4,0},{5,1},{6,2},{7,3},{8,12},{9,13},{10,... | collective-permute-start | bytes 393224 | tf_op jit(solution)/shard_map/ppermute | solution.py:343
  180.8 5.9 %collective-permute-start.8 = (bf16[256,256]{1,0:T(8,128)(2,1)S(1)}, bf16[256,256]{1,0:T(8,128)(2,1)S(1)}, u32[]{:S(2)}, u32[]{:S(2)}) collective-permute-start(bf16[256,256]{1,0:T(8,128)(2,1)S(1)} %shard_map.99.refs_0_), channel_id=1, source_target_pairs={{0,6},{1,7},{2,0},{3,1},{4,2},{5,3},{6,4},{7,5},{8,14},{9,15},{10,... | collective-permute-start | bytes 393224 | tf_op jit(solution)/shard_map/ppermute | solution.py:343
  182.0 4.8 %copy-start.21 = (bf16[256,256]{1,0:T(8,128)(2,1)}, bf16[256,256]{1,0:T(8,128)(2,1)S(1)}, u32[]{:S(2)}) copy-start(bf16[256,256]{1,0:T(8,128)(2,1)S(1)} %collective-permute-done.6.refs_1_) | copy-start | bytes 393220
  186.8 0.7 copy-start.22
  187.4 0.6 copy-start.23
  191.2 5.9 %collective-permute-start.9 = (bf16[256,1024]{1,0:T(8,128)(2,1)}, bf16[256,1024]{1,0:T(8,128)(2,1)S(1)}, u32[]{:S(2)}, u32[]{:S(2)}) collective-permute-start(bf16[256,1024]{1,0:T(8,128)(2,1)} %shard_map.101), channel_id=1, source_target_pairs={{0,1},{1,0},{2,3},{3,2},{4,5},{5,4},{6,7},{7,6},{8,9},{9,8},{10,11... | collective-permute-start | bytes 1572872 | tf_op jit(solution)/shard_map/ppermute | solution.py:430

commit v3 on v2

--- a/solution.py
+++ b/solution.py
@@ -15,6 +15,7 @@
 WIDE = HEADS * HEAD_DIM
 PAIRS = WIDE // LANES
 CORES = 2
+ROUTE = ((1, True), (1, False), (2, True), (3, True), (3, False), (2, False))
 LOW = jnp.bfloat16
 FULL = jnp.float32
 NN = (((1,), (0,)), ((), ()))
@@ -94,8 +95,9 @@
     out_ref,
     *refs,
 ):
-    sent_refs = refs[:-8]
-    lengths_ref, log_ref, x_ref, b_ref, dy_ref, c_ref, sems, sent_sems = refs[-8:]
+    sent_refs = refs[:-10]
+    lengths_ref, log_ref, x_ref, b_ref, dy_ref, c_ref, passing_ref = refs[-10:-3]
+    sems, passing_sems, sent_sems = refs[-3:]
     loads = fetch(
         [
             (lengths_hbm, lengths_ref),
@@ -107,18 +109,17 @@
         ],
         sems,
     )
-    columns = sent_refs[0].shape[0]
-    steps = len(sent_refs) // CORES
+    columns = passing_ref.shape[1]
     me = lax.axis_index("tp")
-    core = lax.rem(me, CORES)
+    core, chips = lax.rem(me, CORES), lax.axis_size("tp") // CORES
     pairs = []
-    for at, sent_ref in enumerate(sent_refs):
-        half = 1 - core if at < steps else core
-        target = lax.rem(me // CORES + at % steps + 1, steps + 1)
+    for at, (step, sibling) in enumerate(ROUTE):
+        half = 1 - core if sibling else core
+        target = lax.rem(me // CORES + step, chips)
         from_row = pl.ds(pl.multiple_of((target * CORES + half) * columns, columns), columns)
-        pairs.append((w_b_hbm.at[from_row, :], sent_ref.at[:, pl.ds(0, STATE)]))
-        pairs.append((w_c_hbm.at[from_row, :], sent_ref.at[:, pl.ds(STATE, STATE)]))
-    sends = fetch(pairs, sent_sems)
+        pairs.append((w_b_hbm.at[from_row, :], passing_ref.at[at, :, pl.ds(0, STATE)]))
+        pairs.append((w_c_hbm.at[from_row, :], passing_ref.at[at, :, pl.ds(STATE, STATE)]))
+    passing = fetch(pairs, passing_sems)
     slices = out_ref.shape[0]
     rows = WIDE // slices
     loads[0].wait()
@@ -126,12 +127,23 @@
     _, _, _, _, enter, leave, total = token_vectors(log_ref, lengths_ref)
     enter_cols = split_columns(enter)
     leave_cols = split_columns(leave)
+    sends = []
     width = 2 * LANES
     for side, (wide_ref, narrow_ref, cols) in enumerate(
         ((x_ref, b_ref, leave_cols), (dy_ref, c_ref, enter_cols))
     ):
         loads[2 + 2 * side].wait()
         loads[3 + 2 * side].wait()
+        if side:
+            for copy in passing:
+                copy.wait()
+            sends = fetch(
+                [
+                    (passing_ref.at[at], sent_refs[at // 3].at[pl.ds(at % 3 * columns, columns), :])
+                    for at in range(len(ROUTE))
+                ],
+                sent_sems,
+            )
         narrow = narrow_ref[...]
         for chunk in range(WIDE // width):
             low = chunk * width
@@ -153,8 +165,7 @@
         send.wait()
 
 
-def scan_kernel(in_ref, *refs):
-    out_ref = refs[-1]
+def scan_kernel(in_ref, out_ref):
     devices, rows = out_ref.shape[0], out_ref.shape[1] // 2
     decays = []
     for at in range(devices):
@@ -275,8 +286,7 @@
     grad_bc_ref[:, STATE:] = mul(table.T.astype(LOW), b)
 
 
-def grad_bc_kernel(x_weighted_ref, dy_weighted_ref, local_ref, edge_ref, *refs):
-    out_ref = refs[-1]
+def grad_bc_kernel(x_weighted_ref, dy_weighted_ref, local_ref, edge_ref, out_ref):
     rows = edge_ref.shape[1] // 2
     start = edge_ref[:, 0:rows, :].reshape(WIDE, STATE)
     end = edge_ref[:, rows : 2 * rows, :].reshape(WIDE, STATE)
@@ -296,25 +306,24 @@
 
 
 def project_kernel(w_b_hbm, w_c_hbm, *refs, sibling):
-    terms = (len(refs) - 3) // 2
-    grads, weights = refs[:terms], refs[terms : 2 * terms - 1]
-    out_ref, grads_ref, weights_ref, sems = refs[-4:]
+    grads, (up, twice, down), (out_ref, grads_ref, weights_ref, sems) = refs[:4], refs[4:7], refs[7:]
     columns = out_ref.shape[1]
     me = lax.axis_index("tp")
     core = lax.rem(me, CORES)
     half = 1 - core if sibling else core
     from_row = pl.ds(pl.multiple_of((me - core + half) * columns, columns), columns)
+    of_half = pl.ds(0 if sibling else columns, columns)
     pairs = [
         (w_b_hbm.at[from_row, :], weights_ref.at[0, :, pl.ds(0, STATE)]),
         (w_c_hbm.at[from_row, :], weights_ref.at[0, :, pl.ds(STATE, STATE)]),
+        (grads[0], grads_ref.at[0]),
     ]
-    for at in range(terms):
-        pairs.append((grads[at], grads_ref.at[at]))
-        if at:
-            pairs.append((weights[at - 1], weights_ref.at[at]))
+    for at, weight in enumerate((up.at[of_half, :], twice, down.at[of_half, :])):
+        pairs.append((grads[at + 1], grads_ref.at[at + 1]))
+        pairs.append((weight, weights_ref.at[at + 1]))
     loads = fetch(pairs, sems)
     total = 0.0
-    for at in range(terms):
+    for at in range(4):
         for load in loads[:3] if at == 0 else loads[1 + 2 * at : 3 + 2 * at]:
             load.wait()
         total += mul(grads_ref[at], weights_ref[at], NT)
@@ -322,11 +331,10 @@
 
 
 BLOCK = pl.BlockSpec(memory_space=pltpu.VMEM)
-WHERE = pl.BlockSpec(memory_space=pl.ANY)
 HBM = pl.BlockSpec(memory_space=pltpu.HBM)
 
 
-def call(body, out_shape, specs, vmem, flops, moved, out_specs=BLOCK, scratch=()):
+def call(body, out_shape, specs, vmem, out_specs=BLOCK, scratch=()):
     return pl.pallas_call(
         body,
         out_shape=out_shape,
@@ -334,7 +342,7 @@
         out_specs=out_specs,
         scratch_shapes=scratch,
         compiler_params=pltpu.CompilerParams(vmem_limit_bytes=vmem),
-        cost_estimate=pl.CostEstimate(flops=flops, bytes_accessed=moved, transcendentals=0),
+        cost_estimate=pl.CostEstimate(flops=1000, bytes_accessed=1000, transcendentals=0),
     )
 
 
@@ -348,7 +356,6 @@
 def per_device(inner_x, in_b, in_c, log_decay, doc_lengths, out_grad, w_b, w_c):
     tokens = inner_x.shape[0]
     devices = lax.axis_size("seq")
-    steps = lax.axis_size("tp") // CORES - 1
     rows = WIDE // devices
     columns = w_b.shape[0] // lax.axis_size("tp")
     local = (doc_lengths, log_decay, inner_x, in_b, out_grad, in_c)
@@ -357,28 +364,28 @@
     held = [pltpu.SMEM(doc_lengths.shape, doc_lengths.dtype)] + [
         pltpu.VMEM(a.shape, a.dtype) for a in local[1:]
     ]
-    sends = CORES * steps
+    blocks = len(ROUTE)
     summary, *sent = call(
         summary_kernel,
         [shape((devices, 2 * rows + 8, STATE), LOW)]
-        + [shape((columns, 2 * STATE), LOW)] * sends,
+        + [shape((blocks // 2 * columns, 2 * STATE), LOW)] * 2,
         [HBM] * 8,
         LARGE_VMEM,
-        2 * 10**8,
-        8 * 10**6,
-        [BLOCK] + [HBM] * sends,
-        held + [dma((6,)), dma((2 * sends,))],
+        [BLOCK, HBM, HBM],
+        held
+        + [pltpu.VMEM((blocks, columns, 2 * STATE), LOW)]
+        + [dma((6,)), dma((2 * blocks,)), dma((blocks,))],
     )(*local, w_b, w_c)
-    weights = [along_x(value, at % steps + 1) for at, value in enumerate(sent)]
+    up, down = along_x(sent[0], 1), along_x(sent[1], 3)
+    up_twice = along_x(up[2 * columns :], 1)
+    down_twice = along_x(down[2 * columns :], 3)
     summary = lax.all_to_all(summary, "seq", 0, 0)
     edges = call(
         scan_kernel,
         shape((devices, 2 * rows, STATE), LOW),
-        [BLOCK] + [WHERE] * steps,
+        [BLOCK],
         4 * MIB,
-        10**6,
-        10**6,
-    )(summary, *weights[:steps])
+    )(summary)
     edges = lax.all_to_all(edges, "seq", 0, 0)
     grad_x, grad_bc, x_weighted, dy_weighted, leave_cols = call(
         local_kernel,
@@ -391,40 +398,33 @@
         ],
         [HBM] * 6,
         16 * MIB,
-        4 * 10**8,
-        3 * 10**6,
         [BLOCK] * 5,
         held + [dma((6,))],
     )(*local)
     grad_bc = call(
         grad_bc_kernel,
         shape((tokens, 2 * STATE), LOW),
-        [BLOCK] * 4 + [WHERE] * steps,
+        [BLOCK] * 4,
         8 * MIB,
-        2 * 10**8,
-        10**6,
-    )(x_weighted, dy_weighted, grad_bc, edges, *weights[steps:])
-    others = [along_x(grad_bc, step + 1) for step in range(steps)]
+    )(x_weighted, dy_weighted, grad_bc, edges)
+    others = [along_x(grad_bc, step) for step in (1, 2, 3)]
     grad_x = call(
-        grad_x_kernel, shape((tokens, WIDE), LOW), [BLOCK] * 4, 8 * MIB, 10**8, 3 * 10**6
+        grad_x_kernel, shape((tokens, WIDE), LOW), [BLOCK] * 4, 8 * MIB
     )(in_b, leave_cols, grad_x, edges)
 
     def project(sibling, kind):
-        terms = steps + 1
         return call(
             functools.partial(project_kernel, sibling=sibling),
             shape((tokens, columns), kind),
-            [HBM] * (2 * terms + 1),
+            [HBM] * 9,
             LARGE_VMEM,
-            6 * 10**8,
-            3 * 10**6,
             BLOCK,
             [
-                pltpu.VMEM((terms, tokens, 2 * STATE), LOW),
-                pltpu.VMEM((terms, columns, 2 * STATE), LOW),
-                dma((2 * terms + 1,)),
+                pltpu.VMEM((4, tokens, 2 * STATE), LOW),
+                pltpu.VMEM((4, columns, 2 * STATE), LOW),
+                dma((9,)),
             ],
-        )(w_b, w_c, grad_bc, *others, *(weights[:steps] if sibling else weights[steps:]))
+        )(w_b, w_c, grad_bc, *others, up, up_twice if sibling else down_twice, down)
 
     partner = [(at, at ^ 1) for at in range(lax.axis_size("tp"))]
     received = lax.ppermute(project(True, LOW), "tp", partner)

time: 200 us -> 90.9 us (0.45)
  Pallas kernels: 110 us -> 18 us
  starting transfers between devices: 36.2 us -> 27.9 us
  waiting for transfers between devices: 40.3 us -> 32.4 us
    pallas_call x1, Pallas kernels: 97.4 us -> 5.5 us  [per_device(): call(summary_kernel, [shape((devices, 2 * rows + 8, STATE), LOW)] + [shap...]
    ppermute x9 -> x7, waiting for transfers between devices: 40.3 us -> 17.9 us  [along_x(): lax.ppermute(value, 'tp', [(at, (at + CORES * step) % devices) for at in...]
    all_to_all x1, waiting for transfers between devices: 0.01 us -> 14.5 us  [per_device(): summary = lax.all_to_all(summary, 'seq', 0, 0)]
    unnamed x48 -> x30, local copies, waits for them, and re-layouts: 9.69 us -> 4.95 us
    ppermute x9 -> x7, starting transfers between devices: 13.6 us -> 8.87 us  [along_x(): lax.ppermute(value, 'tp', [(at, (at + CORES * step) % devices) for at in...]
    all_to_all x1, starting transfers between devices: 9.09 us -> 5.5 us  [per_device(): edges = lax.all_to_all(edges, 'seq', 0, 0)]
    slice x0 -> x2, local copies, waits for them, and re-layouts: none -> 2.97 us  [the longest x1 1.89 us: per_device(): up_twice = along_x(up[2 * columns:], 1)]
  transfers between devices with their start and end apart: 12 -> 10, of which waited for: 5 -> 4; matrix products, arithmetic and copies ran while one was open for 0% -> 3% of each run, Pallas kernels for 4% -> 14%
where the time goes in v3:
time: 90.9 us; the launch traced here: 89.2 us
  waiting for transfers between devices  32.4 us (36%)
  starting transfers between devices  27.9 us (31%)
  Pallas kernels  18 us (20%)
  local copies, waits for them, and re-layouts  7.92 us (9%)
  other arithmetic  2.17 us (2%)
    ppermute x7, waiting for transfers between devices, along_x(): lax.ppermute(value, 'tp', [(at, (at + CORES * step) % devices) for at in...  17.9 us
    all_to_all x1, waiting for transfers between devices, per_device(): summary = lax.all_to_all(summary, 'seq', 0, 0)  14.5 us
    all_to_all x1, starting transfers between devices, per_device(): summary = lax.all_to_all(summary, 'seq', 0, 0)  12 us
    ppermute x7, starting transfers between devices, along_x(): lax.ppermute(value, 'tp', [(at, (at + CORES * step) % devices) for at in...  8.87 us
    pallas_call x2, Pallas kernels, project(): call(functools.partial(project_kernel, sibling=sibling), shape((tokens, c...  6.31 us
    pallas_call x1, Pallas kernels, per_device(): call(summary_kernel, [shape((devices, 2 * rows + 8, STATE), LOW)] + [shap...  5.5 us
    all_to_all x1, starting transfers between devices, per_device(): edges = lax.all_to_all(edges, 'seq', 0, 0)  5.5 us
    unnamed x30, local copies, waits for them, and re-layouts  4.95 us
  transfers between devices with their start and end apart: 10, of which 4 were waited for; matrix products, arithmetic and copies ran while one was open for 3% of the time, Pallas kernels for 14%

profile of v3, /device:TPU:1, one launch (start us, length us, event | category | flops | bytes accessed | tf_op | source)
XLA Modules:
  0.0 89.2 jit_solution(16285490585004980941)
XLA Ops:
  0.6 5.5 %shard_map.96 = (bf16[32,72,128]{2,1,0:T(8,128)(2,1)}, bf16[3072,256]{1,0:T(8,128)(2,1)}, bf16[3072,256]{1,0:T(8,128)(2,1)}) custom-call(s32[4]{0:T(128)} %lengths_hbm.3, f32[16,256]{1,0:T(8,128)} %log_hbm.3, bf16[256,1024]{1,0:T(8,128)(2,1)} %x_hbm.3, bf16[256,128]{1,0:T(8,128)(2,1)} %b_ref.1, bf16[256,1024]{1,0:T(8,128)(2,1)} %dy_hbm.3, ...), custom_call_target="tpu_custom_call" | custom-call | flops 1000 | bytes 1000 | tf_op jit(solution)/shard_map/pallas_call | solution.py:368
  6.1 12.0 %all-to-all-start = ((bf16[32,72,128]{2,1,0:T(8,128)(2,1)}), bf16[32,72,128]{2,1,0:T(8,128)(2,1)S(1)}, u32[]{:S(2)}, u32[]{:S(2)}) async-start(bf16[32,72,128]{2,1,0:T(8,128)(2,1)} %get-tuple-element.12), calls=%async_computation | async-start | bytes 1179648 | tf_op jit(solution)/shard_map/all_to_all | solution.py:382
  18.2 1.3 %collective-permute-start.3 = (bf16[3072,256]{1,0:T(8,128)(2,1)}, bf16[3072,256]{1,0:T(8,128)(2,1)}, u32[]{:S(2)}, u32[]{:S(2)}) collective-permute-start(bf16[3072,256]{1,0:T(8,128)(2,1)} %get-tuple-element.16), channel_id=1, source_target_pairs={{0,2},{1,3},{2,4},{3,5},{4,6},{5,7},{6,0},{7,1},{8,10},{9,11},{10,... | collective-permute-start | bytes 4718600 | tf_op jit(solution)/shard_map/ppermute | solution.py:351
  19.5 0.0 copy-start.9
  19.6 0.0 copy-start.10
  19.6 1.5 %collective-permute-start.4 = (bf16[3072,256]{1,0:T(8,128)(2,1)}, bf16[3072,256]{1,0:T(8,128)(2,1)}, u32[]{:S(2)}, u32[]{:S(2)}) collective-permute-start(bf16[3072,256]{1,0:T(8,128)(2,1)} %get-tuple-element.17), channel_id=1, source_target_pairs={{0,6},{1,7},{2,0},{3,1},{4,2},{5,3},{6,4},{7,5},{8,14},{9,15},{10,... | collective-permute-start | bytes 4718600 | tf_op jit(solution)/shard_map/ppermute | solution.py:351
  21.1 14.5 %all-to-all-done.in_ref = bf16[32,72,128]{2,1,0:T(8,128)(2,1)S(1)} async-done(((bf16[32,72,128]{2,1,0:T(8,128)(2,1)}), bf16[32,72,128]{2,1,0:T(8,128)(2,1)S(1)}, u32[]{:S(2)}, u32[]{:S(2)}) %all-to-all-start) | async-done | bytes 589856 | tf_op jit(solution)/shard_map/all_to_all | solution.py:382
  35.6 0.9 %shard_map.97 = bf16[32,64,128]{2,1,0:T(8,128)(2,1)} custom-call(bf16[32,72,128]{2,1,0:T(8,128)(2,1)S(1)} %all-to-all-done.in_ref), custom_call_target="tpu_custom_call" | custom-call | flops 1000 | bytes 1000 | tf_op jit(solution)/shard_map/pallas_call | solution.py:383
  36.5 5.5 %all-to-all-start.1 = ((bf16[32,64,128]{2,1,0:T(8,128)(2,1)}), bf16[32,64,128]{2,1,0:T(8,128)(2,1)S(1)}, u32[]{:S(2)}, u32[]{:S(2)}) async-start(bf16[32,64,128]{2,1,0:T(8,128)(2,1)} %shard_map.97), calls=%async_computation.1 | async-start | bytes 1048576 | tf_op jit(solution)/shard_map/all_to_all | solution.py:389
  42.0 12.7 %collective-permute-done.3.refs_4_ = bf16[3072,256]{1,0:T(8,128)(2,1)} collective-permute-done((bf16[3072,256]{1,0:T(8,128)(2,1)}, bf16[3072,256]{1,0:T(8,128)(2,1)}, u32[]{:S(2)}, u32[]{:S(2)}) %collective-permute-start.3) | collective-permute-done | bytes 1572896 | tf_op jit(solution)/shard_map/ppermute | solution.py:351
  54.7 1.9 %slice.9 = bf16[1024,256]{1,0:T(8,128)(2,1)} slice(bf16[3072,256]{1,0:T(8,128)(2,1)} %collective-permute-done.3.refs_4_), slice={[2048:3072], [0:256]} | slice | bytes 1048576 | tf_op jit(solution)/shard_map/slice | solution.py:380
  56.6 0.1 collective-permute-start.6
  56.7 0.0 copy-done
  56.7 0.0 copy-done.1
  56.7 0.0 copy-done.3
  56.7 0.0 copy-done.6
  56.7 0.0 copy-done.9
  56.8 0.0 copy-done.10
  56.8 3.6 %shard_map.95 = (f32[256,1024]{1,0:T(8,128)S(1)}, f32[256,256]{1,0:T(8,128)S(1)}, bf16[256,1024]{1,0:T(8,128)(2,1)S(1)}, bf16[256,1024]{1,0:T(8,128)(2,1)S(1)}, bf16[256,32]{1,0:T(8,128)(2,1)S(1)}) custom-call(s32[4]{0:T(128)S(1)} %copy-done.10, f32[16,256]{1,0:T(8,128)S(1)} %copy-done.9, bf16[256,1024]{1,0:T(8,128)(2,1)S(1)} %copy-done, ...), custom_call_target="tpu_custom_call" | custom-call | flops 1000 | bytes 1000 | tf_op jit(solution)/shard_map/pallas_call | solution.py:390
  60.4 0.0 copy-start.4
  60.4 0.8 copy-done.4
  61.2 0.7 copy-done.7
  61.9 0.0 all-to-all-done.1.edge_ref
  61.9 1.0 %copy-done.5 = bf16[256,1024]{1,0:T(8,128)(2,1)S(1)} copy-done((bf16[256,1024]{1,0:T(8,128)(2,1)S(1)}, bf16[256,1024]{1,0:T(8,128)(2,1)}, u32[]{:S(2)}) %copy-start.5) | copy-done | bytes 524312
  63.0 0.9 %copy-done.8 = f32[256,256]{1,0:T(8,128)S(1)} copy-done((f32[256,256]{1,0:T(8,128)S(1)}, f32[256,256]{1,0:T(8,128)}, u32[]{:S(2)}) %copy-start.8) | copy-done | bytes 262168
  63.9 0.4 shard_map.99.refs_0_
  64.3 0.0 copy-start.2
  64.3 2.6 %collective-permute-start.2 = (bf16[256,256]{1,0:T(8,128)(2,1)S(1)}, bf16[256,256]{1,0:T(8,128)(2,1)S(1)}, u32[]{:S(2)}, u32[]{:S(2)}) collective-permute-start(bf16[256,256]{1,0:T(8,128)(2,1)S(1)} %shard_map.99.refs_0_), channel_id=1, source_target_pairs={{0,6},{1,7},{2,0},{3,1},{4,2},{5,3},{6,4},{7,5},{8,14},{9,15},{10,... | collective-permute-start | bytes 393224 | tf_op jit(solution)/shard_map/ppermute | solution.py:351
  67.0 0.5 collective-permute-start.1
  67.5 0.1 collective-permute-start
  67.7 0.0 collective-permute-done.4.refs_6_
  67.7 1.1 %slice.8 = bf16[1024,256]{1,0:T(8,128)(2,1)S(1)} slice(bf16[3072,256]{1,0:T(8,128)(2,1)} %collective-permute-done.4.refs_6_), slice={[2048:3072], [0:256]} | slice | bytes 1048576 | tf_op jit(solution)/shard_map/slice | solution.py:381
  68.7 2.6 %collective-permute-start.5 = (bf16[1024,256]{1,0:T(8,128)(2,1)S(1)}, bf16[1024,256]{1,0:T(8,128)(2,1)S(1)}, u32[]{:S(2)}, u32[]{:S(2)}) collective-permute-start(bf16[1024,256]{1,0:T(8,128)(2,1)S(1)} %slice.8), channel_id=1, source_target_pairs={{0,6},{1,7},{2,0},{3,1},{4,2},{5,3},{6,4},{7,5},{8,14},{9,15},{10,... | collective-permute-start | bytes 1572872 | tf_op jit(solution)/shard_map/ppermute | solution.py:351
  71.3 0.0 collective-permute-done.6.refs_5_
  71.3 0.0 collective-permute-done.2.refs_3_
  71.4 1.6 %collective-permute-done.1.refs_2_ = bf16[256,256]{1,0:T(8,128)(2,1)S(1)} collective-permute-done((bf16[256,256]{1,0:T(8,128)(2,1)S(1)}, bf16[256,256]{1,0:T(8,128)(2,1)S(1)}, u32[]{:S(2)}, u32[]{:S(2)}) %collective-permute-start.1) | collective-permute-done | bytes 131104 | tf_op jit(solution)/shard_map/ppermute | solution.py:351
  73.0 3.6 %collective-permute-done.refs_1_ = bf16[256,256]{1,0:T(8,128)(2,1)S(1)} collective-permute-done((bf16[256,256]{1,0:T(8,128)(2,1)S(1)}, bf16[256,256]{1,0:T(8,128)(2,1)S(1)}, u32[]{:S(2)}, u32[]{:S(2)}) %collective-permute-start) | collective-permute-done | bytes 131104 | tf_op jit(solution)/shard_map/ppermute | solution.py:351
  76.5 0.0 copy-done.2
  76.5 0.0 copy-done.11
  76.6 0.6 copy-done.13
  77.2 3.1 %shard_map.101 = bf16[256,1024]{1,0:T(8,128)(2,1)} custom-call(bf16[8192,128]{1,0:T(8,128)(2,1)} %w_b_hbm.5, bf16[8192,128]{1,0:T(8,128)(2,1)} %w_c_hbm.5, bf16[256,256]{1,0:T(8,128)(2,1)} %copy-done.2, bf16[256,256]{1,0:T(8,128)(2,1)} %copy-done.13, bf16[256,256]{1,0:T(8,128)(2,1)} %copy-done.12, bf16[256,256]{1,0:T(8,128)(2,1)} %copy-done.11, ...), custom_call_target="tpu_custom_call" | custom-call | flops 1000 | bytes 1000 | tf_op jit(solution)/shard_map/pallas_call | solution.py:416
  80.3 1.5 %collective-permute-start.7 = (bf16[256,1024]{1,0:T(8,128)(2,1)}, bf16[256,1024]{1,0:T(8,128)(2,1)S(1)}, u32[]{:S(2)}, u32[]{:S(2)}) collective-permute-start(bf16[256,1024]{1,0:T(8,128)(2,1)} %shard_map.101), channel_id=1, source_target_pairs={{0,1},{1,0},{2,3},{3,2},{4,5},{5,4},{6,7},{7,6},{8,9},{9,8},{10,11... | collective-permute-start | bytes 1572872 | tf_op jit(solution)/shard_map/ppermute | solution.py:430
  81.8 1.2 %shard_map.98 = bf16[256,1024]{1,0:T(8,128)(2,1)} custom-call(bf16[256,128]{1,0:T(8,128)(2,1)S(1)} %copy-done.3, bf16[256,32]{1,0:T(8,128)(2,1)S(1)} %get-tuple-element.10.leave_ref, f32[256,1024]{1,0:T(8,128)S(1)} %get-tuple-element.11.local_ref, bf16[32,64,128]{2,1,0:T(8,128)(2,1)S(1)} %all-to-all-done.1.edge_ref), custom_call_target="tpu_custom_call" | custom-call | flops 1000 | bytes 1000 | tf_op jit(solution)/shard_map/pallas_call | solution.py:411
  83.0 0.0 collective-permute-done.5.refs_5_
  83.0 0.8 copy-done.14
  83.8 3.2 %shard_map.100 = f32[256,1024]{1,0:T(8,128)} custom-call(bf16[8192,128]{1,0:T(8,128)(2,1)} %w_b_hbm.5, bf16[8192,128]{1,0:T(8,128)(2,1)} %w_c_hbm.5, bf16[256,256]{1,0:T(8,128)(2,1)} %copy-done.2, bf16[256,256]{1,0:T(8,128)(2,1)} %copy-done.13, bf16[256,256]{1,0:T(8,128)(2,1)} %copy-done.12, bf16[256,256]{1,0:T(8,128)(2,1)} %copy-done.11, ...), custom_call_target="tpu_custom_call" | custom-call | flops 1000 | bytes 1000 | tf_op jit(solution)/shard_map/pallas_call | solution.py:416
  87.1 0.0 collective-permute-done.7
  87.1 2.2 %add_convert_fusion = bf16[256,1024]{1,0:T(8,128)(2,1)} fusion(f32[256,1024]{1,0:T(8,128)} %shard_map.100, bf16[256,1024]{1,0:T(8,128)(2,1)S(1)} %collective-permute-done.7), kind=kLoop, calls=%fused_computation | loop fusion | flops 786432 | bytes 2097152 | tf_op jit(solution)/shard_map/convert_element_type | solution.py:431
  (12 shorter events, 0.0 us)
Async XLA Ops:
  6.1 29.5 %all-to-all-start = ((bf16[32,72,128]{2,1,0:T(8,128)(2,1)}), bf16[32,72,128]{2,1,0:T(8,128)(2,1)S(1)}, u32[]{:S(2)}, u32[]{:S(2)}) async-start(bf16[32,72,128]{2,1,0:T(8,128)(2,1)} %get-tuple-element.12), calls=%async_computation | async-start | bytes 1179648 | tf_op jit(solution)/shard_map/all_to_all | solution.py:382
  18.2 36.5 %collective-permute-start.3 = (bf16[3072,256]{1,0:T(8,128)(2,1)}, bf16[3072,256]{1,0:T(8,128)(2,1)}, u32[]{:S(2)}, u32[]{:S(2)}) collective-permute-start(bf16[3072,256]{1,0:T(8,128)(2,1)} %get-tuple-element.16), channel_id=1, source_target_pairs={{0,2},{1,3},{2,4},{3,5},{4,6},{5,7},{6,0},{7,1},{8,10},{9,11},{10,... | collective-permute-start | bytes 4718600 | tf_op jit(solution)/shard_map/ppermute | solution.py:351
  19.5 37.2 %copy-start = (bf16[256,1024]{1,0:T(8,128)(2,1)S(1)}, bf16[256,1024]{1,0:T(8,128)(2,1)}, u32[]{:S(2)}) copy-start(bf16[256,1024]{1,0:T(8,128)(2,1)} %x_hbm.3) | copy-start | bytes 1572868
  19.5 37.2 %copy-start.1 = (bf16[256,1024]{1,0:T(8,128)(2,1)S(1)}, bf16[256,1024]{1,0:T(8,128)(2,1)}, u32[]{:S(2)}) copy-start(bf16[256,1024]{1,0:T(8,128)(2,1)} %dy_hbm.3) | copy-start | bytes 1572868
  19.5 37.2 %copy-start.3 = (bf16[256,128]{1,0:T(8,128)(2,1)S(1)}, bf16[256,128]{1,0:T(8,128)(2,1)}, u32[]{:S(2)}) copy-start(bf16[256,128]{1,0:T(8,128)(2,1)} %b_ref.1) | copy-start | bytes 196612
  19.5 37.2 %copy-start.6 = (bf16[256,128]{1,0:T(8,128)(2,1)S(1)}, bf16[256,128]{1,0:T(8,128)(2,1)}, u32[]{:S(2)}) copy-start(bf16[256,128]{1,0:T(8,128)(2,1)} %c_hbm.3) | copy-start | bytes 196612
  19.5 37.2 %copy-start.9 = (f32[16,256]{1,0:T(8,128)S(1)}, f32[16,256]{1,0:T(8,128)}, u32[]{:S(2)}) copy-start(f32[16,256]{1,0:T(8,128)} %log_hbm.3) | copy-start | bytes 49156
  19.6 37.2 %copy-start.10 = (s32[4]{0:T(128)S(1)}, s32[4]{0:T(128)}, u32[]{:S(2)}) copy-start(s32[4]{0:T(128)} %lengths_hbm.3) | copy-start | bytes 52
  19.6 48.1 %collective-permute-start.4 = (bf16[3072,256]{1,0:T(8,128)(2,1)}, bf16[3072,256]{1,0:T(8,128)(2,1)}, u32[]{:S(2)}, u32[]{:S(2)}) collective-permute-start(bf16[3072,256]{1,0:T(8,128)(2,1)} %get-tuple-element.17), channel_id=1, source_target_pairs={{0,6},{1,7},{2,0},{3,1},{4,2},{5,3},{6,4},{7,5},{8,14},{9,15},{10,... | collective-permute-start | bytes 4718600 | tf_op jit(solution)/shard_map/ppermute | solution.py:351
  36.5 25.4 %all-to-all-start.1 = ((bf16[32,64,128]{2,1,0:T(8,128)(2,1)}), bf16[32,64,128]{2,1,0:T(8,128)(2,1)S(1)}, u32[]{:S(2)}, u32[]{:S(2)}) async-start(bf16[32,64,128]{2,1,0:T(8,128)(2,1)} %shard_map.97), calls=%async_computation.1 | async-start | bytes 1048576 | tf_op jit(solution)/shard_map/all_to_all | solution.py:389
  56.6 14.7 %collective-permute-start.6 = (bf16[1024,256]{1,0:T(8,128)(2,1)}, bf16[1024,256]{1,0:T(8,128)(2,1)}, u32[]{:S(2)}, u32[]{:S(2)}) collective-permute-start(bf16[1024,256]{1,0:T(8,128)(2,1)} %slice.9), channel_id=1, source_target_pairs={{0,2},{1,3},{2,4},{3,5},{4,6},{5,7},{6,0},{7,1},{8,10},{9,11},{10,... | collective-permute-start | bytes 1572872 | tf_op jit(solution)/shard_map/ppermute | solution.py:351
  60.4 0.8 copy-start.4
  61.2 0.7 copy-start.7
  61.9 1.0 %copy-start.5 = (bf16[256,1024]{1,0:T(8,128)(2,1)S(1)}, bf16[256,1024]{1,0:T(8,128)(2,1)}, u32[]{:S(2)}) copy-start(bf16[256,1024]{1,0:T(8,128)(2,1)} %copy-done.4) | copy-start | bytes 1572868
  63.0 0.9 %copy-start.8 = (f32[256,256]{1,0:T(8,128)S(1)}, f32[256,256]{1,0:T(8,128)}, u32[]{:S(2)}) copy-start(f32[256,256]{1,0:T(8,128)} %copy-done.7) | copy-start | bytes 786436
  64.3 12.2 %copy-start.2 = (bf16[256,256]{1,0:T(8,128)(2,1)}, bf16[256,256]{1,0:T(8,128)(2,1)S(1)}, u32[]{:S(2)}) copy-start(bf16[256,256]{1,0:T(8,128)(2,1)S(1)} %shard_map.99.refs_0_) | copy-start | bytes 393220
  64.3 7.0 %collective-permute-start.2 = (bf16[256,256]{1,0:T(8,128)(2,1)S(1)}, bf16[256,256]{1,0:T(8,128)(2,1)S(1)}, u32[]{:S(2)}, u32[]{:S(2)}) collective-permute-start(bf16[256,256]{1,0:T(8,128)(2,1)S(1)} %shard_map.99.refs_0_), channel_id=1, source_target_pairs={{0,6},{1,7},{2,0},{3,1},{4,2},{5,3},{6,4},{7,5},{8,14},{9,15},{10,... | collective-permute-start | bytes 393224 | tf_op jit(solution)/shard_map/ppermute | solution.py:351
  67.0 6.0 %collective-permute-start.1 = (bf16[256,256]{1,0:T(8,128)(2,1)S(1)}, bf16[256,256]{1,0:T(8,128)(2,1)S(1)}, u32[]{:S(2)}, u32[]{:S(2)}) collective-permute-start(bf16[256,256]{1,0:T(8,128)(2,1)S(1)} %shard_map.99.refs_0_), channel_id=1, source_target_pairs={{0,4},{1,5},{2,6},{3,7},{4,0},{5,1},{6,2},{7,3},{8,12},{9,13},{10,... | collective-permute-start | bytes 393224 | tf_op jit(solution)/shard_map/ppermute | solution.py:351
  67.5 9.0 %collective-permute-start = (bf16[256,256]{1,0:T(8,128)(2,1)S(1)}, bf16[256,256]{1,0:T(8,128)(2,1)S(1)}, u32[]{:S(2)}, u32[]{:S(2)}) collective-permute-start(bf16[256,256]{1,0:T(8,128)(2,1)S(1)} %shard_map.99.refs_0_), channel_id=1, source_target_pairs={{0,2},{1,3},{2,4},{3,5},{4,6},{5,7},{6,0},{7,1},{8,10},{9,11},{10,... | collective-permute-start | bytes 393224 | tf_op jit(solution)/shard_map/ppermute | solution.py:351
  68.7 14.3 %collective-permute-start.5 = (bf16[1024,256]{1,0:T(8,128)(2,1)S(1)}, bf16[1024,256]{1,0:T(8,128)(2,1)S(1)}, u32[]{:S(2)}, u32[]{:S(2)}) collective-permute-start(bf16[1024,256]{1,0:T(8,128)(2,1)S(1)} %slice.8), channel_id=1, source_target_pairs={{0,6},{1,7},{2,0},{3,1},{4,2},{5,3},{6,4},{7,5},{8,14},{9,15},{10,... | collective-permute-start | bytes 1572872 | tf_op jit(solution)/shard_map/ppermute | solution.py:351
  71.4 5.2 %copy-start.11 = (bf16[256,256]{1,0:T(8,128)(2,1)}, bf16[256,256]{1,0:T(8,128)(2,1)S(1)}, u32[]{:S(2)}) copy-start(bf16[256,256]{1,0:T(8,128)(2,1)S(1)} %collective-permute-done.2.refs_3_) | copy-start | bytes 393220
  73.0 3.6 %copy-start.12 = (bf16[256,256]{1,0:T(8,128)(2,1)}, bf16[256,256]{1,0:T(8,128)(2,1)S(1)}, u32[]{:S(2)}) copy-start(bf16[256,256]{1,0:T(8,128)(2,1)S(1)} %collective-permute-done.1.refs_2_) | copy-start | bytes 393220
  76.6 0.7 copy-start.13
  80.3 6.8 %collective-permute-start.7 = (bf16[256,1024]{1,0:T(8,128)(2,1)}, bf16[256,1024]{1,0:T(8,128)(2,1)S(1)}, u32[]{:S(2)}, u32[]{:S(2)}) collective-permute-start(bf16[256,1024]{1,0:T(8,128)(2,1)} %shard_map.101), channel_id=1, source_target_pairs={{0,1},{1,0},{2,3},{3,2},{4,5},{5,4},{6,7},{7,6},{8,9},{9,8},{10,11... | collective-permute-start | bytes 1572872 | tf_op jit(solution)/shard_map/ppermute | solution.py:430
  83.0 0.8 copy-start.14

commit v4 on v3

--- a/solution.py
+++ b/solution.py
@@ -90,14 +90,15 @@
     b_hbm,
     dy_hbm,
     c_hbm,
-    w_b_hbm,
-    w_c_hbm,
     out_ref,
-    *refs,
+    lengths_ref,
+    log_ref,
+    x_ref,
+    b_ref,
+    dy_ref,
+    c_ref,
+    sems,
 ):
-    sent_refs = refs[:-10]
-    lengths_ref, log_ref, x_ref, b_ref, dy_ref, c_ref, passing_ref = refs[-10:-3]
-    sems, passing_sems, sent_sems = refs[-3:]
     loads = fetch(
         [
             (lengths_hbm, lengths_ref),
@@ -109,17 +110,6 @@
         ],
         sems,
     )
-    columns = passing_ref.shape[1]
-    me = lax.axis_index("tp")
-    core, chips = lax.rem(me, CORES), lax.axis_size("tp") // CORES
-    pairs = []
-    for at, (step, sibling) in enumerate(ROUTE):
-        half = 1 - core if sibling else core
-        target = lax.rem(me // CORES + step, chips)
-        from_row = pl.ds(pl.multiple_of((target * CORES + half) * columns, columns), columns)
-        pairs.append((w_b_hbm.at[from_row, :], passing_ref.at[at, :, pl.ds(0, STATE)]))
-        pairs.append((w_c_hbm.at[from_row, :], passing_ref.at[at, :, pl.ds(STATE, STATE)]))
-    passing = fetch(pairs, passing_sems)
     slices = out_ref.shape[0]
     rows = WIDE // slices
     loads[0].wait()
@@ -127,23 +117,12 @@
     _, _, _, _, enter, leave, total = token_vectors(log_ref, lengths_ref)
     enter_cols = split_columns(enter)
     leave_cols = split_columns(leave)
-    sends = []
     width = 2 * LANES
     for side, (wide_ref, narrow_ref, cols) in enumerate(
         ((x_ref, b_ref, leave_cols), (dy_ref, c_ref, enter_cols))
     ):
         loads[2 + 2 * side].wait()
         loads[3 + 2 * side].wait()
-        if side:
-            for copy in passing:
-                copy.wait()
-            sends = fetch(
-                [
-                    (passing_ref.at[at], sent_refs[at // 3].at[pl.ds(at % 3 * columns, columns), :])
-                    for at in range(len(ROUTE))
-                ],
-                sent_sems,
-            )
         narrow = narrow_ref[...]
         for chunk in range(WIDE // width):
             low = chunk * width
@@ -161,11 +140,32 @@
         tile = jnp.where(iota((8, STATE), 0) == 0, high[head : head + 1], rest).astype(LOW)
         for part in range(per_head):
             out_ref[head * per_head + part, 2 * rows : 2 * rows + 8, :] = tile
+
+
+def stage_kernel(_, w_b_hbm, w_c_hbm, up_hbm, down_hbm, passing_ref, passing_sems, sent_sems):
+    columns = passing_ref.shape[1]
+    me = lax.axis_index("tp")
+    core, chips = lax.rem(me, CORES), lax.axis_size("tp") // CORES
+    pairs = []
+    for at, (step, sibling) in enumerate(ROUTE):
+        half = 1 - core if sibling else core
+        target = lax.rem(me // CORES + step, chips)
+        from_row = pl.ds(pl.multiple_of((target * CORES + half) * columns, columns), columns)
+        pairs.append((w_b_hbm.at[from_row, :], passing_ref.at[at, :, pl.ds(0, STATE)]))
+        pairs.append((w_c_hbm.at[from_row, :], passing_ref.at[at, :, pl.ds(STATE, STATE)]))
+    loads = fetch(pairs, passing_sems)
+    sends = []
+    for at in range(len(ROUTE)):
+        target = (up_hbm, down_hbm)[at // 3].at[pl.ds(at % 3 * columns, columns), :]
+        loads[2 * at].wait()
+        loads[2 * at + 1].wait()
+        sends.append(pltpu.make_async_copy(passing_ref.at[at], target, sent_sems.at[at]))
+        sends[-1].start()
     for send in sends:
         send.wait()
 
 
-def scan_kernel(in_ref, out_ref):
+def scan_kernel(in_ref, _, out_ref):
     devices, rows = out_ref.shape[0], out_ref.shape[1] // 2
     decays = []
     for at in range(devices):
@@ -306,7 +306,8 @@
 
 
 def project_kernel(w_b_hbm, w_c_hbm, *refs, sibling):
-    grads, (up, twice, down), (out_ref, grads_ref, weights_ref, sems) = refs[:4], refs[4:7], refs[7:]
+    grads, (up, up_twice, down, down_twice) = refs[:4], refs[4:8]
+    received, (out_ref, grads_ref, weights_ref, received_ref, sems) = refs[8:-5], refs[-5:]
     columns = out_ref.shape[1]
     me = lax.axis_index("tp")
     core = lax.rem(me, CORES)
@@ -318,16 +319,21 @@
         (w_c_hbm.at[from_row, :], weights_ref.at[0, :, pl.ds(STATE, STATE)]),
         (grads[0], grads_ref.at[0]),
     ]
+    twice = up_twice if sibling else down_twice
     for at, weight in enumerate((up.at[of_half, :], twice, down.at[of_half, :])):
         pairs.append((grads[at + 1], grads_ref.at[at + 1]))
         pairs.append((weight, weights_ref.at[at + 1]))
+    pairs += [(ref, received_ref) for ref in received]
     loads = fetch(pairs, sems)
     total = 0.0
     for at in range(4):
         for load in loads[:3] if at == 0 else loads[1 + 2 * at : 3 + 2 * at]:
             load.wait()
         total += mul(grads_ref[at], weights_ref[at], NT)
-    out_ref[...] = total.astype(out_ref.dtype)
+    for load in loads[9:]:
+        load.wait()
+        total += received_ref[...].astype(FULL)
+    out_ref[...] = total.astype(LOW)
 
 
 BLOCK = pl.BlockSpec(memory_space=pltpu.VMEM)
@@ -365,28 +371,26 @@
         pltpu.VMEM(a.shape, a.dtype) for a in local[1:]
     ]
     blocks = len(ROUTE)
-    summary, *sent = call(
+    summary = call(
         summary_kernel,
-        [shape((devices, 2 * rows + 8, STATE), LOW)]
-        + [shape((blocks // 2 * columns, 2 * STATE), LOW)] * 2,
-        [HBM] * 8,
+        shape((devices, 2 * rows + 8, STATE), LOW),
+        [HBM] * 6,
         LARGE_VMEM,
-        [BLOCK, HBM, HBM],
-        held
-        + [pltpu.VMEM((blocks, columns, 2 * STATE), LOW)]
-        + [dma((6,)), dma((2 * blocks,)), dma((blocks,))],
-    )(*local, w_b, w_c)
+        BLOCK,
+        held + [dma((6,))],
+    )(*local)
+    sent = call(
+        stage_kernel,
+        [shape((blocks // 2 * columns, 2 * STATE), LOW)] * 2,
+        [HBM] * 3,
+        LARGE_VMEM,
+        [HBM, HBM],
+        [pltpu.VMEM((blocks, columns, 2 * STATE), LOW), dma((2 * blocks,)), dma((blocks,))],
+    )(summary, w_b, w_c)
     up, down = along_x(sent[0], 1), along_x(sent[1], 3)
     up_twice = along_x(up[2 * columns :], 1)
     down_twice = along_x(down[2 * columns :], 3)
     summary = lax.all_to_all(summary, "seq", 0, 0)
-    edges = call(
-        scan_kernel,
-        shape((devices, 2 * rows, STATE), LOW),
-        [BLOCK],
-        4 * MIB,
-    )(summary)
-    edges = lax.all_to_all(edges, "seq", 0, 0)
     grad_x, grad_bc, x_weighted, dy_weighted, leave_cols = call(
         local_kernel,
         [
@@ -401,6 +405,13 @@
         [BLOCK] * 5,
         held + [dma((6,))],
     )(*local)
+    edges = call(
+        scan_kernel,
+        shape((devices, 2 * rows, STATE), LOW),
+        [BLOCK, HBM],
+        4 * MIB,
+    )(summary, leave_cols)
+    edges = lax.all_to_all(edges, "seq", 0, 0)
     grad_bc = call(
         grad_bc_kernel,
         shape((tokens, 2 * STATE), LOW),
@@ -412,23 +423,23 @@
         grad_x_kernel, shape((tokens, WIDE), LOW), [BLOCK] * 4, 8 * MIB
     )(in_b, leave_cols, grad_x, edges)
 
-    def project(sibling, kind):
+    def project(*received):
         return call(
-            functools.partial(project_kernel, sibling=sibling),
-            shape((tokens, columns), kind),
-            [HBM] * 9,
+            functools.partial(project_kernel, sibling=not received),
+            shape((tokens, columns), LOW),
+            [HBM] * (10 + len(received)),
             LARGE_VMEM,
             BLOCK,
             [
                 pltpu.VMEM((4, tokens, 2 * STATE), LOW),
                 pltpu.VMEM((4, columns, 2 * STATE), LOW),
-                dma((9,)),
+                pltpu.VMEM((tokens, columns), LOW),
+                dma((9 + len(received),)),
             ],
-        )(w_b, w_c, grad_bc, *others, up, up_twice if sibling else down_twice, down)
+        )(w_b, w_c, grad_bc, *others, up, up_twice, down, down_twice, *received)
 
     partner = [(at, at ^ 1) for at in range(lax.axis_size("tp"))]
-    received = lax.ppermute(project(True, LOW), "tp", partner)
-    grad_input = (project(False, FULL) + received.astype(FULL)).astype(LOW)
+    grad_input = project(lax.ppermute(project(), "tp", partner))
     return grad_x, grad_input
 
 

time: 90.9 us -> 91.1 us (level); the launches traced: 89.2 us -> 90.6 us
  waiting for transfers between devices: 32.4 us -> 35.3 us
  other arithmetic: 2.17 us -> 0 us
  local copies, waits for them, and re-layouts: 7.92 us -> 5.93 us
  starting transfers between devices: 27.9 us -> 29.5 us
  Pallas kernels: 18 us -> 19.2 us
    ppermute x7, waiting for transfers between devices: 17.9 us -> 26.8 us  [along_x(): lax.ppermute(value, 'tp', [(at, (at + CORES * step) % devices) for at in...]
    all_to_all x1, waiting for transfers between devices: 14.5 us -> 7.94 us  [per_device(): summary = lax.all_to_all(summary, 'seq', 0, 0)]
    ppermute x1, starting transfers between devices: 1.52 us -> 5 us  [per_device(): grad_input = project(lax.ppermute(project(), 'tp', partner))]
    unnamed x30 -> x22, local copies, waits for them, and re-layouts: 4.95 us -> 2.2 us
    convert_element_type x1 -> x0, other arithmetic: 2.17 us -> none  [per_device(): grad_input = (project(False, FULL) + received.astype(FULL)).astype(LOW)]
    ppermute x7, starting transfers between devices: 8.87 us -> 6.98 us  [along_x(): lax.ppermute(value, 'tp', [(at, (at + CORES * step) % devices) for at in...]
    pallas_call x4 -> x5, Pallas kernels: 12.7 us -> 13.9 us  [the longest x2 6.22 us: project(): call(functools.partial(project_kernel, sibling=not received), shape((toke...]
  transfers between devices with their start and end apart: 10 -> 10, of which waited for: 4 -> 6; matrix products, arithmetic and copies ran while one was open for 3% -> 4% of each run, Pallas kernels for 14% -> 10%
where the time goes in v4:
time: 91.1 us; the launch traced here: 90.6 us
  waiting for transfers between devices  35.3 us (39%)
  starting transfers between devices  29.5 us (32%)
  Pallas kernels  19.2 us (21%)
  local copies, waits for them, and re-layouts  5.93 us (7%)
    ppermute x7, waiting for transfers between devices, along_x(): lax.ppermute(value, 'tp', [(at, (at + CORES * step) % devices) for at in...  26.8 us
    all_to_all x1, starting transfers between devices, per_device(): summary = lax.all_to_all(summary, 'seq', 0, 0)  12 us
    all_to_all x1, waiting for transfers between devices, per_device(): summary = lax.all_to_all(summary, 'seq', 0, 0)  7.94 us
    ppermute x7, starting transfers between devices, along_x(): lax.ppermute(value, 'tp', [(at, (at + CORES * step) % devices) for at in...  6.98 us
    pallas_call x2, Pallas kernels, project(): call(functools.partial(project_kernel, sibling=not received), shape((toke...  6.22 us
    all_to_all x1, starting transfers between devices, per_device(): edges = lax.all_to_all(edges, 'seq', 0, 0)  5.46 us
    ppermute x1, starting transfers between devices, per_device(): grad_input = project(lax.ppermute(project(), 'tp', partner))  5 us
    pallas_call x1, Pallas kernels, per_device(): call(summary_kernel, shape((devices, 2 * rows + 8, STATE), LOW), [HBM] *...  3.71 us
  transfers between devices with their start and end apart: 10, of which 6 were waited for; matrix products, arithmetic and copies ran while one was open for 4% of the time, Pallas kernels for 10%

profile of v4, /device:TPU:1, one launch (start us, length us, event | category | flops | bytes accessed | tf_op | source)
XLA Modules:
  0.0 90.6 jit_solution(13205859635819802398)
XLA Ops:
  0.6 3.7 %shard_map.96._ = bf16[32,72,128]{2,1,0:T(8,128)(2,1)} custom-call(s32[4]{0:T(128)} %lengths_hbm.3, f32[16,256]{1,0:T(8,128)} %log_hbm.3, bf16[256,1024]{1,0:T(8,128)(2,1)} %x_hbm.3, bf16[256,128]{1,0:T(8,128)(2,1)} %b_ref.1, bf16[256,1024]{1,0:T(8,128)(2,1)} %dy_hbm.3, bf16[256,128]{1,0:T(8,128)(2,1)} %c_hbm.3), custom_call_target="tpu_custom_call" | custom-call | flops 1000 | bytes 1000 | tf_op jit(solution)/shard_map/pallas_call | solution.py:374
  4.3 12.0 %all-to-all-start = ((bf16[32,72,128]{2,1,0:T(8,128)(2,1)}), bf16[32,72,128]{2,1,0:T(8,128)(2,1)S(1)}, u32[]{:S(2)}, u32[]{:S(2)}) async-start(bf16[32,72,128]{2,1,0:T(8,128)(2,1)} %shard_map.96._), calls=%async_computation | async-start | bytes 1179648 | tf_op jit(solution)/shard_map/all_to_all | solution.py:393
  16.4 0.0 copy-start
  16.4 0.0 copy-start.1
  16.4 0.0 copy-start.3
  16.4 0.0 copy-start.4
  16.4 0.0 copy-start.5
  16.5 0.0 copy-start.6
  16.5 3.0 %shard_map.100 = (bf16[3072,256]{1,0:T(8,128)(2,1)}, bf16[3072,256]{1,0:T(8,128)(2,1)}) custom-call(bf16[32,72,128]{2,1,0:T(8,128)(2,1)} %shard_map.96._, bf16[8192,128]{1,0:T(8,128)(2,1)} %w_b_hbm.5, bf16[8192,128]{1,0:T(8,128)(2,1)} %w_c_hbm.5), custom_call_target="tpu_custom_call" | custom-call | flops 1000 | bytes 1000 | tf_op jit(solution)/shard_map/pallas_call | solution.py:382
  19.5 1.3 %collective-permute-start.3 = (bf16[3072,256]{1,0:T(8,128)(2,1)}, bf16[3072,256]{1,0:T(8,128)(2,1)}, u32[]{:S(2)}, u32[]{:S(2)}) collective-permute-start(bf16[3072,256]{1,0:T(8,128)(2,1)} %get-tuple-element.14), channel_id=1, source_target_pairs={{0,2},{1,3},{2,4},{3,5},{4,6},{5,7},{6,0},{7,1},{8,10},{9,11},{10,... | collective-permute-start | bytes 4718600 | tf_op jit(solution)/shard_map/ppermute | solution.py:357
  20.8 1.5 %collective-permute-start.5 = (bf16[3072,256]{1,0:T(8,128)(2,1)}, bf16[3072,256]{1,0:T(8,128)(2,1)}, u32[]{:S(2)}, u32[]{:S(2)}) collective-permute-start(bf16[3072,256]{1,0:T(8,128)(2,1)} %get-tuple-element.15), channel_id=1, source_target_pairs={{0,6},{1,7},{2,0},{3,1},{4,2},{5,3},{6,4},{7,5},{8,14},{9,15},{10,... | collective-permute-start | bytes 4718600 | tf_op jit(solution)/shard_map/ppermute | solution.py:357
  22.2 0.0 copy-done
  22.2 0.0 copy-done.1
  22.2 0.0 copy-done.3
  22.2 0.0 copy-done.4
  22.2 0.0 copy-done.5
  22.2 0.0 copy-done.6
  22.2 3.7 %shard_map.95 = (f32[256,1024]{1,0:T(8,128)S(1)}, f32[256,256]{1,0:T(8,128)S(1)}, bf16[256,1024]{1,0:T(8,128)(2,1)S(1)}, bf16[256,1024]{1,0:T(8,128)(2,1)S(1)}, bf16[256,32]{1,0:T(8,128)(2,1)S(1)}) custom-call(s32[4]{0:T(128)S(1)} %copy-done.6, f32[16,256]{1,0:T(8,128)S(1)} %copy-done.5, bf16[256,1024]{1,0:T(8,128)(2,1)S(1)} %copy-done, ...), custom_call_target="tpu_custom_call" | custom-call | flops 1000 | bytes 1000 | tf_op jit(solution)/shard_map/pallas_call | solution.py:394
  25.9 7.9 %all-to-all-done.in_ref = bf16[32,72,128]{2,1,0:T(8,128)(2,1)S(1)} async-done(((bf16[32,72,128]{2,1,0:T(8,128)(2,1)}), bf16[32,72,128]{2,1,0:T(8,128)(2,1)S(1)}, u32[]{:S(2)}, u32[]{:S(2)}) %all-to-all-start) | async-done | bytes 589856 | tf_op jit(solution)/shard_map/all_to_all | solution.py:393
  33.9 0.9 %shard_map.97 = bf16[32,64,128]{2,1,0:T(8,128)(2,1)} custom-call(bf16[32,72,128]{2,1,0:T(8,128)(2,1)S(1)} %all-to-all-done.in_ref, bf16[256,32]{1,0:T(8,128)(2,1)S(1)} %get-tuple-element.9._.leave_ref), custom_call_target="tpu_custom_call" | custom-call | flops 1000 | bytes 1000 | tf_op jit(solution)/shard_map/pallas_call | solution.py:408
  34.8 5.5 %all-to-all-start.1 = ((bf16[32,64,128]{2,1,0:T(8,128)(2,1)}), bf16[32,64,128]{2,1,0:T(8,128)(2,1)S(1)}, u32[]{:S(2)}, u32[]{:S(2)}) async-start(bf16[32,64,128]{2,1,0:T(8,128)(2,1)} %shard_map.97), calls=%async_computation.1 | async-start | bytes 1048576 | tf_op jit(solution)/shard_map/all_to_all | solution.py:414
  40.3 15.7 %collective-permute-done.3.refs_4_ = bf16[3072,256]{1,0:T(8,128)(2,1)} collective-permute-done((bf16[3072,256]{1,0:T(8,128)(2,1)}, bf16[3072,256]{1,0:T(8,128)(2,1)}, u32[]{:S(2)}, u32[]{:S(2)}) %collective-permute-start.3) | collective-permute-done | bytes 1572896 | tf_op jit(solution)/shard_map/ppermute | solution.py:357
  56.0 1.9 %slice.8 = bf16[1024,256]{1,0:T(8,128)(2,1)} slice(bf16[3072,256]{1,0:T(8,128)(2,1)} %collective-permute-done.3.refs_4_), slice={[2048:3072], [0:256]} | slice | bytes 1048576 | tf_op jit(solution)/shard_map/slice | solution.py:391
  57.9 0.0 collective-permute-start.4
  57.9 0.0 collective-permute-done.5.refs_6_
  57.9 1.9 %slice.9 = bf16[1024,256]{1,0:T(8,128)(2,1)} slice(bf16[3072,256]{1,0:T(8,128)(2,1)} %collective-permute-done.5.refs_6_), slice={[2048:3072], [0:256]} | slice | bytes 1048576 | tf_op jit(solution)/shard_map/slice | solution.py:392
  59.8 2.7 %collective-permute-start.6 = (bf16[1024,256]{1,0:T(8,128)(2,1)}, bf16[1024,256]{1,0:T(8,128)(2,1)}, u32[]{:S(2)}, u32[]{:S(2)}) collective-permute-start(bf16[1024,256]{1,0:T(8,128)(2,1)} %slice.9), channel_id=1, source_target_pairs={{0,6},{1,7},{2,0},{3,1},{4,2},{5,3},{6,4},{7,5},{8,14},{9,15},{10,... | collective-permute-start | bytes 1572872 | tf_op jit(solution)/shard_map/ppermute | solution.py:357
  62.4 0.0 all-to-all-done.1.edge_ref
  62.4 0.4 shard_map.99.refs_0_
  62.8 0.0 copy-start.2
  62.8 0.1 collective-permute-start.2
  63.0 0.5 collective-permute-start.1
  63.5 0.9 collective-permute-start
  64.4 6.8 %collective-permute-done.4.refs_5_ = bf16[1024,256]{1,0:T(8,128)(2,1)} collective-permute-done((bf16[1024,256]{1,0:T(8,128)(2,1)}, bf16[1024,256]{1,0:T(8,128)(2,1)}, u32[]{:S(2)}, u32[]{:S(2)}) %collective-permute-start.4) | collective-permute-done | bytes 524320 | tf_op jit(solution)/shard_map/ppermute | solution.py:357
  71.1 0.6 collective-permute-done.6.refs_7_
  71.8 3.7 %collective-permute-done.2.refs_3_ = bf16[256,256]{1,0:T(8,128)(2,1)S(1)} collective-permute-done((bf16[256,256]{1,0:T(8,128)(2,1)S(1)}, bf16[256,256]{1,0:T(8,128)(2,1)S(1)}, u32[]{:S(2)}, u32[]{:S(2)}) %collective-permute-start.2) | collective-permute-done | bytes 131104 | tf_op jit(solution)/shard_map/ppermute | solution.py:357
  75.5 0.0 collective-permute-done.1.refs_2_
  75.5 0.0 collective-permute-done.refs_1_
  75.5 0.0 copy-done.2
  75.5 0.6 copy-done.7
  76.1 0.1 copy-done.8
  76.2 0.7 copy-done.9
  76.8 3.1 %shard_map.101 = bf16[256,1024]{1,0:T(8,128)(2,1)} custom-call(bf16[8192,128]{1,0:T(8,128)(2,1)} %w_b_hbm.5, bf16[8192,128]{1,0:T(8,128)(2,1)} %w_c_hbm.5, bf16[256,256]{1,0:T(8,128)(2,1)} %copy-done.2, bf16[256,256]{1,0:T(8,128)(2,1)} %copy-done.9, bf16[256,256]{1,0:T(8,128)(2,1)} %copy-done.8, bf16[256,256]{1,0:T(8,128)(2,1)} %copy-done.7, ...), custom_call_target="tpu_custom_call" | custom-call | flops 1000 | bytes 1000 | tf_op jit(solution)/shard_map/pallas_call | solution.py:427
  79.9 5.0 %collective-permute-start.7 = (bf16[256,1024]{1,0:T(8,128)(2,1)}, bf16[256,1024]{1,0:T(8,128)(2,1)S(1)}, u32[]{:S(2)}, u32[]{:S(2)}) collective-permute-start(bf16[256,1024]{1,0:T(8,128)(2,1)} %shard_map.101), channel_id=1, source_target_pairs={{0,1},{1,0},{2,3},{3,2},{4,5},{5,4},{6,7},{7,6},{8,9},{9,8},{10,11... | collective-permute-start | bytes 1572872 | tf_op jit(solution)/shard_map/ppermute | solution.py:442
  84.9 1.2 %shard_map.98 = bf16[256,1024]{1,0:T(8,128)(2,1)} custom-call(bf16[256,128]{1,0:T(8,128)(2,1)S(1)} %copy-done.3, bf16[256,32]{1,0:T(8,128)(2,1)S(1)} %get-tuple-element.9._.leave_ref, f32[256,1024]{1,0:T(8,128)S(1)} %get-tuple-element.10.local_ref, bf16[32,64,128]{2,1,0:T(8,128)(2,1)S(1)} %all-to-all-done.1.edge_ref), custom_call_target="tpu_custom_call" | custom-call | flops 1000 | bytes 1000 | tf_op jit(solution)/shard_map/pallas_call | solution.py:422
  86.1 0.5 collective-permute-done.7.refs_8_
  86.7 0.8 copy-done.10
  87.5 3.2 %shard_map.102 = bf16[256,1024]{1,0:T(8,128)(2,1)} custom-call(bf16[8192,128]{1,0:T(8,128)(2,1)} %w_b_hbm.5, bf16[8192,128]{1,0:T(8,128)(2,1)} %w_c_hbm.5, bf16[256,256]{1,0:T(8,128)(2,1)} %copy-done.2, bf16[256,256]{1,0:T(8,128)(2,1)} %copy-done.9, bf16[256,256]{1,0:T(8,128)(2,1)} %copy-done.8, bf16[256,256]{1,0:T(8,128)(2,1)} %copy-done.7, ...), custom_call_target="tpu_custom_call" | custom-call | flops 1000 | bytes 1000 | tf_op jit(solution)/shard_map/pallas_call | solution.py:427
  (4 shorter events, 0.0 us)
Async XLA Ops:
  4.3 29.5 %all-to-all-start = ((bf16[32,72,128]{2,1,0:T(8,128)(2,1)}), bf16[32,72,128]{2,1,0:T(8,128)(2,1)S(1)}, u32[]{:S(2)}, u32[]{:S(2)}) async-start(bf16[32,72,128]{2,1,0:T(8,128)(2,1)} %shard_map.96._), calls=%async_computation | async-start | bytes 1179648 | tf_op jit(solution)/shard_map/all_to_all | solution.py:393
  16.4 5.8 %copy-start = (bf16[256,1024]{1,0:T(8,128)(2,1)S(1)}, bf16[256,1024]{1,0:T(8,128)(2,1)}, u32[]{:S(2)}) copy-start(bf16[256,1024]{1,0:T(8,128)(2,1)} %x_hbm.3) | copy-start | bytes 1572868
  16.4 5.8 %copy-start.1 = (bf16[256,1024]{1,0:T(8,128)(2,1)S(1)}, bf16[256,1024]{1,0:T(8,128)(2,1)}, u32[]{:S(2)}) copy-start(bf16[256,1024]{1,0:T(8,128)(2,1)} %dy_hbm.3) | copy-start | bytes 1572868
  16.4 5.8 %copy-start.3 = (bf16[256,128]{1,0:T(8,128)(2,1)S(1)}, bf16[256,128]{1,0:T(8,128)(2,1)}, u32[]{:S(2)}) copy-start(bf16[256,128]{1,0:T(8,128)(2,1)} %b_ref.1) | copy-start | bytes 196612
  16.4 5.8 %copy-start.4 = (bf16[256,128]{1,0:T(8,128)(2,1)S(1)}, bf16[256,128]{1,0:T(8,128)(2,1)}, u32[]{:S(2)}) copy-start(bf16[256,128]{1,0:T(8,128)(2,1)} %c_hbm.3) | copy-start | bytes 196612
  16.4 5.8 %copy-start.5 = (f32[16,256]{1,0:T(8,128)S(1)}, f32[16,256]{1,0:T(8,128)}, u32[]{:S(2)}) copy-start(f32[16,256]{1,0:T(8,128)} %log_hbm.3) | copy-start | bytes 49156
  16.5 5.8 %copy-start.6 = (s32[4]{0:T(128)S(1)}, s32[4]{0:T(128)}, u32[]{:S(2)}) copy-start(s32[4]{0:T(128)} %lengths_hbm.3) | copy-start | bytes 52
  19.5 36.5 %collective-permute-start.3 = (bf16[3072,256]{1,0:T(8,128)(2,1)}, bf16[3072,256]{1,0:T(8,128)(2,1)}, u32[]{:S(2)}, u32[]{:S(2)}) collective-permute-start(bf16[3072,256]{1,0:T(8,128)(2,1)} %get-tuple-element.14), channel_id=1, source_target_pairs={{0,2},{1,3},{2,4},{3,5},{4,6},{5,7},{6,0},{7,1},{8,10},{9,11},{10,... | collective-permute-start | bytes 4718600 | tf_op jit(solution)/shard_map/ppermute | solution.py:357
  20.8 37.1 %collective-permute-start.5 = (bf16[3072,256]{1,0:T(8,128)(2,1)}, bf16[3072,256]{1,0:T(8,128)(2,1)}, u32[]{:S(2)}, u32[]{:S(2)}) collective-permute-start(bf16[3072,256]{1,0:T(8,128)(2,1)} %get-tuple-element.15), channel_id=1, source_target_pairs={{0,6},{1,7},{2,0},{3,1},{4,2},{5,3},{6,4},{7,5},{8,14},{9,15},{10,... | collective-permute-start | bytes 4718600 | tf_op jit(solution)/shard_map/ppermute | solution.py:357
  34.8 27.6 %all-to-all-start.1 = ((bf16[32,64,128]{2,1,0:T(8,128)(2,1)}), bf16[32,64,128]{2,1,0:T(8,128)(2,1)S(1)}, u32[]{:S(2)}, u32[]{:S(2)}) async-start(bf16[32,64,128]{2,1,0:T(8,128)(2,1)} %shard_map.97), calls=%async_computation.1 | async-start | bytes 1048576 | tf_op jit(solution)/shard_map/all_to_all | solution.py:414
  57.9 13.3 %collective-permute-start.4 = (bf16[1024,256]{1,0:T(8,128)(2,1)}, bf16[1024,256]{1,0:T(8,128)(2,1)}, u32[]{:S(2)}, u32[]{:S(2)}) collective-permute-start(bf16[1024,256]{1,0:T(8,128)(2,1)} %slice.8), channel_id=1, source_target_pairs={{0,2},{1,3},{2,4},{3,5},{4,6},{5,7},{6,0},{7,1},{8,10},{9,11},{10,... | collective-permute-start | bytes 1572872 | tf_op jit(solution)/shard_map/ppermute | solution.py:357
  59.8 12.0 %collective-permute-start.6 = (bf16[1024,256]{1,0:T(8,128)(2,1)}, bf16[1024,256]{1,0:T(8,128)(2,1)}, u32[]{:S(2)}, u32[]{:S(2)}) collective-permute-start(bf16[1024,256]{1,0:T(8,128)(2,1)} %slice.9), channel_id=1, source_target_pairs={{0,6},{1,7},{2,0},{3,1},{4,2},{5,3},{6,4},{7,5},{8,14},{9,15},{10,... | collective-permute-start | bytes 1572872 | tf_op jit(solution)/shard_map/ppermute | solution.py:357
  62.8 12.6 %copy-start.2 = (bf16[256,256]{1,0:T(8,128)(2,1)}, bf16[256,256]{1,0:T(8,128)(2,1)S(1)}, u32[]{:S(2)}) copy-start(bf16[256,256]{1,0:T(8,128)(2,1)S(1)} %shard_map.99.refs_0_) | copy-start | bytes 393220
  62.8 12.6 %collective-permute-start.2 = (bf16[256,256]{1,0:T(8,128)(2,1)S(1)}, bf16[256,256]{1,0:T(8,128)(2,1)S(1)}, u32[]{:S(2)}, u32[]{:S(2)}) collective-permute-start(bf16[256,256]{1,0:T(8,128)(2,1)S(1)} %shard_map.99.refs_0_), channel_id=1, source_target_pairs={{0,6},{1,7},{2,0},{3,1},{4,2},{5,3},{6,4},{7,5},{8,14},{9,15},{10,... | collective-permute-start | bytes 393224 | tf_op jit(solution)/shard_map/ppermute | solution.py:357
  63.0 12.5 %collective-permute-start.1 = (bf16[256,256]{1,0:T(8,128)(2,1)S(1)}, bf16[256,256]{1,0:T(8,128)(2,1)S(1)}, u32[]{:S(2)}, u32[]{:S(2)}) collective-permute-start(bf16[256,256]{1,0:T(8,128)(2,1)S(1)} %shard_map.99.refs_0_), channel_id=1, source_target_pairs={{0,4},{1,5},{2,6},{3,7},{4,0},{5,1},{6,2},{7,3},{8,12},{9,13},{10,... | collective-permute-start | bytes 393224 | tf_op jit(solution)/shard_map/ppermute | solution.py:357
  63.5 11.9 %collective-permute-start = (bf16[256,256]{1,0:T(8,128)(2,1)S(1)}, bf16[256,256]{1,0:T(8,128)(2,1)S(1)}, u32[]{:S(2)}, u32[]{:S(2)}) collective-permute-start(bf16[256,256]{1,0:T(8,128)(2,1)S(1)} %shard_map.99.refs_0_), channel_id=1, source_target_pairs={{0,2},{1,3},{2,4},{3,5},{4,6},{5,7},{6,0},{7,1},{8,10},{9,11},{10,... | collective-permute-start | bytes 393224 | tf_op jit(solution)/shard_map/ppermute | solution.py:357
  75.5 0.6 copy-start.7
  75.5 0.7 copy-start.8
  76.2 0.7 copy-start.9
  79.9 6.8 %collective-permute-start.7 = (bf16[256,1024]{1,0:T(8,128)(2,1)}, bf16[256,1024]{1,0:T(8,128)(2,1)S(1)}, u32[]{:S(2)}, u32[]{:S(2)}) collective-permute-start(bf16[256,1024]{1,0:T(8,128)(2,1)} %shard_map.101), channel_id=1, source_target_pairs={{0,1},{1,0},{2,3},{3,2},{4,5},{5,4},{6,7},{7,6},{8,9},{9,8},{10,11... | collective-permute-start | bytes 1572872 | tf_op jit(solution)/shard_map/ppermute | solution.py:442
  86.7 0.8 copy-start.10

commit v5 on v4

--- a/solution.py
+++ b/solution.py
@@ -15,7 +15,7 @@
 WIDE = HEADS * HEAD_DIM
 PAIRS = WIDE // LANES
 CORES = 2
-ROUTE = ((1, True), (1, False), (2, True), (3, True), (3, False), (2, False))
+ROUTE = ((2, True), (2, False), (1, True), (1, False), (3, True), (3, False), (0, True), (0, False))
 LOW = jnp.bfloat16
 FULL = jnp.float32
 NN = (((1,), (0,)), ((), ()))
@@ -142,7 +142,9 @@
             out_ref[head * per_head + part, 2 * rows : 2 * rows + 8, :] = tile
 
 
-def stage_kernel(_, w_b_hbm, w_c_hbm, up_hbm, down_hbm, passing_ref, passing_sems, sent_sems):
+def stage_kernel(_, w_b_hbm, w_c_hbm, *refs):
+    up_twice_hbm, down_twice_hbm, up_hbm, down_hbm, own_hbm = refs[:5]
+    passing_ref, passing_sems, sent_sems = refs[5:]
     columns = passing_ref.shape[1]
     me = lax.axis_index("tp")
     core, chips = lax.rem(me, CORES), lax.axis_size("tp") // CORES
@@ -155,8 +157,10 @@
         pairs.append((w_c_hbm.at[from_row, :], passing_ref.at[at, :, pl.ds(STATE, STATE)]))
     loads = fetch(pairs, passing_sems)
     sends = []
-    for at in range(len(ROUTE)):
-        target = (up_hbm, down_hbm)[at // 3].at[pl.ds(at % 3 * columns, columns), :]
+    targets = [up_twice_hbm, down_twice_hbm]
+    for whole in (up_hbm, down_hbm, own_hbm):
+        targets += [whole.at[pl.ds(0, columns), :], whole.at[pl.ds(columns, columns), :]]
+    for at, target in enumerate(targets):
         loads[2 * at].wait()
         loads[2 * at + 1].wait()
         sends.append(pltpu.make_async_copy(passing_ref.at[at], target, sent_sems.at[at]))
@@ -190,8 +194,7 @@
     c_hbm,
     grad_x_ref,
     grad_bc_ref,
-    x_weighted_ref,
-    dy_weighted_ref,
+    weighted_ref,
     leave_ref,
     lengths_ref,
     log_ref,
@@ -250,12 +253,9 @@
     for pair in range(PAIRS):
         low = pair * LANES
         x, dy = x_ref[:, low : low + LANES], dy_ref[:, low : low + LANES]
-        for wide, cols, weighted_ref in (
-            (x, leave_cols, x_weighted_ref),
-            (dy, enter_cols, dy_weighted_ref),
-        ):
+        for side, (wide, cols) in enumerate(((x, leave_cols), (dy, enter_cols))):
             weighted = (wide.astype(FULL) * spread(cols, low, LANES)).astype(LOW)
-            weighted_ref[:, low : low + LANES] = weighted
+            weighted_ref[side, :, low : low + LANES] = weighted
         first_wide = spread(leave_first, low, LANES)
         x_first = (x[:SPAN].astype(FULL) * first_wide).astype(LOW)
         dy_second = (dy[SPAN:].astype(FULL) * spread(enter_second, low, LANES)).astype(LOW)
@@ -286,12 +286,13 @@
     grad_bc_ref[:, STATE:] = mul(table.T.astype(LOW), b)
 
 
-def grad_bc_kernel(x_weighted_ref, dy_weighted_ref, local_ref, edge_ref, out_ref):
+def grad_bc_kernel(weighted_ref, local_ref, edge_ref, *refs):
+    out_ref = refs[-1]
     rows = edge_ref.shape[1] // 2
     start = edge_ref[:, 0:rows, :].reshape(WIDE, STATE)
     end = edge_ref[:, rows : 2 * rows, :].reshape(WIDE, STATE)
-    out_ref[:, :STATE] = (local_ref[:, :STATE] + mul(x_weighted_ref[...], end)).astype(LOW)
-    out_ref[:, STATE:] = (local_ref[:, STATE:] + mul(dy_weighted_ref[...], start)).astype(LOW)
+    out_ref[:, :STATE] = (local_ref[:, :STATE] + mul(weighted_ref[0], end)).astype(LOW)
+    out_ref[:, STATE:] = (local_ref[:, STATE:] + mul(weighted_ref[1], start)).astype(LOW)
 
 
 def grad_x_kernel(b_ref, leave_ref, local_ref, edge_ref, out_ref):
@@ -305,34 +306,17 @@
         out_ref[:, low : low + width] = (local_ref[:, low : low + width] + later).astype(LOW)
 
 
-def project_kernel(w_b_hbm, w_c_hbm, *refs, sibling):
-    grads, (up, up_twice, down, down_twice) = refs[:4], refs[4:8]
-    received, (out_ref, grads_ref, weights_ref, received_ref, sems) = refs[8:-5], refs[-5:]
+def project_kernel(*refs, sibling):
+    grads, (own, up, down), relayed = refs[:4], refs[4:7], refs[7:9]
+    received, out_ref = refs[9:-1], refs[-1]
     columns = out_ref.shape[1]
-    me = lax.axis_index("tp")
-    core = lax.rem(me, CORES)
-    half = 1 - core if sibling else core
-    from_row = pl.ds(pl.multiple_of((me - core + half) * columns, columns), columns)
-    of_half = pl.ds(0 if sibling else columns, columns)
-    pairs = [
-        (w_b_hbm.at[from_row, :], weights_ref.at[0, :, pl.ds(0, STATE)]),
-        (w_c_hbm.at[from_row, :], weights_ref.at[0, :, pl.ds(STATE, STATE)]),
-        (grads[0], grads_ref.at[0]),
-    ]
-    twice = up_twice if sibling else down_twice
-    for at, weight in enumerate((up.at[of_half, :], twice, down.at[of_half, :])):
-        pairs.append((grads[at + 1], grads_ref.at[at + 1]))
-        pairs.append((weight, weights_ref.at[at + 1]))
-    pairs += [(ref, received_ref) for ref in received]
-    loads = fetch(pairs, sems)
-    total = 0.0
-    for at in range(4):
-        for load in loads[:3] if at == 0 else loads[1 + 2 * at : 3 + 2 * at]:
-            load.wait()
-        total += mul(grads_ref[at], weights_ref[at], NT)
-    for load in loads[9:]:
-        load.wait()
-        total += received_ref[...].astype(FULL)
+    half = slice(0, columns) if sibling else slice(columns, 2 * columns)
+    total = mul(grads[0][...], own[half, :], NT)
+    total += mul(grads[1][...], up[half, :], NT)
+    total += mul(grads[2][...], relayed[0 if sibling else 1][...], NT)
+    total += mul(grads[3][...], down[half, :], NT)
+    for ref in received:
+        total += ref[...].astype(FULL)
     out_ref[...] = total.astype(LOW)
 
 
@@ -381,28 +365,27 @@
     )(*local)
     sent = call(
         stage_kernel,
-        [shape((blocks // 2 * columns, 2 * STATE), LOW)] * 2,
+        [shape((columns, 2 * STATE), LOW)] * 2 + [shape((2 * columns, 2 * STATE), LOW)] * 3,
         [HBM] * 3,
         LARGE_VMEM,
-        [HBM, HBM],
+        [HBM] * 5,
         [pltpu.VMEM((blocks, columns, 2 * STATE), LOW), dma((2 * blocks,)), dma((blocks,))],
     )(summary, w_b, w_c)
-    up, down = along_x(sent[0], 1), along_x(sent[1], 3)
-    up_twice = along_x(up[2 * columns :], 1)
-    down_twice = along_x(down[2 * columns :], 3)
+    up_twice, down_twice = along_x(sent[0], 1), along_x(sent[1], 3)
+    up, down = along_x(sent[2], 1), along_x(sent[3], 3)
+    up_twice, down_twice = along_x(up_twice, 1), along_x(down_twice, 3)
     summary = lax.all_to_all(summary, "seq", 0, 0)
-    grad_x, grad_bc, x_weighted, dy_weighted, leave_cols = call(
+    grad_x, grad_bc, weighted, leave_cols = call(
         local_kernel,
         [
             shape((tokens, WIDE), FULL),
             shape((tokens, 2 * STATE), FULL),
-            shape((tokens, WIDE), LOW),
-            shape((tokens, WIDE), LOW),
+            shape((2, tokens, WIDE), LOW),
             shape((tokens, 2 * HEADS), LOW),
         ],
         [HBM] * 6,
         16 * MIB,
-        [BLOCK] * 5,
+        [BLOCK] * 4,
         held + [dma((6,))],
     )(*local)
     edges = call(
@@ -415,9 +398,9 @@
     grad_bc = call(
         grad_bc_kernel,
         shape((tokens, 2 * STATE), LOW),
-        [BLOCK] * 4,
+        [BLOCK] * 3 + [HBM] * 2,
         8 * MIB,
-    )(x_weighted, dy_weighted, grad_bc, edges)
+    )(weighted, grad_bc, edges, up, down)
     others = [along_x(grad_bc, step) for step in (1, 2, 3)]
     grad_x = call(
         grad_x_kernel, shape((tokens, WIDE), LOW), [BLOCK] * 4, 8 * MIB
@@ -427,16 +410,9 @@
         return call(
             functools.partial(project_kernel, sibling=not received),
             shape((tokens, columns), LOW),
-            [HBM] * (10 + len(received)),
-            LARGE_VMEM,
-            BLOCK,
-            [
-                pltpu.VMEM((4, tokens, 2 * STATE), LOW),
-                pltpu.VMEM((4, columns, 2 * STATE), LOW),
-                pltpu.VMEM((tokens, columns), LOW),
-                dma((9 + len(received),)),
-            ],
-        )(w_b, w_c, grad_bc, *others, up, up_twice, down, down_twice, *received)
+            [BLOCK] * (9 + len(received)),
+            16 * MIB,
+        )(grad_bc, *others, sent[4], up, down, up_twice, down_twice, *received)
 
     partner = [(at, at ^ 1) for at in range(lax.axis_size("tp"))]
     grad_input = project(lax.ppermute(project(), "tp", partner))

time: 91.1 us -> 84.6 us (0.929)
  waiting for transfers between devices: 35.3 us -> 30.4 us
  local copies, waits for them, and re-layouts: 5.93 us -> 3.35 us
  starting transfers between devices: 29.5 us -> 31.5 us
  Pallas kernels: 19.2 us -> 18.1 us
    slice x2 -> x0, local copies, waits for them, and re-layouts: 3.73 us -> none  [the longest x1 1.87 us: per_device(): up_twice = along_x(up[2 * columns:], 1)]
    all_to_all x1, waiting for transfers between devices: 7.94 us -> 5.17 us  [per_device(): summary = lax.all_to_all(summary, 'seq', 0, 0)]
    ppermute x7 -> x9, starting transfers between devices: 6.98 us -> 9.73 us  [along_x(): lax.ppermute(value, 'tp', [(at, (at + CORES * step) % devices) for at in...]
    ppermute x7 -> x9, waiting for transfers between devices: 26.8 us -> 24.9 us  [along_x(): lax.ppermute(value, 'tp', [(at, (at + CORES * step) % devices) for at in...]
    pallas_call x2, Pallas kernels: 6.22 us -> 4.44 us  [project(): call(functools.partial(project_kernel, sibling=not received), shape((toke...]
    unnamed x22, local copies, waits for them, and re-layouts: 2.2 us -> 3.35 us
  transfers between devices with their start and end apart: 10 -> 12, of which waited for: 6 -> 6; matrix products, arithmetic and copies ran while one was open for 4% -> 0% of each run, Pallas kernels for 10% -> 12%
where the time goes in v5:
time: 84.6 us; the launch traced here: 84.2 us
  starting transfers between devices  31.5 us (37%)
  waiting for transfers between devices  30.4 us (36%)
  Pallas kernels  18.1 us (21%)
  local copies, waits for them, and re-layouts  3.35 us (4%)
    ppermute x9, waiting for transfers between devices, along_x(): lax.ppermute(value, 'tp', [(at, (at + CORES * step) % devices) for at in...  24.9 us
    all_to_all x1, starting transfers between devices, per_device(): summary = lax.all_to_all(summary, 'seq', 0, 0)  12 us
    ppermute x9, starting transfers between devices, along_x(): lax.ppermute(value, 'tp', [(at, (at + CORES * step) % devices) for at in...  9.73 us
    all_to_all x1, starting transfers between devices, per_device(): edges = lax.all_to_all(edges, 'seq', 0, 0)  5.46 us
    all_to_all x1, waiting for transfers between devices, per_device(): summary = lax.all_to_all(summary, 'seq', 0, 0)  5.17 us
    pallas_call x2, Pallas kernels, project(): call(functools.partial(project_kernel, sibling=not received), shape((toke...  4.44 us
    ppermute x1, starting transfers between devices, per_device(): grad_input = project(lax.ppermute(project(), 'tp', partner))  4.29 us
    pallas_call x1, Pallas kernels, per_device(): call(stage_kernel, [shape((columns, 2 * STATE), LOW)] * 2 + [shape((2 * c...  3.76 us
  transfers between devices with their start and end apart: 12, of which 6 were waited for; matrix products, arithmetic and copies ran while one was open for 0% of the time, Pallas kernels for 12%

profile of v5, /device:TPU:1, one launch (start us, length us, event | category | flops | bytes accessed | tf_op | source)
XLA Modules:
  0.0 84.2 jit_solution(1921960602027692054)
XLA Ops:
  0.6 3.7 %shard_map.96._ = bf16[32,72,128]{2,1,0:T(8,128)(2,1)} custom-call(s32[4]{0:T(128)} %lengths_hbm.3, f32[16,256]{1,0:T(8,128)} %log_hbm.3, bf16[256,1024]{1,0:T(8,128)(2,1)} %x_hbm.3, bf16[256,128]{1,0:T(8,128)(2,1)} %b_ref.1, bf16[256,1024]{1,0:T(8,128)(2,1)} %dy_hbm.3, bf16[256,128]{1,0:T(8,128)(2,1)} %c_hbm.3), custom_call_target="tpu_custom_call" | custom-call | flops 1000 | bytes 1000 | tf_op jit(solution)/shard_map/pallas_call | solution.py:358
  4.4 12.0 %all-to-all-start = ((bf16[32,72,128]{2,1,0:T(8,128)(2,1)}), bf16[32,72,128]{2,1,0:T(8,128)(2,1)S(1)}, u32[]{:S(2)}, u32[]{:S(2)}) async-start(bf16[32,72,128]{2,1,0:T(8,128)(2,1)} %shard_map.96._), calls=%async_computation | async-start | bytes 1179648 | tf_op jit(solution)/shard_map/all_to_all | solution.py:377
  16.4 0.0 copy-start.1
  16.4 0.0 copy-start.2
  16.4 0.0 copy-start.7
  16.4 0.0 copy-start.8
  16.4 0.0 copy-start.9
  16.5 0.0 copy-start.10
  16.5 3.8 %shard_map.99 = (bf16[1024,256]{1,0:T(8,128)(2,1)}, bf16[1024,256]{1,0:T(8,128)(2,1)}, bf16[2048,256]{1,0:T(8,128)(2,1)}, bf16[2048,256]{1,0:T(8,128)(2,1)}, bf16[2048,256]{1,0:T(8,128)(2,1)}) custom-call(bf16[32,72,128]{2,1,0:T(8,128)(2,1)} %shard_map.96._, bf16[8192,128]{1,0:T(8,128)(2,1)} %w_b_hbm.1, bf16[8192,128]{1,0:T(8,128)(2,1)} %w_c_hbm.1), custom_call_target="tpu_custom_call" | custom-call | flops 1000 | bytes 1000 | tf_op jit(solution)/shard_map/pallas_call | solution.py:366
  20.2 1.3 %collective-permute-start = (bf16[2048,256]{1,0:T(8,128)(2,1)}, bf16[2048,256]{1,0:T(8,128)(2,1)S(1)}, u32[]{:S(2)}, u32[]{:S(2)}) collective-permute-start(bf16[2048,256]{1,0:T(8,128)(2,1)} %get-tuple-element.15), channel_id=1, source_target_pairs={{0,2},{1,3},{2,4},{3,5},{4,6},{5,7},{6,0},{7,1},{8,10},{9,11},{10,... | collective-permute-start | bytes 3145736 | tf_op jit(solution)/shard_map/ppermute | solution.py:341
  21.5 1.5 %collective-permute-start.1 = (bf16[2048,256]{1,0:T(8,128)(2,1)}, bf16[2048,256]{1,0:T(8,128)(2,1)S(1)}, u32[]{:S(2)}, u32[]{:S(2)}) collective-permute-start(bf16[2048,256]{1,0:T(8,128)(2,1)} %get-tuple-element.16), channel_id=1, source_target_pairs={{0,6},{1,7},{2,0},{3,1},{4,2},{5,3},{6,4},{7,5},{8,14},{9,15},{10,... | collective-permute-start | bytes 3145736 | tf_op jit(solution)/shard_map/ppermute | solution.py:341
  23.0 0.0 copy-done.1
  23.0 0.0 copy-done.2
  23.0 0.0 copy-done.7
  23.0 0.0 copy-done.8
  23.0 0.0 copy-done.9
  23.0 3.7 %shard_map.95 = (f32[256,1024]{1,0:T(8,128)S(1)}, f32[256,256]{1,0:T(8,128)S(1)}, bf16[2,256,1024]{2,1,0:T(8,128)(2,1)S(1)}, bf16[256,32]{1,0:T(8,128)(2,1)S(1)}) custom-call(s32[4]{0:T(128)S(1)} %copy-done.10, f32[16,256]{1,0:T(8,128)S(1)} %copy-done.9, bf16[256,1024]{1,0:T(8,128)(2,1)S(1)} %copy-done.1, bf16[256,128]{1,0:T(8,128)(2,1)S(1)} %copy-done.7, ...), custom_call_target="tpu_custom_call" | custom-call | flops 1000 | bytes 1000 | tf_op jit(solution)/shard_map/pallas_call | solution.py:378
  26.7 0.0 copy-start.3
  26.7 1.0 %copy-done.3 = f32[256,1024]{1,0:T(8,128)} copy-done((f32[256,1024]{1,0:T(8,128)}, f32[256,1024]{1,0:T(8,128)S(1)}, u32[]{:S(2)}) %copy-start.3) | copy-done | bytes 1048600
  27.7 1.0 %copy-done.5 = bf16[2,256,1024]{2,1,0:T(8,128)(2,1)} copy-done((bf16[2,256,1024]{2,1,0:T(8,128)(2,1)}, bf16[2,256,1024]{2,1,0:T(8,128)(2,1)S(1)}, u32[]{:S(2)}) %copy-start.5) | copy-done | bytes 1048600
  28.7 5.2 %all-to-all-done.in_ref = bf16[32,72,128]{2,1,0:T(8,128)(2,1)S(1)} async-done(((bf16[32,72,128]{2,1,0:T(8,128)(2,1)}), bf16[32,72,128]{2,1,0:T(8,128)(2,1)S(1)}, u32[]{:S(2)}, u32[]{:S(2)}) %all-to-all-start) | async-done | bytes 589856 | tf_op jit(solution)/shard_map/all_to_all | solution.py:377
  33.9 0.9 %shard_map.97 = bf16[32,64,128]{2,1,0:T(8,128)(2,1)} custom-call(bf16[32,72,128]{2,1,0:T(8,128)(2,1)S(1)} %all-to-all-done.in_ref, bf16[256,32]{1,0:T(8,128)(2,1)S(1)} %get-tuple-element.11._.leave_ref), custom_call_target="tpu_custom_call" | custom-call | flops 1000 | bytes 1000 | tf_op jit(solution)/shard_map/pallas_call | solution.py:391
  34.8 5.5 %all-to-all-start.1 = ((bf16[32,64,128]{2,1,0:T(8,128)(2,1)}), bf16[32,64,128]{2,1,0:T(8,128)(2,1)S(1)}, u32[]{:S(2)}, u32[]{:S(2)}) async-start(bf16[32,64,128]{2,1,0:T(8,128)(2,1)} %shard_map.97), calls=%async_computation.1 | async-start | bytes 1048576 | tf_op jit(solution)/shard_map/all_to_all | solution.py:397
  40.3 1.3 %collective-permute-start.5 = (bf16[1024,256]{1,0:T(8,128)(2,1)}, bf16[1024,256]{1,0:T(8,128)(2,1)}, u32[]{:S(2)}, u32[]{:S(2)}) collective-permute-start(bf16[1024,256]{1,0:T(8,128)(2,1)} %get-tuple-element.18), channel_id=1, source_target_pairs={{0,2},{1,3},{2,4},{3,5},{4,6},{5,7},{6,0},{7,1},{8,10},{9,11},{10,... | collective-permute-start | bytes 1572872 | tf_op jit(solution)/shard_map/ppermute | solution.py:341
  41.6 1.5 %collective-permute-start.7 = (bf16[1024,256]{1,0:T(8,128)(2,1)}, bf16[1024,256]{1,0:T(8,128)(2,1)}, u32[]{:S(2)}, u32[]{:S(2)}) collective-permute-start(bf16[1024,256]{1,0:T(8,128)(2,1)} %get-tuple-element.19), channel_id=1, source_target_pairs={{0,6},{1,7},{2,0},{3,1},{4,2},{5,3},{6,4},{7,5},{8,14},{9,15},{10,... | collective-permute-start | bytes 1572872 | tf_op jit(solution)/shard_map/ppermute | solution.py:341
  43.0 13.7 %collective-permute-done.5 = bf16[1024,256]{1,0:T(8,128)(2,1)} collective-permute-done((bf16[1024,256]{1,0:T(8,128)(2,1)}, bf16[1024,256]{1,0:T(8,128)(2,1)}, u32[]{:S(2)}, u32[]{:S(2)}) %collective-permute-start.5) | collective-permute-done | bytes 524320 | tf_op jit(solution)/shard_map/ppermute | solution.py:341
  56.8 0.0 collective-permute-start.6
  56.8 0.0 collective-permute-done.7
  56.8 2.7 %collective-permute-start.8 = (bf16[1024,256]{1,0:T(8,128)(2,1)}, bf16[1024,256]{1,0:T(8,128)(2,1)}, u32[]{:S(2)}, u32[]{:S(2)}) collective-permute-start(bf16[1024,256]{1,0:T(8,128)(2,1)} %collective-permute-done.7), channel_id=1, source_target_pairs={{0,6},{1,7},{2,0},{3,1},{4,2},{5,3},{6,4},{7,5},{8,14},{9,15},{10,... | collective-permute-start | bytes 1572872 | tf_op jit(solution)/shard_map/ppermute | solution.py:341
  59.5 0.0 collective-permute-done.refs_0_.refs_5_
  59.5 0.0 collective-permute-done.1.refs_1_.refs_6_
  59.5 0.0 all-to-all-done.1.edge_ref
  59.5 1.3 %copy-done.6 = bf16[2,256,1024]{2,1,0:T(8,128)(2,1)S(1)} copy-done((bf16[2,256,1024]{2,1,0:T(8,128)(2,1)S(1)}, bf16[2,256,1024]{2,1,0:T(8,128)(2,1)}, u32[]{:S(2)}) %copy-start.6) | copy-done | bytes 1048600
  60.8 0.4 shard_map.100.refs_0_
  61.2 0.1 collective-permute-start.4
  61.4 0.5 collective-permute-start.3
  61.9 0.9 %collective-permute-start.2 = (bf16[256,256]{1,0:T(8,128)(2,1)S(1)}, bf16[256,256]{1,0:T(8,128)(2,1)S(1)}, u32[]{:S(2)}, u32[]{:S(2)}) collective-permute-start(bf16[256,256]{1,0:T(8,128)(2,1)S(1)} %shard_map.100.refs_0_), channel_id=1, source_target_pairs={{0,2},{1,3},{2,4},{3,5},{4,6},{5,7},{6,0},{7,1},{8,10},{9,11},{10,... | collective-permute-start | bytes 393224 | tf_op jit(solution)/shard_map/ppermute | solution.py:341
  62.8 7.2 %collective-permute-done.6.refs_7_ = bf16[1024,256]{1,0:T(8,128)(2,1)S(1)} collective-permute-done((bf16[1024,256]{1,0:T(8,128)(2,1)}, bf16[1024,256]{1,0:T(8,128)(2,1)S(1)}, u32[]{:S(2)}, u32[]{:S(2)}) %collective-permute-start.6) | collective-permute-done | bytes 524320 | tf_op jit(solution)/shard_map/ppermute | solution.py:341
  69.9 0.0 collective-permute-done.8.refs_8_
  70.0 2.5 %collective-permute-done.4.refs_3_ = bf16[256,256]{1,0:T(8,128)(2,1)S(1)} collective-permute-done((bf16[256,256]{1,0:T(8,128)(2,1)S(1)}, bf16[256,256]{1,0:T(8,128)(2,1)S(1)}, u32[]{:S(2)}, u32[]{:S(2)}) %collective-permute-start.4) | collective-permute-done | bytes 131104 | tf_op jit(solution)/shard_map/ppermute | solution.py:341
  72.5 0.0 collective-permute-done.3.refs_2_
  72.5 1.4 %collective-permute-done.2.refs_1_ = bf16[256,256]{1,0:T(8,128)(2,1)S(1)} collective-permute-done((bf16[256,256]{1,0:T(8,128)(2,1)S(1)}, bf16[256,256]{1,0:T(8,128)(2,1)S(1)}, u32[]{:S(2)}, u32[]{:S(2)}) %collective-permute-start.2) | collective-permute-done | bytes 131104 | tf_op jit(solution)/shard_map/ppermute | solution.py:341
  73.9 0.0 copy-done
  74.0 1.9 %shard_map.101 = bf16[256,1024]{1,0:T(8,128)(2,1)S(1)} custom-call(bf16[256,256]{1,0:T(8,128)(2,1)S(1)} %shard_map.100.refs_0_, bf16[256,256]{1,0:T(8,128)(2,1)S(1)} %collective-permute-done.2.refs_1_, bf16[256,256]{1,0:T(8,128)(2,1)S(1)} %collective-permute-done.3.refs_2_, bf16[256,256]{1,0:T(8,128)(2,1)S(1)} %collective-permute-done.4.refs_3_, ...), custom_call_target="tpu_custom_call" | custom-call | flops 1000 | bytes 1000 | tf_op jit(solution)/shard_map/pallas_call | solution.py:410
  75.8 4.3 %collective-permute-start.9 = (bf16[256,1024]{1,0:T(8,128)(2,1)S(1)}, bf16[256,1024]{1,0:T(8,128)(2,1)S(1)}, u32[]{:S(2)}, u32[]{:S(2)}) collective-permute-start(bf16[256,1024]{1,0:T(8,128)(2,1)S(1)} %shard_map.101), channel_id=1, source_target_pairs={{0,1},{1,0},{2,3},{3,2},{4,5},{5,4},{6,7},{7,6},{8,9},{9,8},{10,11... | collective-permute-start | bytes 1572872 | tf_op jit(solution)/shard_map/ppermute | solution.py:418
  80.1 1.2 %shard_map.98 = bf16[256,1024]{1,0:T(8,128)(2,1)} custom-call(bf16[256,128]{1,0:T(8,128)(2,1)S(1)} %copy-done.7, bf16[256,32]{1,0:T(8,128)(2,1)S(1)} %get-tuple-element.11._.leave_ref, f32[256,1024]{1,0:T(8,128)S(1)} %copy-done.4, bf16[32,64,128]{2,1,0:T(8,128)(2,1)S(1)} %all-to-all-done.1.edge_ref), custom_call_target="tpu_custom_call" | custom-call | flops 1000 | bytes 1000 | tf_op jit(solution)/shard_map/pallas_call | solution.py:405
  81.3 0.3 collective-permute-done.9.refs_9_
  81.7 2.6 %shard_map.102 = bf16[256,1024]{1,0:T(8,128)(2,1)} custom-call(bf16[256,256]{1,0:T(8,128)(2,1)S(1)} %shard_map.100.refs_0_, bf16[256,256]{1,0:T(8,128)(2,1)S(1)} %collective-permute-done.2.refs_1_, bf16[256,256]{1,0:T(8,128)(2,1)S(1)} %collective-permute-done.3.refs_2_, bf16[256,256]{1,0:T(8,128)(2,1)S(1)} %collective-permute-done.4.refs_3_, ...), custom_call_target="tpu_custom_call" | custom-call | flops 1000 | bytes 1000 | tf_op jit(solution)/shard_map/pallas_call | solution.py:410
  (6 shorter events, 0.0 us)
Async XLA Ops:
  4.4 29.5 %all-to-all-start = ((bf16[32,72,128]{2,1,0:T(8,128)(2,1)}), bf16[32,72,128]{2,1,0:T(8,128)(2,1)S(1)}, u32[]{:S(2)}, u32[]{:S(2)}) async-start(bf16[32,72,128]{2,1,0:T(8,128)(2,1)} %shard_map.96._), calls=%async_computation | async-start | bytes 1179648 | tf_op jit(solution)/shard_map/all_to_all | solution.py:377
  16.4 6.6 %copy-start.1 = (bf16[256,1024]{1,0:T(8,128)(2,1)S(1)}, bf16[256,1024]{1,0:T(8,128)(2,1)}, u32[]{:S(2)}) copy-start(bf16[256,1024]{1,0:T(8,128)(2,1)} %x_hbm.3) | copy-start | bytes 1572868
  16.4 6.6 %copy-start.2 = (bf16[256,1024]{1,0:T(8,128)(2,1)S(1)}, bf16[256,1024]{1,0:T(8,128)(2,1)}, u32[]{:S(2)}) copy-start(bf16[256,1024]{1,0:T(8,128)(2,1)} %dy_hbm.3) | copy-start | bytes 1572868
  16.4 6.6 %copy-start.7 = (bf16[256,128]{1,0:T(8,128)(2,1)S(1)}, bf16[256,128]{1,0:T(8,128)(2,1)}, u32[]{:S(2)}) copy-start(bf16[256,128]{1,0:T(8,128)(2,1)} %b_ref.1) | copy-start | bytes 196612
  16.4 6.6 %copy-start.8 = (bf16[256,128]{1,0:T(8,128)(2,1)S(1)}, bf16[256,128]{1,0:T(8,128)(2,1)}, u32[]{:S(2)}) copy-start(bf16[256,128]{1,0:T(8,128)(2,1)} %c_hbm.3) | copy-start | bytes 196612
  16.4 6.6 %copy-start.9 = (f32[16,256]{1,0:T(8,128)S(1)}, f32[16,256]{1,0:T(8,128)}, u32[]{:S(2)}) copy-start(f32[16,256]{1,0:T(8,128)} %log_hbm.3) | copy-start | bytes 49156
  16.5 6.6 %copy-start.10 = (s32[4]{0:T(128)S(1)}, s32[4]{0:T(128)}, u32[]{:S(2)}) copy-start(s32[4]{0:T(128)} %lengths_hbm.3) | copy-start | bytes 52
  20.2 39.2 %collective-permute-start = (bf16[2048,256]{1,0:T(8,128)(2,1)}, bf16[2048,256]{1,0:T(8,128)(2,1)S(1)}, u32[]{:S(2)}, u32[]{:S(2)}) collective-permute-start(bf16[2048,256]{1,0:T(8,128)(2,1)} %get-tuple-element.15), channel_id=1, source_target_pairs={{0,2},{1,3},{2,4},{3,5},{4,6},{5,7},{6,0},{7,1},{8,10},{9,11},{10,... | collective-permute-start | bytes 3145736 | tf_op jit(solution)/shard_map/ppermute | solution.py:341
  21.5 37.9 %collective-permute-start.1 = (bf16[2048,256]{1,0:T(8,128)(2,1)}, bf16[2048,256]{1,0:T(8,128)(2,1)S(1)}, u32[]{:S(2)}, u32[]{:S(2)}) collective-permute-start(bf16[2048,256]{1,0:T(8,128)(2,1)} %get-tuple-element.16), channel_id=1, source_target_pairs={{0,6},{1,7},{2,0},{3,1},{4,2},{5,3},{6,4},{7,5},{8,14},{9,15},{10,... | collective-permute-start | bytes 3145736 | tf_op jit(solution)/shard_map/ppermute | solution.py:341
  26.7 1.0 %copy-start.3 = (f32[256,1024]{1,0:T(8,128)}, f32[256,1024]{1,0:T(8,128)S(1)}, u32[]{:S(2)}) copy-start(f32[256,1024]{1,0:T(8,128)S(1)} %get-tuple-element.12.local_ref) | copy-start | bytes 3145732
  27.7 1.0 %copy-start.5 = (bf16[2,256,1024]{2,1,0:T(8,128)(2,1)}, bf16[2,256,1024]{2,1,0:T(8,128)(2,1)S(1)}, u32[]{:S(2)}) copy-start(bf16[2,256,1024]{2,1,0:T(8,128)(2,1)S(1)} %get-tuple-element.13.weighted_ref) | copy-start | bytes 3145732
  34.8 24.7 %all-to-all-start.1 = ((bf16[32,64,128]{2,1,0:T(8,128)(2,1)}), bf16[32,64,128]{2,1,0:T(8,128)(2,1)S(1)}, u32[]{:S(2)}, u32[]{:S(2)}) async-start(bf16[32,64,128]{2,1,0:T(8,128)(2,1)} %shard_map.97), calls=%async_computation.1 | async-start | bytes 1048576 | tf_op jit(solution)/shard_map/all_to_all | solution.py:397
  40.3 16.5 %collective-permute-start.5 = (bf16[1024,256]{1,0:T(8,128)(2,1)}, bf16[1024,256]{1,0:T(8,128)(2,1)}, u32[]{:S(2)}, u32[]{:S(2)}) collective-permute-start(bf16[1024,256]{1,0:T(8,128)(2,1)} %get-tuple-element.18), channel_id=1, source_target_pairs={{0,2},{1,3},{2,4},{3,5},{4,6},{5,7},{6,0},{7,1},{8,10},{9,11},{10,... | collective-permute-start | bytes 1572872 | tf_op jit(solution)/shard_map/ppermute | solution.py:341
  41.6 15.2 %collective-permute-start.7 = (bf16[1024,256]{1,0:T(8,128)(2,1)}, bf16[1024,256]{1,0:T(8,128)(2,1)}, u32[]{:S(2)}, u32[]{:S(2)}) collective-permute-start(bf16[1024,256]{1,0:T(8,128)(2,1)} %get-tuple-element.19), channel_id=1, source_target_pairs={{0,6},{1,7},{2,0},{3,1},{4,2},{5,3},{6,4},{7,5},{8,14},{9,15},{10,... | collective-permute-start | bytes 1572872 | tf_op jit(solution)/shard_map/ppermute | solution.py:341
  56.8 13.2 %collective-permute-start.6 = (bf16[1024,256]{1,0:T(8,128)(2,1)}, bf16[1024,256]{1,0:T(8,128)(2,1)S(1)}, u32[]{:S(2)}, u32[]{:S(2)}) collective-permute-start(bf16[1024,256]{1,0:T(8,128)(2,1)} %collective-permute-done.5), channel_id=1, source_target_pairs={{0,2},{1,3},{2,4},{3,5},{4,6},{5,7},{6,0},{7,1},{8,10},{9,11},{10,... | collective-permute-start | bytes 1572872 | tf_op jit(solution)/shard_map/ppermute | solution.py:341
  56.8 13.2 %collective-permute-start.8 = (bf16[1024,256]{1,0:T(8,128)(2,1)}, bf16[1024,256]{1,0:T(8,128)(2,1)}, u32[]{:S(2)}, u32[]{:S(2)}) collective-permute-start(bf16[1024,256]{1,0:T(8,128)(2,1)} %collective-permute-done.7), channel_id=1, source_target_pairs={{0,6},{1,7},{2,0},{3,1},{4,2},{5,3},{6,4},{7,5},{8,14},{9,15},{10,... | collective-permute-start | bytes 1572872 | tf_op jit(solution)/shard_map/ppermute | solution.py:341
  59.5 14.5 %copy-start = (bf16[2048,256]{1,0:T(8,128)(2,1)S(1)}, bf16[2048,256]{1,0:T(8,128)(2,1)}, u32[]{:S(2)}) copy-start(bf16[2048,256]{1,0:T(8,128)(2,1)} %get-tuple-element.17.refs_4_) | copy-start | bytes 3145732
  59.5 1.3 %copy-start.6 = (bf16[2,256,1024]{2,1,0:T(8,128)(2,1)S(1)}, bf16[2,256,1024]{2,1,0:T(8,128)(2,1)}, u32[]{:S(2)}) copy-start(bf16[2,256,1024]{2,1,0:T(8,128)(2,1)} %copy-done.5) | copy-start | bytes 3145732
  61.2 11.3 %collective-permute-start.4 = (bf16[256,256]{1,0:T(8,128)(2,1)S(1)}, bf16[256,256]{1,0:T(8,128)(2,1)S(1)}, u32[]{:S(2)}, u32[]{:S(2)}) collective-permute-start(bf16[256,256]{1,0:T(8,128)(2,1)S(1)} %shard_map.100.refs_0_), channel_id=1, source_target_pairs={{0,6},{1,7},{2,0},{3,1},{4,2},{5,3},{6,4},{7,5},{8,14},{9,15},{10,... | collective-permute-start | bytes 393224 | tf_op jit(solution)/shard_map/ppermute | solution.py:341
  61.4 11.2 %collective-permute-start.3 = (bf16[256,256]{1,0:T(8,128)(2,1)S(1)}, bf16[256,256]{1,0:T(8,128)(2,1)S(1)}, u32[]{:S(2)}, u32[]{:S(2)}) collective-permute-start(bf16[256,256]{1,0:T(8,128)(2,1)S(1)} %shard_map.100.refs_0_), channel_id=1, source_target_pairs={{0,4},{1,5},{2,6},{3,7},{4,0},{5,1},{6,2},{7,3},{8,12},{9,13},{10,... | collective-permute-start | bytes 393224 | tf_op jit(solution)/shard_map/ppermute | solution.py:341
  61.9 12.1 %collective-permute-start.2 = (bf16[256,256]{1,0:T(8,128)(2,1)S(1)}, bf16[256,256]{1,0:T(8,128)(2,1)S(1)}, u32[]{:S(2)}, u32[]{:S(2)}) collective-permute-start(bf16[256,256]{1,0:T(8,128)(2,1)S(1)} %shard_map.100.refs_0_), channel_id=1, source_target_pairs={{0,2},{1,3},{2,4},{3,5},{4,6},{5,7},{6,0},{7,1},{8,10},{9,11},{10,... | collective-permute-start | bytes 393224 | tf_op jit(solution)/shard_map/ppermute | solution.py:341
  74.0 6.2 %copy-start.4 = (f32[256,1024]{1,0:T(8,128)S(1)}, f32[256,1024]{1,0:T(8,128)}, u32[]{:S(2)}) copy-start(f32[256,1024]{1,0:T(8,128)} %copy-done.3) | copy-start | bytes 3145732
  75.8 5.8 %collective-permute-start.9 = (bf16[256,1024]{1,0:T(8,128)(2,1)S(1)}, bf16[256,1024]{1,0:T(8,128)(2,1)S(1)}, u32[]{:S(2)}, u32[]{:S(2)}) collective-permute-start(bf16[256,1024]{1,0:T(8,128)(2,1)S(1)} %shard_map.101), channel_id=1, source_target_pairs={{0,1},{1,0},{2,3},{3,2},{4,5},{5,4},{6,7},{7,6},{8,9},{9,8},{10,11... | collective-permute-start | bytes 1572872 | tf_op jit(solution)/shard_map/ppermute | solution.py:418

commit v6 on v5

--- a/solution.py
+++ b/solution.py
@@ -15,7 +15,8 @@
 WIDE = HEADS * HEAD_DIM
 PAIRS = WIDE // LANES
 CORES = 2
-ROUTE = ((2, True), (2, False), (1, True), (1, False), (3, True), (3, False), (0, True), (0, False))
+ALONG_Y = 4
+ROUTE = ((2, 0, 1), (2, 1, 1), (1, 0, 2), (3, 0, 2))
 LOW = jnp.bfloat16
 FULL = jnp.float32
 NN = (((1,), (0,)), ((), ()))
@@ -142,34 +143,54 @@
             out_ref[head * per_head + part, 2 * rows : 2 * rows + 8, :] = tile
 
 
-def stage_kernel(_, w_b_hbm, w_c_hbm, *refs):
-    up_twice_hbm, down_twice_hbm, up_hbm, down_hbm, own_hbm = refs[:5]
-    passing_ref, passing_sems, sent_sems = refs[5:]
-    columns = passing_ref.shape[1]
-    me = lax.axis_index("tp")
-    core, chips = lax.rem(me, CORES), lax.axis_size("tp") // CORES
+def fetches_sibling():
+    return lax.rem(lax.axis_index("seq"), 2) == 0
+
+
+def pass_through(pieces, w_b_hbm, w_c_hbm, load_sems, sent_sems):
     pairs = []
-    for at, (step, sibling) in enumerate(ROUTE):
-        half = 1 - core if sibling else core
-        target = lax.rem(me // CORES + step, chips)
-        from_row = pl.ds(pl.multiple_of((target * CORES + half) * columns, columns), columns)
-        pairs.append((w_b_hbm.at[from_row, :], passing_ref.at[at, :, pl.ds(0, STATE)]))
-        pairs.append((w_c_hbm.at[from_row, :], passing_ref.at[at, :, pl.ds(STATE, STATE)]))
-    loads = fetch(pairs, passing_sems)
+    for rows, held_ref, _ in pieces:
+        pairs.append((w_b_hbm.at[rows, :], held_ref.at[:, pl.ds(0, STATE)]))
+        pairs.append((w_c_hbm.at[rows, :], held_ref.at[:, pl.ds(STATE, STATE)]))
+    loads = fetch(pairs, load_sems)
     sends = []
-    targets = [up_twice_hbm, down_twice_hbm]
-    for whole in (up_hbm, down_hbm, own_hbm):
-        targets += [whole.at[pl.ds(0, columns), :], whole.at[pl.ds(columns, columns), :]]
-    for at, target in enumerate(targets):
+    for at, (_, held_ref, sent_ref) in enumerate(pieces):
         loads[2 * at].wait()
         loads[2 * at + 1].wait()
-        sends.append(pltpu.make_async_copy(passing_ref.at[at], target, sent_sems.at[at]))
+        sends.append(pltpu.make_async_copy(held_ref, sent_ref, sent_sems.at[at]))
         sends[-1].start()
     for send in sends:
         send.wait()
 
 
-def scan_kernel(in_ref, _, out_ref):
+def stage_kernel(_, w_b_hbm, w_c_hbm, *refs):
+    sent_refs, held_refs, sems = refs[: len(ROUTE)], refs[len(ROUTE) : -2], refs[-2:]
+    part = sent_refs[0].shape[0]
+    me = lax.axis_index("tp")
+    core, chips = lax.rem(me, CORES), lax.axis_size("tp") // CORES
+    half = lax.rem(core + 1 + lax.rem(lax.axis_index("seq"), 2), CORES)
+    pieces = []
+    for (step, first, parts), held_ref, sent_ref in zip(ROUTE, held_refs, sent_refs):
+        target = lax.rem(me // CORES + step, chips)
+        row = (target * CORES + half) * 2 * part + first * part
+        pieces.append((pl.ds(pl.multiple_of(row, part), parts * part), held_ref, sent_ref))
+    pass_through(pieces, w_b_hbm, w_c_hbm, *sems)
+
+
+def own_kernel(w_b_hbm, w_c_hbm, out_ref, held_ref, *sems):
+    columns = out_ref.shape[0] // CORES
+    me = lax.axis_index("tp")
+    core = lax.rem(me, CORES)
+    pieces = []
+    for which, other in enumerate((1 - core, core)):
+        row = pl.multiple_of((me - core + other) * columns, columns)
+        to = pl.ds(which * columns, columns)
+        pieces.append((pl.ds(row, columns), held_ref.at[to, :], out_ref.at[to, :]))
+    pass_through(pieces, w_b_hbm, w_c_hbm, *sems)
+
+
+def scan_kernel(in_ref, *refs):
+    out_ref = refs[-1]
     devices, rows = out_ref.shape[0], out_ref.shape[1] // 2
     decays = []
     for at in range(devices):
@@ -193,8 +214,7 @@
     dy_hbm,
     c_hbm,
     grad_x_ref,
-    grad_bc_ref,
-    weighted_ref,
+    terms_ref,
     leave_ref,
     lengths_ref,
     log_ref,
@@ -255,7 +275,7 @@
         x, dy = x_ref[:, low : low + LANES], dy_ref[:, low : low + LANES]
         for side, (wide, cols) in enumerate(((x, leave_cols), (dy, enter_cols))):
             weighted = (wide.astype(FULL) * spread(cols, low, LANES)).astype(LOW)
-            weighted_ref[side, :, low : low + LANES] = weighted
+            terms_ref[:, side * WIDE + low : side * WIDE + low + LANES] = weighted
         first_wide = spread(leave_first, low, LANES)
         x_first = (x[:SPAN].astype(FULL) * first_wide).astype(LOW)
         dy_second = (dy[SPAN:].astype(FULL) * spread(enter_second, low, LANES)).astype(LOW)
@@ -282,20 +302,27 @@
         ],
         axis=0,
     )
-    grad_bc_ref[:, :STATE] = mul(table.astype(LOW), c)
-    grad_bc_ref[:, STATE:] = mul(table.T.astype(LOW), b)
-
-
-def grad_bc_kernel(weighted_ref, local_ref, edge_ref, *refs):
-    out_ref = refs[-1]
+    for side, part in enumerate((mul(table.astype(LOW), c), mul(table.T.astype(LOW), b))):
+        high = part.astype(LOW)
+        low = 2 * (WIDE + side * STATE)
+        terms_ref[:, low : low + STATE] = high
+        terms_ref[:, low + STATE : low + 2 * STATE] = (part - high.astype(FULL)).astype(LOW)
+
+
+def grad_bc_kernel(terms_ref, edge_ref, out_ref):
     rows = edge_ref.shape[1] // 2
-    start = edge_ref[:, 0:rows, :].reshape(WIDE, STATE)
-    end = edge_ref[:, rows : 2 * rows, :].reshape(WIDE, STATE)
-    out_ref[:, :STATE] = (local_ref[:, :STATE] + mul(weighted_ref[0], end)).astype(LOW)
-    out_ref[:, STATE:] = (local_ref[:, STATE:] + mul(weighted_ref[1], start)).astype(LOW)
-
-
-def grad_x_kernel(b_ref, leave_ref, local_ref, edge_ref, out_ref):
+    for side in range(2):
+        which = slice(rows, 2 * rows) if side == 0 else slice(0, rows)
+        edge = edge_ref[:, which, :].reshape(WIDE, STATE)
+        total = mul(terms_ref[:, side * WIDE : (side + 1) * WIDE], edge)
+        low = 2 * (WIDE + side * STATE)
+        for part in range(2):
+            total += terms_ref[:, low + part * STATE : low + (part + 1) * STATE].astype(FULL)
+        out_ref[:, side * STATE : (side + 1) * STATE] = total.astype(LOW)
+
+
+def grad_x_kernel(b_ref, leave_ref, local_ref, edge_ref, out_ref, done_ref):
+    done_ref[...] = jnp.zeros_like(done_ref)
     rows = edge_ref.shape[1] // 2
     width = 2 * LANES
     for chunk in range(WIDE // width):
@@ -307,17 +334,25 @@
 
 
 def project_kernel(*refs, sibling):
-    grads, (own, up, down), relayed = refs[:4], refs[4:7], refs[7:9]
-    received, out_ref = refs[9:-1], refs[-1]
+    grads, own, fetched, given, (_, out_ref) = refs[:4], refs[4], refs[5:9], refs[9:13], refs[13:]
     columns = out_ref.shape[1]
     half = slice(0, columns) if sibling else slice(columns, 2 * columns)
-    total = mul(grads[0][...], own[half, :], NT)
-    total += mul(grads[1][...], up[half, :], NT)
-    total += mul(grads[2][...], relayed[0 if sibling else 1][...], NT)
-    total += mul(grads[3][...], down[half, :], NT)
-    for ref in received:
-        total += ref[...].astype(FULL)
-    out_ref[...] = total.astype(LOW)
+
+    def products(weights):
+        twice_first, twice_second, up, down = weights
+        total = mul(grads[0][...], own[half, :], NT)
+        total += mul(grads[1][...], up[...], NT)
+        total += mul(grads[3][...], down[...], NT)
+        twice = [mul(grads[2][...], part[...], NT) for part in (twice_first, twice_second)]
+        out_ref[...] = (total + jnp.concatenate(twice, axis=1)).astype(out_ref.dtype)
+
+    here = fetches_sibling() if sibling else jnp.logical_not(fetches_sibling())
+    pl.when(here)(lambda: products(fetched))
+    pl.when(jnp.logical_not(here))(lambda: products(given))
+
+
+def sum_kernel(kept_ref, received_ref, out_ref):
+    out_ref[...] = (kept_ref[...] + received_ref[...].astype(FULL)).astype(LOW)
 
 
 BLOCK = pl.BlockSpec(memory_space=pltpu.VMEM)
@@ -341,6 +376,14 @@
     return lax.ppermute(
         value, "tp", [(at, (at + CORES * step) % devices) for at in range(devices)]
     )
+
+
+def along_y(value, step):
+    pairs = []
+    for at in range(lax.axis_size("seq")):
+        y = at % ALONG_Y
+        pairs.append((at, at - y + (y + step) % ALONG_Y))
+    return lax.ppermute(value, "seq", pairs)
 
 
 def per_device(inner_x, in_b, in_c, log_decay, doc_lengths, out_grad, w_b, w_c):
@@ -354,7 +397,6 @@
     held = [pltpu.SMEM(doc_lengths.shape, doc_lengths.dtype)] + [
         pltpu.VMEM(a.shape, a.dtype) for a in local[1:]
     ]
-    blocks = len(ROUTE)
     summary = call(
         summary_kernel,
         shape((devices, 2 * rows + 8, STATE), LOW),
@@ -363,59 +405,78 @@
         BLOCK,
         held + [dma((6,))],
     )(*local)
+    pieces = [(parts * columns // 2, 2 * STATE) for _, _, parts in ROUTE]
+    own = (CORES * columns, 2 * STATE)
     sent = call(
         stage_kernel,
-        [shape((columns, 2 * STATE), LOW)] * 2 + [shape((2 * columns, 2 * STATE), LOW)] * 3,
+        [shape(piece, LOW) for piece in pieces],
         [HBM] * 3,
         LARGE_VMEM,
-        [HBM] * 5,
-        [pltpu.VMEM((blocks, columns, 2 * STATE), LOW), dma((2 * blocks,)), dma((blocks,))],
+        [HBM] * len(pieces),
+        [pltpu.VMEM(piece, LOW) for piece in pieces]
+        + [dma((2 * len(pieces),)), dma((len(pieces),))],
     )(summary, w_b, w_c)
-    up_twice, down_twice = along_x(sent[0], 1), along_x(sent[1], 3)
-    up, down = along_x(sent[2], 1), along_x(sent[3], 3)
-    up_twice, down_twice = along_x(up_twice, 1), along_x(down_twice, 3)
+    own = call(
+        own_kernel,
+        shape(own, LOW),
+        [HBM] * 2,
+        LARGE_VMEM,
+        HBM,
+        [pltpu.VMEM(own, LOW), dma((4,)), dma((2,))],
+    )(w_b, w_c)
+    ways = (1, 3, 1, 3)
+    fetched = [along_x(piece, way) for piece, way in zip(sent, ways)]
+    early = list(fetched)
+    fetched[:2] = [along_x(piece, way) for piece, way in zip(fetched[:2], ways)]
+    given = [along_y(piece, way) for piece, way in zip(fetched, ways)]
     summary = lax.all_to_all(summary, "seq", 0, 0)
-    grad_x, grad_bc, weighted, leave_cols = call(
+    grad_x, terms, leave_cols = call(
         local_kernel,
         [
             shape((tokens, WIDE), FULL),
-            shape((tokens, 2 * STATE), FULL),
-            shape((2, tokens, WIDE), LOW),
+            shape((tokens, 2 * WIDE + 4 * STATE), LOW),
             shape((tokens, 2 * HEADS), LOW),
         ],
         [HBM] * 6,
         16 * MIB,
-        [BLOCK] * 4,
+        [BLOCK] * 3,
         held + [dma((6,))],
     )(*local)
     edges = call(
         scan_kernel,
         shape((devices, 2 * rows, STATE), LOW),
-        [BLOCK, HBM],
+        [BLOCK] + [HBM] * (1 + len(early)),
         4 * MIB,
-    )(summary, leave_cols)
+    )(summary, leave_cols, *early)
     edges = lax.all_to_all(edges, "seq", 0, 0)
     grad_bc = call(
         grad_bc_kernel,
         shape((tokens, 2 * STATE), LOW),
-        [BLOCK] * 3 + [HBM] * 2,
+        [BLOCK] * 2,
         8 * MIB,
-    )(weighted, grad_bc, edges, up, down)
+    )(terms, edges)
     others = [along_x(grad_bc, step) for step in (1, 2, 3)]
-    grad_x = call(
-        grad_x_kernel, shape((tokens, WIDE), LOW), [BLOCK] * 4, 8 * MIB
+    grad_x, done = call(
+        grad_x_kernel,
+        [shape((tokens, WIDE), LOW), shape((8, LANES), FULL)],
+        [BLOCK] * 4,
+        8 * MIB,
+        [BLOCK] * 2,
     )(in_b, leave_cols, grad_x, edges)
 
-    def project(*received):
+    def project(sibling, kind):
         return call(
-            functools.partial(project_kernel, sibling=not received),
-            shape((tokens, columns), LOW),
-            [BLOCK] * (9 + len(received)),
+            functools.partial(project_kernel, sibling=sibling),
+            shape((tokens, columns), kind),
+            [BLOCK] * 14,
             16 * MIB,
-        )(grad_bc, *others, sent[4], up, down, up_twice, down_twice, *received)
+        )(grad_bc, *others, own, *fetched, *given, done)
 
     partner = [(at, at ^ 1) for at in range(lax.axis_size("tp"))]
-    grad_input = project(lax.ppermute(project(), "tp", partner))
+    received = lax.ppermute(project(True, LOW), "tp", partner)
+    grad_input = call(sum_kernel, shape((tokens, columns), LOW), [BLOCK] * 2, 8 * MIB)(
+        project(False, FULL), received
+    )
     return grad_x, grad_input
 
 

time: 84.6 us -> 89.2 us (1.054)
  starting transfers between devices: 31.5 us -> 41.4 us
  waiting for transfers between devices: 30.4 us -> 24.4 us
    ppermute x9, waiting for transfers between devices: 24.9 us -> 9.86 us  [along_x(): lax.ppermute(value, 'tp', [(at, (at + CORES * step) % devices) for at in...]
    ppermute x1 -> x5, waiting for transfers between devices: 0.32 us -> 9.56 us  [the longest x4 9.56 us: along_y(): return lax.ppermute(value, 'seq', pairs)]
    all_to_all x1, waiting for transfers between devices: 5.17 us -> 0.01 us  [per_device(): summary = lax.all_to_all(summary, 'seq', 0, 0)]
    all_to_all x1, waiting for transfers between devices: 0.01 us -> 4.97 us  [per_device(): edges = lax.all_to_all(edges, 'seq', 0, 0)]
    ppermute x1 -> x5, starting transfers between devices: 4.29 us -> 9.03 us  [the longest x4 5.35 us: along_y(): return lax.ppermute(value, 'seq', pairs)]
    all_to_all x1, starting transfers between devices: 5.46 us -> 8.93 us  [per_device(): edges = lax.all_to_all(edges, 'seq', 0, 0)]
    ppermute x9, starting transfers between devices: 9.73 us -> 11.4 us  [along_x(): lax.ppermute(value, 'tp', [(at, (at + CORES * step) % devices) for at in...]
    pallas_call x7 -> x9, Pallas kernels: 14.4 us -> 15 us  [the longest x1 3.65 us: per_device(): call(local_kernel, [shape((tokens, WIDE), FULL), shape((tokens, 2 * WIDE...]
  transfers between devices with their start and end apart: 12 -> 16, of which waited for: 6 -> 5; matrix products, arithmetic and copies ran while one was open for 0% -> 0% of each run, Pallas kernels for 12% -> 13%
where the time goes in v6:
time: 89.2 us; the launch traced here: 88.7 us
  starting transfers between devices  41.4 us (46%)
  waiting for transfers between devices  24.4 us (27%)
  Pallas kernels  18.7 us (21%)
  local copies, waits for them, and re-layouts  3.43 us (4%)
    all_to_all x1, starting transfers between devices, per_device(): summary = lax.all_to_all(summary, 'seq', 0, 0)  12.1 us
    ppermute x9, starting transfers between devices, along_x(): lax.ppermute(value, 'tp', [(at, (at + CORES * step) % devices) for at in...  11.4 us
    ppermute x9, waiting for transfers between devices, along_x(): lax.ppermute(value, 'tp', [(at, (at + CORES * step) % devices) for at in...  9.86 us
    ppermute x4, waiting for transfers between devices, along_y(): return lax.ppermute(value, 'seq', pairs)  9.56 us
    all_to_all x1, starting transfers between devices, per_device(): edges = lax.all_to_all(edges, 'seq', 0, 0)  8.93 us
    ppermute x4, starting transfers between devices, along_y(): return lax.ppermute(value, 'seq', pairs)  5.35 us
    all_to_all x1, waiting for transfers between devices, per_device(): edges = lax.all_to_all(edges, 'seq', 0, 0)  4.97 us
    pallas_call x1, Pallas kernels, per_device(): call(summary_kernel, shape((devices, 2 * rows + 8, STATE), LOW), [HBM] *...  3.68 us
  transfers between devices with their start and end apart: 16, of which 5 were waited for; matrix products, arithmetic and copies ran while one was open for 0% of the time, Pallas kernels for 13%

profile of v6, /device:TPU:1, one launch (start us, length us, event | category | flops | bytes accessed | tf_op | source)
XLA Modules:
  0.0 88.7 jit_solution(1273957808970932379)
XLA Ops:
  0.6 3.7 %shard_map.96._ = bf16[32,72,128]{2,1,0:T(8,128)(2,1)} custom-call(s32[4]{0:T(128)} %lengths_hbm.3, f32[16,256]{1,0:T(8,128)} %log_hbm.3, bf16[256,1024]{1,0:T(8,128)(2,1)} %x_hbm.3, bf16[256,128]{1,0:T(8,128)(2,1)} %b_ref.1, bf16[256,1024]{1,0:T(8,128)(2,1)} %dy_hbm.3, bf16[256,128]{1,0:T(8,128)(2,1)} %c_hbm.3), custom_call_target="tpu_custom_call" | custom-call | flops 1000 | bytes 1000 | tf_op jit(solution)/shard_map/pallas_call | solution.py:400
  4.3 12.1 %all-to-all-start = ((bf16[32,72,128]{2,1,0:T(8,128)(2,1)}), bf16[32,72,128]{2,1,0:T(8,128)(2,1)S(1)}, u32[]{:S(2)}, u32[]{:S(2)}) async-start(bf16[32,72,128]{2,1,0:T(8,128)(2,1)} %shard_map.96._), calls=%async_computation | async-start | bytes 1179648 | tf_op jit(solution)/shard_map/all_to_all | solution.py:432
  16.4 0.0 copy-start.1
  16.4 0.0 copy-start.2
  16.4 0.0 copy-start.7
  16.4 0.0 copy-start.8
  16.4 0.0 copy-start.9
  16.4 0.0 copy-start.10
  16.5 2.5 %shard_map.97 = (bf16[512,256]{1,0:T(8,128)(2,1)}, bf16[512,256]{1,0:T(8,128)(2,1)}, bf16[1024,256]{1,0:T(8,128)(2,1)}, bf16[1024,256]{1,0:T(8,128)(2,1)}) custom-call(bf16[32,72,128]{2,1,0:T(8,128)(2,1)} %shard_map.96._, bf16[8192,128]{1,0:T(8,128)(2,1)} %w_b_hbm.3, bf16[8192,128]{1,0:T(8,128)(2,1)} %w_c_hbm.3), custom_call_target="tpu_custom_call" | custom-call | flops 1000 | bytes 1000 | tf_op jit(solution)/shard_map/pallas_call | solution.py:410
  18.9 1.3 %collective-permute-start.2 = (bf16[1024,256]{1,0:T(8,128)(2,1)}, bf16[1024,256]{1,0:T(8,128)(2,1)S(1)}, u32[]{:S(2)}, u32[]{:S(2)}) collective-permute-start(bf16[1024,256]{1,0:T(8,128)(2,1)} %get-tuple-element.15), channel_id=1, source_target_pairs={{0,2},{1,3},{2,4},{3,5},{4,6},{5,7},{6,0},{7,1},{8,10},{9,11},{10,... | collective-permute-start | bytes 1572872 | tf_op jit(solution)/shard_map/ppermute | solution.py:376
  20.2 1.5 %collective-permute-start.3 = (bf16[1024,256]{1,0:T(8,128)(2,1)}, bf16[1024,256]{1,0:T(8,128)(2,1)S(1)}, u32[]{:S(2)}, u32[]{:S(2)}) collective-permute-start(bf16[1024,256]{1,0:T(8,128)(2,1)} %get-tuple-element.16), channel_id=1, source_target_pairs={{0,6},{1,7},{2,0},{3,1},{4,2},{5,3},{6,4},{7,5},{8,14},{9,15},{10,... | collective-permute-start | bytes 1572872 | tf_op jit(solution)/shard_map/ppermute | solution.py:376
  21.7 0.0 collective-permute-start
  21.7 2.7 %collective-permute-start.1 = (bf16[512,256]{1,0:T(8,128)(2,1)}, bf16[512,256]{1,0:T(8,128)(2,1)}, u32[]{:S(2)}, u32[]{:S(2)}) collective-permute-start(bf16[512,256]{1,0:T(8,128)(2,1)} %get-tuple-element.14), channel_id=1, source_target_pairs={{0,6},{1,7},{2,0},{3,1},{4,2},{5,3},{6,4},{7,5},{8,14},{9,15},{10,... | collective-permute-start | bytes 786440 | tf_op jit(solution)/shard_map/ppermute | solution.py:376
  24.4 3.6 %shard_map.95 = (f32[256,1024]{1,0:T(8,128)S(1)}, bf16[256,2560]{1,0:T(8,128)(2,1)S(1)}, bf16[256,32]{1,0:T(8,128)(2,1)S(1)}) custom-call(s32[4]{0:T(128)S(1)} %copy-done.10, f32[16,256]{1,0:T(8,128)S(1)} %copy-done.9, bf16[256,1024]{1,0:T(8,128)(2,1)S(1)} %copy-done.1, bf16[256,128]{1,0:T(8,128)(2,1)S(1)} %copy-done.7, bf16[256,1024]{1,0:T(8,128)(2,1)S(1)} %copy-done.2, ...), custom_call_target="tpu_custom_call" | custom-call | flops 1000 | bytes 1000 | tf_op jit(solution)/shard_map/pallas_call | solution.py:433
  28.0 1.1 %copy-done.3 = bf16[256,2560]{1,0:T(8,128)(2,1)} copy-done((bf16[256,2560]{1,0:T(8,128)(2,1)}, bf16[256,2560]{1,0:T(8,128)(2,1)S(1)}, u32[]{:S(2)}) %copy-start.3) | copy-done | bytes 1310744
  29.1 1.0 %copy-done.5 = f32[256,1024]{1,0:T(8,128)} copy-done((f32[256,1024]{1,0:T(8,128)}, f32[256,1024]{1,0:T(8,128)S(1)}, u32[]{:S(2)}) %copy-start.5) | copy-done | bytes 1048600
  30.1 8.4 %collective-permute-done.refs_1_ = bf16[512,256]{1,0:T(8,128)(2,1)S(1)} collective-permute-done((bf16[512,256]{1,0:T(8,128)(2,1)}, bf16[512,256]{1,0:T(8,128)(2,1)S(1)}, u32[]{:S(2)}, u32[]{:S(2)}) %collective-permute-start) | collective-permute-done | bytes 262176 | tf_op jit(solution)/shard_map/ppermute | solution.py:376
  38.5 0.0 collective-permute-done.2.refs_3_.refs_7_
  38.5 0.0 collective-permute-done.3.refs_4_.refs_8_
  38.5 0.0 all-to-all-done.in_ref
  38.5 0.9 %shard_map.98 = bf16[32,64,128]{2,1,0:T(8,128)(2,1)} custom-call(bf16[32,72,128]{2,1,0:T(8,128)(2,1)S(1)} %all-to-all-done.in_ref, bf16[256,32]{1,0:T(8,128)(2,1)S(1)} %get-tuple-element.11.refs_0_.leave_ref, bf16[512,256]{1,0:T(8,128)(2,1)S(1)} %collective-permute-done.refs_1_, bf16[512,256]{1,0:T(8,128)(2,1)} %collective-permute-done.1.refs_2_, ...), custom_call_target="tpu_custom_call" | custom-call | flops 1000 | bytes 1000 | tf_op jit(solution)/shard_map/pallas_call | solution.py:445
  39.5 8.9 %all-to-all-start.1 = ((bf16[32,64,128]{2,1,0:T(8,128)(2,1)}), bf16[32,64,128]{2,1,0:T(8,128)(2,1)S(1)}, u32[]{:S(2)}, u32[]{:S(2)}) async-start(bf16[32,64,128]{2,1,0:T(8,128)(2,1)} %shard_map.98), calls=%async_computation.1 | async-start | bytes 1048576 | tf_op jit(solution)/shard_map/all_to_all | solution.py:451
  48.4 1.1 %collective-permute-start.7 = (bf16[512,256]{1,0:T(8,128)(2,1)S(1)}, bf16[512,256]{1,0:T(8,128)(2,1)S(1)}, u32[]{:S(2)}, u32[]{:S(2)}) collective-permute-start(bf16[512,256]{1,0:T(8,128)(2,1)S(1)} %collective-permute-done.refs_1_), channel_id=1, source_target_pairs={{0,2},{1,3},{2,4},{3,5},{4,6},{5,7},{6,0},{7,1},{8,10},{9,11},{10,... | collective-permute-start | bytes 786440 | tf_op jit(solution)/shard_map/ppermute | solution.py:376
  49.5 1.7 %collective-permute-start.8 = (bf16[512,256]{1,0:T(8,128)(2,1)}, bf16[512,256]{1,0:T(8,128)(2,1)S(1)}, u32[]{:S(2)}, u32[]{:S(2)}) collective-permute-start(bf16[512,256]{1,0:T(8,128)(2,1)} %collective-permute-done.1.refs_2_), channel_id=1, source_target_pairs={{0,6},{1,7},{2,0},{3,1},{4,2},{5,3},{6,4},{7,5},{8,14},{9,15},{10,... | collective-permute-start | bytes 786440 | tf_op jit(solution)/shard_map/ppermute | solution.py:376
  51.2 1.2 %collective-permute-start.11 = (bf16[1024,256]{1,0:T(8,128)(2,1)S(1)}, bf16[1024,256]{1,0:T(8,128)(2,1)S(1)}, u32[]{:S(2)}, u32[]{:S(2)}) collective-permute-start(bf16[1024,256]{1,0:T(8,128)(2,1)S(1)} %collective-permute-done.2.refs_3_.refs_7_), channel_id=1, source_target_pairs={{0,8},{8,16},{16,24},{24,0},{32,40},{40,48},{48,56},{56,32},{64,72... | collective-permute-start | bytes 1572872 | tf_op jit(solution)/shard_map/ppermute | solution.py:386
  52.4 1.4 %collective-permute-start.12 = (bf16[1024,256]{1,0:T(8,128)(2,1)S(1)}, bf16[1024,256]{1,0:T(8,128)(2,1)S(1)}, u32[]{:S(2)}, u32[]{:S(2)}) collective-permute-start(bf16[1024,256]{1,0:T(8,128)(2,1)S(1)} %collective-permute-done.3.refs_4_.refs_8_), channel_id=1, source_target_pairs={{0,24},{8,0},{16,8},{24,16},{32,56},{40,32},{48,40},{56,48},{64,88... | collective-permute-start | bytes 1572872 | tf_op jit(solution)/shard_map/ppermute | solution.py:386
  53.8 1.4 %collective-permute-done.7.refs_5_ = bf16[512,256]{1,0:T(8,128)(2,1)S(1)} collective-permute-done((bf16[512,256]{1,0:T(8,128)(2,1)S(1)}, bf16[512,256]{1,0:T(8,128)(2,1)S(1)}, u32[]{:S(2)}, u32[]{:S(2)}) %collective-permute-start.7) | collective-permute-done | bytes 262176 | tf_op jit(solution)/shard_map/ppermute | solution.py:376
  55.2 1.1 %collective-permute-start.9 = (bf16[512,256]{1,0:T(8,128)(2,1)S(1)}, bf16[512,256]{1,0:T(8,128)(2,1)S(1)}, u32[]{:S(2)}, u32[]{:S(2)}) collective-permute-start(bf16[512,256]{1,0:T(8,128)(2,1)S(1)} %collective-permute-done.7.refs_5_), channel_id=1, source_target_pairs={{0,8},{8,16},{16,24},{24,0},{32,40},{40,48},{48,56},{56,32},{64,72... | collective-permute-start | bytes 786440 | tf_op jit(solution)/shard_map/ppermute | solution.py:386
  56.3 0.0 collective-permute-done.8.refs_6_
  56.3 1.6 %collective-permute-start.10 = (bf16[512,256]{1,0:T(8,128)(2,1)S(1)}, bf16[512,256]{1,0:T(8,128)(2,1)}, u32[]{:S(2)}, u32[]{:S(2)}) collective-permute-start(bf16[512,256]{1,0:T(8,128)(2,1)S(1)} %collective-permute-done.8.refs_6_), channel_id=1, source_target_pairs={{0,24},{8,0},{16,8},{24,16},{32,56},{40,32},{48,40},{56,48},{64,88... | collective-permute-start | bytes 786440 | tf_op jit(solution)/shard_map/ppermute | solution.py:386
  57.9 5.0 %all-to-all-done.1.edge_ref = bf16[32,64,128]{2,1,0:T(8,128)(2,1)S(1)} async-done(((bf16[32,64,128]{2,1,0:T(8,128)(2,1)}), bf16[32,64,128]{2,1,0:T(8,128)(2,1)S(1)}, u32[]{:S(2)}, u32[]{:S(2)}) %all-to-all-start.1) | async-done | bytes 524320 | tf_op jit(solution)/shard_map/all_to_all | solution.py:451
  62.9 1.3 %copy-done.4 = bf16[256,2560]{1,0:T(8,128)(2,1)S(1)} copy-done((bf16[256,2560]{1,0:T(8,128)(2,1)S(1)}, bf16[256,2560]{1,0:T(8,128)(2,1)}, u32[]{:S(2)}) %copy-start.4) | copy-done | bytes 1310744
  64.2 0.4 shard_map.100.refs_0_
  64.6 0.7 collective-permute-start.4
  65.3 9.5 %collective-permute-done.9.refs_9_ = bf16[512,256]{1,0:T(8,128)(2,1)S(1)} collective-permute-done((bf16[512,256]{1,0:T(8,128)(2,1)S(1)}, bf16[512,256]{1,0:T(8,128)(2,1)S(1)}, u32[]{:S(2)}, u32[]{:S(2)}) %collective-permute-start.9) | collective-permute-done | bytes 262176 | tf_op jit(solution)/shard_map/ppermute | solution.py:386
  74.9 1.3 %collective-permute-start.5 = (bf16[256,256]{1,0:T(8,128)(2,1)S(1)}, bf16[256,256]{1,0:T(8,128)(2,1)S(1)}, u32[]{:S(2)}, u32[]{:S(2)}) collective-permute-start(bf16[256,256]{1,0:T(8,128)(2,1)S(1)} %shard_map.100.refs_0_), channel_id=1, source_target_pairs={{0,4},{1,5},{2,6},{3,7},{4,0},{5,1},{6,2},{7,3},{8,12},{9,13},{10,... | collective-permute-start | bytes 393224 | tf_op jit(solution)/shard_map/ppermute | solution.py:376
  76.2 1.1 %collective-permute-start.6 = (bf16[256,256]{1,0:T(8,128)(2,1)S(1)}, bf16[256,256]{1,0:T(8,128)(2,1)S(1)}, u32[]{:S(2)}, u32[]{:S(2)}) collective-permute-start(bf16[256,256]{1,0:T(8,128)(2,1)S(1)} %shard_map.100.refs_0_), channel_id=1, source_target_pairs={{0,6},{1,7},{2,0},{3,1},{4,2},{5,3},{6,4},{7,5},{8,14},{9,15},{10,... | collective-permute-start | bytes 393224 | tf_op jit(solution)/shard_map/ppermute | solution.py:376
  77.4 2.1 %shard_map.101.refs_4_ = bf16[2048,256]{1,0:T(8,128)(2,1)} custom-call(bf16[8192,128]{1,0:T(8,128)(2,1)} %w_b_hbm.3, bf16[8192,128]{1,0:T(8,128)(2,1)} %w_c_hbm.3), custom_call_target="tpu_custom_call" | custom-call | flops 1000 | bytes 1000 | tf_op jit(solution)/shard_map/pallas_call | solution.py:419
  79.4 1.2 %shard_map.99 = (bf16[256,1024]{1,0:T(8,128)(2,1)}, f32[8,128]{1,0:T(8,128)S(1)}) custom-call(bf16[256,128]{1,0:T(8,128)(2,1)S(1)} %copy-done.7, bf16[256,32]{1,0:T(8,128)(2,1)S(1)} %get-tuple-element.11.refs_0_.leave_ref, f32[256,1024]{1,0:T(8,128)S(1)} %copy-done.6, bf16[32,64,128]{2,1,0:T(8,128)(2,1)S(1)} %all-to-all-done.1.edge_ref), custom_call_target="tpu_custom_call" | custom-call | flops 1000 | bytes 1000 | tf_op jit(solution)/shard_map/pallas_call | solution.py:459
  80.7 0.0 collective-permute-done.11.refs_11_
  80.7 0.0 collective-permute-done.12.refs_12_
  80.7 0.0 collective-permute-done.4.refs_1_
  80.7 0.0 collective-permute-done.5.refs_2_
  80.7 0.1 collective-permute-done.6.refs_3_
  80.8 1.7 %shard_map.103 = bf16[256,1024]{1,0:T(8,128)(2,1)S(1)} custom-call(bf16[256,256]{1,0:T(8,128)(2,1)S(1)} %shard_map.100.refs_0_, bf16[256,256]{1,0:T(8,128)(2,1)S(1)} %collective-permute-done.4.refs_1_, bf16[256,256]{1,0:T(8,128)(2,1)S(1)} %collective-permute-done.5.refs_2_, bf16[256,256]{1,0:T(8,128)(2,1)S(1)} %collective-permute-done.6.refs_3_, ...), custom_call_target="tpu_custom_call" | custom-call | flops 1000 | bytes 1000 | tf_op jit(solution)/shard_map/pallas_call | solution.py:468
  82.5 3.7 %collective-permute-start.13 = (bf16[256,1024]{1,0:T(8,128)(2,1)S(1)}, bf16[256,1024]{1,0:T(8,128)(2,1)S(1)}, u32[]{:S(2)}, u32[]{:S(2)}) collective-permute-start(bf16[256,1024]{1,0:T(8,128)(2,1)S(1)} %shard_map.103), channel_id=1, source_target_pairs={{0,1},{1,0},{2,3},{3,2},{4,5},{5,4},{6,7},{7,6},{8,9},{9,8},{10,11... | collective-permute-start | bytes 1572872 | tf_op jit(solution)/shard_map/ppermute | solution.py:476
  86.1 1.7 %shard_map.102.kept_ref = f32[256,1024]{1,0:T(8,128)S(1)} custom-call(bf16[256,256]{1,0:T(8,128)(2,1)S(1)} %shard_map.100.refs_0_, bf16[256,256]{1,0:T(8,128)(2,1)S(1)} %collective-permute-done.4.refs_1_, bf16[256,256]{1,0:T(8,128)(2,1)S(1)} %collective-permute-done.5.refs_2_, bf16[256,256]{1,0:T(8,128)(2,1)S(1)} %collective-permute-done.6.refs_3_, ...), custom_call_target="tpu_custom_call" | custom-call | flops 1000 | bytes 1000 | tf_op jit(solution)/shard_map/pallas_call | solution.py:468
  87.8 0.9 shard_map.104
  (16 shorter events, 0.0 us)
Async XLA Ops:
  4.3 34.2 %all-to-all-start = ((bf16[32,72,128]{2,1,0:T(8,128)(2,1)}), bf16[32,72,128]{2,1,0:T(8,128)(2,1)S(1)}, u32[]{:S(2)}, u32[]{:S(2)}) async-start(bf16[32,72,128]{2,1,0:T(8,128)(2,1)} %shard_map.96._), calls=%async_computation | async-start | bytes 1179648 | tf_op jit(solution)/shard_map/all_to_all | solution.py:432
  16.4 8.0 %copy-start.1 = (bf16[256,1024]{1,0:T(8,128)(2,1)S(1)}, bf16[256,1024]{1,0:T(8,128)(2,1)}, u32[]{:S(2)}) copy-start(bf16[256,1024]{1,0:T(8,128)(2,1)} %x_hbm.3) | copy-start | bytes 1572868
  16.4 8.0 %copy-start.2 = (bf16[256,1024]{1,0:T(8,128)(2,1)S(1)}, bf16[256,1024]{1,0:T(8,128)(2,1)}, u32[]{:S(2)}) copy-start(bf16[256,1024]{1,0:T(8,128)(2,1)} %dy_hbm.3) | copy-start | bytes 1572868
  16.4 7.9 %copy-start.7 = (bf16[256,128]{1,0:T(8,128)(2,1)S(1)}, bf16[256,128]{1,0:T(8,128)(2,1)}, u32[]{:S(2)}) copy-start(bf16[256,128]{1,0:T(8,128)(2,1)} %b_ref.1) | copy-start | bytes 196612
  16.4 7.9 %copy-start.8 = (bf16[256,128]{1,0:T(8,128)(2,1)S(1)}, bf16[256,128]{1,0:T(8,128)(2,1)}, u32[]{:S(2)}) copy-start(bf16[256,128]{1,0:T(8,128)(2,1)} %c_hbm.3) | copy-start | bytes 196612
  16.4 7.9 %copy-start.9 = (f32[16,256]{1,0:T(8,128)S(1)}, f32[16,256]{1,0:T(8,128)}, u32[]{:S(2)}) copy-start(f32[16,256]{1,0:T(8,128)} %log_hbm.3) | copy-start | bytes 49156
  16.4 7.9 %copy-start.10 = (s32[4]{0:T(128)S(1)}, s32[4]{0:T(128)}, u32[]{:S(2)}) copy-start(s32[4]{0:T(128)} %lengths_hbm.3) | copy-start | bytes 52
  18.9 19.6 %collective-permute-start.2 = (bf16[1024,256]{1,0:T(8,128)(2,1)}, bf16[1024,256]{1,0:T(8,128)(2,1)S(1)}, u32[]{:S(2)}, u32[]{:S(2)}) collective-permute-start(bf16[1024,256]{1,0:T(8,128)(2,1)} %get-tuple-element.15), channel_id=1, source_target_pairs={{0,2},{1,3},{2,4},{3,5},{4,6},{5,7},{6,0},{7,1},{8,10},{9,11},{10,... | collective-permute-start | bytes 1572872 | tf_op jit(solution)/shard_map/ppermute | solution.py:376
  20.2 18.3 %collective-permute-start.3 = (bf16[1024,256]{1,0:T(8,128)(2,1)}, bf16[1024,256]{1,0:T(8,128)(2,1)S(1)}, u32[]{:S(2)}, u32[]{:S(2)}) collective-permute-start(bf16[1024,256]{1,0:T(8,128)(2,1)} %get-tuple-element.16), channel_id=1, source_target_pairs={{0,6},{1,7},{2,0},{3,1},{4,2},{5,3},{6,4},{7,5},{8,14},{9,15},{10,... | collective-permute-start | bytes 1572872 | tf_op jit(solution)/shard_map/ppermute | solution.py:376
  21.7 16.8 %collective-permute-start = (bf16[512,256]{1,0:T(8,128)(2,1)}, bf16[512,256]{1,0:T(8,128)(2,1)S(1)}, u32[]{:S(2)}, u32[]{:S(2)}) collective-permute-start(bf16[512,256]{1,0:T(8,128)(2,1)} %get-tuple-element.13), channel_id=1, source_target_pairs={{0,2},{1,3},{2,4},{3,5},{4,6},{5,7},{6,0},{7,1},{8,10},{9,11},{10,... | collective-permute-start | bytes 786440 | tf_op jit(solution)/shard_map/ppermute | solution.py:376
  21.7 16.8 %collective-permute-start.1 = (bf16[512,256]{1,0:T(8,128)(2,1)}, bf16[512,256]{1,0:T(8,128)(2,1)}, u32[]{:S(2)}, u32[]{:S(2)}) collective-permute-start(bf16[512,256]{1,0:T(8,128)(2,1)} %get-tuple-element.14), channel_id=1, source_target_pairs={{0,6},{1,7},{2,0},{3,1},{4,2},{5,3},{6,4},{7,5},{8,14},{9,15},{10,... | collective-permute-start | bytes 786440 | tf_op jit(solution)/shard_map/ppermute | solution.py:376
  28.0 1.1 %copy-start.3 = (bf16[256,2560]{1,0:T(8,128)(2,1)}, bf16[256,2560]{1,0:T(8,128)(2,1)S(1)}, u32[]{:S(2)}) copy-start(bf16[256,2560]{1,0:T(8,128)(2,1)S(1)} %get-tuple-element.18.terms_ref) | copy-start | bytes 3932164
  29.1 1.0 %copy-start.5 = (f32[256,1024]{1,0:T(8,128)}, f32[256,1024]{1,0:T(8,128)S(1)}, u32[]{:S(2)}) copy-start(f32[256,1024]{1,0:T(8,128)S(1)} %get-tuple-element.12.local_ref) | copy-start | bytes 3145732
  39.5 23.4 %all-to-all-start.1 = ((bf16[32,64,128]{2,1,0:T(8,128)(2,1)}), bf16[32,64,128]{2,1,0:T(8,128)(2,1)S(1)}, u32[]{:S(2)}, u32[]{:S(2)}) async-start(bf16[32,64,128]{2,1,0:T(8,128)(2,1)} %shard_map.98), calls=%async_computation.1 | async-start | bytes 1048576 | tf_op jit(solution)/shard_map/all_to_all | solution.py:451
  48.4 6.8 %collective-permute-start.7 = (bf16[512,256]{1,0:T(8,128)(2,1)S(1)}, bf16[512,256]{1,0:T(8,128)(2,1)S(1)}, u32[]{:S(2)}, u32[]{:S(2)}) collective-permute-start(bf16[512,256]{1,0:T(8,128)(2,1)S(1)} %collective-permute-done.refs_1_), channel_id=1, source_target_pairs={{0,2},{1,3},{2,4},{3,5},{4,6},{5,7},{6,0},{7,1},{8,10},{9,11},{10,... | collective-permute-start | bytes 786440 | tf_op jit(solution)/shard_map/ppermute | solution.py:376
  49.5 6.8 %collective-permute-start.8 = (bf16[512,256]{1,0:T(8,128)(2,1)}, bf16[512,256]{1,0:T(8,128)(2,1)S(1)}, u32[]{:S(2)}, u32[]{:S(2)}) collective-permute-start(bf16[512,256]{1,0:T(8,128)(2,1)} %collective-permute-done.1.refs_2_), channel_id=1, source_target_pairs={{0,6},{1,7},{2,0},{3,1},{4,2},{5,3},{6,4},{7,5},{8,14},{9,15},{10,... | collective-permute-start | bytes 786440 | tf_op jit(solution)/shard_map/ppermute | solution.py:376
  51.2 29.5 %collective-permute-start.11 = (bf16[1024,256]{1,0:T(8,128)(2,1)S(1)}, bf16[1024,256]{1,0:T(8,128)(2,1)S(1)}, u32[]{:S(2)}, u32[]{:S(2)}) collective-permute-start(bf16[1024,256]{1,0:T(8,128)(2,1)S(1)} %collective-permute-done.2.refs_3_.refs_7_), channel_id=1, source_target_pairs={{0,8},{8,16},{16,24},{24,0},{32,40},{40,48},{48,56},{56,32},{64,72... | collective-permute-start | bytes 1572872 | tf_op jit(solution)/shard_map/ppermute | solution.py:386
  52.4 28.3 %collective-permute-start.12 = (bf16[1024,256]{1,0:T(8,128)(2,1)S(1)}, bf16[1024,256]{1,0:T(8,128)(2,1)S(1)}, u32[]{:S(2)}, u32[]{:S(2)}) collective-permute-start(bf16[1024,256]{1,0:T(8,128)(2,1)S(1)} %collective-permute-done.3.refs_4_.refs_8_), channel_id=1, source_target_pairs={{0,24},{8,0},{16,8},{24,16},{32,56},{40,32},{48,40},{56,48},{64,88... | collective-permute-start | bytes 1572872 | tf_op jit(solution)/shard_map/ppermute | solution.py:386
  55.2 19.7 %collective-permute-start.9 = (bf16[512,256]{1,0:T(8,128)(2,1)S(1)}, bf16[512,256]{1,0:T(8,128)(2,1)S(1)}, u32[]{:S(2)}, u32[]{:S(2)}) collective-permute-start(bf16[512,256]{1,0:T(8,128)(2,1)S(1)} %collective-permute-done.7.refs_5_), channel_id=1, source_target_pairs={{0,8},{8,16},{16,24},{24,0},{32,40},{40,48},{48,56},{56,32},{64,72... | collective-permute-start | bytes 786440 | tf_op jit(solution)/shard_map/ppermute | solution.py:386
  56.3 19.9 %collective-permute-start.10 = (bf16[512,256]{1,0:T(8,128)(2,1)S(1)}, bf16[512,256]{1,0:T(8,128)(2,1)}, u32[]{:S(2)}, u32[]{:S(2)}) collective-permute-start(bf16[512,256]{1,0:T(8,128)(2,1)S(1)} %collective-permute-done.8.refs_6_), channel_id=1, source_target_pairs={{0,24},{8,0},{16,8},{24,16},{32,56},{40,32},{48,40},{56,48},{64,88... | collective-permute-start | bytes 786440 | tf_op jit(solution)/shard_map/ppermute | solution.py:386
  62.9 1.3 %copy-start.4 = (bf16[256,2560]{1,0:T(8,128)(2,1)S(1)}, bf16[256,2560]{1,0:T(8,128)(2,1)}, u32[]{:S(2)}) copy-start(bf16[256,2560]{1,0:T(8,128)(2,1)} %copy-done.3) | copy-start | bytes 3932164
  64.6 14.8 %copy-start.6 = (f32[256,1024]{1,0:T(8,128)S(1)}, f32[256,1024]{1,0:T(8,128)}, u32[]{:S(2)}) copy-start(f32[256,1024]{1,0:T(8,128)} %copy-done.5) | copy-start | bytes 3145732
  64.6 16.1 %collective-permute-start.4 = (bf16[256,256]{1,0:T(8,128)(2,1)S(1)}, bf16[256,256]{1,0:T(8,128)(2,1)S(1)}, u32[]{:S(2)}, u32[]{:S(2)}) collective-permute-start(bf16[256,256]{1,0:T(8,128)(2,1)S(1)} %shard_map.100.refs_0_), channel_id=1, source_target_pairs={{0,2},{1,3},{2,4},{3,5},{4,6},{5,7},{6,0},{7,1},{8,10},{9,11},{10,... | collective-permute-start | bytes 393224 | tf_op jit(solution)/shard_map/ppermute | solution.py:376
  74.9 5.8 %collective-permute-start.5 = (bf16[256,256]{1,0:T(8,128)(2,1)S(1)}, bf16[256,256]{1,0:T(8,128)(2,1)S(1)}, u32[]{:S(2)}, u32[]{:S(2)}) collective-permute-start(bf16[256,256]{1,0:T(8,128)(2,1)S(1)} %shard_map.100.refs_0_), channel_id=1, source_target_pairs={{0,4},{1,5},{2,6},{3,7},{4,0},{5,1},{6,2},{7,3},{8,12},{9,13},{10,... | collective-permute-start | bytes 393224 | tf_op jit(solution)/shard_map/ppermute | solution.py:376
  76.2 4.6 %collective-permute-start.6 = (bf16[256,256]{1,0:T(8,128)(2,1)S(1)}, bf16[256,256]{1,0:T(8,128)(2,1)S(1)}, u32[]{:S(2)}, u32[]{:S(2)}) collective-permute-start(bf16[256,256]{1,0:T(8,128)(2,1)S(1)} %shard_map.100.refs_0_), channel_id=1, source_target_pairs={{0,6},{1,7},{2,0},{3,1},{4,2},{5,3},{6,4},{7,5},{8,14},{9,15},{10,... | collective-permute-start | bytes 393224 | tf_op jit(solution)/shard_map/ppermute | solution.py:376
  79.4 1.3 %copy-start = (bf16[2048,256]{1,0:T(8,128)(2,1)S(1)}, bf16[2048,256]{1,0:T(8,128)(2,1)}, u32[]{:S(2)}) copy-start(bf16[2048,256]{1,0:T(8,128)(2,1)} %shard_map.101.refs_4_) | copy-start | bytes 3145732
  82.5 5.4 %collective-permute-start.13 = (bf16[256,1024]{1,0:T(8,128)(2,1)S(1)}, bf16[256,1024]{1,0:T(8,128)(2,1)S(1)}, u32[]{:S(2)}, u32[]{:S(2)}) collective-permute-start(bf16[256,1024]{1,0:T(8,128)(2,1)S(1)} %shard_map.103), channel_id=1, source_target_pairs={{0,1},{1,0},{2,3},{3,2},{4,5},{5,4},{6,7},{7,6},{8,9},{9,8},{10,11... | collective-permute-start | bytes 1572872 | tf_op jit(solution)/shard_map/ppermute | solution.py:476

commit v7 on v6

--- a/solution.py
+++ b/solution.py
@@ -16,7 +16,7 @@
 PAIRS = WIDE // LANES
 CORES = 2
 ALONG_Y = 4
-ROUTE = ((2, 0, 1), (2, 1, 1), (1, 0, 2), (3, 0, 2))
+ROUTE = ((2, 1), (2, 1), (1, 4), (3, 4))
 LOW = jnp.bfloat16
 FULL = jnp.float32
 NN = (((1,), (0,)), ((), ()))
@@ -166,14 +166,21 @@
 def stage_kernel(_, w_b_hbm, w_c_hbm, *refs):
     sent_refs, held_refs, sems = refs[: len(ROUTE)], refs[len(ROUTE) : -2], refs[-2:]
     part = sent_refs[0].shape[0]
+    columns = 2 * part
     me = lax.axis_index("tp")
     core, chips = lax.rem(me, CORES), lax.axis_size("tp") // CORES
     half = lax.rem(core + 1 + lax.rem(lax.axis_index("seq"), 2), CORES)
     pieces = []
-    for (step, first, parts), held_ref, sent_ref in zip(ROUTE, held_refs, sent_refs):
-        target = lax.rem(me // CORES + step, chips)
-        row = (target * CORES + half) * 2 * part + first * part
-        pieces.append((pl.ds(pl.multiple_of(row, part), parts * part), held_ref, sent_ref))
+    for at, ((step, _), held_ref, sent_ref) in enumerate(zip(ROUTE, held_refs, sent_refs)):
+        first = lax.rem(me // CORES + step, chips) * CORES
+        if at < 2:
+            row = pl.multiple_of((first + half) * columns + at * part, part)
+            pieces.append((pl.ds(row, part), held_ref, sent_ref))
+        else:
+            for which, other in enumerate((1 - core, core)):
+                row = pl.multiple_of((first + other) * columns, columns)
+                to = pl.ds(which * columns, columns)
+                pieces.append((pl.ds(row, columns), held_ref.at[to, :], sent_ref.at[to, :]))
     pass_through(pieces, w_b_hbm, w_c_hbm, *sems)
 
 
@@ -189,8 +196,7 @@
     pass_through(pieces, w_b_hbm, w_c_hbm, *sems)
 
 
-def scan_kernel(in_ref, *refs):
-    out_ref = refs[-1]
+def scan_kernel(in_ref, _, out_ref):
     devices, rows = out_ref.shape[0], out_ref.shape[1] // 2
     decays = []
     for at in range(devices):
@@ -309,7 +315,8 @@
         terms_ref[:, low + STATE : low + 2 * STATE] = (part - high.astype(FULL)).astype(LOW)
 
 
-def grad_bc_kernel(terms_ref, edge_ref, out_ref):
+def grad_bc_kernel(terms_ref, edge_ref, *refs):
+    out_ref = refs[-1]
     rows = edge_ref.shape[1] // 2
     for side in range(2):
         which = slice(rows, 2 * rows) if side == 0 else slice(0, rows)
@@ -334,21 +341,26 @@
 
 
 def project_kernel(*refs, sibling):
-    grads, own, fetched, given, (_, out_ref) = refs[:4], refs[4], refs[5:9], refs[9:13], refs[13:]
+    grads, (own, up, down), fetched, given, (_, out_ref) = (
+        refs[:4],
+        refs[4:7],
+        refs[7:9],
+        refs[9:11],
+        refs[11:],
+    )
     columns = out_ref.shape[1]
     half = slice(0, columns) if sibling else slice(columns, 2 * columns)
-
-    def products(weights):
-        twice_first, twice_second, up, down = weights
-        total = mul(grads[0][...], own[half, :], NT)
-        total += mul(grads[1][...], up[...], NT)
-        total += mul(grads[3][...], down[...], NT)
-        twice = [mul(grads[2][...], part[...], NT) for part in (twice_first, twice_second)]
-        out_ref[...] = (total + jnp.concatenate(twice, axis=1)).astype(out_ref.dtype)
+    total = mul(grads[0][...], own[half, :], NT)
+    total += mul(grads[1][...], up[half, :], NT)
+    total += mul(grads[3][...], down[half, :], NT)
+
+    def finish(pieces):
+        twice = jnp.concatenate([mul(grads[2][...], piece[...], NT) for piece in pieces], axis=1)
+        out_ref[...] = (total + twice).astype(out_ref.dtype)
 
     here = fetches_sibling() if sibling else jnp.logical_not(fetches_sibling())
-    pl.when(here)(lambda: products(fetched))
-    pl.when(jnp.logical_not(here))(lambda: products(given))
+    pl.when(here)(lambda: finish(fetched))
+    pl.when(jnp.logical_not(here))(lambda: finish(given))
 
 
 def sum_kernel(kept_ref, received_ref, out_ref):
@@ -405,7 +417,7 @@
         BLOCK,
         held + [dma((6,))],
     )(*local)
-    pieces = [(parts * columns // 2, 2 * STATE) for _, _, parts in ROUTE]
+    pieces = [(parts * columns // 2, 2 * STATE) for _, parts in ROUTE]
     own = (CORES * columns, 2 * STATE)
     sent = call(
         stage_kernel,
@@ -414,7 +426,7 @@
         LARGE_VMEM,
         [HBM] * len(pieces),
         [pltpu.VMEM(piece, LOW) for piece in pieces]
-        + [dma((2 * len(pieces),)), dma((len(pieces),))],
+        + [dma((12,)), dma((6,))],
     )(summary, w_b, w_c)
     own = call(
         own_kernel,
@@ -424,10 +436,10 @@
         HBM,
         [pltpu.VMEM(own, LOW), dma((4,)), dma((2,))],
     )(w_b, w_c)
-    ways = (1, 3, 1, 3)
-    fetched = [along_x(piece, way) for piece, way in zip(sent, ways)]
-    early = list(fetched)
-    fetched[:2] = [along_x(piece, way) for piece, way in zip(fetched[:2], ways)]
+    ways = (1, 3)
+    up, down = [along_x(piece, way) for piece, way in zip(sent[2:], ways)]
+    fetched = [along_x(piece, way) for piece, way in zip(sent[:2], ways)]
+    fetched = [along_x(piece, way) for piece, way in zip(fetched, ways)]
     given = [along_y(piece, way) for piece, way in zip(fetched, ways)]
     summary = lax.all_to_all(summary, "seq", 0, 0)
     grad_x, terms, leave_cols = call(
@@ -445,16 +457,16 @@
     edges = call(
         scan_kernel,
         shape((devices, 2 * rows, STATE), LOW),
-        [BLOCK] + [HBM] * (1 + len(early)),
+        [BLOCK, HBM],
         4 * MIB,
-    )(summary, leave_cols, *early)
+    )(summary, leave_cols)
     edges = lax.all_to_all(edges, "seq", 0, 0)
     grad_bc = call(
         grad_bc_kernel,
         shape((tokens, 2 * STATE), LOW),
-        [BLOCK] * 2,
+        [BLOCK, BLOCK, HBM, HBM],
         8 * MIB,
-    )(terms, edges)
+    )(terms, edges, up, down)
     others = [along_x(grad_bc, step) for step in (1, 2, 3)]
     grad_x, done = call(
         grad_x_kernel,
@@ -468,9 +480,9 @@
         return call(
             functools.partial(project_kernel, sibling=sibling),
             shape((tokens, columns), kind),
-            [BLOCK] * 14,
+            [BLOCK] * 12,
             16 * MIB,
-        )(grad_bc, *others, own, *fetched, *given, done)
+        )(grad_bc, *others, own, up, down, *fetched, *given, done)
 
     partner = [(at, at ^ 1) for at in range(lax.axis_size("tp"))]
     received = lax.ppermute(project(True, LOW), "tp", partner)

time: 89.2 us -> 79.2 us (0.89)
  waiting for transfers between devices: 24.4 us -> 18.3 us
  starting transfers between devices: 41.4 us -> 36.7 us
    ppermute x4 -> x2, waiting for transfers between devices: 9.56 us -> 0.01 us  [along_y(): return lax.ppermute(value, 'seq', pairs)]
    all_to_all x1, waiting for transfers between devices: 0.01 us -> 6.01 us  [per_device(): summary = lax.all_to_all(summary, 'seq', 0, 0)]
    all_to_all x1, waiting for transfers between devices: 4.97 us -> 0.01 us  [per_device(): edges = lax.all_to_all(edges, 'seq', 0, 0)]
    all_to_all x1, starting transfers between devices: 8.93 us -> 5.45 us  [per_device(): edges = lax.all_to_all(edges, 'seq', 0, 0)]
    ppermute x4 -> x2, starting transfers between devices: 5.35 us -> 2.68 us  [along_y(): return lax.ppermute(value, 'seq', pairs)]
    ppermute x9, waiting for transfers between devices: 9.86 us -> 12.3 us  [along_x(): lax.ppermute(value, 'tp', [(at, (at + CORES * step) % devices) for at in...]
    ppermute x1, starting transfers between devices: 3.68 us -> 5.09 us  [per_device(): received = lax.ppermute(project(True, LOW), 'tp', partner)]
    unnamed x22 -> x26, local copies, waits for them, and re-layouts: 3.43 us -> 3.43 us
  transfers between devices with their start and end apart: 16 -> 14, of which waited for: 5 -> 5; matrix products, arithmetic and copies ran while one was open for 0% -> 0% of each run, Pallas kernels for 13% -> 17%
where the time goes in v7:
time: 79.2 us; the launch traced here: 78.8 us
  starting transfers between devices  36.7 us (46%)
  Pallas kernels  19.5 us (25%)
  waiting for transfers between devices  18.3 us (23%)
  local copies, waits for them, and re-layouts  3.43 us (4%)
  between operations  0.87 us (1%)
    ppermute x9, waiting for transfers between devices, along_x(): lax.ppermute(value, 'tp', [(at, (at + CORES * step) % devices) for at in...  12.3 us
    all_to_all x1, starting transfers between devices, per_device(): summary = lax.all_to_all(summary, 'seq', 0, 0)  12.1 us
    ppermute x9, starting transfers between devices, along_x(): lax.ppermute(value, 'tp', [(at, (at + CORES * step) % devices) for at in...  11.4 us
    all_to_all x1, waiting for transfers between devices, per_device(): summary = lax.all_to_all(summary, 'seq', 0, 0)  6.01 us
    all_to_all x1, starting transfers between devices, per_device(): edges = lax.all_to_all(edges, 'seq', 0, 0)  5.45 us
    ppermute x1, starting transfers between devices, per_device(): received = lax.ppermute(project(True, LOW), 'tp', partner)  5.09 us
    pallas_call x2, Pallas kernels, project(): call(functools.partial(project_kernel, sibling=sibling), shape((tokens, c...  3.78 us
    pallas_call x1, Pallas kernels, per_device(): call(summary_kernel, shape((devices, 2 * rows + 8, STATE), LOW), [HBM] *...  3.69 us
  transfers between devices with their start and end apart: 14, of which 5 were waited for; matrix products, arithmetic and copies ran while one was open for 0% of the time, Pallas kernels for 17%

profile of v7, /device:TPU:1, one launch (start us, length us, event | category | flops | bytes accessed | tf_op | source)
XLA Modules:
  0.0 78.8 jit_solution(10015538851595189208)
XLA Ops:
  0.6 3.7 %shard_map.96._ = bf16[32,72,128]{2,1,0:T(8,128)(2,1)} custom-call(s32[4]{0:T(128)} %lengths_hbm.3, f32[16,256]{1,0:T(8,128)} %log_hbm.3, bf16[256,1024]{1,0:T(8,128)(2,1)} %x_hbm.3, bf16[256,128]{1,0:T(8,128)(2,1)} %b_ref.1, bf16[256,1024]{1,0:T(8,128)(2,1)} %dy_hbm.3, bf16[256,128]{1,0:T(8,128)(2,1)} %c_hbm.3), custom_call_target="tpu_custom_call" | custom-call | flops 1000 | bytes 1000 | tf_op jit(solution)/shard_map/pallas_call | solution.py:412
  4.3 12.1 %all-to-all-start = ((bf16[32,72,128]{2,1,0:T(8,128)(2,1)}), bf16[32,72,128]{2,1,0:T(8,128)(2,1)S(1)}, u32[]{:S(2)}, u32[]{:S(2)}) async-start(bf16[32,72,128]{2,1,0:T(8,128)(2,1)} %shard_map.96._), calls=%async_computation | async-start | bytes 1179648 | tf_op jit(solution)/shard_map/all_to_all | solution.py:444
  16.4 0.0 copy-start.1
  16.4 0.0 copy-start.2
  16.4 0.0 copy-start.7
  16.4 0.0 copy-start.8
  16.4 0.0 copy-start.9
  16.4 0.0 copy-start.10
  16.5 2.9 %shard_map.99 = (bf16[512,256]{1,0:T(8,128)(2,1)}, bf16[512,256]{1,0:T(8,128)(2,1)}, bf16[2048,256]{1,0:T(8,128)(2,1)}, bf16[2048,256]{1,0:T(8,128)(2,1)}) custom-call(bf16[32,72,128]{2,1,0:T(8,128)(2,1)} %shard_map.96._, bf16[8192,128]{1,0:T(8,128)(2,1)} %w_b_hbm.3, bf16[8192,128]{1,0:T(8,128)(2,1)} %w_c_hbm.3), custom_call_target="tpu_custom_call" | custom-call | flops 1000 | bytes 1000 | tf_op jit(solution)/shard_map/pallas_call | solution.py:422
  19.3 0.0 copy-start.12
  19.3 1.3 %collective-permute-start = (bf16[2048,256]{1,0:T(8,128)(2,1)}, bf16[2048,256]{1,0:T(8,128)(2,1)S(1)}, u32[]{:S(2)}, u32[]{:S(2)}) collective-permute-start(bf16[2048,256]{1,0:T(8,128)(2,1)} %get-tuple-element.15), channel_id=1, source_target_pairs={{0,2},{1,3},{2,4},{3,5},{4,6},{5,7},{6,0},{7,1},{8,10},{9,11},{10,... | collective-permute-start | bytes 3145736 | tf_op jit(solution)/shard_map/ppermute | solution.py:388
  20.6 1.5 %collective-permute-start.1 = (bf16[2048,256]{1,0:T(8,128)(2,1)}, bf16[2048,256]{1,0:T(8,128)(2,1)S(1)}, u32[]{:S(2)}, u32[]{:S(2)}) collective-permute-start(bf16[2048,256]{1,0:T(8,128)(2,1)} %get-tuple-element.16), channel_id=1, source_target_pairs={{0,6},{1,7},{2,0},{3,1},{4,2},{5,3},{6,4},{7,5},{8,14},{9,15},{10,... | collective-permute-start | bytes 3145736 | tf_op jit(solution)/shard_map/ppermute | solution.py:388
  22.1 3.6 %shard_map.95 = (f32[256,1024]{1,0:T(8,128)S(1)}, bf16[256,2560]{1,0:T(8,128)(2,1)S(1)}, bf16[256,32]{1,0:T(8,128)(2,1)S(1)}) custom-call(s32[4]{0:T(128)S(1)} %copy-done.10, f32[16,256]{1,0:T(8,128)S(1)} %copy-done.9, bf16[256,1024]{1,0:T(8,128)(2,1)S(1)} %copy-done.1, bf16[256,128]{1,0:T(8,128)(2,1)S(1)} %copy-done.7, bf16[256,1024]{1,0:T(8,128)(2,1)S(1)} %copy-done.2, ...), custom_call_target="tpu_custom_call" | custom-call | flops 1000 | bytes 1000 | tf_op jit(solution)/shard_map/pallas_call | solution.py:445
  25.8 1.1 %copy-done.3 = bf16[256,2560]{1,0:T(8,128)(2,1)} copy-done((bf16[256,2560]{1,0:T(8,128)(2,1)}, bf16[256,2560]{1,0:T(8,128)(2,1)S(1)}, u32[]{:S(2)}) %copy-start.3) | copy-done | bytes 1310744
  26.9 1.0 %copy-done.5 = f32[256,1024]{1,0:T(8,128)} copy-done((f32[256,1024]{1,0:T(8,128)}, f32[256,1024]{1,0:T(8,128)S(1)}, u32[]{:S(2)}) %copy-start.5) | copy-done | bytes 1048600
  27.9 6.0 %all-to-all-done.in_ref = bf16[32,72,128]{2,1,0:T(8,128)(2,1)S(1)} async-done(((bf16[32,72,128]{2,1,0:T(8,128)(2,1)}), bf16[32,72,128]{2,1,0:T(8,128)(2,1)S(1)}, u32[]{:S(2)}, u32[]{:S(2)}) %all-to-all-start) | async-done | bytes 589856 | tf_op jit(solution)/shard_map/all_to_all | solution.py:444
  33.9 0.9 %shard_map.97 = bf16[32,64,128]{2,1,0:T(8,128)(2,1)} custom-call(bf16[32,72,128]{2,1,0:T(8,128)(2,1)S(1)} %all-to-all-done.in_ref, bf16[256,32]{1,0:T(8,128)(2,1)S(1)} %get-tuple-element.11._.leave_ref), custom_call_target="tpu_custom_call" | custom-call | flops 1000 | bytes 1000 | tf_op jit(solution)/shard_map/pallas_call | solution.py:457
  34.8 5.4 %all-to-all-start.1 = ((bf16[32,64,128]{2,1,0:T(8,128)(2,1)}), bf16[32,64,128]{2,1,0:T(8,128)(2,1)S(1)}, u32[]{:S(2)}, u32[]{:S(2)}) async-start(bf16[32,64,128]{2,1,0:T(8,128)(2,1)} %shard_map.97), calls=%async_computation.1 | async-start | bytes 1048576 | tf_op jit(solution)/shard_map/all_to_all | solution.py:463
  40.3 1.3 %collective-permute-start.5 = (bf16[512,256]{1,0:T(8,128)(2,1)S(1)}, bf16[512,256]{1,0:T(8,128)(2,1)S(1)}, u32[]{:S(2)}, u32[]{:S(2)}) collective-permute-start(bf16[512,256]{1,0:T(8,128)(2,1)S(1)} %copy-done.12), channel_id=1, source_target_pairs={{0,2},{1,3},{2,4},{3,5},{4,6},{5,7},{6,0},{7,1},{8,10},{9,11},{10,... | collective-permute-start | bytes 786440 | tf_op jit(solution)/shard_map/ppermute | solution.py:388
  41.6 1.5 %collective-permute-start.7 = (bf16[512,256]{1,0:T(8,128)(2,1)S(1)}, bf16[512,256]{1,0:T(8,128)(2,1)S(1)}, u32[]{:S(2)}, u32[]{:S(2)}) collective-permute-start(bf16[512,256]{1,0:T(8,128)(2,1)S(1)} %copy-done.11), channel_id=1, source_target_pairs={{0,6},{1,7},{2,0},{3,1},{4,2},{5,3},{6,4},{7,5},{8,14},{9,15},{10,... | collective-permute-start | bytes 786440 | tf_op jit(solution)/shard_map/ppermute | solution.py:388
  43.0 7.1 %collective-permute-done.5 = bf16[512,256]{1,0:T(8,128)(2,1)S(1)} collective-permute-done((bf16[512,256]{1,0:T(8,128)(2,1)S(1)}, bf16[512,256]{1,0:T(8,128)(2,1)S(1)}, u32[]{:S(2)}, u32[]{:S(2)}) %collective-permute-start.5) | collective-permute-done | bytes 262176 | tf_op jit(solution)/shard_map/ppermute | solution.py:388
  50.2 0.0 collective-permute-start.6
  50.2 0.0 collective-permute-done.7
  50.2 2.7 %collective-permute-start.8 = (bf16[512,256]{1,0:T(8,128)(2,1)S(1)}, bf16[512,256]{1,0:T(8,128)(2,1)S(1)}, u32[]{:S(2)}, u32[]{:S(2)}) collective-permute-start(bf16[512,256]{1,0:T(8,128)(2,1)S(1)} %collective-permute-done.7), channel_id=1, source_target_pairs={{0,6},{1,7},{2,0},{3,1},{4,2},{5,3},{6,4},{7,5},{8,14},{9,15},{10,... | collective-permute-start | bytes 786440 | tf_op jit(solution)/shard_map/ppermute | solution.py:388
  52.8 4.5 %collective-permute-done.6.refs_7_ = bf16[512,256]{1,0:T(8,128)(2,1)S(1)} collective-permute-done((bf16[512,256]{1,0:T(8,128)(2,1)S(1)}, bf16[512,256]{1,0:T(8,128)(2,1)S(1)}, u32[]{:S(2)}, u32[]{:S(2)}) %collective-permute-start.6) | collective-permute-done | bytes 262176 | tf_op jit(solution)/shard_map/ppermute | solution.py:388
  57.3 0.8 %collective-permute-start.9 = (bf16[512,256]{1,0:T(8,128)(2,1)S(1)}, bf16[512,256]{1,0:T(8,128)(2,1)S(1)}, u32[]{:S(2)}, u32[]{:S(2)}) collective-permute-start(bf16[512,256]{1,0:T(8,128)(2,1)S(1)} %collective-permute-done.6.refs_7_), channel_id=1, source_target_pairs={{0,8},{8,16},{16,24},{24,0},{32,40},{40,48},{48,56},{56,32},{64,72... | collective-permute-start | bytes 786440 | tf_op jit(solution)/shard_map/ppermute | solution.py:398
  58.1 0.0 collective-permute-done.8.refs_8_
  58.1 1.9 %collective-permute-start.10 = (bf16[512,256]{1,0:T(8,128)(2,1)S(1)}, bf16[512,256]{1,0:T(8,128)(2,1)}, u32[]{:S(2)}, u32[]{:S(2)}) collective-permute-start(bf16[512,256]{1,0:T(8,128)(2,1)S(1)} %collective-permute-done.8.refs_8_), channel_id=1, source_target_pairs={{0,24},{8,0},{16,8},{24,16},{32,56},{40,32},{48,40},{56,48},{64,88... | collective-permute-start | bytes 786440 | tf_op jit(solution)/shard_map/ppermute | solution.py:398
  60.0 0.0 collective-permute-done.refs_0_.refs_5_
  60.0 0.0 collective-permute-done.1.refs_1_.refs_6_
  60.0 0.0 all-to-all-done.1.edge_ref
  60.0 1.3 %copy-done.4 = bf16[256,2560]{1,0:T(8,128)(2,1)S(1)} copy-done((bf16[256,2560]{1,0:T(8,128)(2,1)S(1)}, bf16[256,2560]{1,0:T(8,128)(2,1)}, u32[]{:S(2)}) %copy-start.4) | copy-done | bytes 1310744
  61.3 0.4 shard_map.100.refs_0_
  61.8 0.3 collective-permute-start.2
  62.0 3.0 %collective-permute-start.3 = (bf16[256,256]{1,0:T(8,128)(2,1)S(1)}, bf16[256,256]{1,0:T(8,128)(2,1)S(1)}, u32[]{:S(2)}, u32[]{:S(2)}) collective-permute-start(bf16[256,256]{1,0:T(8,128)(2,1)S(1)} %shard_map.100.refs_0_), channel_id=1, source_target_pairs={{0,4},{1,5},{2,6},{3,7},{4,0},{5,1},{6,2},{7,3},{8,12},{9,13},{10,... | collective-permute-start | bytes 393224 | tf_op jit(solution)/shard_map/ppermute | solution.py:388
  65.0 0.0 collective-permute-start.4
  65.0 2.1 %shard_map.101.refs_4_ = bf16[2048,256]{1,0:T(8,128)(2,1)} custom-call(bf16[8192,128]{1,0:T(8,128)(2,1)} %w_b_hbm.3, bf16[8192,128]{1,0:T(8,128)(2,1)} %w_c_hbm.3), custom_call_target="tpu_custom_call" | custom-call | flops 1000 | bytes 1000 | tf_op jit(solution)/shard_map/pallas_call | solution.py:431
  67.1 1.2 %shard_map.98 = (bf16[256,1024]{1,0:T(8,128)(2,1)}, f32[8,128]{1,0:T(8,128)S(1)}) custom-call(bf16[256,128]{1,0:T(8,128)(2,1)S(1)} %copy-done.7, bf16[256,32]{1,0:T(8,128)(2,1)S(1)} %get-tuple-element.11._.leave_ref, f32[256,1024]{1,0:T(8,128)S(1)} %copy-done.6, bf16[32,64,128]{2,1,0:T(8,128)(2,1)S(1)} %all-to-all-done.1.edge_ref), custom_call_target="tpu_custom_call" | custom-call | flops 1000 | bytes 1000 | tf_op jit(solution)/shard_map/pallas_call | solution.py:471
  68.3 0.0 collective-permute-done.9.refs_9_
  68.3 0.0 collective-permute-done.10.refs_10_
  68.3 0.0 collective-permute-done.2.refs_1_
  68.3 0.4 collective-permute-done.3.refs_2_
  68.8 0.3 collective-permute-done.4.refs_3_
  69.0 1.9 %shard_map.103 = bf16[256,1024]{1,0:T(8,128)(2,1)S(1)} custom-call(bf16[256,256]{1,0:T(8,128)(2,1)S(1)} %shard_map.100.refs_0_, bf16[256,256]{1,0:T(8,128)(2,1)S(1)} %collective-permute-done.2.refs_1_, bf16[256,256]{1,0:T(8,128)(2,1)S(1)} %collective-permute-done.3.refs_2_, bf16[256,256]{1,0:T(8,128)(2,1)S(1)} %collective-permute-done.4.refs_3_, ...), custom_call_target="tpu_custom_call" | custom-call | flops 1000 | bytes 1000 | tf_op jit(solution)/shard_map/pallas_call | solution.py:480
  70.9 5.1 %collective-permute-start.11 = (bf16[256,1024]{1,0:T(8,128)(2,1)S(1)}, bf16[256,1024]{1,0:T(8,128)(2,1)S(1)}, u32[]{:S(2)}, u32[]{:S(2)}) collective-permute-start(bf16[256,1024]{1,0:T(8,128)(2,1)S(1)} %shard_map.103), channel_id=1, source_target_pairs={{0,1},{1,0},{2,3},{3,2},{4,5},{5,4},{6,7},{7,6},{8,9},{9,8},{10,11... | collective-permute-start | bytes 1572872 | tf_op jit(solution)/shard_map/ppermute | solution.py:488
  76.0 1.9 %shard_map.102.kept_ref = f32[256,1024]{1,0:T(8,128)S(1)} custom-call(bf16[256,256]{1,0:T(8,128)(2,1)S(1)} %shard_map.100.refs_0_, bf16[256,256]{1,0:T(8,128)(2,1)S(1)} %collective-permute-done.2.refs_1_, bf16[256,256]{1,0:T(8,128)(2,1)S(1)} %collective-permute-done.3.refs_2_, bf16[256,256]{1,0:T(8,128)(2,1)S(1)} %collective-permute-done.4.refs_3_, ...), custom_call_target="tpu_custom_call" | custom-call | flops 1000 | bytes 1000 | tf_op jit(solution)/shard_map/pallas_call | solution.py:480
  77.9 0.0 collective-permute-done.11.received_ref
  77.9 0.9 %shard_map.104 = bf16[256,1024]{1,0:T(8,128)(2,1)} custom-call(f32[256,1024]{1,0:T(8,128)S(1)} %shard_map.102.kept_ref, bf16[256,1024]{1,0:T(8,128)(2,1)S(1)} %collective-permute-done.11.received_ref), custom_call_target="tpu_custom_call" | custom-call | flops 1000 | bytes 1000 | tf_op jit(solution)/shard_map/pallas_call | solution.py:489
  (16 shorter events, 0.0 us)
Async XLA Ops:
  4.3 29.6 %all-to-all-start = ((bf16[32,72,128]{2,1,0:T(8,128)(2,1)}), bf16[32,72,128]{2,1,0:T(8,128)(2,1)S(1)}, u32[]{:S(2)}, u32[]{:S(2)}) async-start(bf16[32,72,128]{2,1,0:T(8,128)(2,1)} %shard_map.96._), calls=%async_computation | async-start | bytes 1179648 | tf_op jit(solution)/shard_map/all_to_all | solution.py:444
  16.4 5.7 %copy-start.1 = (bf16[256,1024]{1,0:T(8,128)(2,1)S(1)}, bf16[256,1024]{1,0:T(8,128)(2,1)}, u32[]{:S(2)}) copy-start(bf16[256,1024]{1,0:T(8,128)(2,1)} %x_hbm.3) | copy-start | bytes 1572868
  16.4 5.7 %copy-start.2 = (bf16[256,1024]{1,0:T(8,128)(2,1)S(1)}, bf16[256,1024]{1,0:T(8,128)(2,1)}, u32[]{:S(2)}) copy-start(bf16[256,1024]{1,0:T(8,128)(2,1)} %dy_hbm.3) | copy-start | bytes 1572868
  16.4 5.7 %copy-start.7 = (bf16[256,128]{1,0:T(8,128)(2,1)S(1)}, bf16[256,128]{1,0:T(8,128)(2,1)}, u32[]{:S(2)}) copy-start(bf16[256,128]{1,0:T(8,128)(2,1)} %b_ref.1) | copy-start | bytes 196612
  16.4 5.7 %copy-start.8 = (bf16[256,128]{1,0:T(8,128)(2,1)S(1)}, bf16[256,128]{1,0:T(8,128)(2,1)}, u32[]{:S(2)}) copy-start(bf16[256,128]{1,0:T(8,128)(2,1)} %c_hbm.3) | copy-start | bytes 196612
  16.4 5.7 %copy-start.9 = (f32[16,256]{1,0:T(8,128)S(1)}, f32[16,256]{1,0:T(8,128)}, u32[]{:S(2)}) copy-start(f32[16,256]{1,0:T(8,128)} %log_hbm.3) | copy-start | bytes 49156
  16.4 5.7 %copy-start.10 = (s32[4]{0:T(128)S(1)}, s32[4]{0:T(128)}, u32[]{:S(2)}) copy-start(s32[4]{0:T(128)} %lengths_hbm.3) | copy-start | bytes 52
  19.3 21.0 %copy-start.12 = (bf16[512,256]{1,0:T(8,128)(2,1)S(1)}, bf16[512,256]{1,0:T(8,128)(2,1)}, u32[]{:S(2)}) copy-start(bf16[512,256]{1,0:T(8,128)(2,1)} %get-tuple-element.17) | copy-start | bytes 786436
  19.3 22.2 %copy-start.11 = (bf16[512,256]{1,0:T(8,128)(2,1)S(1)}, bf16[512,256]{1,0:T(8,128)(2,1)}, u32[]{:S(2)}) copy-start(bf16[512,256]{1,0:T(8,128)(2,1)} %get-tuple-element.18) | copy-start | bytes 786436
  19.3 40.7 %collective-permute-start = (bf16[2048,256]{1,0:T(8,128)(2,1)}, bf16[2048,256]{1,0:T(8,128)(2,1)S(1)}, u32[]{:S(2)}, u32[]{:S(2)}) collective-permute-start(bf16[2048,256]{1,0:T(8,128)(2,1)} %get-tuple-element.15), channel_id=1, source_target_pairs={{0,2},{1,3},{2,4},{3,5},{4,6},{5,7},{6,0},{7,1},{8,10},{9,11},{10,... | collective-permute-start | bytes 3145736 | tf_op jit(solution)/shard_map/ppermute | solution.py:388
  20.6 39.4 %collective-permute-start.1 = (bf16[2048,256]{1,0:T(8,128)(2,1)}, bf16[2048,256]{1,0:T(8,128)(2,1)S(1)}, u32[]{:S(2)}, u32[]{:S(2)}) collective-permute-start(bf16[2048,256]{1,0:T(8,128)(2,1)} %get-tuple-element.16), channel_id=1, source_target_pairs={{0,6},{1,7},{2,0},{3,1},{4,2},{5,3},{6,4},{7,5},{8,14},{9,15},{10,... | collective-permute-start | bytes 3145736 | tf_op jit(solution)/shard_map/ppermute | solution.py:388
  25.8 1.1 %copy-start.3 = (bf16[256,2560]{1,0:T(8,128)(2,1)}, bf16[256,2560]{1,0:T(8,128)(2,1)S(1)}, u32[]{:S(2)}) copy-start(bf16[256,2560]{1,0:T(8,128)(2,1)S(1)} %get-tuple-element.14.terms_ref) | copy-start | bytes 3932164
  26.9 1.0 %copy-start.5 = (f32[256,1024]{1,0:T(8,128)}, f32[256,1024]{1,0:T(8,128)S(1)}, u32[]{:S(2)}) copy-start(f32[256,1024]{1,0:T(8,128)S(1)} %get-tuple-element.12.local_ref) | copy-start | bytes 3145732
  34.8 25.2 %all-to-all-start.1 = ((bf16[32,64,128]{2,1,0:T(8,128)(2,1)}), bf16[32,64,128]{2,1,0:T(8,128)(2,1)S(1)}, u32[]{:S(2)}, u32[]{:S(2)}) async-start(bf16[32,64,128]{2,1,0:T(8,128)(2,1)} %shard_map.97), calls=%async_computation.1 | async-start | bytes 1048576 | tf_op jit(solution)/shard_map/all_to_all | solution.py:463
  40.3 9.9 %collective-permute-start.5 = (bf16[512,256]{1,0:T(8,128)(2,1)S(1)}, bf16[512,256]{1,0:T(8,128)(2,1)S(1)}, u32[]{:S(2)}, u32[]{:S(2)}) collective-permute-start(bf16[512,256]{1,0:T(8,128)(2,1)S(1)} %copy-done.12), channel_id=1, source_target_pairs={{0,2},{1,3},{2,4},{3,5},{4,6},{5,7},{6,0},{7,1},{8,10},{9,11},{10,... | collective-permute-start | bytes 786440 | tf_op jit(solution)/shard_map/ppermute | solution.py:388
  41.6 8.6 %collective-permute-start.7 = (bf16[512,256]{1,0:T(8,128)(2,1)S(1)}, bf16[512,256]{1,0:T(8,128)(2,1)S(1)}, u32[]{:S(2)}, u32[]{:S(2)}) collective-permute-start(bf16[512,256]{1,0:T(8,128)(2,1)S(1)} %copy-done.11), channel_id=1, source_target_pairs={{0,6},{1,7},{2,0},{3,1},{4,2},{5,3},{6,4},{7,5},{8,14},{9,15},{10,... | collective-permute-start | bytes 786440 | tf_op jit(solution)/shard_map/ppermute | solution.py:388
  50.2 7.1 %collective-permute-start.6 = (bf16[512,256]{1,0:T(8,128)(2,1)S(1)}, bf16[512,256]{1,0:T(8,128)(2,1)S(1)}, u32[]{:S(2)}, u32[]{:S(2)}) collective-permute-start(bf16[512,256]{1,0:T(8,128)(2,1)S(1)} %collective-permute-done.5), channel_id=1, source_target_pairs={{0,2},{1,3},{2,4},{3,5},{4,6},{5,7},{6,0},{7,1},{8,10},{9,11},{10,... | collective-permute-start | bytes 786440 | tf_op jit(solution)/shard_map/ppermute | solution.py:388
  50.2 8.0 %collective-permute-start.8 = (bf16[512,256]{1,0:T(8,128)(2,1)S(1)}, bf16[512,256]{1,0:T(8,128)(2,1)S(1)}, u32[]{:S(2)}, u32[]{:S(2)}) collective-permute-start(bf16[512,256]{1,0:T(8,128)(2,1)S(1)} %collective-permute-done.7), channel_id=1, source_target_pairs={{0,6},{1,7},{2,0},{3,1},{4,2},{5,3},{6,4},{7,5},{8,14},{9,15},{10,... | collective-permute-start | bytes 786440 | tf_op jit(solution)/shard_map/ppermute | solution.py:388
  57.3 11.0 %collective-permute-start.9 = (bf16[512,256]{1,0:T(8,128)(2,1)S(1)}, bf16[512,256]{1,0:T(8,128)(2,1)S(1)}, u32[]{:S(2)}, u32[]{:S(2)}) collective-permute-start(bf16[512,256]{1,0:T(8,128)(2,1)S(1)} %collective-permute-done.6.refs_7_), channel_id=1, source_target_pairs={{0,8},{8,16},{16,24},{24,0},{32,40},{40,48},{48,56},{56,32},{64,72... | collective-permute-start | bytes 786440 | tf_op jit(solution)/shard_map/ppermute | solution.py:398
  58.1 10.2 %collective-permute-start.10 = (bf16[512,256]{1,0:T(8,128)(2,1)S(1)}, bf16[512,256]{1,0:T(8,128)(2,1)}, u32[]{:S(2)}, u32[]{:S(2)}) collective-permute-start(bf16[512,256]{1,0:T(8,128)(2,1)S(1)} %collective-permute-done.8.refs_8_), channel_id=1, source_target_pairs={{0,24},{8,0},{16,8},{24,16},{32,56},{40,32},{48,40},{56,48},{64,88... | collective-permute-start | bytes 786440 | tf_op jit(solution)/shard_map/ppermute | solution.py:398
  60.0 1.3 %copy-start.4 = (bf16[256,2560]{1,0:T(8,128)(2,1)S(1)}, bf16[256,2560]{1,0:T(8,128)(2,1)}, u32[]{:S(2)}) copy-start(bf16[256,2560]{1,0:T(8,128)(2,1)} %copy-done.3) | copy-start | bytes 3932164
  61.8 5.4 %copy-start.6 = (f32[256,1024]{1,0:T(8,128)S(1)}, f32[256,1024]{1,0:T(8,128)}, u32[]{:S(2)}) copy-start(f32[256,1024]{1,0:T(8,128)} %copy-done.5) | copy-start | bytes 3145732
  61.8 6.6 %collective-permute-start.2 = (bf16[256,256]{1,0:T(8,128)(2,1)S(1)}, bf16[256,256]{1,0:T(8,128)(2,1)S(1)}, u32[]{:S(2)}, u32[]{:S(2)}) collective-permute-start(bf16[256,256]{1,0:T(8,128)(2,1)S(1)} %shard_map.100.refs_0_), channel_id=1, source_target_pairs={{0,2},{1,3},{2,4},{3,5},{4,6},{5,7},{6,0},{7,1},{8,10},{9,11},{10,... | collective-permute-start | bytes 393224 | tf_op jit(solution)/shard_map/ppermute | solution.py:388
  62.0 6.7 %collective-permute-start.3 = (bf16[256,256]{1,0:T(8,128)(2,1)S(1)}, bf16[256,256]{1,0:T(8,128)(2,1)S(1)}, u32[]{:S(2)}, u32[]{:S(2)}) collective-permute-start(bf16[256,256]{1,0:T(8,128)(2,1)S(1)} %shard_map.100.refs_0_), channel_id=1, source_target_pairs={{0,4},{1,5},{2,6},{3,7},{4,0},{5,1},{6,2},{7,3},{8,12},{9,13},{10,... | collective-permute-start | bytes 393224 | tf_op jit(solution)/shard_map/ppermute | solution.py:388
  65.0 4.0 %collective-permute-start.4 = (bf16[256,256]{1,0:T(8,128)(2,1)S(1)}, bf16[256,256]{1,0:T(8,128)(2,1)S(1)}, u32[]{:S(2)}, u32[]{:S(2)}) collective-permute-start(bf16[256,256]{1,0:T(8,128)(2,1)S(1)} %shard_map.100.refs_0_), channel_id=1, source_target_pairs={{0,6},{1,7},{2,0},{3,1},{4,2},{5,3},{6,4},{7,5},{8,14},{9,15},{10,... | collective-permute-start | bytes 393224 | tf_op jit(solution)/shard_map/ppermute | solution.py:388
  67.1 1.9 %copy-start = (bf16[2048,256]{1,0:T(8,128)(2,1)S(1)}, bf16[2048,256]{1,0:T(8,128)(2,1)}, u32[]{:S(2)}) copy-start(bf16[2048,256]{1,0:T(8,128)(2,1)} %shard_map.101.refs_4_) | copy-start | bytes 3145732
  70.9 7.0 %collective-permute-start.11 = (bf16[256,1024]{1,0:T(8,128)(2,1)S(1)}, bf16[256,1024]{1,0:T(8,128)(2,1)S(1)}, u32[]{:S(2)}, u32[]{:S(2)}) collective-permute-start(bf16[256,1024]{1,0:T(8,128)(2,1)S(1)} %shard_map.103), channel_id=1, source_target_pairs={{0,1},{1,0},{2,3},{3,2},{4,5},{5,4},{6,7},{7,6},{8,9},{9,8},{10,11... | collective-permute-start | bytes 1572872 | tf_op jit(solution)/shard_map/ppermute | solution.py:488

commit v8 on v7

--- a/solution.py
+++ b/solution.py
@@ -341,26 +341,37 @@
 
 
 def project_kernel(*refs, sibling):
-    grads, (own, up, down), fetched, given, (_, out_ref) = (
-        refs[:4],
-        refs[4:7],
-        refs[7:9],
-        refs[9:11],
-        refs[11:],
-    )
+    grads, (own, up, down), fetched, given = refs[:4], refs[4:7], refs[7:9], refs[9:11]
+    _, out_ref, held_ref, total_ref, sems = refs[11:]
     columns = out_ref.shape[1]
-    half = slice(0, columns) if sibling else slice(columns, 2 * columns)
-    total = mul(grads[0][...], own[half, :], NT)
-    total += mul(grads[1][...], up[half, :], NT)
-    total += mul(grads[3][...], down[half, :], NT)
-
-    def finish(pieces):
-        twice = jnp.concatenate([mul(grads[2][...], piece[...], NT) for piece in pieces], axis=1)
-        out_ref[...] = (total + twice).astype(out_ref.dtype)
-
+    part = columns // 2
     here = fetches_sibling() if sibling else jnp.logical_not(fetches_sibling())
-    pl.when(here)(lambda: finish(fetched))
-    pl.when(jnp.logical_not(here))(lambda: finish(given))
+
+    def copies(pieces):
+        return [
+            pltpu.make_async_copy(piece, held_ref.at[pl.ds(at * part, part), :], sems.at[at])
+            for at, piece in enumerate(pieces)
+        ]
+
+    def start(pieces):
+        for copy in copies(pieces):
+            copy.start()
+
+    pl.when(here)(lambda: start(fetched))
+    pl.when(jnp.logical_not(here))(lambda: start(given))
+    width = 2 * LANES
+    first = 0 if sibling else columns
+    for low in range(0, columns, width):
+        half = slice(first + low, first + low + width)
+        total = mul(grads[0][...], own[half, :], NT)
+        total += mul(grads[1][...], up[half, :], NT)
+        total_ref[:, low : low + width] = total + mul(grads[3][...], down[half, :], NT)
+    for copy in copies(fetched):
+        copy.wait()
+    for low in range(0, columns, width):
+        to = slice(low, low + width)
+        total = total_ref[:, to] + mul(grads[2][...], held_ref[to, :], NT)
+        out_ref[:, to] = total.astype(out_ref.dtype)
 
 
 def sum_kernel(kept_ref, received_ref, out_ref):
@@ -458,8 +469,8 @@
         scan_kernel,
         shape((devices, 2 * rows, STATE), LOW),
         [BLOCK, HBM],
-        4 * MIB,
-    )(summary, leave_cols)
+        54 * MIB,
+    )(summary, terms)
     edges = lax.all_to_all(edges, "seq", 0, 0)
     grad_bc = call(
         grad_bc_kernel,
@@ -480,8 +491,14 @@
         return call(
             functools.partial(project_kernel, sibling=sibling),
             shape((tokens, columns), kind),
-            [BLOCK] * 12,
+            [BLOCK] * 7 + [HBM] * 4 + [BLOCK],
             16 * MIB,
+            BLOCK,
+            [
+                pltpu.VMEM((columns, 2 * STATE), LOW),
+                pltpu.VMEM((tokens, columns), FULL),
+                dma((2,)),
+            ],
         )(grad_bc, *others, own, up, down, *fetched, *given, done)
 
     partner = [(at, at ^ 1) for at in range(lax.axis_size("tp"))]

time: 79.2 us -> 78.7 us (level)
  waiting for transfers between devices: 18.3 us -> 15.4 us
  Pallas kernels: 19.5 us -> 22.4 us
  local copies, waits for them, and re-layouts: 3.43 us -> 2.1 us
  starting transfers between devices: 36.7 us -> 37.5 us
    ppermute x9, waiting for transfers between devices: 12.3 us -> 9.34 us  [along_x(): lax.ppermute(value, 'tp', [(at, (at + CORES * step) % devices) for at in...]
    unnamed x26 -> x22, local copies, waits for them, and re-layouts: 3.43 us -> 2.1 us
    pallas_call x1, Pallas kernels: 0.94 us -> 2.1 us  [per_device(): call(scan_kernel, shape((devices, 2 * rows, STATE), LOW), [BLOCK, HBM], 5...]
    pallas_call x1, Pallas kernels: 1.22 us -> 2.34 us  [per_device(): call(grad_x_kernel, [shape((tokens, WIDE), LOW), shape((8, LANES), FULL)]...]
    pallas_call x1, Pallas kernels: 0.42 us -> 1.46 us  [per_device(): call(grad_bc_kernel, shape((tokens, 2 * STATE), LOW), [BLOCK, BLOCK, HBM,...]
  transfers between devices with their start and end apart: 14 -> 14, of which waited for: 5 -> 3; matrix products, arithmetic and copies ran while one was open for 0% -> 0% of each run, Pallas kernels for 17% -> 21%
where the time goes in v8:
time: 78.7 us; the launch traced here: 78.3 us
  starting transfers between devices  37.5 us (48%)
  Pallas kernels  22.4 us (28%)
  waiting for transfers between devices  15.4 us (20%)
  local copies, waits for them, and re-layouts  2.1 us (3%)
  between operations  0.86 us (1%)
    all_to_all x1, starting transfers between devices, per_device(): summary = lax.all_to_all(summary, 'seq', 0, 0)  12.2 us
    ppermute x9, starting transfers between devices, along_x(): lax.ppermute(value, 'tp', [(at, (at + CORES * step) % devices) for at in...  11.8 us
    ppermute x9, waiting for transfers between devices, along_x(): lax.ppermute(value, 'tp', [(at, (at + CORES * step) % devices) for at in...  9.34 us
    all_to_all x1, waiting for transfers between devices, per_device(): summary = lax.all_to_all(summary, 'seq', 0, 0)  6.05 us
    all_to_all x1, starting transfers between devices, per_device(): edges = lax.all_to_all(edges, 'seq', 0, 0)  5.58 us
    ppermute x1, starting transfers between devices, per_device(): received = lax.ppermute(project(True, LOW), 'tp', partner)  5.23 us
    pallas_call x1, Pallas kernels, per_device(): call(summary_kernel, shape((devices, 2 * rows + 8, STATE), LOW), [HBM] *...  3.72 us
    pallas_call x1, Pallas kernels, per_device(): call(local_kernel, [shape((tokens, WIDE), FULL), shape((tokens, 2 * WIDE...  3.65 us
  transfers between devices with their start and end apart: 14, of which 3 were waited for; matrix products, arithmetic and copies ran while one was open for 0% of the time, Pallas kernels for 21%

profile of v8, /device:TPU:1, one launch (start us, length us, event | category | flops | bytes accessed | tf_op | source)
XLA Modules:
  0.0 78.3 jit_solution(6789793495213683519)
XLA Ops:
  0.6 3.7 %shard_map.96._ = bf16[32,72,128]{2,1,0:T(8,128)(2,1)} custom-call(s32[4]{0:T(128)} %lengths_hbm.3, f32[16,256]{1,0:T(8,128)} %log_hbm.3, bf16[256,1024]{1,0:T(8,128)(2,1)} %x_hbm.3, bf16[256,128]{1,0:T(8,128)(2,1)} %b_ref.1, bf16[256,1024]{1,0:T(8,128)(2,1)} %dy_hbm.3, bf16[256,128]{1,0:T(8,128)(2,1)} %c_hbm.3), custom_call_target="tpu_custom_call" | custom-call | flops 1000 | bytes 1000 | tf_op jit(solution)/shard_map/pallas_call | solution.py:423
  4.4 12.2 %all-to-all-start = ((bf16[32,72,128]{2,1,0:T(8,128)(2,1)}), bf16[32,72,128]{2,1,0:T(8,128)(2,1)}, u32[]{:S(2)}, u32[]{:S(2)}) async-start(bf16[32,72,128]{2,1,0:T(8,128)(2,1)} %shard_map.96._), calls=%async_computation | async-start | bytes 1179648 | tf_op jit(solution)/shard_map/all_to_all | solution.py:455
  16.5 0.0 copy-start.3
  16.5 0.0 copy-start.4
  16.6 0.0 copy-start.7
  16.6 0.0 copy-start.8
  16.6 0.0 copy-start.9
  16.6 0.0 copy-start.10
  16.6 2.8 %shard_map.99 = (bf16[512,256]{1,0:T(8,128)(2,1)}, bf16[512,256]{1,0:T(8,128)(2,1)}, bf16[2048,256]{1,0:T(8,128)(2,1)}, bf16[2048,256]{1,0:T(8,128)(2,1)}) custom-call(bf16[32,72,128]{2,1,0:T(8,128)(2,1)} %shard_map.96._, bf16[8192,128]{1,0:T(8,128)(2,1)} %w_b_hbm.3, bf16[8192,128]{1,0:T(8,128)(2,1)} %w_c_hbm.3), custom_call_target="tpu_custom_call" | custom-call | flops 1000 | bytes 1000 | tf_op jit(solution)/shard_map/pallas_call | solution.py:433
  19.5 1.3 %collective-permute-start = (bf16[2048,256]{1,0:T(8,128)(2,1)}, bf16[2048,256]{1,0:T(8,128)(2,1)S(1)}, u32[]{:S(2)}, u32[]{:S(2)}) collective-permute-start(bf16[2048,256]{1,0:T(8,128)(2,1)} %get-tuple-element.15), channel_id=1, source_target_pairs={{0,2},{1,3},{2,4},{3,5},{4,6},{5,7},{6,0},{7,1},{8,10},{9,11},{10,... | collective-permute-start | bytes 3145736 | tf_op jit(solution)/shard_map/ppermute | solution.py:399
  20.7 1.5 %collective-permute-start.1 = (bf16[2048,256]{1,0:T(8,128)(2,1)}, bf16[2048,256]{1,0:T(8,128)(2,1)S(1)}, u32[]{:S(2)}, u32[]{:S(2)}) collective-permute-start(bf16[2048,256]{1,0:T(8,128)(2,1)} %get-tuple-element.16), channel_id=1, source_target_pairs={{0,6},{1,7},{2,0},{3,1},{4,2},{5,3},{6,4},{7,5},{8,14},{9,15},{10,... | collective-permute-start | bytes 3145736 | tf_op jit(solution)/shard_map/ppermute | solution.py:399
  22.2 0.0 copy-done.3
  22.2 0.0 copy-done.9
  22.2 3.6 %shard_map.95 = (f32[256,1024]{1,0:T(8,128)S(1)}, bf16[256,2560]{1,0:T(8,128)(2,1)S(1)}, bf16[256,32]{1,0:T(8,128)(2,1)S(1)}) custom-call(s32[4]{0:T(128)S(1)} %copy-done.10, f32[16,256]{1,0:T(8,128)S(1)} %copy-done.9, bf16[256,1024]{1,0:T(8,128)(2,1)S(1)} %copy-done.3, bf16[256,128]{1,0:T(8,128)(2,1)S(1)} %copy-done.7, bf16[256,1024]{1,0:T(8,128)(2,1)S(1)} %copy-done.4, ...), custom_call_target="tpu_custom_call" | custom-call | flops 1000 | bytes 1000 | tf_op jit(solution)/shard_map/pallas_call | solution.py:456
  25.9 1.1 %copy-done.1 = bf16[256,2560]{1,0:T(8,128)(2,1)} copy-done((bf16[256,2560]{1,0:T(8,128)(2,1)}, bf16[256,2560]{1,0:T(8,128)(2,1)S(1)}, u32[]{:S(2)}) %copy-start.1) | copy-done | bytes 1310744
  27.0 1.0 %copy-done.5 = f32[256,1024]{1,0:T(8,128)} copy-done((f32[256,1024]{1,0:T(8,128)}, f32[256,1024]{1,0:T(8,128)S(1)}, u32[]{:S(2)}) %copy-start.5) | copy-done | bytes 1048600
  28.0 6.1 %all-to-all-done.in_ref = bf16[32,72,128]{2,1,0:T(8,128)(2,1)} async-done(((bf16[32,72,128]{2,1,0:T(8,128)(2,1)}), bf16[32,72,128]{2,1,0:T(8,128)(2,1)}, u32[]{:S(2)}, u32[]{:S(2)}) %all-to-all-start) | async-done | bytes 589856 | tf_op jit(solution)/shard_map/all_to_all | solution.py:455
  34.0 2.1 %shard_map.97 = bf16[32,64,128]{2,1,0:T(8,128)(2,1)} custom-call(bf16[32,72,128]{2,1,0:T(8,128)(2,1)} %all-to-all-done.in_ref, bf16[256,2560]{1,0:T(8,128)(2,1)} %copy-done.1), custom_call_target="tpu_custom_call" | custom-call | flops 1000 | bytes 1000 | tf_op jit(solution)/shard_map/pallas_call | solution.py:468
  36.1 5.6 %all-to-all-start.1 = ((bf16[32,64,128]{2,1,0:T(8,128)(2,1)}), bf16[32,64,128]{2,1,0:T(8,128)(2,1)}, u32[]{:S(2)}, u32[]{:S(2)}) async-start(bf16[32,64,128]{2,1,0:T(8,128)(2,1)} %shard_map.97), calls=%async_computation.1 | async-start | bytes 1048576 | tf_op jit(solution)/shard_map/all_to_all | solution.py:474
  41.7 1.3 %collective-permute-start.5 = (bf16[512,256]{1,0:T(8,128)(2,1)}, bf16[512,256]{1,0:T(8,128)(2,1)S(1)}, u32[]{:S(2)}, u32[]{:S(2)}) collective-permute-start(bf16[512,256]{1,0:T(8,128)(2,1)} %get-tuple-element.17), channel_id=1, source_target_pairs={{0,2},{1,3},{2,4},{3,5},{4,6},{5,7},{6,0},{7,1},{8,10},{9,11},{10,... | collective-permute-start | bytes 786440 | tf_op jit(solution)/shard_map/ppermute | solution.py:399
  43.0 1.5 %collective-permute-start.7 = (bf16[512,256]{1,0:T(8,128)(2,1)}, bf16[512,256]{1,0:T(8,128)(2,1)S(1)}, u32[]{:S(2)}, u32[]{:S(2)}) collective-permute-start(bf16[512,256]{1,0:T(8,128)(2,1)} %get-tuple-element.18), channel_id=1, source_target_pairs={{0,6},{1,7},{2,0},{3,1},{4,2},{5,3},{6,4},{7,5},{8,14},{9,15},{10,... | collective-permute-start | bytes 786440 | tf_op jit(solution)/shard_map/ppermute | solution.py:399
  44.5 5.2 %collective-permute-done.5 = bf16[512,256]{1,0:T(8,128)(2,1)S(1)} collective-permute-done((bf16[512,256]{1,0:T(8,128)(2,1)}, bf16[512,256]{1,0:T(8,128)(2,1)S(1)}, u32[]{:S(2)}, u32[]{:S(2)}) %collective-permute-start.5) | collective-permute-done | bytes 262176 | tf_op jit(solution)/shard_map/ppermute | solution.py:399
  49.6 0.1 collective-permute-start.6
  49.7 0.0 collective-permute-done.7
  49.7 2.6 %collective-permute-start.8 = (bf16[512,256]{1,0:T(8,128)(2,1)S(1)}, bf16[512,256]{1,0:T(8,128)(2,1)}, u32[]{:S(2)}, u32[]{:S(2)}) collective-permute-start(bf16[512,256]{1,0:T(8,128)(2,1)S(1)} %collective-permute-done.7), channel_id=1, source_target_pairs={{0,6},{1,7},{2,0},{3,1},{4,2},{5,3},{6,4},{7,5},{8,14},{9,15},{10,... | collective-permute-start | bytes 786440 | tf_op jit(solution)/shard_map/ppermute | solution.py:399
  52.3 4.2 %collective-permute-done.6.refs_7_ = bf16[512,256]{1,0:T(8,128)(2,1)} collective-permute-done((bf16[512,256]{1,0:T(8,128)(2,1)S(1)}, bf16[512,256]{1,0:T(8,128)(2,1)}, u32[]{:S(2)}, u32[]{:S(2)}) %collective-permute-start.6) | collective-permute-done | bytes 262176 | tf_op jit(solution)/shard_map/ppermute | solution.py:399
  56.5 0.9 %collective-permute-start.9 = (bf16[512,256]{1,0:T(8,128)(2,1)}, bf16[512,256]{1,0:T(8,128)(2,1)}, u32[]{:S(2)}, u32[]{:S(2)}) collective-permute-start(bf16[512,256]{1,0:T(8,128)(2,1)} %collective-permute-done.6.refs_7_), channel_id=1, source_target_pairs={{0,8},{8,16},{16,24},{24,0},{32,40},{40,48},{48,56},{56,32},{64,72... | collective-permute-start | bytes 786440 | tf_op jit(solution)/shard_map/ppermute | solution.py:409
  57.4 0.0 collective-permute-done.8.refs_8_
  57.4 1.8 %collective-permute-start.10 = (bf16[512,256]{1,0:T(8,128)(2,1)}, bf16[512,256]{1,0:T(8,128)(2,1)}, u32[]{:S(2)}, u32[]{:S(2)}) collective-permute-start(bf16[512,256]{1,0:T(8,128)(2,1)} %collective-permute-done.8.refs_8_), channel_id=1, source_target_pairs={{0,24},{8,0},{16,8},{24,16},{32,56},{40,32},{48,40},{56,48},{64,88... | collective-permute-start | bytes 786440 | tf_op jit(solution)/shard_map/ppermute | solution.py:409
  59.1 0.0 collective-permute-done.refs_0_.refs_5_
  59.1 0.0 collective-permute-done.1.refs_1_.refs_6_
  59.2 0.0 all-to-all-done.1.edge_ref
  59.2 1.5 %shard_map.100.refs_0_ = bf16[256,256]{1,0:T(8,128)(2,1)S(1)} custom-call(bf16[256,2560]{1,0:T(8,128)(2,1)S(1)} %copy-done.2, bf16[32,64,128]{2,1,0:T(8,128)(2,1)} %all-to-all-done.1.edge_ref, bf16[2048,256]{1,0:T(8,128)(2,1)S(1)} %collective-permute-done.refs_0_.refs_5_, bf16[2048,256]{1,0:T(8,128)(2,1)S(1)} %collective-permute-done.1.refs_1_.refs_6_), custom_call_target="tpu_custom_call" | custom-call | flops 1000 | bytes 1000 | tf_op jit(solution)/shard_map/pallas_call | solution.py:475
  60.6 0.3 collective-permute-start.2
  60.9 3.4 %collective-permute-start.3 = (bf16[256,256]{1,0:T(8,128)(2,1)S(1)}, bf16[256,256]{1,0:T(8,128)(2,1)S(1)}, u32[]{:S(2)}, u32[]{:S(2)}) collective-permute-start(bf16[256,256]{1,0:T(8,128)(2,1)S(1)} %shard_map.100.refs_0_), channel_id=1, source_target_pairs={{0,4},{1,5},{2,6},{3,7},{4,0},{5,1},{6,2},{7,3},{8,12},{9,13},{10,... | collective-permute-start | bytes 393224 | tf_op jit(solution)/shard_map/ppermute | solution.py:399
  64.3 0.0 collective-permute-start.4
  64.3 2.1 %shard_map.101.refs_4_ = bf16[2048,256]{1,0:T(8,128)(2,1)} custom-call(bf16[8192,128]{1,0:T(8,128)(2,1)} %w_b_hbm.3, bf16[8192,128]{1,0:T(8,128)(2,1)} %w_c_hbm.3), custom_call_target="tpu_custom_call" | custom-call | flops 1000 | bytes 1000 | tf_op jit(solution)/shard_map/pallas_call | solution.py:442
  66.4 2.3 %shard_map.98 = (bf16[256,1024]{1,0:T(8,128)(2,1)}, f32[8,128]{1,0:T(8,128)S(1)}) custom-call(bf16[256,128]{1,0:T(8,128)(2,1)S(1)} %copy-done.7, bf16[256,32]{1,0:T(8,128)(2,1)S(1)} %get-tuple-element.11.leave_ref, f32[256,1024]{1,0:T(8,128)S(1)} %copy-done.6, bf16[32,64,128]{2,1,0:T(8,128)(2,1)} %all-to-all-done.1.edge_ref), custom_call_target="tpu_custom_call" | custom-call | flops 1000 | bytes 1000 | tf_op jit(solution)/shard_map/pallas_call | solution.py:482
  68.7 0.0 collective-permute-done.9.refs_9_
  68.7 0.0 collective-permute-done.10.refs_10_
  68.7 0.0 collective-permute-done.2.refs_1_
  68.8 0.0 collective-permute-done.3.refs_2_
  68.8 0.0 collective-permute-done.4.refs_3_
  68.8 1.7 %shard_map.103 = bf16[256,1024]{1,0:T(8,128)(2,1)S(1)} custom-call(bf16[256,256]{1,0:T(8,128)(2,1)S(1)} %shard_map.100.refs_0_, bf16[256,256]{1,0:T(8,128)(2,1)S(1)} %collective-permute-done.2.refs_1_, bf16[256,256]{1,0:T(8,128)(2,1)S(1)} %collective-permute-done.3.refs_2_, bf16[256,256]{1,0:T(8,128)(2,1)S(1)} %collective-permute-done.4.refs_3_, ...), custom_call_target="tpu_custom_call" | custom-call | flops 1000 | bytes 1000 | tf_op jit(solution)/shard_map/pallas_call | solution.py:491
  70.5 5.2 %collective-permute-start.11 = (bf16[256,1024]{1,0:T(8,128)(2,1)S(1)}, bf16[256,1024]{1,0:T(8,128)(2,1)S(1)}, u32[]{:S(2)}, u32[]{:S(2)}) collective-permute-start(bf16[256,1024]{1,0:T(8,128)(2,1)S(1)} %shard_map.103), channel_id=1, source_target_pairs={{0,1},{1,0},{2,3},{3,2},{4,5},{5,4},{6,7},{7,6},{8,9},{9,8},{10,11... | collective-permute-start | bytes 1572872 | tf_op jit(solution)/shard_map/ppermute | solution.py:505
  75.7 1.7 %shard_map.102.kept_ref = f32[256,1024]{1,0:T(8,128)S(1)} custom-call(bf16[256,256]{1,0:T(8,128)(2,1)S(1)} %shard_map.100.refs_0_, bf16[256,256]{1,0:T(8,128)(2,1)S(1)} %collective-permute-done.2.refs_1_, bf16[256,256]{1,0:T(8,128)(2,1)S(1)} %collective-permute-done.3.refs_2_, bf16[256,256]{1,0:T(8,128)(2,1)S(1)} %collective-permute-done.4.refs_3_, ...), custom_call_target="tpu_custom_call" | custom-call | flops 1000 | bytes 1000 | tf_op jit(solution)/shard_map/pallas_call | solution.py:491
  77.4 0.0 collective-permute-done.11.received_ref
  77.4 0.9 %shard_map.104 = bf16[256,1024]{1,0:T(8,128)(2,1)} custom-call(f32[256,1024]{1,0:T(8,128)S(1)} %shard_map.102.kept_ref, bf16[256,1024]{1,0:T(8,128)(2,1)S(1)} %collective-permute-done.11.received_ref), custom_call_target="tpu_custom_call" | custom-call | flops 1000 | bytes 1000 | tf_op jit(solution)/shard_map/pallas_call | solution.py:506
  (12 shorter events, 0.0 us)
Async XLA Ops:
  4.4 29.7 %all-to-all-start = ((bf16[32,72,128]{2,1,0:T(8,128)(2,1)}), bf16[32,72,128]{2,1,0:T(8,128)(2,1)}, u32[]{:S(2)}, u32[]{:S(2)}) async-start(bf16[32,72,128]{2,1,0:T(8,128)(2,1)} %shard_map.96._), calls=%async_computation | async-start | bytes 1179648 | tf_op jit(solution)/shard_map/all_to_all | solution.py:455
  16.5 5.7 %copy-start.3 = (bf16[256,1024]{1,0:T(8,128)(2,1)S(1)}, bf16[256,1024]{1,0:T(8,128)(2,1)}, u32[]{:S(2)}) copy-start(bf16[256,1024]{1,0:T(8,128)(2,1)} %x_hbm.3) | copy-start | bytes 1572868
  16.5 5.7 %copy-start.4 = (bf16[256,1024]{1,0:T(8,128)(2,1)S(1)}, bf16[256,1024]{1,0:T(8,128)(2,1)}, u32[]{:S(2)}) copy-start(bf16[256,1024]{1,0:T(8,128)(2,1)} %dy_hbm.3) | copy-start | bytes 1572868
  16.6 5.7 %copy-start.7 = (bf16[256,128]{1,0:T(8,128)(2,1)S(1)}, bf16[256,128]{1,0:T(8,128)(2,1)}, u32[]{:S(2)}) copy-start(bf16[256,128]{1,0:T(8,128)(2,1)} %b_ref.1) | copy-start | bytes 196612
  16.6 5.7 %copy-start.8 = (bf16[256,128]{1,0:T(8,128)(2,1)S(1)}, bf16[256,128]{1,0:T(8,128)(2,1)}, u32[]{:S(2)}) copy-start(bf16[256,128]{1,0:T(8,128)(2,1)} %c_hbm.3) | copy-start | bytes 196612
  16.6 5.7 %copy-start.9 = (f32[16,256]{1,0:T(8,128)S(1)}, f32[16,256]{1,0:T(8,128)}, u32[]{:S(2)}) copy-start(f32[16,256]{1,0:T(8,128)} %log_hbm.3) | copy-start | bytes 49156
  16.6 5.6 %copy-start.10 = (s32[4]{0:T(128)S(1)}, s32[4]{0:T(128)}, u32[]{:S(2)}) copy-start(s32[4]{0:T(128)} %lengths_hbm.3) | copy-start | bytes 52
  19.5 39.7 %collective-permute-start = (bf16[2048,256]{1,0:T(8,128)(2,1)}, bf16[2048,256]{1,0:T(8,128)(2,1)S(1)}, u32[]{:S(2)}, u32[]{:S(2)}) collective-permute-start(bf16[2048,256]{1,0:T(8,128)(2,1)} %get-tuple-element.15), channel_id=1, source_target_pairs={{0,2},{1,3},{2,4},{3,5},{4,6},{5,7},{6,0},{7,1},{8,10},{9,11},{10,... | collective-permute-start | bytes 3145736 | tf_op jit(solution)/shard_map/ppermute | solution.py:399
  20.7 38.4 %collective-permute-start.1 = (bf16[2048,256]{1,0:T(8,128)(2,1)}, bf16[2048,256]{1,0:T(8,128)(2,1)S(1)}, u32[]{:S(2)}, u32[]{:S(2)}) collective-permute-start(bf16[2048,256]{1,0:T(8,128)(2,1)} %get-tuple-element.16), channel_id=1, source_target_pairs={{0,6},{1,7},{2,0},{3,1},{4,2},{5,3},{6,4},{7,5},{8,14},{9,15},{10,... | collective-permute-start | bytes 3145736 | tf_op jit(solution)/shard_map/ppermute | solution.py:399
  25.9 1.1 %copy-start.1 = (bf16[256,2560]{1,0:T(8,128)(2,1)}, bf16[256,2560]{1,0:T(8,128)(2,1)S(1)}, u32[]{:S(2)}) copy-start(bf16[256,2560]{1,0:T(8,128)(2,1)S(1)} %get-tuple-element.13._.terms_ref) | copy-start | bytes 3932164
  27.0 1.0 %copy-start.5 = (f32[256,1024]{1,0:T(8,128)}, f32[256,1024]{1,0:T(8,128)S(1)}, u32[]{:S(2)}) copy-start(f32[256,1024]{1,0:T(8,128)S(1)} %get-tuple-element.12.local_ref) | copy-start | bytes 3145732
  34.0 25.1 %copy-start.2 = (bf16[256,2560]{1,0:T(8,128)(2,1)S(1)}, bf16[256,2560]{1,0:T(8,128)(2,1)}, u32[]{:S(2)}) copy-start(bf16[256,2560]{1,0:T(8,128)(2,1)} %copy-done.1) | copy-start | bytes 3932164
  36.1 23.0 %all-to-all-start.1 = ((bf16[32,64,128]{2,1,0:T(8,128)(2,1)}), bf16[32,64,128]{2,1,0:T(8,128)(2,1)}, u32[]{:S(2)}, u32[]{:S(2)}) async-start(bf16[32,64,128]{2,1,0:T(8,128)(2,1)} %shard_map.97), calls=%async_computation.1 | async-start | bytes 1048576 | tf_op jit(solution)/shard_map/all_to_all | solution.py:474
  41.7 7.9 %collective-permute-start.5 = (bf16[512,256]{1,0:T(8,128)(2,1)}, bf16[512,256]{1,0:T(8,128)(2,1)S(1)}, u32[]{:S(2)}, u32[]{:S(2)}) collective-permute-start(bf16[512,256]{1,0:T(8,128)(2,1)} %get-tuple-element.17), channel_id=1, source_target_pairs={{0,2},{1,3},{2,4},{3,5},{4,6},{5,7},{6,0},{7,1},{8,10},{9,11},{10,... | collective-permute-start | bytes 786440 | tf_op jit(solution)/shard_map/ppermute | solution.py:399
  43.0 6.7 %collective-permute-start.7 = (bf16[512,256]{1,0:T(8,128)(2,1)}, bf16[512,256]{1,0:T(8,128)(2,1)S(1)}, u32[]{:S(2)}, u32[]{:S(2)}) collective-permute-start(bf16[512,256]{1,0:T(8,128)(2,1)} %get-tuple-element.18), channel_id=1, source_target_pairs={{0,6},{1,7},{2,0},{3,1},{4,2},{5,3},{6,4},{7,5},{8,14},{9,15},{10,... | collective-permute-start | bytes 786440 | tf_op jit(solution)/shard_map/ppermute | solution.py:399
  49.6 6.8 %collective-permute-start.6 = (bf16[512,256]{1,0:T(8,128)(2,1)S(1)}, bf16[512,256]{1,0:T(8,128)(2,1)}, u32[]{:S(2)}, u32[]{:S(2)}) collective-permute-start(bf16[512,256]{1,0:T(8,128)(2,1)S(1)} %collective-permute-done.5), channel_id=1, source_target_pairs={{0,2},{1,3},{2,4},{3,5},{4,6},{5,7},{6,0},{7,1},{8,10},{9,11},{10,... | collective-permute-start | bytes 786440 | tf_op jit(solution)/shard_map/ppermute | solution.py:399
  49.7 7.6 %collective-permute-start.8 = (bf16[512,256]{1,0:T(8,128)(2,1)S(1)}, bf16[512,256]{1,0:T(8,128)(2,1)}, u32[]{:S(2)}, u32[]{:S(2)}) collective-permute-start(bf16[512,256]{1,0:T(8,128)(2,1)S(1)} %collective-permute-done.7), channel_id=1, source_target_pairs={{0,6},{1,7},{2,0},{3,1},{4,2},{5,3},{6,4},{7,5},{8,14},{9,15},{10,... | collective-permute-start | bytes 786440 | tf_op jit(solution)/shard_map/ppermute | solution.py:399
  56.5 12.3 %collective-permute-start.9 = (bf16[512,256]{1,0:T(8,128)(2,1)}, bf16[512,256]{1,0:T(8,128)(2,1)}, u32[]{:S(2)}, u32[]{:S(2)}) collective-permute-start(bf16[512,256]{1,0:T(8,128)(2,1)} %collective-permute-done.6.refs_7_), channel_id=1, source_target_pairs={{0,8},{8,16},{16,24},{24,0},{32,40},{40,48},{48,56},{56,32},{64,72... | collective-permute-start | bytes 786440 | tf_op jit(solution)/shard_map/ppermute | solution.py:409
  57.4 11.4 %collective-permute-start.10 = (bf16[512,256]{1,0:T(8,128)(2,1)}, bf16[512,256]{1,0:T(8,128)(2,1)}, u32[]{:S(2)}, u32[]{:S(2)}) collective-permute-start(bf16[512,256]{1,0:T(8,128)(2,1)} %collective-permute-done.8.refs_8_), channel_id=1, source_target_pairs={{0,24},{8,0},{16,8},{24,16},{32,56},{40,32},{48,40},{56,48},{64,88... | collective-permute-start | bytes 786440 | tf_op jit(solution)/shard_map/ppermute | solution.py:409
  60.6 5.8 %copy-start.6 = (f32[256,1024]{1,0:T(8,128)S(1)}, f32[256,1024]{1,0:T(8,128)}, u32[]{:S(2)}) copy-start(f32[256,1024]{1,0:T(8,128)} %copy-done.5) | copy-start | bytes 3145732
  60.6 8.1 %collective-permute-start.2 = (bf16[256,256]{1,0:T(8,128)(2,1)S(1)}, bf16[256,256]{1,0:T(8,128)(2,1)S(1)}, u32[]{:S(2)}, u32[]{:S(2)}) collective-permute-start(bf16[256,256]{1,0:T(8,128)(2,1)S(1)} %shard_map.100.refs_0_), channel_id=1, source_target_pairs={{0,2},{1,3},{2,4},{3,5},{4,6},{5,7},{6,0},{7,1},{8,10},{9,11},{10,... | collective-permute-start | bytes 393224 | tf_op jit(solution)/shard_map/ppermute | solution.py:399
  60.9 7.8 %collective-permute-start.3 = (bf16[256,256]{1,0:T(8,128)(2,1)S(1)}, bf16[256,256]{1,0:T(8,128)(2,1)S(1)}, u32[]{:S(2)}, u32[]{:S(2)}) collective-permute-start(bf16[256,256]{1,0:T(8,128)(2,1)S(1)} %shard_map.100.refs_0_), channel_id=1, source_target_pairs={{0,4},{1,5},{2,6},{3,7},{4,0},{5,1},{6,2},{7,3},{8,12},{9,13},{10,... | collective-permute-start | bytes 393224 | tf_op jit(solution)/shard_map/ppermute | solution.py:399
  64.3 4.5 %collective-permute-start.4 = (bf16[256,256]{1,0:T(8,128)(2,1)S(1)}, bf16[256,256]{1,0:T(8,128)(2,1)S(1)}, u32[]{:S(2)}, u32[]{:S(2)}) collective-permute-start(bf16[256,256]{1,0:T(8,128)(2,1)S(1)} %shard_map.100.refs_0_), channel_id=1, source_target_pairs={{0,6},{1,7},{2,0},{3,1},{4,2},{5,3},{6,4},{7,5},{8,14},{9,15},{10,... | collective-permute-start | bytes 393224 | tf_op jit(solution)/shard_map/ppermute | solution.py:399
  66.4 2.4 %copy-start = (bf16[2048,256]{1,0:T(8,128)(2,1)S(1)}, bf16[2048,256]{1,0:T(8,128)(2,1)}, u32[]{:S(2)}) copy-start(bf16[2048,256]{1,0:T(8,128)(2,1)} %shard_map.101.refs_4_) | copy-start | bytes 3145732
  70.5 6.9 %collective-permute-start.11 = (bf16[256,1024]{1,0:T(8,128)(2,1)S(1)}, bf16[256,1024]{1,0:T(8,128)(2,1)S(1)}, u32[]{:S(2)}, u32[]{:S(2)}) collective-permute-start(bf16[256,1024]{1,0:T(8,128)(2,1)S(1)} %shard_map.103), channel_id=1, source_target_pairs={{0,1},{1,0},{2,3},{3,2},{4,5},{5,4},{6,7},{7,6},{8,9},{9,8},{10,11... | collective-permute-start | bytes 1572872 | tf_op jit(solution)/shard_map/ppermute | solution.py:505

commit v9 on v8

--- a/solution.py
+++ b/solution.py
@@ -16,7 +16,6 @@
 PAIRS = WIDE // LANES
 CORES = 2
 ALONG_Y = 4
-ROUTE = ((2, 1), (2, 1), (1, 4), (3, 4))
 LOW = jnp.bfloat16
 FULL = jnp.float32
 NN = (((1,), (0,)), ((), ()))
@@ -163,24 +162,32 @@
         send.wait()
 
 
-def stage_kernel(_, w_b_hbm, w_c_hbm, *refs):
-    sent_refs, held_refs, sems = refs[: len(ROUTE)], refs[len(ROUTE) : -2], refs[-2:]
+def stage_far_kernel(_, w_b_hbm, w_c_hbm, *refs):
+    sent_refs, held_refs, sems = refs[:2], refs[2:4], refs[4:]
     part = sent_refs[0].shape[0]
-    columns = 2 * part
     me = lax.axis_index("tp")
     core, chips = lax.rem(me, CORES), lax.axis_size("tp") // CORES
     half = lax.rem(core + 1 + lax.rem(lax.axis_index("seq"), 2), CORES)
+    first = (lax.rem(me // CORES + 2, chips) * CORES + half) * 2 * part
     pieces = []
-    for at, ((step, _), held_ref, sent_ref) in enumerate(zip(ROUTE, held_refs, sent_refs)):
+    for at in range(2):
+        row = pl.multiple_of(first + at * part, part)
+        pieces.append((pl.ds(row, part), held_refs[at], sent_refs[at]))
+    pass_through(pieces, w_b_hbm, w_c_hbm, *sems)
+
+
+def stage_near_kernel(_, w_b_hbm, w_c_hbm, *refs):
+    sent_refs, held_refs, sems = refs[:2], refs[2:4], refs[4:]
+    columns = sent_refs[0].shape[0] // CORES
+    me = lax.axis_index("tp")
+    core, chips = lax.rem(me, CORES), lax.axis_size("tp") // CORES
+    pieces = []
+    for step, held_ref, sent_ref in zip((1, 3), held_refs, sent_refs):
         first = lax.rem(me // CORES + step, chips) * CORES
-        if at < 2:
-            row = pl.multiple_of((first + half) * columns + at * part, part)
-            pieces.append((pl.ds(row, part), held_ref, sent_ref))
-        else:
-            for which, other in enumerate((1 - core, core)):
-                row = pl.multiple_of((first + other) * columns, columns)
-                to = pl.ds(which * columns, columns)
-                pieces.append((pl.ds(row, columns), held_ref.at[to, :], sent_ref.at[to, :]))
+        for which, other in enumerate((1 - core, core)):
+            row = pl.multiple_of((first + other) * columns, columns)
+            to = pl.ds(which * columns, columns)
+            pieces.append((pl.ds(row, columns), held_ref.at[to, :], sent_ref.at[to, :]))
     pass_through(pieces, w_b_hbm, w_c_hbm, *sems)
 
 
@@ -196,7 +203,8 @@
     pass_through(pieces, w_b_hbm, w_c_hbm, *sems)
 
 
-def scan_kernel(in_ref, _, out_ref):
+def scan_kernel(in_ref, *refs):
+    out_ref = refs[-1]
     devices, rows = out_ref.shape[0], out_ref.shape[1] // 2
     decays = []
     for at in range(devices):
@@ -428,30 +436,30 @@
         BLOCK,
         held + [dma((6,))],
     )(*local)
-    pieces = [(parts * columns // 2, 2 * STATE) for _, parts in ROUTE]
-    own = (CORES * columns, 2 * STATE)
-    sent = call(
-        stage_kernel,
-        [shape(piece, LOW) for piece in pieces],
-        [HBM] * 3,
-        LARGE_VMEM,
-        [HBM] * len(pieces),
-        [pltpu.VMEM(piece, LOW) for piece in pieces]
-        + [dma((12,)), dma((6,))],
-    )(summary, w_b, w_c)
+    both = (CORES * columns, 2 * STATE)
+
+    def stage(kernel, piece, count, after):
+        return call(
+            kernel,
+            [shape(piece, LOW)] * 2,
+            [HBM] * 3,
+            LARGE_VMEM,
+            [HBM] * 2,
+            [pltpu.VMEM(piece, LOW)] * 2 + [dma((2 * count,)), dma((count,))],
+        )(after, w_b, w_c)
+
+    ways = (1, 3)
+    far = stage(stage_far_kernel, (columns // 2, 2 * STATE), 2, summary)
+    fetched = [along_x(piece, 2) for piece in far]
+    given = [along_y(piece, way) for piece, way in zip(fetched, ways)]
     own = call(
         own_kernel,
-        shape(own, LOW),
+        shape(both, LOW),
         [HBM] * 2,
         LARGE_VMEM,
         HBM,
-        [pltpu.VMEM(own, LOW), dma((4,)), dma((2,))],
+        [pltpu.VMEM(both, LOW), dma((4,)), dma((2,))],
     )(w_b, w_c)
-    ways = (1, 3)
-    up, down = [along_x(piece, way) for piece, way in zip(sent[2:], ways)]
-    fetched = [along_x(piece, way) for piece, way in zip(sent[:2], ways)]
-    fetched = [along_x(piece, way) for piece, way in zip(fetched, ways)]
-    given = [along_y(piece, way) for piece, way in zip(fetched, ways)]
     summary = lax.all_to_all(summary, "seq", 0, 0)
     grad_x, terms, leave_cols = call(
         local_kernel,
@@ -465,12 +473,14 @@
         [BLOCK] * 3,
         held + [dma((6,))],
     )(*local)
+    near = stage(stage_near_kernel, both, 4, leave_cols)
+    up, down = [along_x(piece, way) for piece, way in zip(near, ways)]
     edges = call(
         scan_kernel,
         shape((devices, 2 * rows, STATE), LOW),
-        [BLOCK, HBM],
-        54 * MIB,
-    )(summary, terms)
+        [BLOCK] + [HBM] * 3,
+        4 * MIB,
+    )(summary, leave_cols, *fetched)
     edges = lax.all_to_all(edges, "seq", 0, 0)
     grad_bc = call(
         grad_bc_kernel,

time: 78.7 us -> 77.6 us (0.986)
  waiting for transfers between devices: 15.4 us -> 12.9 us
  Pallas kernels: 22.4 us -> 20.2 us
  starting transfers between devices: 37.5 us -> 39.4 us
  local copies, waits for them, and re-layouts: 2.1 us -> 3.75 us
    all_to_all x1, waiting for transfers between devices: 6.05 us -> 1.07 us  [per_device(): summary = lax.all_to_all(summary, 'seq', 0, 0)]
    all_to_all x1, waiting for transfers between devices: 0.01 us -> 2.72 us  [per_device(): edges = lax.all_to_all(edges, 'seq', 0, 0)]
    all_to_all x1, starting transfers between devices: 5.58 us -> 7.79 us  [per_device(): edges = lax.all_to_all(edges, 'seq', 0, 0)]
    ppermute x9 -> x7, starting transfers between devices: 11.8 us -> 10.1 us  [along_x(): lax.ppermute(value, 'tp', [(at, (at + CORES * step) % devices) for at in...]
    unnamed x22 -> x28, local copies, waits for them, and re-layouts: 2.1 us -> 3.75 us
    ppermute x1, starting transfers between devices: 5.23 us -> 6.59 us  [per_device(): received = lax.ppermute(project(True, LOW), 'tp', partner)]
    pallas_call x2, Pallas kernels: 3.37 us -> 2.2 us  [project(): call(functools.partial(project_kernel, sibling=sibling), shape((tokens, c...]
    pallas_call x3 -> x4, Pallas kernels: 7.02 us -> 8.15 us  [the longest x2 4.88 us: stage(): call(kernel, [shape(piece, LOW)] * 2, [HBM] * 3, LARGE_VMEM, [HBM] * 2, [...]
  transfers between devices with their start and end apart: 14 -> 12, of which waited for: 3 -> 7; matrix products, arithmetic and copies ran while one was open for 0% -> 0% of each run, Pallas kernels for 21% -> 19%
where the time goes in v9:
time: 77.6 us; the launch traced here: 77.1 us
  starting transfers between devices  39.4 us (51%)
  Pallas kernels  20.2 us (26%)
  waiting for transfers between devices  12.9 us (17%)
  local copies, waits for them, and re-layouts  3.75 us (5%)
  between operations  0.84 us (1%)
    all_to_all x1, starting transfers between devices, per_device(): summary = lax.all_to_all(summary, 'seq', 0, 0)  12.2 us
    ppermute x7, starting transfers between devices, along_x(): lax.ppermute(value, 'tp', [(at, (at + CORES * step) % devices) for at in...  10.1 us
    ppermute x7, waiting for transfers between devices, along_x(): lax.ppermute(value, 'tp', [(at, (at + CORES * step) % devices) for at in...  8.85 us
    all_to_all x1, starting transfers between devices, per_device(): edges = lax.all_to_all(edges, 'seq', 0, 0)  7.79 us
    ppermute x1, starting transfers between devices, per_device(): received = lax.ppermute(project(True, LOW), 'tp', partner)  6.59 us
    pallas_call x2, Pallas kernels, stage(): call(kernel, [shape(piece, LOW)] * 2, [HBM] * 3, LARGE_VMEM, [HBM] * 2, [...  4.88 us
    unnamed x28, local copies, waits for them, and re-layouts  3.75 us
    pallas_call x1, Pallas kernels, per_device(): call(summary_kernel, shape((devices, 2 * rows + 8, STATE), LOW), [HBM] *...  3.71 us
  transfers between devices with their start and end apart: 12, of which 7 were waited for; matrix products, arithmetic and copies ran while one was open for 0% of the time, Pallas kernels for 19%

profile of v9, /device:TPU:1, one launch (start us, length us, event | category | flops | bytes accessed | tf_op | source)
XLA Modules:
  0.0 77.1 jit_solution(62459315627562592)
XLA Ops:
  0.6 3.7 %shard_map.96._ = bf16[32,72,128]{2,1,0:T(8,128)(2,1)} custom-call(s32[4]{0:T(128)} %lengths_hbm.3, f32[16,256]{1,0:T(8,128)} %log_hbm.3, bf16[256,1024]{1,0:T(8,128)(2,1)} %x_hbm.3, bf16[256,128]{1,0:T(8,128)(2,1)} %b_ref.1, bf16[256,1024]{1,0:T(8,128)(2,1)} %dy_hbm.3, bf16[256,128]{1,0:T(8,128)(2,1)} %c_hbm.3), custom_call_target="tpu_custom_call" | custom-call | flops 1000 | bytes 1000 | tf_op jit(solution)/shard_map/pallas_call | solution.py:431
  4.3 12.2 %all-to-all-start = ((bf16[32,72,128]{2,1,0:T(8,128)(2,1)}), bf16[32,72,128]{2,1,0:T(8,128)(2,1)}, u32[]{:S(2)}, u32[]{:S(2)}) async-start(bf16[32,72,128]{2,1,0:T(8,128)(2,1)} %shard_map.96._), calls=%async_computation | async-start | bytes 1179648 | tf_op jit(solution)/shard_map/all_to_all | solution.py:463
  16.5 0.0 copy-start.2
  16.5 0.0 copy-start.3
  16.5 0.0 copy-start.10
  16.5 0.0 copy-start.11
  16.6 0.0 copy-start.12
  16.6 0.0 copy-start.13
  16.6 1.9 %shard_map.97 = (bf16[512,256]{1,0:T(8,128)(2,1)}, bf16[512,256]{1,0:T(8,128)(2,1)}) custom-call(bf16[32,72,128]{2,1,0:T(8,128)(2,1)} %shard_map.96._, bf16[8192,128]{1,0:T(8,128)(2,1)} %w_b_hbm.5, bf16[8192,128]{1,0:T(8,128)(2,1)} %w_c_hbm.5), custom_call_target="tpu_custom_call" | custom-call | flops 1000 | bytes 1000 | tf_op jit(solution)/shard_map/pallas_call | solution.py:442
  18.5 2.8 %collective-permute-start = (bf16[512,256]{1,0:T(8,128)(2,1)}, bf16[512,256]{1,0:T(8,128)(2,1)S(1)}, u32[]{:S(2)}, u32[]{:S(2)}) collective-permute-start(bf16[512,256]{1,0:T(8,128)(2,1)} %get-tuple-element.13), channel_id=1, source_target_pairs={{0,4},{1,5},{2,6},{3,7},{4,0},{5,1},{6,2},{7,3},{8,12},{9,13},{10,... | collective-permute-start | bytes 786440 | tf_op jit(solution)/shard_map/ppermute | solution.py:407
  21.4 0.2 collective-permute-start.1
  21.6 0.0 copy-done.3
  21.6 0.0 copy-done.11
  21.6 3.6 %shard_map.95 = (f32[256,1024]{1,0:T(8,128)S(1)}, bf16[256,2560]{1,0:T(8,128)(2,1)S(1)}, bf16[256,32]{1,0:T(8,128)(2,1)S(1)}) custom-call(s32[4]{0:T(128)S(1)} %copy-done.13, f32[16,256]{1,0:T(8,128)S(1)} %copy-done.12, bf16[256,1024]{1,0:T(8,128)(2,1)S(1)} %copy-done.2, bf16[256,128]{1,0:T(8,128)(2,1)S(1)} %copy-done.10, bf16[256,1024]{1,0:T(8,128)(2,1)S(1)} %copy-done.3, ...), custom_call_target="tpu_custom_call" | custom-call | flops 1000 | bytes 1000 | tf_op jit(solution)/shard_map/pallas_call | solution.py:464
  25.3 1.0 %copy-done.6 = f32[256,1024]{1,0:T(8,128)} copy-done((f32[256,1024]{1,0:T(8,128)}, f32[256,1024]{1,0:T(8,128)S(1)}, u32[]{:S(2)}) %copy-start.6) | copy-done | bytes 1048600
  26.3 0.6 copy-done.8
  26.9 2.9 %shard_map.100 = (bf16[2048,256]{1,0:T(8,128)(2,1)}, bf16[2048,256]{1,0:T(8,128)(2,1)}) custom-call(bf16[256,32]{1,0:T(8,128)(2,1)} %copy-done.8, bf16[8192,128]{1,0:T(8,128)(2,1)} %w_b_hbm.5, bf16[8192,128]{1,0:T(8,128)(2,1)} %w_c_hbm.5), custom_call_target="tpu_custom_call" | custom-call | flops 1000 | bytes 1000 | tf_op jit(solution)/shard_map/pallas_call | solution.py:442
  29.8 1.3 %collective-permute-start.2 = (bf16[2048,256]{1,0:T(8,128)(2,1)}, bf16[2048,256]{1,0:T(8,128)(2,1)S(1)}, u32[]{:S(2)}, u32[]{:S(2)}) collective-permute-start(bf16[2048,256]{1,0:T(8,128)(2,1)} %get-tuple-element.17), channel_id=1, source_target_pairs={{0,2},{1,3},{2,4},{3,5},{4,6},{5,7},{6,0},{7,1},{8,10},{9,11},{10,... | collective-permute-start | bytes 3145736 | tf_op jit(solution)/shard_map/ppermute | solution.py:407
  31.1 1.5 %collective-permute-start.3 = (bf16[2048,256]{1,0:T(8,128)(2,1)}, bf16[2048,256]{1,0:T(8,128)(2,1)S(1)}, u32[]{:S(2)}, u32[]{:S(2)}) collective-permute-start(bf16[2048,256]{1,0:T(8,128)(2,1)} %get-tuple-element.18), channel_id=1, source_target_pairs={{0,6},{1,7},{2,0},{3,1},{4,2},{5,3},{6,4},{7,5},{8,14},{9,15},{10,... | collective-permute-start | bytes 3145736 | tf_op jit(solution)/shard_map/ppermute | solution.py:407
  32.6 0.0 collective-permute-done.refs_1_.refs_7_
  32.6 0.3 collective-permute-done.1.refs_2_.refs_8_
  32.9 1.1 %all-to-all-done.in_ref = bf16[32,72,128]{2,1,0:T(8,128)(2,1)} async-done(((bf16[32,72,128]{2,1,0:T(8,128)(2,1)}), bf16[32,72,128]{2,1,0:T(8,128)(2,1)}, u32[]{:S(2)}, u32[]{:S(2)}) %all-to-all-start) | async-done | bytes 589856 | tf_op jit(solution)/shard_map/all_to_all | solution.py:463
  34.0 1.2 %shard_map.98 = bf16[32,64,128]{2,1,0:T(8,128)(2,1)S(1)} custom-call(bf16[32,72,128]{2,1,0:T(8,128)(2,1)} %all-to-all-done.in_ref, bf16[256,32]{1,0:T(8,128)(2,1)S(1)} %copy-done.9, bf16[512,256]{1,0:T(8,128)(2,1)S(1)} %collective-permute-done.refs_1_.refs_7_, bf16[512,256]{1,0:T(8,128)(2,1)S(1)} %collective-permute-done.1.refs_2_.refs_8_), custom_call_target="tpu_custom_call" | custom-call | flops 1000 | bytes 1000 | tf_op jit(solution)/shard_map/pallas_call | solution.py:478
  35.2 0.0 copy-start.1
  35.2 0.8 %copy-done.1 = bf16[32,64,128]{2,1,0:T(8,128)(2,1)} copy-done((bf16[32,64,128]{2,1,0:T(8,128)(2,1)}, bf16[32,64,128]{2,1,0:T(8,128)(2,1)S(1)}, u32[]{:S(2)}) %copy-start.1) | copy-done | bytes 524312
  36.0 7.8 %all-to-all-start.1 = ((bf16[32,64,128]{2,1,0:T(8,128)(2,1)}), bf16[32,64,128]{2,1,0:T(8,128)(2,1)S(1)}, u32[]{:S(2)}, u32[]{:S(2)}) async-start(bf16[32,64,128]{2,1,0:T(8,128)(2,1)} %copy-done.1), calls=%async_computation.1 | async-start | bytes 1048576 | tf_op jit(solution)/shard_map/all_to_all | solution.py:484
  43.8 1.3 %collective-permute-start.7 = (bf16[512,256]{1,0:T(8,128)(2,1)S(1)}, bf16[512,256]{1,0:T(8,128)(2,1)S(1)}, u32[]{:S(2)}, u32[]{:S(2)}) collective-permute-start(bf16[512,256]{1,0:T(8,128)(2,1)S(1)} %collective-permute-done.refs_1_.refs_7_), channel_id=1, source_target_pairs={{0,8},{8,16},{16,24},{24,0},{32,40},{40,48},{48,56},{56,32},{64,72... | collective-permute-start | bytes 786440 | tf_op jit(solution)/shard_map/ppermute | solution.py:417
  45.1 1.4 %collective-permute-start.8 = (bf16[512,256]{1,0:T(8,128)(2,1)S(1)}, bf16[512,256]{1,0:T(8,128)(2,1)}, u32[]{:S(2)}, u32[]{:S(2)}) collective-permute-start(bf16[512,256]{1,0:T(8,128)(2,1)S(1)} %collective-permute-done.1.refs_2_.refs_8_), channel_id=1, source_target_pairs={{0,24},{8,0},{16,8},{24,16},{32,56},{40,32},{48,40},{56,48},{64,88... | collective-permute-start | bytes 786440 | tf_op jit(solution)/shard_map/ppermute | solution.py:417
  46.5 8.4 %collective-permute-done.2.refs_0_.refs_5_ = bf16[2048,256]{1,0:T(8,128)(2,1)S(1)} collective-permute-done((bf16[2048,256]{1,0:T(8,128)(2,1)}, bf16[2048,256]{1,0:T(8,128)(2,1)S(1)}, u32[]{:S(2)}, u32[]{:S(2)}) %collective-permute-start.2) | collective-permute-done | bytes 1048608 | tf_op jit(solution)/shard_map/ppermute | solution.py:407
  54.9 0.0 collective-permute-done.3.refs_1_.refs_6_
  54.9 2.7 %all-to-all-done.1.edge_ref = bf16[32,64,128]{2,1,0:T(8,128)(2,1)S(1)} async-done(((bf16[32,64,128]{2,1,0:T(8,128)(2,1)}), bf16[32,64,128]{2,1,0:T(8,128)(2,1)S(1)}, u32[]{:S(2)}, u32[]{:S(2)}) %all-to-all-start.1) | async-done | bytes 524320 | tf_op jit(solution)/shard_map/all_to_all | solution.py:484
  57.7 1.3 %copy-done.5 = bf16[256,2560]{1,0:T(8,128)(2,1)S(1)} copy-done((bf16[256,2560]{1,0:T(8,128)(2,1)S(1)}, bf16[256,2560]{1,0:T(8,128)(2,1)}, u32[]{:S(2)}) %copy-start.5) | copy-done | bytes 1310744
  59.0 0.4 shard_map.101.refs_0_
  59.4 1.8 %collective-permute-start.4 = (bf16[256,256]{1,0:T(8,128)(2,1)S(1)}, bf16[256,256]{1,0:T(8,128)(2,1)S(1)}, u32[]{:S(2)}, u32[]{:S(2)}) collective-permute-start(bf16[256,256]{1,0:T(8,128)(2,1)S(1)} %shard_map.101.refs_0_), channel_id=1, source_target_pairs={{0,2},{1,3},{2,4},{3,5},{4,6},{5,7},{6,0},{7,1},{8,10},{9,11},{10,... | collective-permute-start | bytes 393224 | tf_op jit(solution)/shard_map/ppermute | solution.py:407
  61.2 2.1 %collective-permute-start.5 = (bf16[256,256]{1,0:T(8,128)(2,1)S(1)}, bf16[256,256]{1,0:T(8,128)(2,1)S(1)}, u32[]{:S(2)}, u32[]{:S(2)}) collective-permute-start(bf16[256,256]{1,0:T(8,128)(2,1)S(1)} %shard_map.101.refs_0_), channel_id=1, source_target_pairs={{0,4},{1,5},{2,6},{3,7},{4,0},{5,1},{6,2},{7,3},{8,12},{9,13},{10,... | collective-permute-start | bytes 393224 | tf_op jit(solution)/shard_map/ppermute | solution.py:407
  63.4 0.4 collective-permute-start.6
  63.7 2.1 %shard_map.102.refs_4_ = bf16[2048,256]{1,0:T(8,128)(2,1)} custom-call(bf16[8192,128]{1,0:T(8,128)(2,1)} %w_b_hbm.5, bf16[8192,128]{1,0:T(8,128)(2,1)} %w_c_hbm.5), custom_call_target="tpu_custom_call" | custom-call | flops 1000 | bytes 1000 | tf_op jit(solution)/shard_map/pallas_call | solution.py:455
  65.8 1.2 %shard_map.99 = (bf16[256,1024]{1,0:T(8,128)(2,1)}, f32[8,128]{1,0:T(8,128)S(1)}) custom-call(bf16[256,128]{1,0:T(8,128)(2,1)S(1)} %copy-done.10, bf16[256,32]{1,0:T(8,128)(2,1)S(1)} %copy-done.9, f32[256,1024]{1,0:T(8,128)S(1)} %copy-done.7, bf16[32,64,128]{2,1,0:T(8,128)(2,1)S(1)} %all-to-all-done.1.edge_ref), custom_call_target="tpu_custom_call" | custom-call | flops 1000 | bytes 1000 | tf_op jit(solution)/shard_map/pallas_call | solution.py:492
  67.0 0.0 collective-permute-done.7.refs_9_
  67.0 0.0 collective-permute-done.8.refs_10_
  67.0 0.0 collective-permute-done.4.refs_1_
  67.1 0.1 collective-permute-done.5.refs_2_
  67.1 0.1 collective-permute-done.6.refs_3_
  67.2 0.9 %shard_map.104 = bf16[256,1024]{1,0:T(8,128)(2,1)S(1)} custom-call(bf16[256,256]{1,0:T(8,128)(2,1)S(1)} %shard_map.101.refs_0_, bf16[256,256]{1,0:T(8,128)(2,1)S(1)} %collective-permute-done.4.refs_1_, bf16[256,256]{1,0:T(8,128)(2,1)S(1)} %collective-permute-done.5.refs_2_, bf16[256,256]{1,0:T(8,128)(2,1)S(1)} %collective-permute-done.6.refs_3_, ...), custom_call_target="tpu_custom_call" | custom-call | flops 1000 | bytes 1000 | tf_op jit(solution)/shard_map/pallas_call | solution.py:501
  68.1 6.6 %collective-permute-start.9 = (bf16[256,1024]{1,0:T(8,128)(2,1)S(1)}, bf16[256,1024]{1,0:T(8,128)(2,1)S(1)}, u32[]{:S(2)}, u32[]{:S(2)}) collective-permute-start(bf16[256,1024]{1,0:T(8,128)(2,1)S(1)} %shard_map.104), channel_id=1, source_target_pairs={{0,1},{1,0},{2,3},{3,2},{4,5},{5,4},{6,7},{7,6},{8,9},{9,8},{10,11... | collective-permute-start | bytes 1572872 | tf_op jit(solution)/shard_map/ppermute | solution.py:515
  74.7 1.3 %shard_map.103.kept_ref = f32[256,1024]{1,0:T(8,128)S(1)} custom-call(bf16[256,256]{1,0:T(8,128)(2,1)S(1)} %shard_map.101.refs_0_, bf16[256,256]{1,0:T(8,128)(2,1)S(1)} %collective-permute-done.4.refs_1_, bf16[256,256]{1,0:T(8,128)(2,1)S(1)} %collective-permute-done.5.refs_2_, bf16[256,256]{1,0:T(8,128)(2,1)S(1)} %collective-permute-done.6.refs_3_, ...), custom_call_target="tpu_custom_call" | custom-call | flops 1000 | bytes 1000 | tf_op jit(solution)/shard_map/pallas_call | solution.py:501
  76.0 0.2 collective-permute-done.9.received_ref
  76.2 0.9 %shard_map.105 = bf16[256,1024]{1,0:T(8,128)(2,1)} custom-call(f32[256,1024]{1,0:T(8,128)S(1)} %shard_map.103.kept_ref, bf16[256,1024]{1,0:T(8,128)(2,1)S(1)} %collective-permute-done.9.received_ref), custom_call_target="tpu_custom_call" | custom-call | flops 1000 | bytes 1000 | tf_op jit(solution)/shard_map/pallas_call | solution.py:516
  (15 shorter events, 0.0 us)
Async XLA Ops:
  4.3 29.6 %all-to-all-start = ((bf16[32,72,128]{2,1,0:T(8,128)(2,1)}), bf16[32,72,128]{2,1,0:T(8,128)(2,1)}, u32[]{:S(2)}, u32[]{:S(2)}) async-start(bf16[32,72,128]{2,1,0:T(8,128)(2,1)} %shard_map.96._), calls=%async_computation | async-start | bytes 1179648 | tf_op jit(solution)/shard_map/all_to_all | solution.py:463
  16.5 5.1 %copy-start.2 = (bf16[256,1024]{1,0:T(8,128)(2,1)S(1)}, bf16[256,1024]{1,0:T(8,128)(2,1)}, u32[]{:S(2)}) copy-start(bf16[256,1024]{1,0:T(8,128)(2,1)} %x_hbm.3) | copy-start | bytes 1572868
  16.5 5.1 %copy-start.3 = (bf16[256,1024]{1,0:T(8,128)(2,1)S(1)}, bf16[256,1024]{1,0:T(8,128)(2,1)}, u32[]{:S(2)}) copy-start(bf16[256,1024]{1,0:T(8,128)(2,1)} %dy_hbm.3) | copy-start | bytes 1572868
  16.5 5.1 %copy-start.10 = (bf16[256,128]{1,0:T(8,128)(2,1)S(1)}, bf16[256,128]{1,0:T(8,128)(2,1)}, u32[]{:S(2)}) copy-start(bf16[256,128]{1,0:T(8,128)(2,1)} %b_ref.1) | copy-start | bytes 196612
  16.5 5.1 %copy-start.11 = (bf16[256,128]{1,0:T(8,128)(2,1)S(1)}, bf16[256,128]{1,0:T(8,128)(2,1)}, u32[]{:S(2)}) copy-start(bf16[256,128]{1,0:T(8,128)(2,1)} %c_hbm.3) | copy-start | bytes 196612
  16.6 5.1 %copy-start.12 = (f32[16,256]{1,0:T(8,128)S(1)}, f32[16,256]{1,0:T(8,128)}, u32[]{:S(2)}) copy-start(f32[16,256]{1,0:T(8,128)} %log_hbm.3) | copy-start | bytes 49156
  16.6 5.1 %copy-start.13 = (s32[4]{0:T(128)S(1)}, s32[4]{0:T(128)}, u32[]{:S(2)}) copy-start(s32[4]{0:T(128)} %lengths_hbm.3) | copy-start | bytes 52
  18.5 14.1 %collective-permute-start = (bf16[512,256]{1,0:T(8,128)(2,1)}, bf16[512,256]{1,0:T(8,128)(2,1)S(1)}, u32[]{:S(2)}, u32[]{:S(2)}) collective-permute-start(bf16[512,256]{1,0:T(8,128)(2,1)} %get-tuple-element.13), channel_id=1, source_target_pairs={{0,4},{1,5},{2,6},{3,7},{4,0},{5,1},{6,2},{7,3},{8,12},{9,13},{10,... | collective-permute-start | bytes 786440 | tf_op jit(solution)/shard_map/ppermute | solution.py:407
  21.4 11.5 %collective-permute-start.1 = (bf16[512,256]{1,0:T(8,128)(2,1)}, bf16[512,256]{1,0:T(8,128)(2,1)S(1)}, u32[]{:S(2)}, u32[]{:S(2)}) collective-permute-start(bf16[512,256]{1,0:T(8,128)(2,1)} %get-tuple-element.14), channel_id=1, source_target_pairs={{0,4},{1,5},{2,6},{3,7},{4,0},{5,1},{6,2},{7,3},{8,12},{9,13},{10,... | collective-permute-start | bytes 786440 | tf_op jit(solution)/shard_map/ppermute | solution.py:407
  25.3 1.0 %copy-start.6 = (f32[256,1024]{1,0:T(8,128)}, f32[256,1024]{1,0:T(8,128)S(1)}, u32[]{:S(2)}) copy-start(f32[256,1024]{1,0:T(8,128)S(1)} %get-tuple-element.12.local_ref) | copy-start | bytes 3145732
  26.3 0.6 copy-start.8
  26.9 2.9 %copy-start.4 = (bf16[256,2560]{1,0:T(8,128)(2,1)}, bf16[256,2560]{1,0:T(8,128)(2,1)S(1)}, u32[]{:S(2)}) copy-start(bf16[256,2560]{1,0:T(8,128)(2,1)S(1)} %get-tuple-element.16.terms_ref) | copy-start | bytes 3932164
  26.9 7.1 %copy-start.9 = (bf16[256,32]{1,0:T(8,128)(2,1)S(1)}, bf16[256,32]{1,0:T(8,128)(2,1)}, u32[]{:S(2)}) copy-start(bf16[256,32]{1,0:T(8,128)(2,1)} %copy-done.8) | copy-start | bytes 49156
  29.8 25.1 %collective-permute-start.2 = (bf16[2048,256]{1,0:T(8,128)(2,1)}, bf16[2048,256]{1,0:T(8,128)(2,1)S(1)}, u32[]{:S(2)}, u32[]{:S(2)}) collective-permute-start(bf16[2048,256]{1,0:T(8,128)(2,1)} %get-tuple-element.17), channel_id=1, source_target_pairs={{0,2},{1,3},{2,4},{3,5},{4,6},{5,7},{6,0},{7,1},{8,10},{9,11},{10,... | collective-permute-start | bytes 3145736 | tf_op jit(solution)/shard_map/ppermute | solution.py:407
  31.1 23.8 %collective-permute-start.3 = (bf16[2048,256]{1,0:T(8,128)(2,1)}, bf16[2048,256]{1,0:T(8,128)(2,1)S(1)}, u32[]{:S(2)}, u32[]{:S(2)}) collective-permute-start(bf16[2048,256]{1,0:T(8,128)(2,1)} %get-tuple-element.18), channel_id=1, source_target_pairs={{0,6},{1,7},{2,0},{3,1},{4,2},{5,3},{6,4},{7,5},{8,14},{9,15},{10,... | collective-permute-start | bytes 3145736 | tf_op jit(solution)/shard_map/ppermute | solution.py:407
  35.2 0.8 %copy-start.1 = (bf16[32,64,128]{2,1,0:T(8,128)(2,1)}, bf16[32,64,128]{2,1,0:T(8,128)(2,1)S(1)}, u32[]{:S(2)}) copy-start(bf16[32,64,128]{2,1,0:T(8,128)(2,1)S(1)} %shard_map.98) | copy-start | bytes 1572868
  36.0 21.7 %all-to-all-start.1 = ((bf16[32,64,128]{2,1,0:T(8,128)(2,1)}), bf16[32,64,128]{2,1,0:T(8,128)(2,1)S(1)}, u32[]{:S(2)}, u32[]{:S(2)}) async-start(bf16[32,64,128]{2,1,0:T(8,128)(2,1)} %copy-done.1), calls=%async_computation.1 | async-start | bytes 1048576 | tf_op jit(solution)/shard_map/all_to_all | solution.py:484
  43.8 23.3 %collective-permute-start.7 = (bf16[512,256]{1,0:T(8,128)(2,1)S(1)}, bf16[512,256]{1,0:T(8,128)(2,1)S(1)}, u32[]{:S(2)}, u32[]{:S(2)}) collective-permute-start(bf16[512,256]{1,0:T(8,128)(2,1)S(1)} %collective-permute-done.refs_1_.refs_7_), channel_id=1, source_target_pairs={{0,8},{8,16},{16,24},{24,0},{32,40},{40,48},{48,56},{56,32},{64,72... | collective-permute-start | bytes 786440 | tf_op jit(solution)/shard_map/ppermute | solution.py:417
  45.1 22.0 %collective-permute-start.8 = (bf16[512,256]{1,0:T(8,128)(2,1)S(1)}, bf16[512,256]{1,0:T(8,128)(2,1)}, u32[]{:S(2)}, u32[]{:S(2)}) collective-permute-start(bf16[512,256]{1,0:T(8,128)(2,1)S(1)} %collective-permute-done.1.refs_2_.refs_8_), channel_id=1, source_target_pairs={{0,24},{8,0},{16,8},{24,16},{32,56},{40,32},{48,40},{56,48},{64,88... | collective-permute-start | bytes 786440 | tf_op jit(solution)/shard_map/ppermute | solution.py:417
  57.7 1.3 %copy-start.5 = (bf16[256,2560]{1,0:T(8,128)(2,1)S(1)}, bf16[256,2560]{1,0:T(8,128)(2,1)}, u32[]{:S(2)}) copy-start(bf16[256,2560]{1,0:T(8,128)(2,1)} %copy-done.4) | copy-start | bytes 3932164
  59.4 6.4 %copy-start.7 = (f32[256,1024]{1,0:T(8,128)S(1)}, f32[256,1024]{1,0:T(8,128)}, u32[]{:S(2)}) copy-start(f32[256,1024]{1,0:T(8,128)} %copy-done.6) | copy-start | bytes 3145732
  59.4 7.6 %collective-permute-start.4 = (bf16[256,256]{1,0:T(8,128)(2,1)S(1)}, bf16[256,256]{1,0:T(8,128)(2,1)S(1)}, u32[]{:S(2)}, u32[]{:S(2)}) collective-permute-start(bf16[256,256]{1,0:T(8,128)(2,1)S(1)} %shard_map.101.refs_0_), channel_id=1, source_target_pairs={{0,2},{1,3},{2,4},{3,5},{4,6},{5,7},{6,0},{7,1},{8,10},{9,11},{10,... | collective-permute-start | bytes 393224 | tf_op jit(solution)/shard_map/ppermute | solution.py:407
  61.2 5.9 %collective-permute-start.5 = (bf16[256,256]{1,0:T(8,128)(2,1)S(1)}, bf16[256,256]{1,0:T(8,128)(2,1)S(1)}, u32[]{:S(2)}, u32[]{:S(2)}) collective-permute-start(bf16[256,256]{1,0:T(8,128)(2,1)S(1)} %shard_map.101.refs_0_), channel_id=1, source_target_pairs={{0,4},{1,5},{2,6},{3,7},{4,0},{5,1},{6,2},{7,3},{8,12},{9,13},{10,... | collective-permute-start | bytes 393224 | tf_op jit(solution)/shard_map/ppermute | solution.py:407
  63.4 3.8 %collective-permute-start.6 = (bf16[256,256]{1,0:T(8,128)(2,1)S(1)}, bf16[256,256]{1,0:T(8,128)(2,1)S(1)}, u32[]{:S(2)}, u32[]{:S(2)}) collective-permute-start(bf16[256,256]{1,0:T(8,128)(2,1)S(1)} %shard_map.101.refs_0_), channel_id=1, source_target_pairs={{0,6},{1,7},{2,0},{3,1},{4,2},{5,3},{6,4},{7,5},{8,14},{9,15},{10,... | collective-permute-start | bytes 393224 | tf_op jit(solution)/shard_map/ppermute | solution.py:407
  65.8 1.4 %copy-start = (bf16[2048,256]{1,0:T(8,128)(2,1)S(1)}, bf16[2048,256]{1,0:T(8,128)(2,1)}, u32[]{:S(2)}) copy-start(bf16[2048,256]{1,0:T(8,128)(2,1)} %shard_map.102.refs_4_) | copy-start | bytes 3145732
  68.1 8.1 %collective-permute-start.9 = (bf16[256,1024]{1,0:T(8,128)(2,1)S(1)}, bf16[256,1024]{1,0:T(8,128)(2,1)S(1)}, u32[]{:S(2)}, u32[]{:S(2)}) collective-permute-start(bf16[256,1024]{1,0:T(8,128)(2,1)S(1)} %shard_map.104), channel_id=1, source_target_pairs={{0,1},{1,0},{2,3},{3,2},{4,5},{5,4},{6,7},{7,6},{8,9},{9,8},{10,11... | collective-permute-start | bytes 1572872 | tf_op jit(solution)/shard_map/ppermute | solution.py:515

commit v10 on v9

--- a/solution.py
+++ b/solution.py
@@ -162,18 +162,14 @@
         send.wait()
 
 
-def stage_far_kernel(_, w_b_hbm, w_c_hbm, *refs):
-    sent_refs, held_refs, sems = refs[:2], refs[2:4], refs[4:]
-    part = sent_refs[0].shape[0]
+def stage_far_kernel(_, w_b_hbm, w_c_hbm, sent_ref, held_ref, *sems):
+    columns = sent_ref.shape[0]
     me = lax.axis_index("tp")
     core, chips = lax.rem(me, CORES), lax.axis_size("tp") // CORES
     half = lax.rem(core + 1 + lax.rem(lax.axis_index("seq"), 2), CORES)
-    first = (lax.rem(me // CORES + 2, chips) * CORES + half) * 2 * part
-    pieces = []
-    for at in range(2):
-        row = pl.multiple_of(first + at * part, part)
-        pieces.append((pl.ds(row, part), held_refs[at], sent_refs[at]))
-    pass_through(pieces, w_b_hbm, w_c_hbm, *sems)
+    row = (lax.rem(me // CORES + 2, chips) * CORES + half) * columns
+    from_row = pl.ds(pl.multiple_of(row, columns), columns)
+    pass_through([(from_row, held_ref, sent_ref)], w_b_hbm, w_c_hbm, *sems)
 
 
 def stage_near_kernel(_, w_b_hbm, w_c_hbm, *refs):
@@ -349,8 +345,8 @@
 
 
 def project_kernel(*refs, sibling):
-    grads, (own, up, down), fetched, given = refs[:4], refs[4:7], refs[7:9], refs[9:11]
-    _, out_ref, held_ref, total_ref, sems = refs[11:]
+    grads, (own, up, down), fetched, given = refs[:4], refs[4:7], refs[7], refs[8:10]
+    _, out_ref, held_ref, total_ref, sems = refs[10:]
     columns = out_ref.shape[1]
     part = columns // 2
     here = fetches_sibling() if sibling else jnp.logical_not(fetches_sibling())
@@ -365,6 +361,7 @@
         for copy in copies(pieces):
             copy.start()
 
+    fetched = [fetched.at[pl.ds(at * part, part), :] for at in range(2)]
     pl.when(here)(lambda: start(fetched))
     pl.when(jnp.logical_not(here))(lambda: start(given))
     width = 2 * LANES
@@ -438,20 +435,23 @@
     )(*local)
     both = (CORES * columns, 2 * STATE)
 
-    def stage(kernel, piece, count, after):
+    def stage(kernel, piece, arrays, count, after):
         return call(
             kernel,
-            [shape(piece, LOW)] * 2,
+            [shape(piece, LOW)] * arrays,
             [HBM] * 3,
             LARGE_VMEM,
-            [HBM] * 2,
-            [pltpu.VMEM(piece, LOW)] * 2 + [dma((2 * count,)), dma((count,))],
+            [HBM] * arrays,
+            [pltpu.VMEM(piece, LOW)] * arrays + [dma((2 * count,)), dma((count,))],
         )(after, w_b, w_c)
 
     ways = (1, 3)
-    far = stage(stage_far_kernel, (columns // 2, 2 * STATE), 2, summary)
-    fetched = [along_x(piece, 2) for piece in far]
-    given = [along_y(piece, way) for piece, way in zip(fetched, ways)]
+    [far] = stage(stage_far_kernel, (columns, 2 * STATE), 1, 1, summary)
+    fetched = along_x(far, 2)
+    given = [
+        along_y(piece, way)
+        for piece, way in zip((fetched[: columns // 2], fetched[columns // 2 :]), ways)
+    ]
     own = call(
         own_kernel,
         shape(both, LOW),
@@ -473,14 +473,14 @@
         [BLOCK] * 3,
         held + [dma((6,))],
     )(*local)
-    near = stage(stage_near_kernel, both, 4, leave_cols)
+    near = stage(stage_near_kernel, both, 2, 4, leave_cols)
     up, down = [along_x(piece, way) for piece, way in zip(near, ways)]
     edges = call(
         scan_kernel,
         shape((devices, 2 * rows, STATE), LOW),
-        [BLOCK] + [HBM] * 3,
+        [BLOCK] + [HBM] * 2,
         4 * MIB,
-    )(summary, leave_cols, *fetched)
+    )(summary, leave_cols, fetched)
     edges = lax.all_to_all(edges, "seq", 0, 0)
     grad_bc = call(
         grad_bc_kernel,
@@ -501,7 +501,7 @@
         return call(
             functools.partial(project_kernel, sibling=sibling),
             shape((tokens, columns), kind),
-            [BLOCK] * 7 + [HBM] * 4 + [BLOCK],
+            [BLOCK] * 7 + [HBM] * 3 + [BLOCK],
             16 * MIB,
             BLOCK,
             [
@@ -509,7 +509,7 @@
                 pltpu.VMEM((tokens, columns), FULL),
                 dma((2,)),
             ],
-        )(grad_bc, *others, own, up, down, *fetched, *given, done)
+        )(grad_bc, *others, own, up, down, fetched, *given, done)
 
     partner = [(at, at ^ 1) for at in range(lax.axis_size("tp"))]
     received = lax.ppermute(project(True, LOW), "tp", partner)

time: 77.6 us -> 76.7 us (0.988)
    all_to_all x1, waiting for transfers between devices: 2.72 us -> 0.01 us  [per_device(): edges = lax.all_to_all(edges, 'seq', 0, 0)]
    ppermute x7 -> x6, waiting for transfers between devices: 8.85 us -> 10.8 us  [along_x(): lax.ppermute(value, 'tp', [(at, (at + CORES * step) % devices) for at in...]
    pallas_call x1, Pallas kernels: 1.21 us -> 0.14 us  [per_device(): call(scan_kernel, shape((devices, 2 * rows, STATE), LOW), [BLOCK] + [HBM]...]
    ppermute x7 -> x6, starting transfers between devices: 10.1 us -> 11.2 us  [along_x(): lax.ppermute(value, 'tp', [(at, (at + CORES * step) % devices) for at in...]
    unnamed x28, local copies, waits for them, and re-layouts: 3.75 us -> 2.79 us
    slice x0 -> x1, local copies, waits for them, and re-layouts: none -> 0.86 us  [per_device(): fetched[columns // 2:]]
  transfers between devices with their start and end apart: 12 -> 11, of which waited for: 7 -> 4; matrix products, arithmetic and copies ran while one was open for 0% -> 1% of each run, Pallas kernels for 19% -> 18%
where the time goes in v10:
time: 76.7 us; the launch traced here: 76.3 us
  starting transfers between devices  39.9 us (52%)
  Pallas kernels  19.6 us (26%)
  waiting for transfers between devices  12.2 us (16%)
  local copies, waits for them, and re-layouts  3.64 us (5%)
  between operations  0.87 us (1%)
    all_to_all x1, starting transfers between devices, per_device(): summary = lax.all_to_all(summary, 'seq', 0, 0)  12 us
    ppermute x6, starting transfers between devices, along_x(): lax.ppermute(value, 'tp', [(at, (at + CORES * step) % devices) for at in...  11.2 us
    ppermute x6, waiting for transfers between devices, along_x(): lax.ppermute(value, 'tp', [(at, (at + CORES * step) % devices) for at in...  10.8 us
    all_to_all x1, starting transfers between devices, per_device(): edges = lax.all_to_all(edges, 'seq', 0, 0)  7.75 us
    ppermute x1, starting transfers between devices, per_device(): received = lax.ppermute(project(True, LOW), 'tp', partner)  6.32 us
    pallas_call x2, Pallas kernels, stage(): call(kernel, [shape(piece, LOW)] * arrays, [HBM] * 3, LARGE_VMEM, [HBM] *...  5.29 us
    pallas_call x1, Pallas kernels, per_device(): call(summary_kernel, shape((devices, 2 * rows + 8, STATE), LOW), [HBM] *...  3.7 us
    pallas_call x1, Pallas kernels, per_device(): call(local_kernel, [shape((tokens, WIDE), FULL), shape((tokens, 2 * WIDE...  3.65 us
  transfers between devices with their start and end apart: 11, of which 4 were waited for; matrix products, arithmetic and copies ran while one was open for 1% of the time, Pallas kernels for 18%

profile of v10, /device:TPU:1, one launch (start us, length us, event | category | flops | bytes accessed | tf_op | source)
XLA Modules:
  0.0 76.3 jit_solution(10132800211175238143)
XLA Ops:
  0.6 3.7 %shard_map.96._ = bf16[32,72,128]{2,1,0:T(8,128)(2,1)} custom-call(s32[4]{0:T(128)} %lengths_hbm.3, f32[16,256]{1,0:T(8,128)} %log_hbm.3, bf16[256,1024]{1,0:T(8,128)(2,1)} %x_hbm.3, bf16[256,128]{1,0:T(8,128)(2,1)} %b_ref.1, bf16[256,1024]{1,0:T(8,128)(2,1)} %dy_hbm.3, bf16[256,128]{1,0:T(8,128)(2,1)} %c_hbm.3), custom_call_target="tpu_custom_call" | custom-call | flops 1000 | bytes 1000 | tf_op jit(solution)/shard_map/pallas_call | solution.py:428
  4.3 12.0 %all-to-all-start = ((bf16[32,72,128]{2,1,0:T(8,128)(2,1)}), bf16[32,72,128]{2,1,0:T(8,128)(2,1)S(1)}, u32[]{:S(2)}, u32[]{:S(2)}) async-start(bf16[32,72,128]{2,1,0:T(8,128)(2,1)} %shard_map.96._), calls=%async_computation | async-start | bytes 1179648 | tf_op jit(solution)/shard_map/all_to_all | solution.py:463
  16.4 0.0 copy-start.2
  16.4 0.0 copy-start.3
  16.4 0.0 copy-start.10
  16.4 0.0 copy-start.11
  16.4 0.0 copy-start.12
  16.4 0.0 copy-start.13
  16.5 1.9 %shard_map.97 = bf16[1024,256]{1,0:T(8,128)(2,1)} custom-call(bf16[32,72,128]{2,1,0:T(8,128)(2,1)} %shard_map.96._, bf16[8192,128]{1,0:T(8,128)(2,1)} %w_b_hbm.5, bf16[8192,128]{1,0:T(8,128)(2,1)} %w_c_hbm.5), custom_call_target="tpu_custom_call" | custom-call | flops 1000 | bytes 1000 | tf_op jit(solution)/shard_map/pallas_call | solution.py:439
  18.4 2.8 %collective-permute-start = (bf16[1024,256]{1,0:T(8,128)(2,1)}, bf16[1024,256]{1,0:T(8,128)(2,1)S(1)}, u32[]{:S(2)}, u32[]{:S(2)}) collective-permute-start(bf16[1024,256]{1,0:T(8,128)(2,1)} %shard_map.97), channel_id=1, source_target_pairs={{0,4},{1,5},{2,6},{3,7},{4,0},{5,1},{6,2},{7,3},{8,12},{9,13},{10,... | collective-permute-start | bytes 1572872 | tf_op jit(solution)/shard_map/ppermute | solution.py:404
  21.2 0.0 copy-done.2
  21.3 0.0 copy-done.11
  21.3 3.6 %shard_map.95 = (f32[256,1024]{1,0:T(8,128)S(1)}, bf16[256,2560]{1,0:T(8,128)(2,1)S(1)}, bf16[256,32]{1,0:T(8,128)(2,1)S(1)}) custom-call(s32[4]{0:T(128)S(1)} %copy-done.13, f32[16,256]{1,0:T(8,128)S(1)} %copy-done.12, bf16[256,1024]{1,0:T(8,128)(2,1)S(1)} %copy-done.2, bf16[256,128]{1,0:T(8,128)(2,1)S(1)} %copy-done.10, bf16[256,1024]{1,0:T(8,128)(2,1)S(1)} %copy-done.3, ...), custom_call_target="tpu_custom_call" | custom-call | flops 1000 | bytes 1000 | tf_op jit(solution)/shard_map/pallas_call | solution.py:464
  24.9 0.0 copy-start.8
  25.0 0.6 copy-done.8
  25.6 3.3 %shard_map.100 = (bf16[2048,256]{1,0:T(8,128)(2,1)}, bf16[2048,256]{1,0:T(8,128)(2,1)}) custom-call(bf16[256,32]{1,0:T(8,128)(2,1)} %copy-done.8, bf16[8192,128]{1,0:T(8,128)(2,1)} %w_b_hbm.5, bf16[8192,128]{1,0:T(8,128)(2,1)} %w_c_hbm.5), custom_call_target="tpu_custom_call" | custom-call | flops 1000 | bytes 1000 | tf_op jit(solution)/shard_map/pallas_call | solution.py:439
  28.9 0.4 collective-permute-start.1
  29.3 2.4 %collective-permute-start.2 = (bf16[2048,256]{1,0:T(8,128)(2,1)}, bf16[2048,256]{1,0:T(8,128)(2,1)S(1)}, u32[]{:S(2)}, u32[]{:S(2)}) collective-permute-start(bf16[2048,256]{1,0:T(8,128)(2,1)} %get-tuple-element.14), channel_id=1, source_target_pairs={{0,6},{1,7},{2,0},{3,1},{4,2},{5,3},{6,4},{7,5},{8,14},{9,15},{10,... | collective-permute-start | bytes 3145736 | tf_op jit(solution)/shard_map/ppermute | solution.py:404
  31.7 1.0 %collective-permute-done.refs_1_.refs_7_ = bf16[1024,256]{1,0:T(8,128)(2,1)S(1)} collective-permute-done((bf16[1024,256]{1,0:T(8,128)(2,1)}, bf16[1024,256]{1,0:T(8,128)(2,1)S(1)}, u32[]{:S(2)}, u32[]{:S(2)}) %collective-permute-start) | collective-permute-done | bytes 524320 | tf_op jit(solution)/shard_map/ppermute | solution.py:404
  32.7 1.2 %all-to-all-done.in_ref = bf16[32,72,128]{2,1,0:T(8,128)(2,1)S(1)} async-done(((bf16[32,72,128]{2,1,0:T(8,128)(2,1)}), bf16[32,72,128]{2,1,0:T(8,128)(2,1)S(1)}, u32[]{:S(2)}, u32[]{:S(2)}) %all-to-all-start) | async-done | bytes 589856 | tf_op jit(solution)/shard_map/all_to_all | solution.py:463
  33.9 0.1 shard_map.98
  34.0 0.0 copy-start.1
  34.0 0.8 %copy-done.1 = bf16[32,64,128]{2,1,0:T(8,128)(2,1)} copy-done((bf16[32,64,128]{2,1,0:T(8,128)(2,1)}, bf16[32,64,128]{2,1,0:T(8,128)(2,1)S(1)}, u32[]{:S(2)}) %copy-start.1) | copy-done | bytes 524312
  34.8 7.7 %all-to-all-start.1 = ((bf16[32,64,128]{2,1,0:T(8,128)(2,1)}), bf16[32,64,128]{2,1,0:T(8,128)(2,1)S(1)}, u32[]{:S(2)}, u32[]{:S(2)}) async-start(bf16[32,64,128]{2,1,0:T(8,128)(2,1)} %copy-done.1), calls=%async_computation.1 | async-start | bytes 1048576 | tf_op jit(solution)/shard_map/all_to_all | solution.py:484
  42.6 0.9 %fusion = (bf16[512,256]{1,0:T(8,128)(2,1)}, bf16[512,256]{1,0:T(8,128)(2,1)}) fusion(bf16[1024,256]{1,0:T(8,128)(2,1)S(1)} %collective-permute-done.refs_1_.refs_7_), kind=kLoop, calls=%fused_computation | loop fusion | bytes 1048576 | tf_op jit(solution)/shard_map/slice | solution.py:453
  43.4 1.2 %collective-permute-start.6 = (bf16[512,256]{1,0:T(8,128)(2,1)}, bf16[512,256]{1,0:T(8,128)(2,1)S(1)}, u32[]{:S(2)}, u32[]{:S(2)}) collective-permute-start(bf16[512,256]{1,0:T(8,128)(2,1)} %get-tuple-element.17), channel_id=1, source_target_pairs={{0,8},{8,16},{16,24},{24,0},{32,40},{40,48},{48,56},{56,32},{64,72... | collective-permute-start | bytes 786440 | tf_op jit(solution)/shard_map/ppermute | solution.py:414
  44.6 1.4 %collective-permute-start.7 = (bf16[512,256]{1,0:T(8,128)(2,1)}, bf16[512,256]{1,0:T(8,128)(2,1)}, u32[]{:S(2)}, u32[]{:S(2)}) collective-permute-start(bf16[512,256]{1,0:T(8,128)(2,1)} %get-tuple-element.16), channel_id=1, source_target_pairs={{0,24},{8,0},{16,8},{24,16},{32,56},{40,32},{48,40},{56,48},{64,88... | collective-permute-start | bytes 786440 | tf_op jit(solution)/shard_map/ppermute | solution.py:414
  46.1 9.9 %collective-permute-done.1.refs_0_.refs_5_ = bf16[2048,256]{1,0:T(8,128)(2,1)S(1)} collective-permute-done((bf16[2048,256]{1,0:T(8,128)(2,1)}, bf16[2048,256]{1,0:T(8,128)(2,1)S(1)}, u32[]{:S(2)}, u32[]{:S(2)}) %collective-permute-start.1) | collective-permute-done | bytes 1048608 | tf_op jit(solution)/shard_map/ppermute | solution.py:404
  56.0 0.0 collective-permute-done.2.refs_1_.refs_6_
  56.0 0.0 all-to-all-done.1.edge_ref
  56.0 1.3 %copy-done.5 = bf16[256,2560]{1,0:T(8,128)(2,1)S(1)} copy-done((bf16[256,2560]{1,0:T(8,128)(2,1)S(1)}, bf16[256,2560]{1,0:T(8,128)(2,1)}, u32[]{:S(2)}) %copy-start.5) | copy-done | bytes 1310744
  57.3 0.4 shard_map.101.refs_0_
  57.7 2.0 %collective-permute-start.3 = (bf16[256,256]{1,0:T(8,128)(2,1)S(1)}, bf16[256,256]{1,0:T(8,128)(2,1)S(1)}, u32[]{:S(2)}, u32[]{:S(2)}) collective-permute-start(bf16[256,256]{1,0:T(8,128)(2,1)S(1)} %shard_map.101.refs_0_), channel_id=1, source_target_pairs={{0,2},{1,3},{2,4},{3,5},{4,6},{5,7},{6,0},{7,1},{8,10},{9,11},{10,... | collective-permute-start | bytes 393224 | tf_op jit(solution)/shard_map/ppermute | solution.py:404
  59.7 1.7 %collective-permute-start.4 = (bf16[256,256]{1,0:T(8,128)(2,1)S(1)}, bf16[256,256]{1,0:T(8,128)(2,1)S(1)}, u32[]{:S(2)}, u32[]{:S(2)}) collective-permute-start(bf16[256,256]{1,0:T(8,128)(2,1)S(1)} %shard_map.101.refs_0_), channel_id=1, source_target_pairs={{0,4},{1,5},{2,6},{3,7},{4,0},{5,1},{6,2},{7,3},{8,12},{9,13},{10,... | collective-permute-start | bytes 393224 | tf_op jit(solution)/shard_map/ppermute | solution.py:404
  61.4 1.9 %collective-permute-start.5 = (bf16[256,256]{1,0:T(8,128)(2,1)S(1)}, bf16[256,256]{1,0:T(8,128)(2,1)S(1)}, u32[]{:S(2)}, u32[]{:S(2)}) collective-permute-start(bf16[256,256]{1,0:T(8,128)(2,1)S(1)} %shard_map.101.refs_0_), channel_id=1, source_target_pairs={{0,6},{1,7},{2,0},{3,1},{4,2},{5,3},{6,4},{7,5},{8,14},{9,15},{10,... | collective-permute-start | bytes 393224 | tf_op jit(solution)/shard_map/ppermute | solution.py:404
  63.3 2.1 %shard_map.102.refs_4_ = bf16[2048,256]{1,0:T(8,128)(2,1)} custom-call(bf16[8192,128]{1,0:T(8,128)(2,1)} %w_b_hbm.5, bf16[8192,128]{1,0:T(8,128)(2,1)} %w_c_hbm.5), custom_call_target="tpu_custom_call" | custom-call | flops 1000 | bytes 1000 | tf_op jit(solution)/shard_map/pallas_call | solution.py:455
  65.4 1.2 %shard_map.99 = (bf16[256,1024]{1,0:T(8,128)(2,1)}, f32[8,128]{1,0:T(8,128)S(1)}) custom-call(bf16[256,128]{1,0:T(8,128)(2,1)S(1)} %copy-done.10, bf16[256,32]{1,0:T(8,128)(2,1)S(1)} %copy-done.9, f32[256,1024]{1,0:T(8,128)S(1)} %copy-done.7, bf16[32,64,128]{2,1,0:T(8,128)(2,1)S(1)} %all-to-all-done.1.edge_ref), custom_call_target="tpu_custom_call" | custom-call | flops 1000 | bytes 1000 | tf_op jit(solution)/shard_map/pallas_call | solution.py:492
  66.6 0.0 collective-permute-done.6.refs_8_
  66.6 0.0 collective-permute-done.7.refs_9_
  66.6 0.0 collective-permute-done.3.refs_1_
  66.6 0.0 collective-permute-done.4.refs_2_
  66.6 0.0 collective-permute-done.5.refs_3_
  66.6 0.0 copy-done
  66.6 0.9 %shard_map.104 = bf16[256,1024]{1,0:T(8,128)(2,1)S(1)} custom-call(bf16[256,256]{1,0:T(8,128)(2,1)S(1)} %shard_map.101.refs_0_, bf16[256,256]{1,0:T(8,128)(2,1)S(1)} %collective-permute-done.3.refs_1_, bf16[256,256]{1,0:T(8,128)(2,1)S(1)} %collective-permute-done.4.refs_2_, bf16[256,256]{1,0:T(8,128)(2,1)S(1)} %collective-permute-done.5.refs_3_, ...), custom_call_target="tpu_custom_call" | custom-call | flops 1000 | bytes 1000 | tf_op jit(solution)/shard_map/pallas_call | solution.py:501
  67.6 6.3 %collective-permute-start.8 = (bf16[256,1024]{1,0:T(8,128)(2,1)S(1)}, bf16[256,1024]{1,0:T(8,128)(2,1)S(1)}, u32[]{:S(2)}, u32[]{:S(2)}) collective-permute-start(bf16[256,1024]{1,0:T(8,128)(2,1)S(1)} %shard_map.104), channel_id=1, source_target_pairs={{0,1},{1,0},{2,3},{3,2},{4,5},{5,4},{6,7},{7,6},{8,9},{9,8},{10,11... | collective-permute-start | bytes 1572872 | tf_op jit(solution)/shard_map/ppermute | solution.py:515
  73.9 1.3 %shard_map.103.kept_ref = f32[256,1024]{1,0:T(8,128)S(1)} custom-call(bf16[256,256]{1,0:T(8,128)(2,1)S(1)} %shard_map.101.refs_0_, bf16[256,256]{1,0:T(8,128)(2,1)S(1)} %collective-permute-done.3.refs_1_, bf16[256,256]{1,0:T(8,128)(2,1)S(1)} %collective-permute-done.4.refs_2_, bf16[256,256]{1,0:T(8,128)(2,1)S(1)} %collective-permute-done.5.refs_3_, ...), custom_call_target="tpu_custom_call" | custom-call | flops 1000 | bytes 1000 | tf_op jit(solution)/shard_map/pallas_call | solution.py:501
  75.2 0.2 collective-permute-done.8.received_ref
  75.4 0.9 %shard_map.105 = bf16[256,1024]{1,0:T(8,128)(2,1)} custom-call(f32[256,1024]{1,0:T(8,128)S(1)} %shard_map.103.kept_ref, bf16[256,1024]{1,0:T(8,128)(2,1)S(1)} %collective-permute-done.8.received_ref), custom_call_target="tpu_custom_call" | custom-call | flops 1000 | bytes 1000 | tf_op jit(solution)/shard_map/pallas_call | solution.py:516
  (14 shorter events, 0.0 us)
Async XLA Ops:
  4.3 29.5 %all-to-all-start = ((bf16[32,72,128]{2,1,0:T(8,128)(2,1)}), bf16[32,72,128]{2,1,0:T(8,128)(2,1)S(1)}, u32[]{:S(2)}, u32[]{:S(2)}) async-start(bf16[32,72,128]{2,1,0:T(8,128)(2,1)} %shard_map.96._), calls=%async_computation | async-start | bytes 1179648 | tf_op jit(solution)/shard_map/all_to_all | solution.py:463
  16.4 4.9 %copy-start.2 = (bf16[256,1024]{1,0:T(8,128)(2,1)S(1)}, bf16[256,1024]{1,0:T(8,128)(2,1)}, u32[]{:S(2)}) copy-start(bf16[256,1024]{1,0:T(8,128)(2,1)} %x_hbm.3) | copy-start | bytes 1572868
  16.4 4.9 %copy-start.3 = (bf16[256,1024]{1,0:T(8,128)(2,1)S(1)}, bf16[256,1024]{1,0:T(8,128)(2,1)}, u32[]{:S(2)}) copy-start(bf16[256,1024]{1,0:T(8,128)(2,1)} %dy_hbm.3) | copy-start | bytes 1572868
  16.4 4.8 %copy-start.10 = (bf16[256,128]{1,0:T(8,128)(2,1)S(1)}, bf16[256,128]{1,0:T(8,128)(2,1)}, u32[]{:S(2)}) copy-start(bf16[256,128]{1,0:T(8,128)(2,1)} %b_ref.1) | copy-start | bytes 196612
  16.4 4.8 %copy-start.11 = (bf16[256,128]{1,0:T(8,128)(2,1)S(1)}, bf16[256,128]{1,0:T(8,128)(2,1)}, u32[]{:S(2)}) copy-start(bf16[256,128]{1,0:T(8,128)(2,1)} %c_hbm.3) | copy-start | bytes 196612
  16.4 4.8 %copy-start.12 = (f32[16,256]{1,0:T(8,128)S(1)}, f32[16,256]{1,0:T(8,128)}, u32[]{:S(2)}) copy-start(f32[16,256]{1,0:T(8,128)} %log_hbm.3) | copy-start | bytes 49156
  16.4 4.8 %copy-start.13 = (s32[4]{0:T(128)S(1)}, s32[4]{0:T(128)}, u32[]{:S(2)}) copy-start(s32[4]{0:T(128)} %lengths_hbm.3) | copy-start | bytes 52
  18.4 14.3 %collective-permute-start = (bf16[1024,256]{1,0:T(8,128)(2,1)}, bf16[1024,256]{1,0:T(8,128)(2,1)S(1)}, u32[]{:S(2)}, u32[]{:S(2)}) collective-permute-start(bf16[1024,256]{1,0:T(8,128)(2,1)} %shard_map.97), channel_id=1, source_target_pairs={{0,4},{1,5},{2,6},{3,7},{4,0},{5,1},{6,2},{7,3},{8,12},{9,13},{10,... | collective-permute-start | bytes 1572872 | tf_op jit(solution)/shard_map/ppermute | solution.py:404
  24.9 0.6 copy-start.8
  25.6 3.4 %copy-start.4 = (bf16[256,2560]{1,0:T(8,128)(2,1)}, bf16[256,2560]{1,0:T(8,128)(2,1)S(1)}, u32[]{:S(2)}) copy-start(bf16[256,2560]{1,0:T(8,128)(2,1)S(1)} %get-tuple-element.12.terms_ref) | copy-start | bytes 3932164
  25.6 3.4 %copy-start.6 = (f32[256,1024]{1,0:T(8,128)}, f32[256,1024]{1,0:T(8,128)S(1)}, u32[]{:S(2)}) copy-start(f32[256,1024]{1,0:T(8,128)S(1)} %get-tuple-element.10.local_ref) | copy-start | bytes 3145732
  25.6 8.3 %copy-start.9 = (bf16[256,32]{1,0:T(8,128)(2,1)S(1)}, bf16[256,32]{1,0:T(8,128)(2,1)}, u32[]{:S(2)}) copy-start(bf16[256,32]{1,0:T(8,128)(2,1)} %copy-done.8) | copy-start | bytes 49156
  28.9 27.0 %collective-permute-start.1 = (bf16[2048,256]{1,0:T(8,128)(2,1)}, bf16[2048,256]{1,0:T(8,128)(2,1)S(1)}, u32[]{:S(2)}, u32[]{:S(2)}) collective-permute-start(bf16[2048,256]{1,0:T(8,128)(2,1)} %get-tuple-element.13), channel_id=1, source_target_pairs={{0,2},{1,3},{2,4},{3,5},{4,6},{5,7},{6,0},{7,1},{8,10},{9,11},{10,... | collective-permute-start | bytes 3145736 | tf_op jit(solution)/shard_map/ppermute | solution.py:404
  29.3 26.6 %collective-permute-start.2 = (bf16[2048,256]{1,0:T(8,128)(2,1)}, bf16[2048,256]{1,0:T(8,128)(2,1)S(1)}, u32[]{:S(2)}, u32[]{:S(2)}) collective-permute-start(bf16[2048,256]{1,0:T(8,128)(2,1)} %get-tuple-element.14), channel_id=1, source_target_pairs={{0,6},{1,7},{2,0},{3,1},{4,2},{5,3},{6,4},{7,5},{8,14},{9,15},{10,... | collective-permute-start | bytes 3145736 | tf_op jit(solution)/shard_map/ppermute | solution.py:404
  34.0 0.8 %copy-start.1 = (bf16[32,64,128]{2,1,0:T(8,128)(2,1)}, bf16[32,64,128]{2,1,0:T(8,128)(2,1)S(1)}, u32[]{:S(2)}) copy-start(bf16[32,64,128]{2,1,0:T(8,128)(2,1)S(1)} %shard_map.98) | copy-start | bytes 1572868
  34.8 21.2 %all-to-all-start.1 = ((bf16[32,64,128]{2,1,0:T(8,128)(2,1)}), bf16[32,64,128]{2,1,0:T(8,128)(2,1)S(1)}, u32[]{:S(2)}, u32[]{:S(2)}) async-start(bf16[32,64,128]{2,1,0:T(8,128)(2,1)} %copy-done.1), calls=%async_computation.1 | async-start | bytes 1048576 | tf_op jit(solution)/shard_map/all_to_all | solution.py:484
  43.4 23.2 %collective-permute-start.6 = (bf16[512,256]{1,0:T(8,128)(2,1)}, bf16[512,256]{1,0:T(8,128)(2,1)S(1)}, u32[]{:S(2)}, u32[]{:S(2)}) collective-permute-start(bf16[512,256]{1,0:T(8,128)(2,1)} %get-tuple-element.17), channel_id=1, source_target_pairs={{0,8},{8,16},{16,24},{24,0},{32,40},{40,48},{48,56},{56,32},{64,72... | collective-permute-start | bytes 786440 | tf_op jit(solution)/shard_map/ppermute | solution.py:414
  44.6 22.0 %collective-permute-start.7 = (bf16[512,256]{1,0:T(8,128)(2,1)}, bf16[512,256]{1,0:T(8,128)(2,1)}, u32[]{:S(2)}, u32[]{:S(2)}) collective-permute-start(bf16[512,256]{1,0:T(8,128)(2,1)} %get-tuple-element.16), channel_id=1, source_target_pairs={{0,24},{8,0},{16,8},{24,16},{32,56},{40,32},{48,40},{56,48},{64,88... | collective-permute-start | bytes 786440 | tf_op jit(solution)/shard_map/ppermute | solution.py:414
  56.0 1.3 %copy-start.5 = (bf16[256,2560]{1,0:T(8,128)(2,1)S(1)}, bf16[256,2560]{1,0:T(8,128)(2,1)}, u32[]{:S(2)}) copy-start(bf16[256,2560]{1,0:T(8,128)(2,1)} %copy-done.4) | copy-start | bytes 3932164
  57.7 7.7 %copy-start.7 = (f32[256,1024]{1,0:T(8,128)S(1)}, f32[256,1024]{1,0:T(8,128)}, u32[]{:S(2)}) copy-start(f32[256,1024]{1,0:T(8,128)} %copy-done.6) | copy-start | bytes 3145732
  57.7 8.9 %collective-permute-start.3 = (bf16[256,256]{1,0:T(8,128)(2,1)S(1)}, bf16[256,256]{1,0:T(8,128)(2,1)S(1)}, u32[]{:S(2)}, u32[]{:S(2)}) collective-permute-start(bf16[256,256]{1,0:T(8,128)(2,1)S(1)} %shard_map.101.refs_0_), channel_id=1, source_target_pairs={{0,2},{1,3},{2,4},{3,5},{4,6},{5,7},{6,0},{7,1},{8,10},{9,11},{10,... | collective-permute-start | bytes 393224 | tf_op jit(solution)/shard_map/ppermute | solution.py:404
  59.7 6.9 %collective-permute-start.4 = (bf16[256,256]{1,0:T(8,128)(2,1)S(1)}, bf16[256,256]{1,0:T(8,128)(2,1)S(1)}, u32[]{:S(2)}, u32[]{:S(2)}) collective-permute-start(bf16[256,256]{1,0:T(8,128)(2,1)S(1)} %shard_map.101.refs_0_), channel_id=1, source_target_pairs={{0,4},{1,5},{2,6},{3,7},{4,0},{5,1},{6,2},{7,3},{8,12},{9,13},{10,... | collective-permute-start | bytes 393224 | tf_op jit(solution)/shard_map/ppermute | solution.py:404
  61.4 5.2 %collective-permute-start.5 = (bf16[256,256]{1,0:T(8,128)(2,1)S(1)}, bf16[256,256]{1,0:T(8,128)(2,1)S(1)}, u32[]{:S(2)}, u32[]{:S(2)}) collective-permute-start(bf16[256,256]{1,0:T(8,128)(2,1)S(1)} %shard_map.101.refs_0_), channel_id=1, source_target_pairs={{0,6},{1,7},{2,0},{3,1},{4,2},{5,3},{6,4},{7,5},{8,14},{9,15},{10,... | collective-permute-start | bytes 393224 | tf_op jit(solution)/shard_map/ppermute | solution.py:404
  65.4 1.3 %copy-start = (bf16[2048,256]{1,0:T(8,128)(2,1)S(1)}, bf16[2048,256]{1,0:T(8,128)(2,1)}, u32[]{:S(2)}) copy-start(bf16[2048,256]{1,0:T(8,128)(2,1)} %shard_map.102.refs_4_) | copy-start | bytes 3145732
  67.6 7.9 %collective-permute-start.8 = (bf16[256,1024]{1,0:T(8,128)(2,1)S(1)}, bf16[256,1024]{1,0:T(8,128)(2,1)S(1)}, u32[]{:S(2)}, u32[]{:S(2)}) collective-permute-start(bf16[256,1024]{1,0:T(8,128)(2,1)S(1)} %shard_map.104), channel_id=1, source_target_pairs={{0,1},{1,0},{2,3},{3,2},{4,5},{5,4},{6,7},{7,6},{8,9},{9,8},{10,11... | collective-permute-start | bytes 1572872 | tf_op jit(solution)/shard_map/ppermute | solution.py:515

commit v11 on v10

--- a/solution.py
+++ b/solution.py
@@ -173,29 +173,17 @@
 
 
 def stage_near_kernel(_, w_b_hbm, w_c_hbm, *refs):
-    sent_refs, held_refs, sems = refs[:2], refs[2:4], refs[4:]
+    sent_refs, held_refs, sems = refs[:3], refs[3:6], refs[6:]
     columns = sent_refs[0].shape[0] // CORES
     me = lax.axis_index("tp")
     core, chips = lax.rem(me, CORES), lax.axis_size("tp") // CORES
     pieces = []
-    for step, held_ref, sent_ref in zip((1, 3), held_refs, sent_refs):
+    for step, held_ref, sent_ref in zip((1, 3, 0), held_refs, sent_refs):
         first = lax.rem(me // CORES + step, chips) * CORES
         for which, other in enumerate((1 - core, core)):
             row = pl.multiple_of((first + other) * columns, columns)
             to = pl.ds(which * columns, columns)
             pieces.append((pl.ds(row, columns), held_ref.at[to, :], sent_ref.at[to, :]))
-    pass_through(pieces, w_b_hbm, w_c_hbm, *sems)
-
-
-def own_kernel(w_b_hbm, w_c_hbm, out_ref, held_ref, *sems):
-    columns = out_ref.shape[0] // CORES
-    me = lax.axis_index("tp")
-    core = lax.rem(me, CORES)
-    pieces = []
-    for which, other in enumerate((1 - core, core)):
-        row = pl.multiple_of((me - core + other) * columns, columns)
-        to = pl.ds(which * columns, columns)
-        pieces.append((pl.ds(row, columns), held_ref.at[to, :], out_ref.at[to, :]))
     pass_through(pieces, w_b_hbm, w_c_hbm, *sems)
 
 
@@ -369,13 +357,13 @@
     for low in range(0, columns, width):
         half = slice(first + low, first + low + width)
         total = mul(grads[0][...], own[half, :], NT)
-        total += mul(grads[1][...], up[half, :], NT)
+        total += mul(grads[2][...], up[half, :], NT)
         total_ref[:, low : low + width] = total + mul(grads[3][...], down[half, :], NT)
     for copy in copies(fetched):
         copy.wait()
     for low in range(0, columns, width):
         to = slice(low, low + width)
-        total = total_ref[:, to] + mul(grads[2][...], held_ref[to, :], NT)
+        total = total_ref[:, to] + mul(grads[1][...], held_ref[to, :], NT)
         out_ref[:, to] = total.astype(out_ref.dtype)
 
 
@@ -452,14 +440,6 @@
         along_y(piece, way)
         for piece, way in zip((fetched[: columns // 2], fetched[columns // 2 :]), ways)
     ]
-    own = call(
-        own_kernel,
-        shape(both, LOW),
-        [HBM] * 2,
-        LARGE_VMEM,
-        HBM,
-        [pltpu.VMEM(both, LOW), dma((4,)), dma((2,))],
-    )(w_b, w_c)
     summary = lax.all_to_all(summary, "seq", 0, 0)
     grad_x, terms, leave_cols = call(
         local_kernel,
@@ -473,7 +453,7 @@
         [BLOCK] * 3,
         held + [dma((6,))],
     )(*local)
-    near = stage(stage_near_kernel, both, 2, 4, leave_cols)
+    *near, own = stage(stage_near_kernel, both, 3, 6, leave_cols)
     up, down = [along_x(piece, way) for piece, way in zip(near, ways)]
     edges = call(
         scan_kernel,
@@ -488,7 +468,7 @@
         [BLOCK, BLOCK, HBM, HBM],
         8 * MIB,
     )(terms, edges, up, down)
-    others = [along_x(grad_bc, step) for step in (1, 2, 3)]
+    others = [along_x(grad_bc, step) for step in (2, 1, 3)]
     grad_x, done = call(
         grad_x_kernel,
         [shape((tokens, WIDE), LOW), shape((8, LANES), FULL)],

time: 76.7 us -> 76.8 us (level)
  Pallas kernels: 19.6 us -> 18 us
  starting transfers between devices: 39.9 us -> 41.1 us
    pallas_call x1 -> x0, Pallas kernels: 2.07 us -> none  [per_device(): call(own_kernel, shape(both, LOW), [HBM] * 2, LARGE_VMEM, HBM, [pltpu.VME...]
  transfers between devices with their start and end apart: 11 -> 11, of which waited for: 4 -> 5; matrix products, arithmetic and copies ran while one was open for 1% -> 1% of each run, Pallas kernels for 18% -> 16%
where the time goes in v11:
time: 76.8 us; the launch traced here: 76.4 us
  starting transfers between devices  41.1 us (54%)
  Pallas kernels  18 us (23%)
  waiting for transfers between devices  12.9 us (17%)
  local copies, waits for them, and re-layouts  3.63 us (5%)
  between operations  0.82 us (1%)
    all_to_all x1, starting transfers between devices, per_device(): summary = lax.all_to_all(summary, 'seq', 0, 0)  12 us
    ppermute x6, starting transfers between devices, along_x(): lax.ppermute(value, 'tp', [(at, (at + CORES * step) % devices) for at in...  11.8 us
    ppermute x6, waiting for transfers between devices, along_x(): lax.ppermute(value, 'tp', [(at, (at + CORES * step) % devices) for at in...  11.5 us
    all_to_all x1, starting transfers between devices, per_device(): edges = lax.all_to_all(edges, 'seq', 0, 0)  7.75 us
    ppermute x1, starting transfers between devices, per_device(): received = lax.ppermute(project(True, LOW), 'tp', partner)  6.79 us
    pallas_call x2, Pallas kernels, stage(): call(kernel, [shape(piece, LOW)] * arrays, [HBM] * 3, LARGE_VMEM, [HBM] *...  5.79 us
    pallas_call x1, Pallas kernels, per_device(): call(summary_kernel, shape((devices, 2 * rows + 8, STATE), LOW), [HBM] *...  3.71 us
    pallas_call x1, Pallas kernels, per_device(): call(local_kernel, [shape((tokens, WIDE), FULL), shape((tokens, 2 * WIDE...  3.65 us
  transfers between devices with their start and end apart: 11, of which 5 were waited for; matrix products, arithmetic and copies ran while one was open for 1% of the time, Pallas kernels for 16%

profile of v11, /device:TPU:1, one launch (start us, length us, event | category | flops | bytes accessed | tf_op | source)
XLA Modules:
  0.0 76.4 jit_solution(14937473941720115860)
XLA Ops:
  0.6 3.7 %shard_map.96._ = bf16[32,72,128]{2,1,0:T(8,128)(2,1)} custom-call(s32[4]{0:T(128)} %lengths_hbm.3, f32[16,256]{1,0:T(8,128)} %log_hbm.3, bf16[256,1024]{1,0:T(8,128)(2,1)} %x_hbm.3, bf16[256,128]{1,0:T(8,128)(2,1)} %b_ref.1, bf16[256,1024]{1,0:T(8,128)(2,1)} %dy_hbm.3, bf16[256,128]{1,0:T(8,128)(2,1)} %c_hbm.3), custom_call_target="tpu_custom_call" | custom-call | flops 1000 | bytes 1000 | tf_op jit(solution)/shard_map/pallas_call | solution.py:416
  4.3 12.0 %all-to-all-start = ((bf16[32,72,128]{2,1,0:T(8,128)(2,1)}), bf16[32,72,128]{2,1,0:T(8,128)(2,1)S(1)}, u32[]{:S(2)}, u32[]{:S(2)}) async-start(bf16[32,72,128]{2,1,0:T(8,128)(2,1)} %shard_map.96._), calls=%async_computation | async-start | bytes 1179648 | tf_op jit(solution)/shard_map/all_to_all | solution.py:443
  16.4 0.0 copy-start.2
  16.4 0.0 copy-start.3
  16.4 0.0 copy-start.10
  16.4 0.0 copy-start.11
  16.4 0.0 copy-start.12
  16.5 0.0 copy-start.13
  16.5 1.9 %shard_map.97 = bf16[1024,256]{1,0:T(8,128)(2,1)} custom-call(bf16[32,72,128]{2,1,0:T(8,128)(2,1)} %shard_map.96._, bf16[8192,128]{1,0:T(8,128)(2,1)} %w_b_hbm.3, bf16[8192,128]{1,0:T(8,128)(2,1)} %w_c_hbm.3), custom_call_target="tpu_custom_call" | custom-call | flops 1000 | bytes 1000 | tf_op jit(solution)/shard_map/pallas_call | solution.py:427
  18.4 2.8 %collective-permute-start = (bf16[1024,256]{1,0:T(8,128)(2,1)}, bf16[1024,256]{1,0:T(8,128)(2,1)S(1)}, u32[]{:S(2)}, u32[]{:S(2)}) collective-permute-start(bf16[1024,256]{1,0:T(8,128)(2,1)} %shard_map.97), channel_id=1, source_target_pairs={{0,4},{1,5},{2,6},{3,7},{4,0},{5,1},{6,2},{7,3},{8,12},{9,13},{10,... | collective-permute-start | bytes 1572872 | tf_op jit(solution)/shard_map/ppermute | solution.py:392
  21.3 0.0 copy-done.2
  21.3 0.0 copy-done.3
  21.3 0.0 copy-done.12
  21.3 0.0 copy-done.13
  21.3 3.6 %shard_map.95 = (f32[256,1024]{1,0:T(8,128)S(1)}, bf16[256,2560]{1,0:T(8,128)(2,1)S(1)}, bf16[256,32]{1,0:T(8,128)(2,1)S(1)}) custom-call(s32[4]{0:T(128)S(1)} %copy-done.13, f32[16,256]{1,0:T(8,128)S(1)} %copy-done.12, bf16[256,1024]{1,0:T(8,128)(2,1)S(1)} %copy-done.2, bf16[256,128]{1,0:T(8,128)(2,1)S(1)} %copy-done.10, bf16[256,1024]{1,0:T(8,128)(2,1)S(1)} %copy-done.3, ...), custom_call_target="tpu_custom_call" | custom-call | flops 1000 | bytes 1000 | tf_op jit(solution)/shard_map/pallas_call | solution.py:444
  24.9 0.0 copy-start.8
  25.0 0.6 copy-done.8
  25.6 3.8 %shard_map.100 = (bf16[2048,256]{1,0:T(8,128)(2,1)}, bf16[2048,256]{1,0:T(8,128)(2,1)}, bf16[2048,256]{1,0:T(8,128)(2,1)}) custom-call(bf16[256,32]{1,0:T(8,128)(2,1)} %copy-done.8, bf16[8192,128]{1,0:T(8,128)(2,1)} %w_b_hbm.3, bf16[8192,128]{1,0:T(8,128)(2,1)} %w_c_hbm.3), custom_call_target="tpu_custom_call" | custom-call | flops 1000 | bytes 1000 | tf_op jit(solution)/shard_map/pallas_call | solution.py:427
  29.5 0.4 collective-permute-start.1
  29.8 2.4 %collective-permute-start.2 = (bf16[2048,256]{1,0:T(8,128)(2,1)}, bf16[2048,256]{1,0:T(8,128)(2,1)S(1)}, u32[]{:S(2)}, u32[]{:S(2)}) collective-permute-start(bf16[2048,256]{1,0:T(8,128)(2,1)} %get-tuple-element.15), channel_id=1, source_target_pairs={{0,6},{1,7},{2,0},{3,1},{4,2},{5,3},{6,4},{7,5},{8,14},{9,15},{10,... | collective-permute-start | bytes 3145736 | tf_op jit(solution)/shard_map/ppermute | solution.py:392
  32.2 0.5 collective-permute-done.refs_1_.refs_7_
  32.7 1.2 %all-to-all-done.in_ref = bf16[32,72,128]{2,1,0:T(8,128)(2,1)S(1)} async-done(((bf16[32,72,128]{2,1,0:T(8,128)(2,1)}), bf16[32,72,128]{2,1,0:T(8,128)(2,1)S(1)}, u32[]{:S(2)}, u32[]{:S(2)}) %all-to-all-start) | async-done | bytes 589856 | tf_op jit(solution)/shard_map/all_to_all | solution.py:443
  33.9 0.1 shard_map.98
  34.0 0.0 copy-start.1
  34.0 0.8 %copy-done.1 = bf16[32,64,128]{2,1,0:T(8,128)(2,1)} copy-done((bf16[32,64,128]{2,1,0:T(8,128)(2,1)}, bf16[32,64,128]{2,1,0:T(8,128)(2,1)S(1)}, u32[]{:S(2)}) %copy-start.1) | copy-done | bytes 524312
  34.8 7.7 %all-to-all-start.1 = ((bf16[32,64,128]{2,1,0:T(8,128)(2,1)}), bf16[32,64,128]{2,1,0:T(8,128)(2,1)S(1)}, u32[]{:S(2)}, u32[]{:S(2)}) async-start(bf16[32,64,128]{2,1,0:T(8,128)(2,1)} %copy-done.1), calls=%async_computation.1 | async-start | bytes 1048576 | tf_op jit(solution)/shard_map/all_to_all | solution.py:464
  42.6 0.8 %fusion = (bf16[512,256]{1,0:T(8,128)(2,1)}, bf16[512,256]{1,0:T(8,128)(2,1)}) fusion(bf16[1024,256]{1,0:T(8,128)(2,1)S(1)} %collective-permute-done.refs_1_.refs_7_), kind=kLoop, calls=%fused_computation | loop fusion | bytes 1048576 | tf_op jit(solution)/shard_map/slice | solution.py:441
  43.4 1.2 %collective-permute-start.6 = (bf16[512,256]{1,0:T(8,128)(2,1)}, bf16[512,256]{1,0:T(8,128)(2,1)S(1)}, u32[]{:S(2)}, u32[]{:S(2)}) collective-permute-start(bf16[512,256]{1,0:T(8,128)(2,1)} %get-tuple-element.19), channel_id=1, source_target_pairs={{0,8},{8,16},{16,24},{24,0},{32,40},{40,48},{48,56},{56,32},{64,72... | collective-permute-start | bytes 786440 | tf_op jit(solution)/shard_map/ppermute | solution.py:402
  44.6 1.4 %collective-permute-start.7 = (bf16[512,256]{1,0:T(8,128)(2,1)}, bf16[512,256]{1,0:T(8,128)(2,1)}, u32[]{:S(2)}, u32[]{:S(2)}) collective-permute-start(bf16[512,256]{1,0:T(8,128)(2,1)} %get-tuple-element.18), channel_id=1, source_target_pairs={{0,24},{8,0},{16,8},{24,16},{32,56},{40,32},{48,40},{56,48},{64,88... | collective-permute-start | bytes 786440 | tf_op jit(solution)/shard_map/ppermute | solution.py:402
  46.1 9.9 %collective-permute-done.1.refs_0_.refs_5_ = bf16[2048,256]{1,0:T(8,128)(2,1)S(1)} collective-permute-done((bf16[2048,256]{1,0:T(8,128)(2,1)}, bf16[2048,256]{1,0:T(8,128)(2,1)S(1)}, u32[]{:S(2)}, u32[]{:S(2)}) %collective-permute-start.1) | collective-permute-done | bytes 1048608 | tf_op jit(solution)/shard_map/ppermute | solution.py:392
  55.9 0.0 collective-permute-done.2.refs_1_.refs_6_
  56.0 0.0 all-to-all-done.1.edge_ref
  56.0 1.3 %copy-done.5 = bf16[256,2560]{1,0:T(8,128)(2,1)S(1)} copy-done((bf16[256,2560]{1,0:T(8,128)(2,1)S(1)}, bf16[256,2560]{1,0:T(8,128)(2,1)}, u32[]{:S(2)}) %copy-start.5) | copy-done | bytes 1310744
  57.3 0.4 shard_map.101.refs_0_
  57.7 3.5 %collective-permute-start.3 = (bf16[256,256]{1,0:T(8,128)(2,1)S(1)}, bf16[256,256]{1,0:T(8,128)(2,1)S(1)}, u32[]{:S(2)}, u32[]{:S(2)}) collective-permute-start(bf16[256,256]{1,0:T(8,128)(2,1)S(1)} %shard_map.101.refs_0_), channel_id=1, source_target_pairs={{0,4},{1,5},{2,6},{3,7},{4,0},{5,1},{6,2},{7,3},{8,12},{9,13},{10,... | collective-permute-start | bytes 393224 | tf_op jit(solution)/shard_map/ppermute | solution.py:392
  61.2 0.0 collective-permute-start.4
  61.2 2.7 %collective-permute-start.5 = (bf16[256,256]{1,0:T(8,128)(2,1)S(1)}, bf16[256,256]{1,0:T(8,128)(2,1)S(1)}, u32[]{:S(2)}, u32[]{:S(2)}) collective-permute-start(bf16[256,256]{1,0:T(8,128)(2,1)S(1)} %shard_map.101.refs_0_), channel_id=1, source_target_pairs={{0,6},{1,7},{2,0},{3,1},{4,2},{5,3},{6,4},{7,5},{8,14},{9,15},{10,... | collective-permute-start | bytes 393224 | tf_op jit(solution)/shard_map/ppermute | solution.py:392
  63.9 1.2 %shard_map.99 = (bf16[256,1024]{1,0:T(8,128)(2,1)}, f32[8,128]{1,0:T(8,128)S(1)}) custom-call(bf16[256,128]{1,0:T(8,128)(2,1)S(1)} %copy-done.10, bf16[256,32]{1,0:T(8,128)(2,1)S(1)} %copy-done.9, f32[256,1024]{1,0:T(8,128)S(1)} %copy-done.7, bf16[32,64,128]{2,1,0:T(8,128)(2,1)S(1)} %all-to-all-done.1.edge_ref), custom_call_target="tpu_custom_call" | custom-call | flops 1000 | bytes 1000 | tf_op jit(solution)/shard_map/pallas_call | solution.py:472
  65.1 0.0 collective-permute-done.6.refs_8_
  65.1 0.0 collective-permute-done.7.refs_9_
  65.1 0.0 collective-permute-done.3.refs_1_
  65.1 1.1 %collective-permute-done.4.refs_2_ = bf16[256,256]{1,0:T(8,128)(2,1)S(1)} collective-permute-done((bf16[256,256]{1,0:T(8,128)(2,1)S(1)}, bf16[256,256]{1,0:T(8,128)(2,1)S(1)}, u32[]{:S(2)}, u32[]{:S(2)}) %collective-permute-start.4) | collective-permute-done | bytes 131104 | tf_op jit(solution)/shard_map/ppermute | solution.py:392
  66.3 0.0 collective-permute-done.5.refs_3_
  66.3 0.9 %shard_map.103 = bf16[256,1024]{1,0:T(8,128)(2,1)S(1)} custom-call(bf16[256,256]{1,0:T(8,128)(2,1)S(1)} %shard_map.101.refs_0_, bf16[256,256]{1,0:T(8,128)(2,1)S(1)} %collective-permute-done.3.refs_1_, bf16[256,256]{1,0:T(8,128)(2,1)S(1)} %collective-permute-done.4.refs_2_, bf16[256,256]{1,0:T(8,128)(2,1)S(1)} %collective-permute-done.5.refs_3_, ...), custom_call_target="tpu_custom_call" | custom-call | flops 1000 | bytes 1000 | tf_op jit(solution)/shard_map/pallas_call | solution.py:481
  67.2 6.8 %collective-permute-start.8 = (bf16[256,1024]{1,0:T(8,128)(2,1)S(1)}, bf16[256,1024]{1,0:T(8,128)(2,1)S(1)}, u32[]{:S(2)}, u32[]{:S(2)}) collective-permute-start(bf16[256,1024]{1,0:T(8,128)(2,1)S(1)} %shard_map.103), channel_id=1, source_target_pairs={{0,1},{1,0},{2,3},{3,2},{4,5},{5,4},{6,7},{7,6},{8,9},{9,8},{10,11... | collective-permute-start | bytes 1572872 | tf_op jit(solution)/shard_map/ppermute | solution.py:495
  74.0 1.3 %shard_map.102.kept_ref = f32[256,1024]{1,0:T(8,128)S(1)} custom-call(bf16[256,256]{1,0:T(8,128)(2,1)S(1)} %shard_map.101.refs_0_, bf16[256,256]{1,0:T(8,128)(2,1)S(1)} %collective-permute-done.3.refs_1_, bf16[256,256]{1,0:T(8,128)(2,1)S(1)} %collective-permute-done.4.refs_2_, bf16[256,256]{1,0:T(8,128)(2,1)S(1)} %collective-permute-done.5.refs_3_, ...), custom_call_target="tpu_custom_call" | custom-call | flops 1000 | bytes 1000 | tf_op jit(solution)/shard_map/pallas_call | solution.py:481
  75.3 0.2 collective-permute-done.8.received_ref
  75.5 0.9 %shard_map.104 = bf16[256,1024]{1,0:T(8,128)(2,1)} custom-call(f32[256,1024]{1,0:T(8,128)S(1)} %shard_map.102.kept_ref, bf16[256,1024]{1,0:T(8,128)(2,1)S(1)} %collective-permute-done.8.received_ref), custom_call_target="tpu_custom_call" | custom-call | flops 1000 | bytes 1000 | tf_op jit(solution)/shard_map/pallas_call | solution.py:496
  (13 shorter events, 0.0 us)
Async XLA Ops:
  4.3 29.5 %all-to-all-start = ((bf16[32,72,128]{2,1,0:T(8,128)(2,1)}), bf16[32,72,128]{2,1,0:T(8,128)(2,1)S(1)}, u32[]{:S(2)}, u32[]{:S(2)}) async-start(bf16[32,72,128]{2,1,0:T(8,128)(2,1)} %shard_map.96._), calls=%async_computation | async-start | bytes 1179648 | tf_op jit(solution)/shard_map/all_to_all | solution.py:443
  16.4 4.9 %copy-start.2 = (bf16[256,1024]{1,0:T(8,128)(2,1)S(1)}, bf16[256,1024]{1,0:T(8,128)(2,1)}, u32[]{:S(2)}) copy-start(bf16[256,1024]{1,0:T(8,128)(2,1)} %x_hbm.3) | copy-start | bytes 1572868
  16.4 4.9 %copy-start.3 = (bf16[256,1024]{1,0:T(8,128)(2,1)S(1)}, bf16[256,1024]{1,0:T(8,128)(2,1)}, u32[]{:S(2)}) copy-start(bf16[256,1024]{1,0:T(8,128)(2,1)} %dy_hbm.3) | copy-start | bytes 1572868
  16.4 4.8 %copy-start.10 = (bf16[256,128]{1,0:T(8,128)(2,1)S(1)}, bf16[256,128]{1,0:T(8,128)(2,1)}, u32[]{:S(2)}) copy-start(bf16[256,128]{1,0:T(8,128)(2,1)} %b_ref.1) | copy-start | bytes 196612
  16.4 4.8 %copy-start.11 = (bf16[256,128]{1,0:T(8,128)(2,1)S(1)}, bf16[256,128]{1,0:T(8,128)(2,1)}, u32[]{:S(2)}) copy-start(bf16[256,128]{1,0:T(8,128)(2,1)} %c_hbm.3) | copy-start | bytes 196612
  16.4 4.8 %copy-start.12 = (f32[16,256]{1,0:T(8,128)S(1)}, f32[16,256]{1,0:T(8,128)}, u32[]{:S(2)}) copy-start(f32[16,256]{1,0:T(8,128)} %log_hbm.3) | copy-start | bytes 49156
  16.5 4.8 %copy-start.13 = (s32[4]{0:T(128)S(1)}, s32[4]{0:T(128)}, u32[]{:S(2)}) copy-start(s32[4]{0:T(128)} %lengths_hbm.3) | copy-start | bytes 52
  18.4 14.3 %collective-permute-start = (bf16[1024,256]{1,0:T(8,128)(2,1)}, bf16[1024,256]{1,0:T(8,128)(2,1)S(1)}, u32[]{:S(2)}, u32[]{:S(2)}) collective-permute-start(bf16[1024,256]{1,0:T(8,128)(2,1)} %shard_map.97), channel_id=1, source_target_pairs={{0,4},{1,5},{2,6},{3,7},{4,0},{5,1},{6,2},{7,3},{8,12},{9,13},{10,... | collective-permute-start | bytes 1572872 | tf_op jit(solution)/shard_map/ppermute | solution.py:392
  24.9 0.6 copy-start.8
  25.6 3.9 %copy-start.4 = (bf16[256,2560]{1,0:T(8,128)(2,1)}, bf16[256,2560]{1,0:T(8,128)(2,1)S(1)}, u32[]{:S(2)}) copy-start(bf16[256,2560]{1,0:T(8,128)(2,1)S(1)} %get-tuple-element.13.terms_ref) | copy-start | bytes 3932164
  25.6 3.9 %copy-start.6 = (f32[256,1024]{1,0:T(8,128)}, f32[256,1024]{1,0:T(8,128)S(1)}, u32[]{:S(2)}) copy-start(f32[256,1024]{1,0:T(8,128)S(1)} %get-tuple-element.11.local_ref) | copy-start | bytes 3145732
  25.6 8.3 %copy-start.9 = (bf16[256,32]{1,0:T(8,128)(2,1)S(1)}, bf16[256,32]{1,0:T(8,128)(2,1)}, u32[]{:S(2)}) copy-start(bf16[256,32]{1,0:T(8,128)(2,1)} %copy-done.8) | copy-start | bytes 49156
  29.5 26.5 %collective-permute-start.1 = (bf16[2048,256]{1,0:T(8,128)(2,1)}, bf16[2048,256]{1,0:T(8,128)(2,1)S(1)}, u32[]{:S(2)}, u32[]{:S(2)}) collective-permute-start(bf16[2048,256]{1,0:T(8,128)(2,1)} %get-tuple-element.14), channel_id=1, source_target_pairs={{0,2},{1,3},{2,4},{3,5},{4,6},{5,7},{6,0},{7,1},{8,10},{9,11},{10,... | collective-permute-start | bytes 3145736 | tf_op jit(solution)/shard_map/ppermute | solution.py:392
  29.8 26.1 %collective-permute-start.2 = (bf16[2048,256]{1,0:T(8,128)(2,1)}, bf16[2048,256]{1,0:T(8,128)(2,1)S(1)}, u32[]{:S(2)}, u32[]{:S(2)}) collective-permute-start(bf16[2048,256]{1,0:T(8,128)(2,1)} %get-tuple-element.15), channel_id=1, source_target_pairs={{0,6},{1,7},{2,0},{3,1},{4,2},{5,3},{6,4},{7,5},{8,14},{9,15},{10,... | collective-permute-start | bytes 3145736 | tf_op jit(solution)/shard_map/ppermute | solution.py:392
  34.0 0.8 %copy-start.1 = (bf16[32,64,128]{2,1,0:T(8,128)(2,1)}, bf16[32,64,128]{2,1,0:T(8,128)(2,1)S(1)}, u32[]{:S(2)}) copy-start(bf16[32,64,128]{2,1,0:T(8,128)(2,1)S(1)} %shard_map.98) | copy-start | bytes 1572868
  34.8 21.1 %all-to-all-start.1 = ((bf16[32,64,128]{2,1,0:T(8,128)(2,1)}), bf16[32,64,128]{2,1,0:T(8,128)(2,1)S(1)}, u32[]{:S(2)}, u32[]{:S(2)}) async-start(bf16[32,64,128]{2,1,0:T(8,128)(2,1)} %copy-done.1), calls=%async_computation.1 | async-start | bytes 1048576 | tf_op jit(solution)/shard_map/all_to_all | solution.py:464
  43.4 21.7 %collective-permute-start.6 = (bf16[512,256]{1,0:T(8,128)(2,1)}, bf16[512,256]{1,0:T(8,128)(2,1)S(1)}, u32[]{:S(2)}, u32[]{:S(2)}) collective-permute-start(bf16[512,256]{1,0:T(8,128)(2,1)} %get-tuple-element.19), channel_id=1, source_target_pairs={{0,8},{8,16},{16,24},{24,0},{32,40},{40,48},{48,56},{56,32},{64,72... | collective-permute-start | bytes 786440 | tf_op jit(solution)/shard_map/ppermute | solution.py:402
  44.6 20.5 %collective-permute-start.7 = (bf16[512,256]{1,0:T(8,128)(2,1)}, bf16[512,256]{1,0:T(8,128)(2,1)}, u32[]{:S(2)}, u32[]{:S(2)}) collective-permute-start(bf16[512,256]{1,0:T(8,128)(2,1)} %get-tuple-element.18), channel_id=1, source_target_pairs={{0,24},{8,0},{16,8},{24,16},{32,56},{40,32},{48,40},{56,48},{64,88... | collective-permute-start | bytes 786440 | tf_op jit(solution)/shard_map/ppermute | solution.py:402
  56.0 1.3 %copy-start.5 = (bf16[256,2560]{1,0:T(8,128)(2,1)S(1)}, bf16[256,2560]{1,0:T(8,128)(2,1)}, u32[]{:S(2)}) copy-start(bf16[256,2560]{1,0:T(8,128)(2,1)} %copy-done.4) | copy-start | bytes 3932164
  57.3 6.6 %copy-start.7 = (f32[256,1024]{1,0:T(8,128)S(1)}, f32[256,1024]{1,0:T(8,128)}, u32[]{:S(2)}) copy-start(f32[256,1024]{1,0:T(8,128)} %copy-done.6) | copy-start | bytes 3145732
  57.3 9.0 %copy-start = (bf16[2048,256]{1,0:T(8,128)(2,1)S(1)}, bf16[2048,256]{1,0:T(8,128)(2,1)}, u32[]{:S(2)}) copy-start(bf16[2048,256]{1,0:T(8,128)(2,1)} %get-tuple-element.16.refs_4_) | copy-start | bytes 3145732
  57.7 7.4 %collective-permute-start.3 = (bf16[256,256]{1,0:T(8,128)(2,1)S(1)}, bf16[256,256]{1,0:T(8,128)(2,1)S(1)}, u32[]{:S(2)}, u32[]{:S(2)}) collective-permute-start(bf16[256,256]{1,0:T(8,128)(2,1)S(1)} %shard_map.101.refs_0_), channel_id=1, source_target_pairs={{0,4},{1,5},{2,6},{3,7},{4,0},{5,1},{6,2},{7,3},{8,12},{9,13},{10,... | collective-permute-start | bytes 393224 | tf_op jit(solution)/shard_map/ppermute | solution.py:392
  61.2 5.0 %collective-permute-start.4 = (bf16[256,256]{1,0:T(8,128)(2,1)S(1)}, bf16[256,256]{1,0:T(8,128)(2,1)S(1)}, u32[]{:S(2)}, u32[]{:S(2)}) collective-permute-start(bf16[256,256]{1,0:T(8,128)(2,1)S(1)} %shard_map.101.refs_0_), channel_id=1, source_target_pairs={{0,2},{1,3},{2,4},{3,5},{4,6},{5,7},{6,0},{7,1},{8,10},{9,11},{10,... | collective-permute-start | bytes 393224 | tf_op jit(solution)/shard_map/ppermute | solution.py:392
  61.2 5.0 %collective-permute-start.5 = (bf16[256,256]{1,0:T(8,128)(2,1)S(1)}, bf16[256,256]{1,0:T(8,128)(2,1)S(1)}, u32[]{:S(2)}, u32[]{:S(2)}) collective-permute-start(bf16[256,256]{1,0:T(8,128)(2,1)S(1)} %shard_map.101.refs_0_), channel_id=1, source_target_pairs={{0,6},{1,7},{2,0},{3,1},{4,2},{5,3},{6,4},{7,5},{8,14},{9,15},{10,... | collective-permute-start | bytes 393224 | tf_op jit(solution)/shard_map/ppermute | solution.py:392
  67.2 8.3 %collective-permute-start.8 = (bf16[256,1024]{1,0:T(8,128)(2,1)S(1)}, bf16[256,1024]{1,0:T(8,128)(2,1)S(1)}, u32[]{:S(2)}, u32[]{:S(2)}) collective-permute-start(bf16[256,1024]{1,0:T(8,128)(2,1)S(1)} %shard_map.103), channel_id=1, source_target_pairs={{0,1},{1,0},{2,3},{3,2},{4,5},{5,4},{6,7},{7,6},{8,9},{9,8},{10,11... | collective-permute-start | bytes 1572872 | tf_op jit(solution)/shard_map/ppermute | solution.py:495

commit v12 on v10

--- a/solution.py
+++ b/solution.py
@@ -460,6 +460,7 @@
         HBM,
         [pltpu.VMEM(both, LOW), dma((4,)), dma((2,))],
     )(w_b, w_c)
+    sent = summary
     summary = lax.all_to_all(summary, "seq", 0, 0)
     grad_x, terms, leave_cols = call(
         local_kernel,
@@ -473,7 +474,7 @@
         [BLOCK] * 3,
         held + [dma((6,))],
     )(*local)
-    near = stage(stage_near_kernel, both, 2, 4, leave_cols)
+    near = stage(stage_near_kernel, both, 2, 4, sent)
     up, down = [along_x(piece, way) for piece, way in zip(near, ways)]
     edges = call(
         scan_kernel,

time: 76.7 us -> 76.7 us (level)
  local copies, waits for them, and re-layouts: 3.64 us -> 5.04 us
  Pallas kernels: 19.6 us -> 18.6 us
    unnamed x28 -> x24, local copies, waits for them, and re-layouts: 2.79 us -> 4.21 us
    pallas_call x2, Pallas kernels: 5.29 us -> 4.32 us  [stage(): call(kernel, [shape(piece, LOW)] * arrays, [HBM] * 3, LARGE_VMEM, [HBM] *...]
  transfers between devices with their start and end apart: 11 -> 11, of which waited for: 4 -> 4; matrix products, arithmetic and copies ran while one was open for 1% -> 1% of each run, Pallas kernels for 18% -> 17%
where the time goes in v12:
time: 76.7 us; the launch traced here: 76.3 us
  starting transfers between devices  39.4 us (51%)
  Pallas kernels  18.6 us (24%)
  waiting for transfers between devices  12.4 us (16%)
  local copies, waits for them, and re-layouts  5.04 us (7%)
  between operations  0.86 us (1%)
    all_to_all x1, starting transfers between devices, per_device(): summary = lax.all_to_all(summary, 'seq', 0, 0)  12 us
    ppermute x6, waiting for transfers between devices, along_x(): lax.ppermute(value, 'tp', [(at, (at + CORES * step) % devices) for at in...  10.9 us
    ppermute x6, starting transfers between devices, along_x(): lax.ppermute(value, 'tp', [(at, (at + CORES * step) % devices) for at in...  10.6 us
    all_to_all x1, starting transfers between devices, per_device(): edges = lax.all_to_all(edges, 'seq', 0, 0)  7.71 us
    ppermute x1, starting transfers between devices, per_device(): received = lax.ppermute(project(True, LOW), 'tp', partner)  6.34 us
    pallas_call x2, Pallas kernels, stage(): call(kernel, [shape(piece, LOW)] * arrays, [HBM] * 3, LARGE_VMEM, [HBM] *...  4.32 us
    unnamed x24, local copies, waits for them, and re-layouts  4.21 us
    pallas_call x1, Pallas kernels, per_device(): call(summary_kernel, shape((devices, 2 * rows + 8, STATE), LOW), [HBM] *...  3.69 us
  transfers between devices with their start and end apart: 11, of which 4 were waited for; matrix products, arithmetic and copies ran while one was open for 1% of the time, Pallas kernels for 17%

profile of v12, /device:TPU:1, one launch (start us, length us, event | category | flops | bytes accessed | tf_op | source)
XLA Modules:
  0.0 76.3 jit_solution(11050210177929065088)
XLA Ops:
  0.6 3.7 %shard_map.96._ = bf16[32,72,128]{2,1,0:T(8,128)(2,1)} custom-call(s32[4]{0:T(128)} %lengths_hbm.3, f32[16,256]{1,0:T(8,128)} %log_hbm.3, bf16[256,1024]{1,0:T(8,128)(2,1)} %x_hbm.3, bf16[256,128]{1,0:T(8,128)(2,1)} %b_ref.1, bf16[256,1024]{1,0:T(8,128)(2,1)} %dy_hbm.3, bf16[256,128]{1,0:T(8,128)(2,1)} %c_hbm.3), custom_call_target="tpu_custom_call" | custom-call | flops 1000 | bytes 1000 | tf_op jit(solution)/shard_map/pallas_call | solution.py:428
  4.3 12.0 %all-to-all-start = ((bf16[32,72,128]{2,1,0:T(8,128)(2,1)}), bf16[32,72,128]{2,1,0:T(8,128)(2,1)S(1)}, u32[]{:S(2)}, u32[]{:S(2)}) async-start(bf16[32,72,128]{2,1,0:T(8,128)(2,1)} %shard_map.96._), calls=%async_computation | async-start | bytes 1179648 | tf_op jit(solution)/shard_map/all_to_all | solution.py:464
  16.4 1.9 %shard_map.97 = bf16[1024,256]{1,0:T(8,128)(2,1)} custom-call(bf16[32,72,128]{2,1,0:T(8,128)(2,1)} %shard_map.96._, bf16[8192,128]{1,0:T(8,128)(2,1)} %w_b_hbm.5, bf16[8192,128]{1,0:T(8,128)(2,1)} %w_c_hbm.5), custom_call_target="tpu_custom_call" | custom-call | flops 1000 | bytes 1000 | tf_op jit(solution)/shard_map/pallas_call | solution.py:439
  18.3 0.0 copy-start.2
  18.3 0.0 copy-start.3
  18.3 0.0 copy-start.8
  18.3 0.0 copy-start.9
  18.3 0.0 copy-start.10
  18.3 0.0 copy-start.11
  18.3 2.8 %collective-permute-start = (bf16[1024,256]{1,0:T(8,128)(2,1)}, bf16[1024,256]{1,0:T(8,128)(2,1)S(1)}, u32[]{:S(2)}, u32[]{:S(2)}) collective-permute-start(bf16[1024,256]{1,0:T(8,128)(2,1)} %shard_map.97), channel_id=1, source_target_pairs={{0,4},{1,5},{2,6},{3,7},{4,0},{5,1},{6,2},{7,3},{8,12},{9,13},{10,... | collective-permute-start | bytes 1572872 | tf_op jit(solution)/shard_map/ppermute | solution.py:404
  21.2 2.5 %shard_map.100 = (bf16[2048,256]{1,0:T(8,128)(2,1)}, bf16[2048,256]{1,0:T(8,128)(2,1)}) custom-call(bf16[32,72,128]{2,1,0:T(8,128)(2,1)} %shard_map.96._, bf16[8192,128]{1,0:T(8,128)(2,1)} %w_b_hbm.5, bf16[8192,128]{1,0:T(8,128)(2,1)} %w_c_hbm.5), custom_call_target="tpu_custom_call" | custom-call | flops 1000 | bytes 1000 | tf_op jit(solution)/shard_map/pallas_call | solution.py:439
  23.6 0.4 collective-permute-start.1
  24.0 2.4 %collective-permute-start.2 = (bf16[2048,256]{1,0:T(8,128)(2,1)}, bf16[2048,256]{1,0:T(8,128)(2,1)S(1)}, u32[]{:S(2)}, u32[]{:S(2)}) collective-permute-start(bf16[2048,256]{1,0:T(8,128)(2,1)} %get-tuple-element.14), channel_id=1, source_target_pairs={{0,6},{1,7},{2,0},{3,1},{4,2},{5,3},{6,4},{7,5},{8,14},{9,15},{10,... | collective-permute-start | bytes 3145736 | tf_op jit(solution)/shard_map/ppermute | solution.py:404
  26.4 0.0 copy-done.2
  26.4 0.0 copy-done.10
  26.4 0.0 copy-done.11
  26.4 3.6 %shard_map.95 = (f32[256,1024]{1,0:T(8,128)S(1)}, bf16[256,2560]{1,0:T(8,128)(2,1)S(1)}, bf16[256,32]{1,0:T(8,128)(2,1)S(1)}) custom-call(s32[4]{0:T(128)S(1)} %copy-done.11, f32[16,256]{1,0:T(8,128)S(1)} %copy-done.10, bf16[256,1024]{1,0:T(8,128)(2,1)S(1)} %copy-done.2, bf16[256,128]{1,0:T(8,128)(2,1)S(1)} %copy-done.8, bf16[256,1024]{1,0:T(8,128)(2,1)S(1)} %copy-done.3, ...), custom_call_target="tpu_custom_call" | custom-call | flops 1000 | bytes 1000 | tf_op jit(solution)/shard_map/pallas_call | solution.py:465
  30.1 1.1 %copy-done.4 = bf16[256,2560]{1,0:T(8,128)(2,1)} copy-done((bf16[256,2560]{1,0:T(8,128)(2,1)}, bf16[256,2560]{1,0:T(8,128)(2,1)S(1)}, u32[]{:S(2)}) %copy-start.4) | copy-done | bytes 1310744
  31.1 1.0 %copy-done.6 = f32[256,1024]{1,0:T(8,128)} copy-done((f32[256,1024]{1,0:T(8,128)}, f32[256,1024]{1,0:T(8,128)S(1)}, u32[]{:S(2)}) %copy-start.6) | copy-done | bytes 1048600
  32.1 0.5 collective-permute-done.refs_1_.refs_7_
  32.6 1.2 %all-to-all-done.in_ref = bf16[32,72,128]{2,1,0:T(8,128)(2,1)S(1)} async-done(((bf16[32,72,128]{2,1,0:T(8,128)(2,1)}), bf16[32,72,128]{2,1,0:T(8,128)(2,1)S(1)}, u32[]{:S(2)}, u32[]{:S(2)}) %all-to-all-start) | async-done | bytes 589856 | tf_op jit(solution)/shard_map/all_to_all | solution.py:464
  33.9 0.1 shard_map.98
  34.0 0.0 copy-start.1
  34.0 0.8 %copy-done.1 = bf16[32,64,128]{2,1,0:T(8,128)(2,1)} copy-done((bf16[32,64,128]{2,1,0:T(8,128)(2,1)}, bf16[32,64,128]{2,1,0:T(8,128)(2,1)S(1)}, u32[]{:S(2)}) %copy-start.1) | copy-done | bytes 524312
  34.8 7.7 %all-to-all-start.1 = ((bf16[32,64,128]{2,1,0:T(8,128)(2,1)}), bf16[32,64,128]{2,1,0:T(8,128)(2,1)S(1)}, u32[]{:S(2)}, u32[]{:S(2)}) async-start(bf16[32,64,128]{2,1,0:T(8,128)(2,1)} %copy-done.1), calls=%async_computation.1 | async-start | bytes 1048576 | tf_op jit(solution)/shard_map/all_to_all | solution.py:485
  42.5 0.8 %fusion = (bf16[512,256]{1,0:T(8,128)(2,1)}, bf16[512,256]{1,0:T(8,128)(2,1)}) fusion(bf16[1024,256]{1,0:T(8,128)(2,1)S(1)} %collective-permute-done.refs_1_.refs_7_), kind=kLoop, calls=%fused_computation | loop fusion | bytes 1048576 | tf_op jit(solution)/shard_map/slice | solution.py:453
  43.4 1.2 %collective-permute-start.6 = (bf16[512,256]{1,0:T(8,128)(2,1)}, bf16[512,256]{1,0:T(8,128)(2,1)S(1)}, u32[]{:S(2)}, u32[]{:S(2)}) collective-permute-start(bf16[512,256]{1,0:T(8,128)(2,1)} %get-tuple-element.17), channel_id=1, source_target_pairs={{0,8},{8,16},{16,24},{24,0},{32,40},{40,48},{48,56},{56,32},{64,72... | collective-permute-start | bytes 786440 | tf_op jit(solution)/shard_map/ppermute | solution.py:414
  44.6 1.4 %collective-permute-start.7 = (bf16[512,256]{1,0:T(8,128)(2,1)}, bf16[512,256]{1,0:T(8,128)(2,1)}, u32[]{:S(2)}, u32[]{:S(2)}) collective-permute-start(bf16[512,256]{1,0:T(8,128)(2,1)} %get-tuple-element.16), channel_id=1, source_target_pairs={{0,24},{8,0},{16,8},{24,16},{32,56},{40,32},{48,40},{56,48},{64,88... | collective-permute-start | bytes 786440 | tf_op jit(solution)/shard_map/ppermute | solution.py:414
  46.0 10.4 %collective-permute-done.1.refs_0_.refs_5_ = bf16[2048,256]{1,0:T(8,128)(2,1)S(1)} collective-permute-done((bf16[2048,256]{1,0:T(8,128)(2,1)}, bf16[2048,256]{1,0:T(8,128)(2,1)S(1)}, u32[]{:S(2)}, u32[]{:S(2)}) %collective-permute-start.1) | collective-permute-done | bytes 1048608 | tf_op jit(solution)/shard_map/ppermute | solution.py:404
  56.4 0.0 collective-permute-done.2.refs_1_.refs_6_
  56.5 0.0 all-to-all-done.1.edge_ref
  56.5 1.3 %copy-done.5 = bf16[256,2560]{1,0:T(8,128)(2,1)S(1)} copy-done((bf16[256,2560]{1,0:T(8,128)(2,1)S(1)}, bf16[256,2560]{1,0:T(8,128)(2,1)}, u32[]{:S(2)}) %copy-start.5) | copy-done | bytes 1310744
  57.8 0.4 shard_map.101.refs_0_
  58.2 1.4 %collective-permute-start.3 = (bf16[256,256]{1,0:T(8,128)(2,1)S(1)}, bf16[256,256]{1,0:T(8,128)(2,1)S(1)}, u32[]{:S(2)}, u32[]{:S(2)}) collective-permute-start(bf16[256,256]{1,0:T(8,128)(2,1)S(1)} %shard_map.101.refs_0_), channel_id=1, source_target_pairs={{0,2},{1,3},{2,4},{3,5},{4,6},{5,7},{6,0},{7,1},{8,10},{9,11},{10,... | collective-permute-start | bytes 393224 | tf_op jit(solution)/shard_map/ppermute | solution.py:404
  59.6 2.3 %collective-permute-start.4 = (bf16[256,256]{1,0:T(8,128)(2,1)S(1)}, bf16[256,256]{1,0:T(8,128)(2,1)S(1)}, u32[]{:S(2)}, u32[]{:S(2)}) collective-permute-start(bf16[256,256]{1,0:T(8,128)(2,1)S(1)} %shard_map.101.refs_0_), channel_id=1, source_target_pairs={{0,4},{1,5},{2,6},{3,7},{4,0},{5,1},{6,2},{7,3},{8,12},{9,13},{10,... | collective-permute-start | bytes 393224 | tf_op jit(solution)/shard_map/ppermute | solution.py:404
  61.9 1.3 %collective-permute-start.5 = (bf16[256,256]{1,0:T(8,128)(2,1)S(1)}, bf16[256,256]{1,0:T(8,128)(2,1)S(1)}, u32[]{:S(2)}, u32[]{:S(2)}) collective-permute-start(bf16[256,256]{1,0:T(8,128)(2,1)S(1)} %shard_map.101.refs_0_), channel_id=1, source_target_pairs={{0,6},{1,7},{2,0},{3,1},{4,2},{5,3},{6,4},{7,5},{8,14},{9,15},{10,... | collective-permute-start | bytes 393224 | tf_op jit(solution)/shard_map/ppermute | solution.py:404
  63.2 2.1 %shard_map.102.refs_4_ = bf16[2048,256]{1,0:T(8,128)(2,1)} custom-call(bf16[8192,128]{1,0:T(8,128)(2,1)} %w_b_hbm.5, bf16[8192,128]{1,0:T(8,128)(2,1)} %w_c_hbm.5), custom_call_target="tpu_custom_call" | custom-call | flops 1000 | bytes 1000 | tf_op jit(solution)/shard_map/pallas_call | solution.py:455
  65.3 1.2 %shard_map.99 = (bf16[256,1024]{1,0:T(8,128)(2,1)}, f32[8,128]{1,0:T(8,128)S(1)}) custom-call(bf16[256,128]{1,0:T(8,128)(2,1)S(1)} %copy-done.8, bf16[256,32]{1,0:T(8,128)(2,1)S(1)} %get-tuple-element.9.refs_0_.leave_ref, f32[256,1024]{1,0:T(8,128)S(1)} %copy-done.7, bf16[32,64,128]{2,1,0:T(8,128)(2,1)S(1)} %all-to-all-done.1.edge_ref), custom_call_target="tpu_custom_call" | custom-call | flops 1000 | bytes 1000 | tf_op jit(solution)/shard_map/pallas_call | solution.py:493
  66.5 0.0 collective-permute-done.6.refs_8_
  66.5 0.0 collective-permute-done.7.refs_9_
  66.6 0.0 collective-permute-done.3.refs_1_
  66.6 0.0 collective-permute-done.4.refs_2_
  66.6 0.0 collective-permute-done.5.refs_3_
  66.6 0.9 %shard_map.104 = bf16[256,1024]{1,0:T(8,128)(2,1)S(1)} custom-call(bf16[256,256]{1,0:T(8,128)(2,1)S(1)} %shard_map.101.refs_0_, bf16[256,256]{1,0:T(8,128)(2,1)S(1)} %collective-permute-done.3.refs_1_, bf16[256,256]{1,0:T(8,128)(2,1)S(1)} %collective-permute-done.4.refs_2_, bf16[256,256]{1,0:T(8,128)(2,1)S(1)} %collective-permute-done.5.refs_3_, ...), custom_call_target="tpu_custom_call" | custom-call | flops 1000 | bytes 1000 | tf_op jit(solution)/shard_map/pallas_call | solution.py:502
  67.5 6.3 %collective-permute-start.8 = (bf16[256,1024]{1,0:T(8,128)(2,1)S(1)}, bf16[256,1024]{1,0:T(8,128)(2,1)S(1)}, u32[]{:S(2)}, u32[]{:S(2)}) collective-permute-start(bf16[256,1024]{1,0:T(8,128)(2,1)S(1)} %shard_map.104), channel_id=1, source_target_pairs={{0,1},{1,0},{2,3},{3,2},{4,5},{5,4},{6,7},{7,6},{8,9},{9,8},{10,11... | collective-permute-start | bytes 1572872 | tf_op jit(solution)/shard_map/ppermute | solution.py:516
  73.8 1.3 %shard_map.103.kept_ref = f32[256,1024]{1,0:T(8,128)S(1)} custom-call(bf16[256,256]{1,0:T(8,128)(2,1)S(1)} %shard_map.101.refs_0_, bf16[256,256]{1,0:T(8,128)(2,1)S(1)} %collective-permute-done.3.refs_1_, bf16[256,256]{1,0:T(8,128)(2,1)S(1)} %collective-permute-done.4.refs_2_, bf16[256,256]{1,0:T(8,128)(2,1)S(1)} %collective-permute-done.5.refs_3_, ...), custom_call_target="tpu_custom_call" | custom-call | flops 1000 | bytes 1000 | tf_op jit(solution)/shard_map/pallas_call | solution.py:502
  75.2 0.2 collective-permute-done.8.received_ref
  75.4 0.9 %shard_map.105 = bf16[256,1024]{1,0:T(8,128)(2,1)} custom-call(f32[256,1024]{1,0:T(8,128)S(1)} %shard_map.103.kept_ref, bf16[256,1024]{1,0:T(8,128)(2,1)S(1)} %collective-permute-done.8.received_ref), custom_call_target="tpu_custom_call" | custom-call | flops 1000 | bytes 1000 | tf_op jit(solution)/shard_map/pallas_call | solution.py:517
  (10 shorter events, 0.0 us)
Async XLA Ops:
  4.3 29.5 %all-to-all-start = ((bf16[32,72,128]{2,1,0:T(8,128)(2,1)}), bf16[32,72,128]{2,1,0:T(8,128)(2,1)S(1)}, u32[]{:S(2)}, u32[]{:S(2)}) async-start(bf16[32,72,128]{2,1,0:T(8,128)(2,1)} %shard_map.96._), calls=%async_computation | async-start | bytes 1179648 | tf_op jit(solution)/shard_map/all_to_all | solution.py:464
  18.3 8.1 %copy-start.2 = (bf16[256,1024]{1,0:T(8,128)(2,1)S(1)}, bf16[256,1024]{1,0:T(8,128)(2,1)}, u32[]{:S(2)}) copy-start(bf16[256,1024]{1,0:T(8,128)(2,1)} %x_hbm.3) | copy-start | bytes 1572868
  18.3 8.1 %copy-start.3 = (bf16[256,1024]{1,0:T(8,128)(2,1)S(1)}, bf16[256,1024]{1,0:T(8,128)(2,1)}, u32[]{:S(2)}) copy-start(bf16[256,1024]{1,0:T(8,128)(2,1)} %dy_hbm.3) | copy-start | bytes 1572868
  18.3 8.1 %copy-start.8 = (bf16[256,128]{1,0:T(8,128)(2,1)S(1)}, bf16[256,128]{1,0:T(8,128)(2,1)}, u32[]{:S(2)}) copy-start(bf16[256,128]{1,0:T(8,128)(2,1)} %b_ref.1) | copy-start | bytes 196612
  18.3 8.1 %copy-start.9 = (bf16[256,128]{1,0:T(8,128)(2,1)S(1)}, bf16[256,128]{1,0:T(8,128)(2,1)}, u32[]{:S(2)}) copy-start(bf16[256,128]{1,0:T(8,128)(2,1)} %c_hbm.3) | copy-start | bytes 196612
  18.3 8.1 %copy-start.10 = (f32[16,256]{1,0:T(8,128)S(1)}, f32[16,256]{1,0:T(8,128)}, u32[]{:S(2)}) copy-start(f32[16,256]{1,0:T(8,128)} %log_hbm.3) | copy-start | bytes 49156
  18.3 8.1 %copy-start.11 = (s32[4]{0:T(128)S(1)}, s32[4]{0:T(128)}, u32[]{:S(2)}) copy-start(s32[4]{0:T(128)} %lengths_hbm.3) | copy-start | bytes 52
  18.3 14.3 %collective-permute-start = (bf16[1024,256]{1,0:T(8,128)(2,1)}, bf16[1024,256]{1,0:T(8,128)(2,1)S(1)}, u32[]{:S(2)}, u32[]{:S(2)}) collective-permute-start(bf16[1024,256]{1,0:T(8,128)(2,1)} %shard_map.97), channel_id=1, source_target_pairs={{0,4},{1,5},{2,6},{3,7},{4,0},{5,1},{6,2},{7,3},{8,12},{9,13},{10,... | collective-permute-start | bytes 1572872 | tf_op jit(solution)/shard_map/ppermute | solution.py:404
  23.6 32.8 %collective-permute-start.1 = (bf16[2048,256]{1,0:T(8,128)(2,1)}, bf16[2048,256]{1,0:T(8,128)(2,1)S(1)}, u32[]{:S(2)}, u32[]{:S(2)}) collective-permute-start(bf16[2048,256]{1,0:T(8,128)(2,1)} %get-tuple-element.13), channel_id=1, source_target_pairs={{0,2},{1,3},{2,4},{3,5},{4,6},{5,7},{6,0},{7,1},{8,10},{9,11},{10,... | collective-permute-start | bytes 3145736 | tf_op jit(solution)/shard_map/ppermute | solution.py:404
  24.0 32.4 %collective-permute-start.2 = (bf16[2048,256]{1,0:T(8,128)(2,1)}, bf16[2048,256]{1,0:T(8,128)(2,1)S(1)}, u32[]{:S(2)}, u32[]{:S(2)}) collective-permute-start(bf16[2048,256]{1,0:T(8,128)(2,1)} %get-tuple-element.14), channel_id=1, source_target_pairs={{0,6},{1,7},{2,0},{3,1},{4,2},{5,3},{6,4},{7,5},{8,14},{9,15},{10,... | collective-permute-start | bytes 3145736 | tf_op jit(solution)/shard_map/ppermute | solution.py:404
  30.1 1.1 %copy-start.4 = (bf16[256,2560]{1,0:T(8,128)(2,1)}, bf16[256,2560]{1,0:T(8,128)(2,1)S(1)}, u32[]{:S(2)}) copy-start(bf16[256,2560]{1,0:T(8,128)(2,1)S(1)} %get-tuple-element.12.terms_ref) | copy-start | bytes 3932164
  31.1 1.0 %copy-start.6 = (f32[256,1024]{1,0:T(8,128)}, f32[256,1024]{1,0:T(8,128)S(1)}, u32[]{:S(2)}) copy-start(f32[256,1024]{1,0:T(8,128)S(1)} %get-tuple-element.10.local_ref) | copy-start | bytes 3145732
  34.0 0.8 %copy-start.1 = (bf16[32,64,128]{2,1,0:T(8,128)(2,1)}, bf16[32,64,128]{2,1,0:T(8,128)(2,1)S(1)}, u32[]{:S(2)}) copy-start(bf16[32,64,128]{2,1,0:T(8,128)(2,1)S(1)} %shard_map.98) | copy-start | bytes 1572868
  34.8 21.7 %all-to-all-start.1 = ((bf16[32,64,128]{2,1,0:T(8,128)(2,1)}), bf16[32,64,128]{2,1,0:T(8,128)(2,1)S(1)}, u32[]{:S(2)}, u32[]{:S(2)}) async-start(bf16[32,64,128]{2,1,0:T(8,128)(2,1)} %copy-done.1), calls=%async_computation.1 | async-start | bytes 1048576 | tf_op jit(solution)/shard_map/all_to_all | solution.py:485
  43.4 23.2 %collective-permute-start.6 = (bf16[512,256]{1,0:T(8,128)(2,1)}, bf16[512,256]{1,0:T(8,128)(2,1)S(1)}, u32[]{:S(2)}, u32[]{:S(2)}) collective-permute-start(bf16[512,256]{1,0:T(8,128)(2,1)} %get-tuple-element.17), channel_id=1, source_target_pairs={{0,8},{8,16},{16,24},{24,0},{32,40},{40,48},{48,56},{56,32},{64,72... | collective-permute-start | bytes 786440 | tf_op jit(solution)/shard_map/ppermute | solution.py:414
  44.6 22.0 %collective-permute-start.7 = (bf16[512,256]{1,0:T(8,128)(2,1)}, bf16[512,256]{1,0:T(8,128)(2,1)}, u32[]{:S(2)}, u32[]{:S(2)}) collective-permute-start(bf16[512,256]{1,0:T(8,128)(2,1)} %get-tuple-element.16), channel_id=1, source_target_pairs={{0,24},{8,0},{16,8},{24,16},{32,56},{40,32},{48,40},{56,48},{64,88... | collective-permute-start | bytes 786440 | tf_op jit(solution)/shard_map/ppermute | solution.py:414
  56.5 1.3 %copy-start.5 = (bf16[256,2560]{1,0:T(8,128)(2,1)S(1)}, bf16[256,2560]{1,0:T(8,128)(2,1)}, u32[]{:S(2)}) copy-start(bf16[256,2560]{1,0:T(8,128)(2,1)} %copy-done.4) | copy-start | bytes 3932164
  58.2 7.1 %copy-start.7 = (f32[256,1024]{1,0:T(8,128)S(1)}, f32[256,1024]{1,0:T(8,128)}, u32[]{:S(2)}) copy-start(f32[256,1024]{1,0:T(8,128)} %copy-done.6) | copy-start | bytes 3145732
  58.2 8.3 %collective-permute-start.3 = (bf16[256,256]{1,0:T(8,128)(2,1)S(1)}, bf16[256,256]{1,0:T(8,128)(2,1)S(1)}, u32[]{:S(2)}, u32[]{:S(2)}) collective-permute-start(bf16[256,256]{1,0:T(8,128)(2,1)S(1)} %shard_map.101.refs_0_), channel_id=1, source_target_pairs={{0,2},{1,3},{2,4},{3,5},{4,6},{5,7},{6,0},{7,1},{8,10},{9,11},{10,... | collective-permute-start | bytes 393224 | tf_op jit(solution)/shard_map/ppermute | solution.py:404
  59.6 7.0 %collective-permute-start.4 = (bf16[256,256]{1,0:T(8,128)(2,1)S(1)}, bf16[256,256]{1,0:T(8,128)(2,1)S(1)}, u32[]{:S(2)}, u32[]{:S(2)}) collective-permute-start(bf16[256,256]{1,0:T(8,128)(2,1)S(1)} %shard_map.101.refs_0_), channel_id=1, source_target_pairs={{0,4},{1,5},{2,6},{3,7},{4,0},{5,1},{6,2},{7,3},{8,12},{9,13},{10,... | collective-permute-start | bytes 393224 | tf_op jit(solution)/shard_map/ppermute | solution.py:404
  61.9 4.6 %collective-permute-start.5 = (bf16[256,256]{1,0:T(8,128)(2,1)S(1)}, bf16[256,256]{1,0:T(8,128)(2,1)S(1)}, u32[]{:S(2)}, u32[]{:S(2)}) collective-permute-start(bf16[256,256]{1,0:T(8,128)(2,1)S(1)} %shard_map.101.refs_0_), channel_id=1, source_target_pairs={{0,6},{1,7},{2,0},{3,1},{4,2},{5,3},{6,4},{7,5},{8,14},{9,15},{10,... | collective-permute-start | bytes 393224 | tf_op jit(solution)/shard_map/ppermute | solution.py:404
  65.3 1.3 %copy-start = (bf16[2048,256]{1,0:T(8,128)(2,1)S(1)}, bf16[2048,256]{1,0:T(8,128)(2,1)}, u32[]{:S(2)}) copy-start(bf16[2048,256]{1,0:T(8,128)(2,1)} %shard_map.102.refs_4_) | copy-start | bytes 3145732
  67.5 7.9 %collective-permute-start.8 = (bf16[256,1024]{1,0:T(8,128)(2,1)S(1)}, bf16[256,1024]{1,0:T(8,128)(2,1)S(1)}, u32[]{:S(2)}, u32[]{:S(2)}) collective-permute-start(bf16[256,1024]{1,0:T(8,128)(2,1)S(1)} %shard_map.104), channel_id=1, source_target_pairs={{0,1},{1,0},{2,3},{3,2},{4,5},{5,4},{6,7},{7,6},{8,9},{9,8},{10,11... | collective-permute-start | bytes 1572872 | tf_op jit(solution)/shard_map/ppermute | solution.py:516
